TPU v7x, 32 devices: a whole 2x2x4 slice. The times are simulated.
32 devices in a mesh: groups: 2 (over y), seq: 4 (over z), segment: 2 (over x), cfg: 2 (over core).
Axes of the slice: x: 2, y: 2, z: 4, core: 2. Of those that a mesh axis runs over, the one named last changes fastest.
Arguments:
- latent: float32 [2, 64, 64], P(None, ('groups', 'seq')), parts along dimension 1, may hold values from -0.1 to 0.1
- w_embed: bfloat16 [64, 3072], replicated, may hold values from -0.75 to 0.75
- w_qkv: bfloat16 [2, 9216, 3072], P('segment', 'seq'), may hold values from -0.109375 to 0.109375
- w_out: bfloat16 [2, 3072, 3072], P('segment', 'seq'), may hold values from -0.109375 to 0.109375
- mod_table: bfloat16 [50, 3, 3072], replicated, may hold values from -3 to 3
- cond_mod: float32 [2, 4, 3, 3072], P('cfg', ('groups', 'segment')), parts along dimension 1, may hold values from -3 to 3
- stale_kv: bfloat16 [2, 2, 4, 2, 64, 1536], P('segment', 'cfg', 'seq', None, 'groups'), parts along dimension 4, may hold values from -6 to 6
- w_final: bfloat16 [3072, 64], replicated, may hold values from -0.109375 to 0.109375
- w_conv: bfloat16 [27, 16, 512], P(None, None, ('segment', 'cfg')), may hold values from -0.3125 to 0.3125
- patch_order: int32 [4], P('groups'), parts along dimension 0, may hold values from 0 to 1, each once
- timestep: int32 [2], P('groups'), parts along dimension 0, may hold values from 0 to 49
- slab_rows: int32 [8], P('groups'), parts along dimension 0, may hold values from 1 to 4, 8 in all
Outputs:
- velocity: float32 [2, 64, 64], P(None, ('groups', 'seq')), parts along dimension 1
- decoded: bfloat16 [8, 4, 4, 8, 512], P(('groups', 'seq'), None, None, None, ('segment', 'cfg')), parts along dimension 0
There are 2 independent parts, one for each index of `groups`. A program takes and returns all parts, laid end to end along the dimension named above; an argument that names none is the same for every part. Nothing has to cross between parts.
Inputs may be any that keep to these rules, and one draw needn't show every extreme that they name: `patch_order`: each patch once. `slab_rows`: the rows sum to 8; some slab has exactly 4 rows.
All inputs are finite; a program needn't handle non-finite values.
Results may differ from a plain program's by a relative error of at most 0.03.
Values may be sent and summed in bfloat16 or wider, within the bound.
No kernel may reach another device: no remote copies, remote signals or barrier semaphores. Data moves between devices by JAX's collectives and lax.ppermute only.
A program may use at most 128 MiB of HBM per device.

v0:
```python
import jax
import jax.numpy as jnp
from jax import lax
from jax.sharding import PartitionSpec as P

HEADS = 24
HEAD_DIM = 128
D = 3072
LAT_CH = 16
SCHED_STEPS = 50
MICRO = 2
TOK_DEV = 8
FRAMES = 4
LAT_W = 8


guide_scale = 5.0
norm_eps = 1e-06


def swapped(value, axis, bit):
    return lax.ppermute(value, axis, [(i, i ^ 1 << bit) for i in range(lax.axis_size(axis))])


def passed_along(value, axis, by):
    size = lax.axis_size(axis)
    pairs = [(i, i + by) for i in range(size) if 0 <= i + by < size]
    return lax.ppermute(value, axis, pairs)


def rms_scaled(values):
    wide = values.astype(jnp.float32)
    return wide * lax.rsqrt(jnp.mean(wide * wide, axis=-1, keepdims=True) + norm_eps)


def cycle_join(piece, seq_index, cycle_bits):
    joined = piece
    for bit_number in range(cycle_bits):
        partner = swapped(joined, "seq", bit_number)
        upper_half = (seq_index // 2**bit_number % 2).astype(jnp.int32)
        part_rows = joined.shape[0]
        combined = jnp.zeros((2 * part_rows,) + joined.shape[1:], joined.dtype)
        combined = lax.dynamic_update_slice_in_dim(combined, joined, upper_half * part_rows, 0)
        joined = lax.dynamic_update_slice_in_dim(combined, partner, (1 - upper_half) * part_rows, 0)
    return joined


def shards(
    latent,
    w_embed,
    w_qkv,
    w_out,
    mod_table,
    cond_mod,
    stale_kv,
    w_final,
    w_conv,
    patch_order,
    timestep,
    slab_rows,
):
    seq_count = lax.axis_size("seq")
    segment_count = lax.axis_size("segment")
    seq_index = lax.axis_index("seq")
    segment_index = lax.axis_index("segment")
    branch_index = lax.axis_index("cfg")
    group_count = min(seq_count, 8)
    cycle_size = seq_count // group_count
    cycle_bits = cycle_size.bit_length() - 1
    group_heads = HEADS // group_count
    sub_rows = TOK_DEV // cycle_size
    share_rows = seq_count * sub_rows
    kv_lanes = 2 * group_heads * HEAD_DIM
    table_row = lax.dynamic_index_in_dim(mod_table, timestep[0], 0, keepdims=False).astype(
        jnp.float32
    )
    modulation = table_row + cond_mod[0, 0]
    shift_row = modulation[0]
    scale_row = modulation[1]
    gate_row = modulation[2]
    joined_weights = (
        cycle_join(w_qkv[0], seq_index, cycle_bits),
        cycle_join(w_out[0], seq_index, cycle_bits),
    )
    stale_joined = cycle_join(stale_kv[0, 0], seq_index, cycle_bits)
    cache = jnp.transpose(stale_joined, (1, 0, 2, 3)).reshape(
        MICRO, cycle_size * share_rows, kv_lanes
    )
    received = jnp.zeros((TOK_DEV, D), jnp.bfloat16)
    finished = jnp.zeros((MICRO, TOK_DEV, D), jnp.bfloat16)
    slot_ids = jnp.arange(MICRO)
    tick_count = MICRO + segment_count - 1
    for tick_index in range(tick_count):
        qkv_rows, out_rows = joined_weights
        micro_index = tick_index - segment_index
        active = (micro_index >= 0) & (micro_index < MICRO)
        clipped = jnp.clip(micro_index, 0, MICRO - 1)
        patch_id = jnp.sum(jnp.where(slot_ids == clipped, patch_order, 0))
        own_latent = lax.dynamic_index_in_dim(latent, patch_id, 0, keepdims=False).astype(
            jnp.bfloat16
        )
        embedded = jnp.dot(own_latent, w_embed, preferred_element_type=jnp.float32).astype(
            jnp.bfloat16
        )
        layer_input = jnp.where(segment_index == 0, embedded, received)
        normed = (rms_scaled(layer_input) * (1.0 + scale_row) + shift_row).astype(jnp.bfloat16)
        outgoing = jnp.broadcast_to(
            normed.reshape(1, cycle_size, sub_rows, D), (group_count, cycle_size, sub_rows, D)
        )
        shared = lax.all_to_all(
            outgoing.reshape(share_rows, D), "seq", split_axis=0, concat_axis=0, tiled=True
        )
        projected = lax.dot_general(
            shared, qkv_rows, (((1,), (1,)), ((), ())), preferred_element_type=jnp.float32
        )
        projected = projected.astype(jnp.bfloat16).reshape(share_rows, group_heads, 3, HEAD_DIM)
        queries = projected[:, :, 0]
        fresh_local = jnp.transpose(projected[:, :, 1:], (0, 2, 1, 3)).reshape(
            1, share_rows, kv_lanes
        )
        fresh = cycle_join(fresh_local, seq_index, cycle_bits).reshape(
            cycle_size * share_rows, kv_lanes
        )
        previous = lax.dynamic_index_in_dim(cache, patch_id, 0, keepdims=False)
        cache = lax.dynamic_update_index_in_dim(
            cache, jnp.where(active, fresh, previous), patch_id, 0
        )
        keyvals = cache.reshape(MICRO * cycle_size * share_rows, 2, group_heads, HEAD_DIM)
        scores = jnp.einsum(
            "shd,khd->hsk", queries, keyvals[:, 0], preferred_element_type=jnp.float32
        ) * HEAD_DIM ** (-0.5)
        probs = jax.nn.softmax(scores, axis=-1).astype(jnp.bfloat16)
        attended = jnp.einsum(
            "hsk,khd->shd", probs, keyvals[:, 1], preferred_element_type=jnp.float32
        ).astype(jnp.bfloat16)
        partial_out = jnp.dot(
            attended.reshape(share_rows, group_heads * HEAD_DIM),
            out_rows,
            preferred_element_type=jnp.float32,
        )
        returned = lax.all_to_all(
            partial_out.astype(jnp.bfloat16), "seq", split_axis=0, concat_axis=0, tiled=True
        ).astype(partial_out.dtype)
        mixed = jnp.sum(returned.reshape(group_count, cycle_size, sub_rows, D), axis=0).reshape(
            TOK_DEV, D
        )
        layer_output = (layer_input.astype(jnp.float32) + gate_row * mixed).astype(jnp.bfloat16)
        keep_final = active & (segment_index == segment_count - 1)
        earlier = lax.dynamic_index_in_dim(finished, patch_id, 0, keepdims=False)
        finished = lax.dynamic_update_index_in_dim(
            finished, jnp.where(keep_final, layer_output, earlier), patch_id, 0
        )
        if tick_index + 1 < tick_count:
            received = passed_along(layer_output, "segment", 1)
    final_normed = rms_scaled(finished).astype(jnp.bfloat16)
    predicted = jnp.einsum("mtd,dc->mtc", final_normed, w_final, preferred_element_type=jnp.float32)
    is_last = segment_index == segment_count - 1
    branch_weight = jnp.where(branch_index == 0, 1.0 - guide_scale, guide_scale)
    velocity_term = jnp.where(is_last, branch_weight * predicted, 0.0)
    latent_term = jnp.where(is_last & (branch_index == 0), latent, 0.0)
    velocity_own, latent_own = lax.psum((velocity_term, latent_term), ("segment", "cfg"))
    velocity_full, latent_full = (
        lax.all_gather(velocity_own, "seq", axis=1, tiled=True),
        lax.all_gather(latent_own, "seq", axis=1, tiled=True),
    )
    stepped = latent_full - velocity_full / SCHED_STEPS
    token_rows = MICRO * seq_count * TOK_DEV // (FRAMES * (LAT_W // 2))
    image_rows = 2 * token_rows
    slab_most = 2 * image_rows // seq_count
    image = stepped.reshape(FRAMES, token_rows, LAT_W // 2, 2, 2, LAT_CH)
    image = (
        jnp.transpose(image, (0, 1, 3, 2, 4, 5))
        .reshape(FRAMES, image_rows, LAT_W, LAT_CH)
        .astype(jnp.bfloat16)
    )
    padded = jnp.concatenate([image[:1], image[:1], image], 0)
    padded = jnp.pad(padded, ((0, 0), (1, 1 + slab_most), (1, 1), (0, 0)))
    positions = jnp.arange(seq_count)
    slab_count = jnp.sum(jnp.where(positions == seq_index, slab_rows, 0))
    slab_start = jnp.sum(jnp.where(positions < seq_index, slab_rows, 0))
    window = lax.dynamic_slice_in_dim(padded, slab_start, slab_most + 2, 1)
    pieces = []
    for frame_shift in range(3):
        for row_shift in range(3):
            for col_shift in range(3):
                pieces.append(
                    window[
                        frame_shift : frame_shift + FRAMES,
                        row_shift : row_shift + slab_most,
                        col_shift : col_shift + LAT_W,
                    ]
                )
    columns = jnp.concatenate(pieces, -1).reshape(FRAMES * slab_most * LAT_W, 27 * LAT_CH)
    kernel = w_conv.reshape(27 * LAT_CH, w_conv.shape[2])
    features = jnp.dot(columns, kernel, preferred_element_type=jnp.float32).astype(jnp.bfloat16)
    features = features.reshape(FRAMES, slab_most, LAT_W, w_conv.shape[2])
    row_valid = jnp.arange(slab_most)[None, :, None, None] < slab_count
    decoded = jnp.where(row_valid, features, jnp.zeros_like(features))
    return (velocity_own, decoded[None])


def solution(mesh):
    in_specs = (
        P(None, ("groups", "seq"), None),
        P(),
        P("segment", "seq", None),
        P("segment", "seq", None),
        P(),
        P("cfg", ("groups", "segment"), None, None),
        P("segment", "cfg", "seq", None, "groups", None),
        P(),
        P(None, None, ("segment", "cfg")),
        P("groups"),
        P("groups"),
        P("groups"),
    )
    out_specs = (
        P(None, ("groups", "seq"), None),
        P(("groups", "seq"), None, None, None, ("segment", "cfg")),
    )
    return jax.shard_map(shards, mesh=mesh, in_specs=in_specs, out_specs=out_specs, check_vma=False)
```

profile of v0, /device:TPU:0, one launch (start us, length us, event | category | flops | bytes accessed | tf_op | source)
XLA Modules:
  0.0 166.7 jit_solution(4546387687725415421)
XLA Ops:
  0.7 1.5 fusion.111
  7.8 6.3 %all-to-all-start = ((bf16[4,8,3072]{2,1,0:T(8,128)(2,1)}), bf16[4,8,3072]{2,1,0:T(8,128)(2,1)S(1)}, u32[]{:S(2)}, u32[]{:S(2)}) async-start(bf16[4,8,3072]{2,1,0:T(8,128)(2,1)} %all_to_all.42), calls=%async_computation | async-start | bytes 393216 | tf_op jit(solution)/shard_map/all_to_all | solution.py:110
  15.1 6.6 %all-to-all-done = bf16[4,8,3072]{2,1,0:T(8,128)(2,1)S(1)} async-done(((bf16[4,8,3072]{2,1,0:T(8,128)(2,1)}), bf16[4,8,3072]{2,1,0:T(8,128)(2,1)S(1)}, u32[]{:S(2)}, u32[]{:S(2)}) %all-to-all-start) | async-done | bytes 196640 | tf_op jit(solution)/shard_map/all_to_all | solution.py:110
  21.7 9.2 %fusion.24 = bf16[32,2304]{1,0:T(8,128)(2,1)S(1)} fusion(bf16[1,2304,3072]{2,1,0:T(8,128)(2,1)} %param.14, bf16[4,8,3072]{2,1,0:T(8,128)(2,1)S(1)} %all-to-all-done), kind=kOutput, calls=%fused_computation.18 | convolution fusion | flops 453058560 | bytes 14499840 | tf_op jit(solution)/shard_map/dot_general | solution.py:113
  32.4 3.9 %fusion.39 = bf16[4,8,3072]{2,1,0:T(8,128)(2,1)} fusion(bf16[1,768,3072]{2,1,0:T(8,128)(2,1)} %param.15, bf16[6,4,8,128]{3,2,1,0:T(8,128)(2,1)S(1)} %fusion.52), kind=kOutput, calls=%fused_computation.23 | convolution fusion | flops 151093248 | bytes 4964352 | tf_op jit(solution)/shard_map/dot_general | solution.py:136
  36.3 3.5 %all-to-all-start.1 = ((bf16[4,8,3072]{2,1,0:T(8,128)(2,1)}), bf16[4,8,3072]{2,1,0:T(8,128)(2,1)S(1)}, u32[]{:S(2)}, u32[]{:S(2)}) async-start(bf16[4,8,3072]{2,1,0:T(8,128)(2,1)} %fusion.39), calls=%async_computation.1 | async-start | bytes 393216 | tf_op jit(solution)/shard_map/all_to_all | solution.py:141
  39.9 6.2 %all-to-all-done.1 = bf16[4,8,3072]{2,1,0:T(8,128)(2,1)S(1)} async-done(((bf16[4,8,3072]{2,1,0:T(8,128)(2,1)}), bf16[4,8,3072]{2,1,0:T(8,128)(2,1)S(1)}, u32[]{:S(2)}, u32[]{:S(2)}) %all-to-all-start.1) | async-done | bytes 196640 | tf_op jit(solution)/shard_map/all_to_all | solution.py:141
  46.1 3.4 %collective-permute-start = (bf16[8,3072]{1,0:T(8,128)(2,1)S(1)}, bf16[8,3072]{1,0:T(8,128)(2,1)S(1)}, u32[]{:S(2)}, u32[]{:S(2)}) collective-permute-start(bf16[8,3072]{1,0:T(8,128)(2,1)S(1)} %get-tuple-element.14), channel_id=1, source_target_pairs={{0,2},{1,3},{4,6},{5,7},{8,10},{9,11},{12,14},{13,15},{16,18},{17,... | collective-permute-start | bytes 147464 | tf_op jit(solution)/shard_map/ppermute | solution.py:28
  52.5 3.4 %all-to-all-start.2 = ((bf16[4,8,3072]{2,1,0:T(8,128)(2,1)}), bf16[4,8,3072]{2,1,0:T(8,128)(2,1)S(1)}, u32[]{:S(2)}, u32[]{:S(2)}) async-start(bf16[4,8,3072]{2,1,0:T(8,128)(2,1)} %all_to_all.47), calls=%async_computation.2 | async-start | bytes 393216 | tf_op jit(solution)/shard_map/all_to_all | solution.py:110
  58.1 4.0 %all-to-all-done.2 = bf16[4,8,3072]{2,1,0:T(8,128)(2,1)S(1)} async-done(((bf16[4,8,3072]{2,1,0:T(8,128)(2,1)}), bf16[4,8,3072]{2,1,0:T(8,128)(2,1)S(1)}, u32[]{:S(2)}, u32[]{:S(2)}) %all-to-all-start.2) | async-done | bytes 196640 | tf_op jit(solution)/shard_map/all_to_all | solution.py:110
  62.1 9.2 %fusion.27 = bf16[32,2304]{1,0:T(8,128)(2,1)S(1)} fusion(bf16[1,2304,3072]{2,1,0:T(8,128)(2,1)} %param.14, bf16[4,8,3072]{2,1,0:T(8,128)(2,1)S(1)} %all-to-all-done.2), kind=kOutput, calls=%fused_computation.19 | convolution fusion | flops 453058560 | bytes 14499840 | tf_op jit(solution)/shard_map/dot_general | solution.py:113
  72.8 3.9 %fusion.36 = bf16[4,8,3072]{2,1,0:T(8,128)(2,1)} fusion(bf16[1,768,3072]{2,1,0:T(8,128)(2,1)} %param.15, bf16[6,4,8,128]{3,2,1,0:T(8,128)(2,1)S(1)} %fusion.53), kind=kOutput, calls=%fused_computation.22 | convolution fusion | flops 151093248 | bytes 4964352 | tf_op jit(solution)/shard_map/dot_general | solution.py:136
  76.8 3.5 %all-to-all-start.3 = ((bf16[4,8,3072]{2,1,0:T(8,128)(2,1)}), bf16[4,8,3072]{2,1,0:T(8,128)(2,1)S(1)}, u32[]{:S(2)}, u32[]{:S(2)}) async-start(bf16[4,8,3072]{2,1,0:T(8,128)(2,1)} %fusion.36), calls=%async_computation.3 | async-start | bytes 393216 | tf_op jit(solution)/shard_map/all_to_all | solution.py:141
  80.3 6.2 %all-to-all-done.3 = bf16[4,8,3072]{2,1,0:T(8,128)(2,1)S(1)} async-done(((bf16[4,8,3072]{2,1,0:T(8,128)(2,1)}), bf16[4,8,3072]{2,1,0:T(8,128)(2,1)S(1)}, u32[]{:S(2)}, u32[]{:S(2)}) %all-to-all-start.3) | async-done | bytes 196640 | tf_op jit(solution)/shard_map/all_to_all | solution.py:141
  86.6 4.1 %collective-permute-start.1 = (bf16[8,3072]{1,0:T(8,128)(2,1)S(1)}, bf16[8,3072]{1,0:T(8,128)(2,1)S(1)}, u32[]{:S(2)}, u32[]{:S(2)}) collective-permute-start(bf16[8,3072]{1,0:T(8,128)(2,1)S(1)} %get-tuple-element.12), channel_id=1, source_target_pairs={{0,2},{1,3},{4,6},{5,7},{8,10},{9,11},{12,14},{13,15},{16,18},{17,... | collective-permute-start | bytes 147464 | tf_op jit(solution)/shard_map/ppermute | solution.py:28
  94.2 3.5 %all-to-all-start.4 = ((bf16[4,8,3072]{2,1,0:T(8,128)(2,1)}), bf16[4,8,3072]{2,1,0:T(8,128)(2,1)S(1)}, u32[]{:S(2)}, u32[]{:S(2)}) async-start(bf16[4,8,3072]{2,1,0:T(8,128)(2,1)} %all_to_all.52), calls=%async_computation.4 | async-start | bytes 393216 | tf_op jit(solution)/shard_map/all_to_all | solution.py:110
  98.5 5.3 %all-to-all-done.4 = bf16[4,8,3072]{2,1,0:T(8,128)(2,1)S(1)} async-done(((bf16[4,8,3072]{2,1,0:T(8,128)(2,1)}), bf16[4,8,3072]{2,1,0:T(8,128)(2,1)S(1)}, u32[]{:S(2)}, u32[]{:S(2)}) %all-to-all-start.4) | async-done | bytes 196640 | tf_op jit(solution)/shard_map/all_to_all | solution.py:110
  103.8 9.2 %fusion.30 = bf16[32,2304]{1,0:T(8,128)(2,1)S(1)} fusion(bf16[1,2304,3072]{2,1,0:T(8,128)(2,1)} %param.14, bf16[4,8,3072]{2,1,0:T(8,128)(2,1)S(1)} %all-to-all-done.4), kind=kOutput, calls=%fused_computation.20 | convolution fusion | flops 453058560 | bytes 14499840 | tf_op jit(solution)/shard_map/dot_general | solution.py:113
  114.5 3.9 %fusion.33 = bf16[4,8,3072]{2,1,0:T(8,128)(2,1)} fusion(bf16[1,768,3072]{2,1,0:T(8,128)(2,1)} %param.15, bf16[6,4,8,128]{3,2,1,0:T(8,128)(2,1)S(1)} %fusion.54), kind=kOutput, calls=%fused_computation.21 | convolution fusion | flops 151093248 | bytes 4964352 | tf_op jit(solution)/shard_map/dot_general | solution.py:136
  118.5 3.4 %all-to-all-start.5 = ((bf16[4,8,3072]{2,1,0:T(8,128)(2,1)}), bf16[4,8,3072]{2,1,0:T(8,128)(2,1)S(1)}, u32[]{:S(2)}, u32[]{:S(2)}) async-start(bf16[4,8,3072]{2,1,0:T(8,128)(2,1)} %fusion.33), calls=%async_computation.5 | async-start | bytes 393216 | tf_op jit(solution)/shard_map/all_to_all | solution.py:141
  121.8 6.2 %all-to-all-done.5 = bf16[4,8,3072]{2,1,0:T(8,128)(2,1)S(1)} async-done(((bf16[4,8,3072]{2,1,0:T(8,128)(2,1)}), bf16[4,8,3072]{2,1,0:T(8,128)(2,1)S(1)}, u32[]{:S(2)}, u32[]{:S(2)}) %all-to-all-start.5) | async-done | bytes 196640 | tf_op jit(solution)/shard_map/all_to_all | solution.py:141
  128.5 10.2 %all-reduce.1 = (f32[2,8,64]{2,1,0:T(8,128)S(1)}, f32[2,8,64]{2,1,0:T(8,128)S(1)}) all-reduce(f32[2,8,64]{2,1,0:T(8,128)S(1)} %fusion.55, f32[2,8,64]{2,1,0:T(8,128)S(1)} %broadcast_select_fusion.2), channel_id=1, replica_groups=mesh['groups'=2,'seq'=4,'segment'=2,'cfg'=2] {'segment','cfg'}, use_global_device_ids=true, to_apply=%region_16.17 | all-reduce | flops 2048 | bytes 16384 | tf_op jit(solution)/shard_map/psum | solution.py:161
  138.6 13.1 %all_gather.6 = f32[2,32,64]{2,1,0:T(8,128)S(1)} all-gather(f32[2,8,64]{2,1,0:T(8,128)S(1)} %get-tuple-element.8), channel_id=1, replica_groups=mesh['groups'=2,'seq'=4,'segment'=2,'cfg'=2] {'seq'}, dimensions={1}, use_global_device_ids=true | all-gather | bytes 20480 | tf_op jit(solution)/shard_map/all_gather | solution.py:164
  151.8 13.1 %all_gather.7 = f32[2,32,64]{2,1,0:T(8,128)S(1)} all-gather(f32[2,8,64]{2,1,0:T(8,128)S(1)} %get-tuple-element.7), channel_id=1, replica_groups=mesh['groups'=2,'seq'=4,'segment'=2,'cfg'=2] {'seq'}, dimensions={1}, use_global_device_ids=true | all-gather | bytes 20480 | tf_op jit(solution)/shard_map/all_gather | solution.py:163
  (94 shorter events, 14.1 us)
Async XLA Ops:
  0.6 5.5 %copy-start = (bf16[50,3,3072]{2,0,1:T(8,128)(2,1)S(1)}, bf16[50,3,3072]{2,0,1:T(8,128)(2,1)}, u32[]{:S(2)}) copy-start(bf16[50,3,3072]{2,0,1:T(8,128)(2,1)} %param.16) | copy-start | bytes 2764804
  0.6 50.8 %copy-start.5 = (f32[2,8,64]{2,1,0:T(8,128)S(1)}, f32[2,8,64]{2,1,0:T(8,128)}, u32[]{:S(2)}) copy-start(f32[2,8,64]{2,1,0:T(8,128)} %param.12) | copy-start | bytes 12292
  0.7 50.8 %copy-start.1 = (bf16[64,3072]{1,0:T(8,128)(2,1)S(1)}, bf16[64,3072]{1,0:T(8,128)(2,1)}, u32[]{:S(2)}) copy-start(bf16[64,3072]{1,0:T(8,128)(2,1)} %param.13) | copy-start | bytes 1179652
  0.7 30.7 %copy-start.2 = (bf16[1,1,1,2,32,1536]{5,4,3,2,1,0:T(8,128)(2,1)S(1)}, bf16[1,1,1,2,32,1536]{5,4,3,2,1,0:T(8,128)(2,1)}, u32[]{:S(2)}) copy-start(bf16[1,1,1,2,32,1536]{5,4,3,2,1,0:T(8,128)(2,1)} %param.18) | copy-start | bytes 589828
  7.8 13.8 %all-to-all-start = ((bf16[4,8,3072]{2,1,0:T(8,128)(2,1)}), bf16[4,8,3072]{2,1,0:T(8,128)(2,1)S(1)}, u32[]{:S(2)}, u32[]{:S(2)}) async-start(bf16[4,8,3072]{2,1,0:T(8,128)(2,1)} %all_to_all.42), calls=%async_computation | async-start | bytes 393216 | tf_op jit(solution)/shard_map/all_to_all | solution.py:110
  36.3 54.3 %copy-start.7 = (s32[4]{0:T(128)S(1)}, s32[4]{0:T(128)}, u32[]{:S(2)}) copy-start(s32[4]{0:T(128)} %param.23) | copy-start | bytes 52
  36.3 9.7 %all-to-all-start.1 = ((bf16[4,8,3072]{2,1,0:T(8,128)(2,1)}), bf16[4,8,3072]{2,1,0:T(8,128)(2,1)S(1)}, u32[]{:S(2)}, u32[]{:S(2)}) async-start(bf16[4,8,3072]{2,1,0:T(8,128)(2,1)} %fusion.39), calls=%async_computation.1 | async-start | bytes 393216 | tf_op jit(solution)/shard_map/all_to_all | solution.py:141
  46.1 5.3 %collective-permute-start = (bf16[8,3072]{1,0:T(8,128)(2,1)S(1)}, bf16[8,3072]{1,0:T(8,128)(2,1)S(1)}, u32[]{:S(2)}, u32[]{:S(2)}) collective-permute-start(bf16[8,3072]{1,0:T(8,128)(2,1)S(1)} %get-tuple-element.14), channel_id=1, source_target_pairs={{0,2},{1,3},{4,6},{5,7},{8,10},{9,11},{12,14},{13,15},{16,18},{17,... | collective-permute-start | bytes 147464 | tf_op jit(solution)/shard_map/ppermute | solution.py:28
  52.5 9.6 %all-to-all-start.2 = ((bf16[4,8,3072]{2,1,0:T(8,128)(2,1)}), bf16[4,8,3072]{2,1,0:T(8,128)(2,1)S(1)}, u32[]{:S(2)}, u32[]{:S(2)}) async-start(bf16[4,8,3072]{2,1,0:T(8,128)(2,1)} %all_to_all.47), calls=%async_computation.2 | async-start | bytes 393216 | tf_op jit(solution)/shard_map/all_to_all | solution.py:110
  76.8 51.4 %copy-start.3 = (bf16[3072,64]{0,1:T(8,128)(2,1)S(1)}, bf16[3072,64]{0,1:T(8,128)(2,1)}, u32[]{:S(2)}) copy-start(bf16[3072,64]{0,1:T(8,128)(2,1)} %param.19) | copy-start | bytes 1179652
  76.8 9.7 %all-to-all-start.3 = ((bf16[4,8,3072]{2,1,0:T(8,128)(2,1)}), bf16[4,8,3072]{2,1,0:T(8,128)(2,1)S(1)}, u32[]{:S(2)}, u32[]{:S(2)}) async-start(bf16[4,8,3072]{2,1,0:T(8,128)(2,1)} %fusion.36), calls=%async_computation.3 | async-start | bytes 393216 | tf_op jit(solution)/shard_map/all_to_all | solution.py:141
  86.6 6.7 %collective-permute-start.1 = (bf16[8,3072]{1,0:T(8,128)(2,1)S(1)}, bf16[8,3072]{1,0:T(8,128)(2,1)S(1)}, u32[]{:S(2)}, u32[]{:S(2)}) collective-permute-start(bf16[8,3072]{1,0:T(8,128)(2,1)S(1)} %get-tuple-element.12), channel_id=1, source_target_pairs={{0,2},{1,3},{4,6},{5,7},{8,10},{9,11},{12,14},{13,15},{16,18},{17,... | collective-permute-start | bytes 147464 | tf_op jit(solution)/shard_map/ppermute | solution.py:28
  94.2 9.6 %all-to-all-start.4 = ((bf16[4,8,3072]{2,1,0:T(8,128)(2,1)}), bf16[4,8,3072]{2,1,0:T(8,128)(2,1)S(1)}, u32[]{:S(2)}, u32[]{:S(2)}) async-start(bf16[4,8,3072]{2,1,0:T(8,128)(2,1)} %all_to_all.52), calls=%async_computation.4 | async-start | bytes 393216 | tf_op jit(solution)/shard_map/all_to_all | solution.py:110
  97.7 68.0 %copy-start.4 = (bf16[27,16,128]{2,1,0:T(8,128)(2,1)S(1)}, bf16[27,16,128]{2,1,0:T(8,128)(2,1)}, u32[]{:S(2)}) copy-start(bf16[27,16,128]{2,1,0:T(8,128)(2,1)} %param.20) | copy-start | bytes 331780
  118.5 9.6 %all-to-all-start.5 = ((bf16[4,8,3072]{2,1,0:T(8,128)(2,1)}), bf16[4,8,3072]{2,1,0:T(8,128)(2,1)S(1)}, u32[]{:S(2)}, u32[]{:S(2)}) async-start(bf16[4,8,3072]{2,1,0:T(8,128)(2,1)} %fusion.33), calls=%async_computation.5 | async-start | bytes 393216 | tf_op jit(solution)/shard_map/all_to_all | solution.py:141
  138.6 28.0 %copy-start.6 = (f32[2,8,64]{2,1,0:T(8,128)}, f32[2,8,64]{2,1,0:T(8,128)S(1)}, u32[]{:S(2)}) copy-start(f32[2,8,64]{2,1,0:T(8,128)S(1)} %get-tuple-element.7) | copy-start | bytes 12292
where the time goes:
time: 168 us; the launch traced here: 167 us
  matrix products  43.2 us (26%)
  blocking collectives  36.4 us (22%)
  waiting for transfers between devices  34.5 us (21%)
  starting transfers between devices  31.1 us (19%)
  between operations  9.58 us (6%)
  other arithmetic  6.12 us (4%)
  local copies, waits for them, and re-layouts  5.78 us (3%)
    dot_general x3, matrix products, shards(): lax.dot_general(shared, qkv_rows, (((1,), (1,)), ((), ())), preferred_ele...  27.7 us
    all_to_all x3, waiting for transfers between devices, shards(): lax.all_to_all(partial_out.astype(jnp.bfloat16), 'seq', split_axis=0, con...  18.6 us
    all_to_all x3, waiting for transfers between devices, shards(): lax.all_to_all(outgoing.reshape(share_rows, D), 'seq', split_axis=0, conc...  15.9 us
    all_to_all x3, starting transfers between devices, shards(): lax.all_to_all(outgoing.reshape(share_rows, D), 'seq', split_axis=0, conc...  13.2 us
    all_gather x1, blocking collectives, shards(): lax.all_gather(velocity_own, 'seq', axis=1, tiled=True)  13.1 us
    all_gather x1, blocking collectives, shards(): lax.all_gather(latent_own, 'seq', axis=1, tiled=True)  13.1 us
    dot_general x3, matrix products, shards(): jnp.dot(attended.reshape(share_rows, group_heads * HEAD_DIM), out_rows, p...  11.8 us
    all_to_all x3, starting transfers between devices, shards(): lax.all_to_all(partial_out.astype(jnp.bfloat16), 'seq', split_axis=0, con...  10.4 us
  transfers between devices with their start and end apart: 8, of which 6 were waited for; matrix products, arithmetic and copies ran while one was open for 2% of the time, Pallas kernels for 0%

commit v1 on v0

--- a/solution.py
+++ b/solution.py
@@ -1,6 +1,8 @@
 import jax
 import jax.numpy as jnp
 from jax import lax
+from jax.experimental import pallas as pl
+from jax.experimental.pallas import tpu as pltpu
 from jax.sharding import PartitionSpec as P
 
 HEADS = 24
@@ -45,7 +47,7 @@
     return joined
 
 
-def shards(
+def cycled_shards(
     latent,
     w_embed,
     w_qkv,
@@ -163,7 +165,203 @@
         lax.all_gather(velocity_own, "seq", axis=1, tiled=True),
         lax.all_gather(latent_own, "seq", axis=1, tiled=True),
     )
-    stepped = latent_full - velocity_full / SCHED_STEPS
+    stepped = (latent_full - velocity_full / SCHED_STEPS).astype(jnp.bfloat16)
+    decoded = decoder_input(stepped, w_conv, slab_rows, seq_index, seq_count)
+    return (velocity_own, decoded)
+
+
+def nt_kernel(lhs_ref, weight_ref, out_ref):
+    out_ref[...] = lax.dot_general(
+        lhs_ref[...],
+        weight_ref[...],
+        (((1,), (1,)), ((), ())),
+        preferred_element_type=jnp.float32,
+    )
+
+
+def nt_dot(lhs, weight, tile):
+    rows, depth = lhs.shape
+    columns = weight.shape[0]
+    return pl.pallas_call(
+        nt_kernel,
+        grid=(columns // tile,),
+        in_specs=[
+            pl.BlockSpec((rows, depth), lambda i: (0, 0)),
+            pl.BlockSpec((tile, depth), lambda i: (i, 0)),
+        ],
+        out_specs=pl.BlockSpec((rows, tile), lambda i: (0, i)),
+        out_shape=jax.ShapeDtypeStruct((rows, columns), jnp.float32),
+        cost_estimate=pl.CostEstimate(
+            flops=2 * rows * depth * columns,
+            bytes_accessed=2 * depth * columns,
+            transcendentals=0,
+        ),
+        compiler_params=pltpu.CompilerParams(vmem_limit_bytes=32 * 2**20),
+    )(lhs, weight)
+
+
+def exchanged(value_for, axis, pairs_for, count):
+    return [lax.ppermute(value_for(k), axis, pairs_for(k)) for k in range(count)]
+
+
+def shards(
+    latent,
+    w_embed,
+    w_qkv,
+    w_out,
+    mod_table,
+    cond_mod,
+    stale_kv,
+    w_final,
+    w_conv,
+    patch_order,
+    timestep,
+    slab_rows,
+):
+    seq_count = lax.axis_size("seq")
+    segment_count = lax.axis_size("segment")
+    seq_index = lax.axis_index("seq")
+    segment_index = lax.axis_index("segment")
+    branch_index = lax.axis_index("cfg")
+    group_heads = HEADS // seq_count
+    lanes = group_heads * HEAD_DIM
+    rows_dev = MICRO * TOK_DEV
+    rows = seq_count * rows_dev
+    patch_rows = seq_count * TOK_DEV
+    table_row = lax.dynamic_index_in_dim(mod_table, timestep[0], 0, keepdims=False).astype(
+        jnp.float32
+    )
+    modulation = table_row + cond_mod[0, 0]
+    shift_row = modulation[0]
+    scale_row = 1.0 + modulation[1]
+    gate_row = modulation[2]
+    flipped = patch_order[0] == 1
+
+    def micro_ordered(value):
+        return jnp.where(flipped, value[::-1], value)
+
+    def within(k):
+        return [(i, i ^ k) for i in range(seq_count)]
+
+    def seq_ordered(pieces):
+        stacked = jnp.stack(pieces)
+        return jnp.take(stacked, jnp.arange(seq_count) ^ seq_index, axis=0)
+
+    own_latent = micro_ordered(latent).astype(jnp.bfloat16).reshape(rows_dev, -1)
+    latents = seq_ordered(
+        [own_latent]
+        + [lax.ppermute(own_latent, "seq", within(k)) for k in range(1, seq_count)]
+    ).reshape(rows, -1)
+
+    spare = 16 - 1
+    embed_rows = w_embed.shape[0]
+    scaled_embed = (w_embed.astype(jnp.float32) * scale_row).astype(jnp.bfloat16)
+    lhs = jnp.concatenate(
+        [scaled_embed, shift_row[None].astype(jnp.bfloat16), jnp.zeros((spare, D), jnp.bfloat16)]
+    )
+    head_embed = nt_dot(lhs, w_qkv[0], 256)
+    shift_term = head_embed[embed_rows : embed_rows + 1]
+
+    embedded = jnp.dot(latents, w_embed, preferred_element_type=jnp.float32).astype(jnp.bfloat16)
+    wide = embedded.astype(jnp.float32)
+    norm = lax.rsqrt(jnp.mean(wide * wide, axis=-1, keepdims=True) + norm_eps)
+    projected = (
+        norm
+        * jnp.dot(
+            latents,
+            head_embed[:embed_rows].astype(jnp.bfloat16),
+            preferred_element_type=jnp.float32,
+        )
+        + shift_term
+    ).astype(jnp.bfloat16)
+
+    stale = jnp.where(flipped, stale_kv[0, 0, 0, 0], stale_kv[0, 0, 0, 1])
+    stale = stale.reshape(patch_rows, 2, group_heads, HEAD_DIM)
+    row_micro = jnp.arange(rows) // TOK_DEV % MICRO
+    fresh_seen = row_micro[:, None] >= row_micro[None, :]
+    stale_seen = jnp.broadcast_to(row_micro[:, None] == 0, (rows, patch_rows))
+    seen = jnp.concatenate([fresh_seen, stale_seen], axis=1)
+
+    def attention(projected):
+        heads = projected.reshape(rows, group_heads, 3, HEAD_DIM)
+        keys = jnp.concatenate([heads[:, :, 1], stale[:, 0]], axis=0)
+        values = jnp.concatenate([heads[:, :, 2], stale[:, 1]], axis=0)
+        scores = jnp.einsum(
+            "shd,khd->hsk", heads[:, :, 0], keys, preferred_element_type=jnp.float32
+        ) * HEAD_DIM ** (-0.5)
+        scores = jnp.where(seen[None], scores, -jnp.inf)
+        probs = jax.nn.softmax(scores, axis=-1).astype(jnp.bfloat16)
+        attended = jnp.einsum(
+            "hsk,khd->shd", probs, values, preferred_element_type=jnp.float32
+        ).astype(jnp.bfloat16)
+        return attended.reshape(rows, lanes)
+
+    columns = D // seq_count
+    hidden = embedded
+    for step in range(segment_count):
+        partial_out = jnp.dot(
+            attention(projected), w_out[0], preferred_element_type=jnp.float32
+        ).astype(jnp.bfloat16)
+        if step + 1 == segment_count:
+            break
+
+        def column_block(value, place):
+            return lax.dynamic_slice_in_dim(value, place * columns, columns, value.ndim - 1)
+
+        mixed = column_block(partial_out, seq_index).astype(jnp.float32)
+        for k in range(1, seq_count):
+            mixed = mixed + lax.ppermute(
+                column_block(partial_out, seq_index ^ k), "seq", within(k)
+            ).astype(jnp.float32)
+        block = (
+            column_block(hidden, seq_index).astype(jnp.float32)
+            + column_block(gate_row, seq_index) * mixed
+        ).astype(jnp.bfloat16)
+        pieces = []
+        for k in range(seq_count):
+            pairs = [
+                (i * segment_count + step, (i ^ k) * segment_count + step + 1)
+                for i in range(seq_count)
+            ]
+            pieces.append(lax.ppermute(block, ("seq", "segment"), pairs))
+        hidden = jnp.transpose(seq_ordered(pieces), (1, 0, 2)).reshape(rows, D)
+        wide = hidden.astype(jnp.float32)
+        norm = lax.rsqrt(jnp.mean(wide * wide, axis=-1, keepdims=True) + norm_eps)
+        scaled = (wide * scale_row).astype(jnp.bfloat16)
+        projected = (norm * nt_dot(scaled, w_qkv[0], 256) + shift_term).astype(jnp.bfloat16)
+
+    def row_block(value, place):
+        return lax.dynamic_slice_in_dim(value, place * rows_dev, rows_dev, 0)
+
+    mixed = row_block(partial_out, seq_index).astype(jnp.float32)
+    for k in range(1, seq_count):
+        mixed = mixed + lax.ppermute(
+            row_block(partial_out, seq_index ^ k), "seq", within(k)
+        ).astype(jnp.float32)
+    final = (row_block(hidden, seq_index).astype(jnp.float32) + gate_row * mixed).astype(
+        jnp.bfloat16
+    )
+    predicted = jnp.dot(
+        rms_scaled(final).astype(jnp.bfloat16), w_final, preferred_element_type=jnp.float32
+    )
+    term = jnp.where(branch_index == 0, 1.0 - guide_scale, guide_scale) * predicted
+    velocity_own = term + swapped(term, "cfg", 0)
+    hop = [(segment_count - 1, i) for i in range(segment_count - 1)]
+    for pair in hop:
+        moved = lax.ppermute(velocity_own, "segment", [pair])
+        velocity_own = jnp.where(segment_index == pair[1], moved, velocity_own)
+    velocity_own = micro_ordered(velocity_own.reshape(MICRO, TOK_DEV, -1))
+    stepped_own = (latent - velocity_own / SCHED_STEPS).astype(jnp.bfloat16)
+    stepped = seq_ordered(
+        [stepped_own]
+        + [lax.ppermute(stepped_own, "seq", within(k)) for k in range(1, seq_count)]
+    )
+    stepped = jnp.transpose(stepped, (1, 0, 2, 3))
+    decoded = decoder_input(stepped, w_conv, slab_rows, seq_index, seq_count)
+    return (velocity_own, decoded)
+
+
+def decoder_input(stepped, w_conv, slab_rows, seq_index, seq_count):
     token_rows = MICRO * seq_count * TOK_DEV // (FRAMES * (LAT_W // 2))
     image_rows = 2 * token_rows
     slab_most = 2 * image_rows // seq_count
@@ -171,7 +369,6 @@
     image = (
         jnp.transpose(image, (0, 1, 3, 2, 4, 5))
         .reshape(FRAMES, image_rows, LAT_W, LAT_CH)
-        .astype(jnp.bfloat16)
     )
     padded = jnp.concatenate([image[:1], image[:1], image], 0)
     padded = jnp.pad(padded, ((0, 0), (1, 1 + slab_most), (1, 1), (0, 0)))
@@ -196,7 +393,7 @@
     features = features.reshape(FRAMES, slab_most, LAT_W, w_conv.shape[2])
     row_valid = jnp.arange(slab_most)[None, :, None, None] < slab_count
     decoded = jnp.where(row_valid, features, jnp.zeros_like(features))
-    return (velocity_own, decoded[None])
+    return decoded[None]
 
 
 def solution(mesh):
@@ -218,4 +415,6 @@
         P(None, ("groups", "seq"), None),
         P(("groups", "seq"), None, None, None, ("segment", "cfg")),
     )
-    return jax.shard_map(shards, mesh=mesh, in_specs=in_specs, out_specs=out_specs, check_vma=False)
+    whole_groups = HEADS % mesh.shape["seq"] == 0 and mesh.shape["seq"] <= 8
+    program = shards if whole_groups else cycled_shards
+    return jax.shard_map(program, mesh=mesh, in_specs=in_specs, out_specs=out_specs, check_vma=False)

time: 168 us -> 99.4 us (0.59)
  blocking collectives: 36.4 us -> 0 us
  matrix products: 43.2 us -> 8.87 us
  waiting for transfers between devices: 34.5 us -> 21.9 us
  Pallas kernels: 0 us -> 11 us
  local copies, waits for them, and re-layouts: 5.78 us -> 14.3 us
  between operations: 9.58 us -> 4.35 us
    dot_general x17 -> x8, matrix products: 43.2 us -> 8.1 us  [the longest x2 6.6 us: shards(): jnp.dot(attention(projected), w_out[0], preferred_element_type=jnp.float32)]
    all_to_all x6 -> x0, waiting for transfers between devices: 34.5 us -> none  [the longest x3 18.6 us: shards(): lax.all_to_all(partial_out.astype(jnp.bfloat16), 'seq', split_axis=0, con...]
    all_gather x2 -> x0, blocking collectives: 26.2 us -> none  [the longest x1 13.1 us: shards(): lax.all_gather(velocity_own, 'seq', axis=1, tiled=True)]
    ppermute x2 -> x18, starting transfers between devices: 7.49 us -> 31.4 us  [the longest x4 9.33 us: shards(): pieces.append(lax.ppermute(block, ('seq', 'segment'), pairs))]
    all_to_all x6 -> x0, starting transfers between devices: 23.6 us -> none  [the longest x3 13.2 us: shards(): lax.all_to_all(outgoing.reshape(share_rows, D), 'seq', split_axis=0, conc...]
    ppermute x2 -> x18, waiting for transfers between devices: 0.01 us -> 21.9 us  [the longest x3 6.91 us: shards(): lax.ppermute(column_block(partial_out, seq_index ^ k), 'seq', within(k))]
    pallas_call x0 -> x2, Pallas kernels: none -> 11 us  [nt_dot(): pl.pallas_call(nt_kernel, grid=(columns // tile,), in_specs=[pl.BlockSpec...]
    psum x1 -> x0, blocking collectives: 10.2 us -> none  [shards(): lax.psum((velocity_term, latent_term), ('segment', 'cfg'))]
  transfers between devices with their start and end apart: 8 -> 18, of which waited for: 6 -> 9; matrix products, arithmetic and copies ran while one was open for 2% -> 4% of each run, Pallas kernels for 0% -> 6%
where the time goes in v1:
time: 99.4 us; the launch traced here: 98.9 us
  starting transfers between devices  31.4 us (32%)
  waiting for transfers between devices  21.9 us (22%)
  local copies, waits for them, and re-layouts  14.3 us (14%)
  Pallas kernels  11 us (11%)
  matrix products  8.87 us (9%)
  other arithmetic  7.02 us (7%)
  between operations  4.35 us (4%)
    pallas_call x2, Pallas kernels, nt_dot(): pl.pallas_call(nt_kernel, grid=(columns // tile,), in_specs=[pl.BlockSpec...  11 us
    unnamed x20, local copies, waits for them, and re-layouts  10.1 us
    ppermute x4, starting transfers between devices, shards(): pieces.append(lax.ppermute(block, ('seq', 'segment'), pairs))  9.33 us
    ppermute x3, waiting for transfers between devices, shards(): lax.ppermute(column_block(partial_out, seq_index ^ k), 'seq', within(k))  6.91 us
    ppermute x3, waiting for transfers between devices, shards(): lax.ppermute(row_block(partial_out, seq_index ^ k), 'seq', within(k))  6.62 us
    dot_general x2, matrix products, shards(): jnp.dot(attention(projected), w_out[0], preferred_element_type=jnp.float32)  6.6 us
    ppermute x3, starting transfers between devices, shards(): lax.ppermute(row_block(partial_out, seq_index ^ k), 'seq', within(k))  6.34 us
    ppermute x3, starting transfers between devices, shards(): lax.ppermute(own_latent, 'seq', within(k))  5.62 us
  transfers between devices with their start and end apart: 18, of which 9 were waited for; matrix products, arithmetic and copies ran while one was open for 4% of the time, Pallas kernels for 6%

profile of v1, /device:TPU:0, one launch (start us, length us, event | category | flops | bytes accessed | tf_op | source)
XLA Modules:
  0.0 98.9 jit_solution(14269893156948927628)
XLA Ops:
  2.2 3.0 %collective-permute-start = (bf16[16,64]{1,0:T(8,128)(2,1)S(1)}, bf16[16,64]{1,0:T(8,128)(2,1)S(1)}, u32[]{:S(2)}, u32[]{:S(2)}) collective-permute-start(bf16[16,64]{1,0:T(8,128)(2,1)S(1)} %get-tuple-element.52), channel_id=1, source_target_pairs={{0,4},{4,0},{8,12},{12,8},{1,5},{5,1},{9,13},{13,9},{2,6},{6,2},{1... | collective-permute-start | bytes 6152 | tf_op jit(solution)/shard_map/ppermute | solution.py:253
  5.2 2.6 %collective-permute-start.1 = (bf16[16,64]{1,0:T(8,128)(2,1)S(1)}, bf16[16,64]{1,0:T(8,128)(2,1)S(1)}, u32[]{:S(2)}, u32[]{:S(2)}) collective-permute-start(bf16[16,64]{1,0:T(8,128)(2,1)S(1)} %get-tuple-element.52), channel_id=1, source_target_pairs={{0,8},{4,12},{8,0},{12,4},{1,9},{5,13},{9,1},{13,5},{2,10},{6,14},... | collective-permute-start | bytes 6152 | tf_op jit(solution)/shard_map/ppermute | solution.py:253
  10.7 5.0 %copy-done.1 = bf16[1,2304,3072]{2,1,0:T(8,128)(2,1)S(1)} copy-done((bf16[1,2304,3072]{2,1,0:T(8,128)(2,1)S(1)}, bf16[1,2304,3072]{2,1,0:T(8,128)(2,1)}, u32[]{:S(2)}) %copy-start.1) | copy-done | bytes 14155800
  15.7 5.5 %shard_map.131 = f32[80,2304]{1,0:T(8,128)S(1)} custom-call(bf16[80,3072]{1,0:T(8,128)(2,1)S(1)} %maximum_maximum_fusion.lhs_ref, bf16[2304,3072]{1,0:T(8,128)(2,1)S(1)} %bitcast.113), custom_call_target="tpu_custom_call" | custom-call | flops 1132462080 | bytes 14155776 | tf_op jit(solution)/shard_map/pallas_call | solution.py:185
  24.5 3.3 %fusion.8 = bf16[64,3072]{1,0:T(8,128)(2,1)S(1)} fusion(bf16[1,768,3072]{2,1,0:T(8,128)(2,1)} %param.15, bf16[6,8,8,128]{3,2,1,0:T(8,128)(2,1)S(1)} %fusion.20), kind=kOutput, calls=%fused_computation.12 | convolution fusion | flops 302186496 | bytes 5210112 | tf_op jit(solution)/shard_map/dot_general | solution.py:302
  28.8 3.5 %collective-permute-start.4 = (bf16[64,768]{1,0:T(8,128)(2,1)S(1)}, bf16[64,768]{1,0:T(8,128)(2,1)S(1)}, u32[]{:S(2)}, u32[]{:S(2)}) collective-permute-start(bf16[64,768]{1,0:T(8,128)(2,1)S(1)} %get-tuple-element.16), channel_id=1, source_target_pairs={{0,8},{4,12},{8,0},{12,4},{1,9},{5,13},{9,1},{13,5},{2,10},{6,14},... | collective-permute-start | bytes 294920 | tf_op jit(solution)/shard_map/ppermute | solution.py:313
  32.3 1.1 %collective-permute-done.3 = bf16[64,768]{1,0:T(8,128)(2,1)S(1)} collective-permute-done((bf16[64,768]{1,0:T(8,128)(2,1)S(1)}, bf16[64,768]{1,0:T(8,128)(2,1)S(1)}, u32[]{:S(2)}, u32[]{:S(2)}) %collective-permute-start.3) | collective-permute-done | bytes 98336 | tf_op jit(solution)/shard_map/ppermute | solution.py:313
  33.4 5.8 %collective-permute-done.4 = bf16[64,768]{1,0:T(8,128)(2,1)S(1)} collective-permute-done((bf16[64,768]{1,0:T(8,128)(2,1)S(1)}, bf16[64,768]{1,0:T(8,128)(2,1)S(1)}, u32[]{:S(2)}, u32[]{:S(2)}) %collective-permute-start.4) | collective-permute-done | bytes 98336 | tf_op jit(solution)/shard_map/ppermute | solution.py:313
  39.3 3.4 %collective-permute-start.6 = (bf16[64,768]{1,0:T(8,128)(2,1)S(1)}, bf16[64,768]{1,0:T(8,128)(2,1)S(1)}, u32[]{:S(2)}, u32[]{:S(2)}) collective-permute-start(bf16[64,768]{1,0:T(8,128)(2,1)S(1)} %add_convert_fusion.2), channel_id=1, source_target_pairs={{0,2},{4,6},{8,10},{12,14},{1,3},{5,7},{9,11},{13,15},{16,18},{20,... | collective-permute-start | bytes 294920 | tf_op jit(solution)/shard_map/ppermute | solution.py:326
  42.7 2.3 %collective-permute-start.7 = (bf16[64,768]{1,0:T(8,128)(2,1)S(1)}, bf16[64,768]{1,0:T(8,128)(2,1)S(1)}, u32[]{:S(2)}, u32[]{:S(2)}) collective-permute-start(bf16[64,768]{1,0:T(8,128)(2,1)S(1)} %add_convert_fusion.2), channel_id=1, source_target_pairs={{0,6},{4,2},{8,14},{12,10},{1,7},{5,3},{9,15},{13,11},{16,22},{20,... | collective-permute-start | bytes 294920 | tf_op jit(solution)/shard_map/ppermute | solution.py:326
  45.0 2.3 %collective-permute-start.8 = (bf16[64,768]{1,0:T(8,128)(2,1)S(1)}, bf16[64,768]{1,0:T(8,128)(2,1)S(1)}, u32[]{:S(2)}, u32[]{:S(2)}) collective-permute-start(bf16[64,768]{1,0:T(8,128)(2,1)S(1)} %add_convert_fusion.2), channel_id=1, source_target_pairs={{0,10},{4,14},{8,2},{12,6},{1,11},{5,15},{9,3},{13,7},{16,26},{20,... | collective-permute-start | bytes 294920 | tf_op jit(solution)/shard_map/ppermute | solution.py:326
  47.3 1.3 %collective-permute-start.9 = (bf16[64,768]{1,0:T(8,128)(2,1)S(1)}, bf16[64,768]{1,0:T(8,128)(2,1)S(1)}, u32[]{:S(2)}, u32[]{:S(2)}) collective-permute-start(bf16[64,768]{1,0:T(8,128)(2,1)S(1)} %add_convert_fusion.2), channel_id=1, source_target_pairs={{0,14},{4,10},{8,6},{12,2},{1,15},{5,11},{9,7},{13,3},{16,30},{20,... | collective-permute-start | bytes 294920 | tf_op jit(solution)/shard_map/ppermute | solution.py:326
  48.7 1.5 %collective-permute-done.8 = bf16[64,768]{1,0:T(8,128)(2,1)S(1)} collective-permute-done((bf16[64,768]{1,0:T(8,128)(2,1)S(1)}, bf16[64,768]{1,0:T(8,128)(2,1)S(1)}, u32[]{:S(2)}, u32[]{:S(2)}) %collective-permute-start.8) | collective-permute-done | bytes 98336 | tf_op jit(solution)/shard_map/ppermute | solution.py:326
  52.4 5.0 %copy-done.2 = bf16[1,2304,3072]{2,1,0:T(8,128)(2,1)S(1)} copy-done((bf16[1,2304,3072]{2,1,0:T(8,128)(2,1)S(1)}, bf16[1,2304,3072]{2,1,0:T(8,128)(2,1)}, u32[]{:S(2)}) %copy-start.2) | copy-done | bytes 14155800
  57.4 5.5 %shard_map.132 = f32[64,2304]{1,0:T(8,128)S(1)} custom-call(bf16[64,3072]{1,0:T(8,128)(2,1)S(1)} %multiply_convert_fusion.lhs_ref, bf16[2304,3072]{1,0:T(8,128)(2,1)S(1)} %bitcast.114), custom_call_target="tpu_custom_call" | custom-call | flops 905969664 | bytes 14155776 | tf_op jit(solution)/shard_map/pallas_call | solution.py:185
  64.4 3.3 %fusion.11 = bf16[64,3072]{1,0:T(8,128)(2,1)S(1)} fusion(bf16[1,768,3072]{2,1,0:T(8,128)(2,1)} %param.15, bf16[6,8,8,128]{3,2,1,0:T(8,128)(2,1)S(1)} %fusion.21), kind=kOutput, calls=%fused_computation.13 | convolution fusion | flops 302186496 | bytes 5210112 | tf_op jit(solution)/shard_map/dot_general | solution.py:302
  67.7 3.9 %collective-permute-start.10 = (bf16[16,3072]{1,0:T(8,128)(2,1)S(1)}, bf16[16,3072]{1,0:T(8,128)(2,1)S(1)}, u32[]{:S(2)}, u32[]{:S(2)}) collective-permute-start(bf16[16,3072]{1,0:T(8,128)(2,1)S(1)} %get-tuple-element.8), channel_id=1, source_target_pairs={{0,4},{4,0},{8,12},{12,8},{1,5},{5,1},{9,13},{13,9},{2,6},{6,2},{1... | collective-permute-start | bytes 294920 | tf_op jit(solution)/shard_map/ppermute | solution.py:338
  71.6 2.4 %collective-permute-start.12 = (bf16[16,3072]{1,0:T(8,128)(2,1)S(1)}, bf16[16,3072]{1,0:T(8,128)(2,1)S(1)}, u32[]{:S(2)}, u32[]{:S(2)}) collective-permute-start(bf16[16,3072]{1,0:T(8,128)(2,1)S(1)} %get-tuple-element.9), channel_id=1, source_target_pairs={{0,12},{4,8},{8,4},{12,0},{1,13},{5,9},{9,5},{13,1},{2,14},{6,10},... | collective-permute-start | bytes 294920 | tf_op jit(solution)/shard_map/ppermute | solution.py:338
  74.6 6.1 %collective-permute-done.11 = bf16[16,3072]{1,0:T(8,128)(2,1)S(1)} collective-permute-done((bf16[16,3072]{1,0:T(8,128)(2,1)S(1)}, bf16[16,3072]{1,0:T(8,128)(2,1)S(1)}, u32[]{:S(2)}, u32[]{:S(2)}) %collective-permute-start.11) | collective-permute-done | bytes 98336 | tf_op jit(solution)/shard_map/ppermute | solution.py:338
  82.4 1.3 %collective-permute-start.14 = (f32[16,64]{1,0:T(8,128)S(1)}, f32[16,64]{1,0:T(8,128)S(1)}, u32[]{:S(2)}, u32[]{:S(2)}) collective-permute-start(f32[16,64]{1,0:T(8,128)S(1)} %add.193), channel_id=1, source_target_pairs={{2,0},{3,1},{6,4},{7,5},{10,8},{11,9},{14,12},{15,13},{18,16},{19,... | collective-permute-start | bytes 12296 | tf_op jit(solution)/shard_map/ppermute | solution.py:351
  84.3 3.6 %collective-permute-done.14 = f32[16,64]{1,0:T(8,128)S(1)} collective-permute-done((f32[16,64]{1,0:T(8,128)S(1)}, f32[16,64]{1,0:T(8,128)S(1)}, u32[]{:S(2)}, u32[]{:S(2)}) %collective-permute-start.14) | collective-permute-done | bytes 4128 | tf_op jit(solution)/shard_map/ppermute | solution.py:351
  88.5 1.7 %collective-permute-start.15 = (bf16[2,8,64]{2,1,0:T(8,128)(2,1)S(1)}, bf16[2,8,64]{2,1,0:T(8,128)(2,1)S(1)}, u32[]{:S(2)}, u32[]{:S(2)}) collective-permute-start(bf16[2,8,64]{2,1,0:T(8,128)(2,1)S(1)} %get-tuple-element.4), channel_id=1, source_target_pairs={{0,4},{4,0},{8,12},{12,8},{1,5},{5,1},{9,13},{13,9},{2,6},{6,2},{1... | collective-permute-start | bytes 6152 | tf_op jit(solution)/shard_map/ppermute | solution.py:357
  91.0 1.9 %collective-permute-start.17 = (bf16[2,8,64]{2,1,0:T(8,128)(2,1)S(1)}, bf16[2,8,64]{2,1,0:T(8,128)(2,1)S(1)}, u32[]{:S(2)}, u32[]{:S(2)}) collective-permute-start(bf16[2,8,64]{2,1,0:T(8,128)(2,1)S(1)} %get-tuple-element.4), channel_id=1, source_target_pairs={{0,12},{4,8},{8,4},{12,0},{1,13},{5,9},{9,5},{13,1},{2,14},{6,10},... | collective-permute-start | bytes 6152 | tf_op jit(solution)/shard_map/ppermute | solution.py:357
  95.2 1.2 %collective-permute-done.17 = bf16[2,8,64]{2,1,0:T(8,128)(2,1)S(1)} collective-permute-done((bf16[2,8,64]{2,1,0:T(8,128)(2,1)S(1)}, bf16[2,8,64]{2,1,0:T(8,128)(2,1)S(1)}, u32[]{:S(2)}, u32[]{:S(2)}) %collective-permute-start.17) | collective-permute-done | bytes 2080 | tf_op jit(solution)/shard_map/ppermute | solution.py:357
  (110 shorter events, 17.9 us)
Async XLA Ops:
  0.6 7.8 %copy-start = (bf16[50,3,3072]{2,0,1:T(8,128)(2,1)S(1)}, bf16[50,3,3072]{2,0,1:T(8,128)(2,1)}, u32[]{:S(2)}) copy-start(bf16[50,3,3072]{2,0,1:T(8,128)(2,1)} %param.16) | copy-start | bytes 2764804
  2.2 19.8 %collective-permute-start = (bf16[16,64]{1,0:T(8,128)(2,1)S(1)}, bf16[16,64]{1,0:T(8,128)(2,1)S(1)}, u32[]{:S(2)}, u32[]{:S(2)}) collective-permute-start(bf16[16,64]{1,0:T(8,128)(2,1)S(1)} %get-tuple-element.52), channel_id=1, source_target_pairs={{0,4},{4,0},{8,12},{12,8},{1,5},{5,1},{9,13},{13,9},{2,6},{6,2},{1... | collective-permute-start | bytes 6152 | tf_op jit(solution)/shard_map/ppermute | solution.py:253
  5.2 16.8 %collective-permute-start.1 = (bf16[16,64]{1,0:T(8,128)(2,1)S(1)}, bf16[16,64]{1,0:T(8,128)(2,1)S(1)}, u32[]{:S(2)}, u32[]{:S(2)}) collective-permute-start(bf16[16,64]{1,0:T(8,128)(2,1)S(1)} %get-tuple-element.52), channel_id=1, source_target_pairs={{0,8},{4,12},{8,0},{12,4},{1,9},{5,13},{9,1},{13,5},{2,10},{6,14},... | collective-permute-start | bytes 6152 | tf_op jit(solution)/shard_map/ppermute | solution.py:253
  7.8 14.2 %collective-permute-start.2 = (bf16[16,64]{1,0:T(8,128)(2,1)S(1)}, bf16[16,64]{1,0:T(8,128)(2,1)S(1)}, u32[]{:S(2)}, u32[]{:S(2)}) collective-permute-start(bf16[16,64]{1,0:T(8,128)(2,1)S(1)} %get-tuple-element.52), channel_id=1, source_target_pairs={{0,12},{4,8},{8,4},{12,0},{1,13},{5,9},{9,5},{13,1},{2,14},{6,10},... | collective-permute-start | bytes 6152 | tf_op jit(solution)/shard_map/ppermute | solution.py:253
  15.7 6.9 %copy-start.3 = (bf16[64,3072]{1,0:T(8,128)(2,1)S(1)}, bf16[64,3072]{1,0:T(8,128)(2,1)}, u32[]{:S(2)}) copy-start(bf16[64,3072]{1,0:T(8,128)(2,1)} %param.13) | copy-start | bytes 1179652
  27.8 5.6 %collective-permute-start.3 = (bf16[64,768]{1,0:T(8,128)(2,1)S(1)}, bf16[64,768]{1,0:T(8,128)(2,1)S(1)}, u32[]{:S(2)}, u32[]{:S(2)}) collective-permute-start(bf16[64,768]{1,0:T(8,128)(2,1)S(1)} %get-tuple-element.14), channel_id=1, source_target_pairs={{0,4},{4,0},{8,12},{12,8},{1,5},{5,1},{9,13},{13,9},{2,6},{6,2},{1... | collective-permute-start | bytes 294920 | tf_op jit(solution)/shard_map/ppermute | solution.py:313
  28.8 10.4 %collective-permute-start.4 = (bf16[64,768]{1,0:T(8,128)(2,1)S(1)}, bf16[64,768]{1,0:T(8,128)(2,1)S(1)}, u32[]{:S(2)}, u32[]{:S(2)}) collective-permute-start(bf16[64,768]{1,0:T(8,128)(2,1)S(1)} %get-tuple-element.16), channel_id=1, source_target_pairs={{0,8},{4,12},{8,0},{12,4},{1,9},{5,13},{9,1},{13,5},{2,10},{6,14},... | collective-permute-start | bytes 294920 | tf_op jit(solution)/shard_map/ppermute | solution.py:313
  32.3 6.9 %collective-permute-start.5 = (bf16[64,768]{1,0:T(8,128)(2,1)S(1)}, bf16[64,768]{1,0:T(8,128)(2,1)S(1)}, u32[]{:S(2)}, u32[]{:S(2)}) collective-permute-start(bf16[64,768]{1,0:T(8,128)(2,1)S(1)} %get-tuple-element.15), channel_id=1, source_target_pairs={{0,12},{4,8},{8,4},{12,0},{1,13},{5,9},{9,5},{13,1},{2,14},{6,10},... | collective-permute-start | bytes 294920 | tf_op jit(solution)/shard_map/ppermute | solution.py:313
  39.3 9.4 %collective-permute-start.6 = (bf16[64,768]{1,0:T(8,128)(2,1)S(1)}, bf16[64,768]{1,0:T(8,128)(2,1)S(1)}, u32[]{:S(2)}, u32[]{:S(2)}) collective-permute-start(bf16[64,768]{1,0:T(8,128)(2,1)S(1)} %add_convert_fusion.2), channel_id=1, source_target_pairs={{0,2},{4,6},{8,10},{12,14},{1,3},{5,7},{9,11},{13,15},{16,18},{20,... | collective-permute-start | bytes 294920 | tf_op jit(solution)/shard_map/ppermute | solution.py:326
  42.7 6.0 %collective-permute-start.7 = (bf16[64,768]{1,0:T(8,128)(2,1)S(1)}, bf16[64,768]{1,0:T(8,128)(2,1)S(1)}, u32[]{:S(2)}, u32[]{:S(2)}) collective-permute-start(bf16[64,768]{1,0:T(8,128)(2,1)S(1)} %add_convert_fusion.2), channel_id=1, source_target_pairs={{0,6},{4,2},{8,14},{12,10},{1,7},{5,3},{9,15},{13,11},{16,22},{20,... | collective-permute-start | bytes 294920 | tf_op jit(solution)/shard_map/ppermute | solution.py:326
  45.0 5.2 %collective-permute-start.8 = (bf16[64,768]{1,0:T(8,128)(2,1)S(1)}, bf16[64,768]{1,0:T(8,128)(2,1)S(1)}, u32[]{:S(2)}, u32[]{:S(2)}) collective-permute-start(bf16[64,768]{1,0:T(8,128)(2,1)S(1)} %add_convert_fusion.2), channel_id=1, source_target_pairs={{0,10},{4,14},{8,2},{12,6},{1,11},{5,15},{9,3},{13,7},{16,26},{20,... | collective-permute-start | bytes 294920 | tf_op jit(solution)/shard_map/ppermute | solution.py:326
  47.3 3.9 %collective-permute-start.9 = (bf16[64,768]{1,0:T(8,128)(2,1)S(1)}, bf16[64,768]{1,0:T(8,128)(2,1)S(1)}, u32[]{:S(2)}, u32[]{:S(2)}) collective-permute-start(bf16[64,768]{1,0:T(8,128)(2,1)S(1)} %add_convert_fusion.2), channel_id=1, source_target_pairs={{0,14},{4,10},{8,6},{12,2},{1,15},{5,11},{9,7},{13,3},{16,30},{20,... | collective-permute-start | bytes 294920 | tf_op jit(solution)/shard_map/ppermute | solution.py:326
  63.2 17.7 %copy-start.4 = (bf16[3072,64]{0,1:T(8,128)(2,1)S(1)}, bf16[3072,64]{0,1:T(8,128)(2,1)}, u32[]{:S(2)}) copy-start(bf16[3072,64]{0,1:T(8,128)(2,1)} %param.19) | copy-start | bytes 1179652
  63.6 20.0 %copy-start.8 = (s32[4]{0:T(128)S(1)}, s32[4]{0:T(128)}, u32[]{:S(2)}) copy-start(s32[4]{0:T(128)} %param.23) | copy-start | bytes 52
  63.6 24.3 %copy-start.7 = (f32[2,8,64]{2,1,0:T(8,128)S(1)}, f32[2,8,64]{2,1,0:T(8,128)}, u32[]{:S(2)}) copy-start(f32[2,8,64]{2,1,0:T(8,128)} %param.12) | copy-start | bytes 12292
  64.3 33.6 %copy-start.6 = (bf16[27,16,128]{2,1,0:T(8,128)(2,1)S(1)}, bf16[27,16,128]{2,1,0:T(8,128)(2,1)}, u32[]{:S(2)}) copy-start(bf16[27,16,128]{2,1,0:T(8,128)(2,1)} %param.20) | copy-start | bytes 331780
  67.7 6.9 %collective-permute-start.10 = (bf16[16,3072]{1,0:T(8,128)(2,1)S(1)}, bf16[16,3072]{1,0:T(8,128)(2,1)S(1)}, u32[]{:S(2)}, u32[]{:S(2)}) collective-permute-start(bf16[16,3072]{1,0:T(8,128)(2,1)S(1)} %get-tuple-element.8), channel_id=1, source_target_pairs={{0,4},{4,0},{8,12},{12,8},{1,5},{5,1},{9,13},{13,9},{2,6},{6,2},{1... | collective-permute-start | bytes 294920 | tf_op jit(solution)/shard_map/ppermute | solution.py:338
  71.6 9.1 %collective-permute-start.11 = (bf16[16,3072]{1,0:T(8,128)(2,1)S(1)}, bf16[16,3072]{1,0:T(8,128)(2,1)S(1)}, u32[]{:S(2)}, u32[]{:S(2)}) collective-permute-start(bf16[16,3072]{1,0:T(8,128)(2,1)S(1)} %get-tuple-element.10), channel_id=1, source_target_pairs={{0,8},{4,12},{8,0},{12,4},{1,9},{5,13},{9,1},{13,5},{2,10},{6,14},... | collective-permute-start | bytes 294920 | tf_op jit(solution)/shard_map/ppermute | solution.py:338
  71.6 9.0 %collective-permute-start.12 = (bf16[16,3072]{1,0:T(8,128)(2,1)S(1)}, bf16[16,3072]{1,0:T(8,128)(2,1)S(1)}, u32[]{:S(2)}, u32[]{:S(2)}) collective-permute-start(bf16[16,3072]{1,0:T(8,128)(2,1)S(1)} %get-tuple-element.9), channel_id=1, source_target_pairs={{0,12},{4,8},{8,4},{12,0},{1,13},{5,9},{9,5},{13,1},{2,14},{6,10},... | collective-permute-start | bytes 294920 | tf_op jit(solution)/shard_map/ppermute | solution.py:338
  81.2 1.2 %collective-permute-start.13 = (f32[16,64]{1,0:T(8,128)S(1)}, f32[16,64]{1,0:T(8,128)S(1)}, u32[]{:S(2)}, u32[]{:S(2)}) collective-permute-start(f32[16,64]{1,0:T(8,128)S(1)} %convolution_multiply_fusion.3), channel_id=1, source_target_pairs={{0,1},{1,0},{2,3},{3,2},{4,5},{5,4},{6,7},{7,6},{8,9},{9,8},{10,11... | collective-permute-start | bytes 12296 | tf_op jit(solution)/shard_map/ppermute | solution.py:24
  82.4 5.5 %collective-permute-start.14 = (f32[16,64]{1,0:T(8,128)S(1)}, f32[16,64]{1,0:T(8,128)S(1)}, u32[]{:S(2)}, u32[]{:S(2)}) collective-permute-start(f32[16,64]{1,0:T(8,128)S(1)} %add.193), channel_id=1, source_target_pairs={{2,0},{3,1},{6,4},{7,5},{10,8},{11,9},{14,12},{15,13},{18,16},{19,... | collective-permute-start | bytes 12296 | tf_op jit(solution)/shard_map/ppermute | solution.py:351
  88.5 6.7 %collective-permute-start.15 = (bf16[2,8,64]{2,1,0:T(8,128)(2,1)S(1)}, bf16[2,8,64]{2,1,0:T(8,128)(2,1)S(1)}, u32[]{:S(2)}, u32[]{:S(2)}) collective-permute-start(bf16[2,8,64]{2,1,0:T(8,128)(2,1)S(1)} %get-tuple-element.4), channel_id=1, source_target_pairs={{0,4},{4,0},{8,12},{12,8},{1,5},{5,1},{9,13},{13,9},{2,6},{6,2},{1... | collective-permute-start | bytes 6152 | tf_op jit(solution)/shard_map/ppermute | solution.py:357
  90.2 5.0 %collective-permute-start.16 = (bf16[2,8,64]{2,1,0:T(8,128)(2,1)S(1)}, bf16[2,8,64]{2,1,0:T(8,128)(2,1)S(1)}, u32[]{:S(2)}, u32[]{:S(2)}) collective-permute-start(bf16[2,8,64]{2,1,0:T(8,128)(2,1)S(1)} %get-tuple-element.4), channel_id=1, source_target_pairs={{0,8},{4,12},{8,0},{12,4},{1,9},{5,13},{9,1},{13,5},{2,10},{6,14},... | collective-permute-start | bytes 6152 | tf_op jit(solution)/shard_map/ppermute | solution.py:357
  91.0 5.4 %collective-permute-start.17 = (bf16[2,8,64]{2,1,0:T(8,128)(2,1)S(1)}, bf16[2,8,64]{2,1,0:T(8,128)(2,1)S(1)}, u32[]{:S(2)}, u32[]{:S(2)}) collective-permute-start(bf16[2,8,64]{2,1,0:T(8,128)(2,1)S(1)} %get-tuple-element.4), channel_id=1, source_target_pairs={{0,12},{4,8},{8,4},{12,0},{1,13},{5,9},{9,5},{13,1},{2,14},{6,10},... | collective-permute-start | bytes 6152 | tf_op jit(solution)/shard_map/ppermute | solution.py:357
  (3 other events, 15.6 us)

commit v2 on v0

--- a/solution.py
+++ b/solution.py
@@ -1,6 +1,10 @@
+import functools
+
 import jax
 import jax.numpy as jnp
 from jax import lax
+from jax.experimental import pallas as pl
+from jax.experimental.pallas import tpu as pltpu
 from jax.sharding import PartitionSpec as P
 
 HEADS = 24
@@ -45,7 +49,7 @@
     return joined
 
 
-def shards(
+def cycled_shards(
     latent,
     w_embed,
     w_qkv,
@@ -163,7 +167,380 @@
         lax.all_gather(velocity_own, "seq", axis=1, tiled=True),
         lax.all_gather(latent_own, "seq", axis=1, tiled=True),
     )
-    stepped = latent_full - velocity_full / SCHED_STEPS
+    stepped = (latent_full - velocity_full / SCHED_STEPS).astype(jnp.bfloat16)
+    decoded = decoder_input(stepped, w_conv, slab_rows, seq_index, seq_count)
+    return (velocity_own, decoded)
+
+
+VMEM_LIMIT = 24 * 2**20
+NT = (((1,), (1,)), ((), ()))
+
+
+def kernel_params():
+    return pltpu.CompilerParams(vmem_limit_bytes=VMEM_LIMIT)
+
+
+def whole(space=pltpu.VMEM):
+    return pl.BlockSpec(memory_space=space)
+
+
+def prepare_kernel(
+    embed_ref, shift_ref, scale_ref, qkv_hbm, out_hbm, heads_ref, term_ref, qkv_ref, out_ref, lhs, sems
+):
+    tiles = sems.shape[0] - 1
+    tile = qkv_ref.shape[0] // tiles
+
+    def qkv_copy(i):
+        part = pl.ds(i * tile, tile)
+        return pltpu.make_async_copy(qkv_hbm.at[part], qkv_ref.at[part], sems.at[i])
+
+    out_copy = pltpu.make_async_copy(out_hbm, out_ref, sems.at[tiles])
+    for i in range(tiles):
+        qkv_copy(i).start()
+    out_copy.start()
+    count = embed_ref.shape[0]
+    lhs[:count] = (embed_ref[...].astype(jnp.float32) * scale_ref[...]).astype(jnp.bfloat16)
+    lhs[count:] = jnp.broadcast_to(shift_ref[...], (16, lhs.shape[1])).astype(jnp.bfloat16)
+    for i in range(tiles):
+        qkv_copy(i).wait()
+        part = pl.ds(i * tile, tile)
+        product = lax.dot_general(
+            lhs[...], qkv_ref[part, :], NT, preferred_element_type=jnp.float32
+        )
+        heads_ref[:, part] = product[:count].astype(jnp.bfloat16)
+        term_ref[:, part] = product[count:]
+    out_copy.wait()
+
+
+def prepared(w_embed, shift_row, scale_row, qkv, out):
+    count, depth = w_embed.shape
+    lanes = qkv.shape[0]
+    tiles = lanes // 256
+    return pl.pallas_call(
+        prepare_kernel,
+        in_specs=[whole(), whole(), whole(), whole(pltpu.HBM), whole(pltpu.HBM)],
+        out_specs=[whole()] * 4,
+        out_shape=[
+            jax.ShapeDtypeStruct((count, lanes), jnp.bfloat16),
+            jax.ShapeDtypeStruct((16, lanes), jnp.float32),
+            pltpu.VMEM(qkv.shape, qkv.dtype),
+            pltpu.VMEM(out.shape, out.dtype),
+        ],
+        scratch_shapes=[
+            pltpu.VMEM((count + 16, depth), jnp.bfloat16),
+            pltpu.SemaphoreType.DMA((tiles + 1,)),
+        ],
+        cost_estimate=pl.CostEstimate(
+            flops=2 * count * depth * lanes,
+            bytes_accessed=2 * (qkv.size + out.size),
+            transcendentals=0,
+        ),
+        compiler_params=kernel_params(),
+    )(w_embed, shift_row, scale_row, qkv, out)
+
+
+def attend(projected, stale_ref, attended):
+    rows = projected.shape[0]
+    patch_rows = stale_ref.shape[0]
+    lanes = attended.shape[1]
+
+    def micro_of(shape, dim):
+        return lax.broadcasted_iota(jnp.int32, shape, dim) // TOK_DEV % MICRO
+
+    unseen = micro_of((rows, rows), 0) < micro_of((rows, rows), 1)
+    late = micro_of((rows, patch_rows), 0) > 0
+    for head in range(lanes // HEAD_DIM):
+        first = 3 * HEAD_DIM * head
+        queries = projected[:, first : first + HEAD_DIM]
+        keys = projected[:, first + HEAD_DIM : first + 2 * HEAD_DIM]
+        values = projected[:, first + 2 * HEAD_DIM : first + 3 * HEAD_DIM]
+        part = slice(head * HEAD_DIM, (head + 1) * HEAD_DIM)
+        value_part = slice(lanes + head * HEAD_DIM, lanes + (head + 1) * HEAD_DIM)
+        fresh = lax.dot_general(queries, keys, NT, preferred_element_type=jnp.float32)
+        stale = lax.dot_general(
+            queries, stale_ref[:, part], NT, preferred_element_type=jnp.float32
+        )
+        fresh = jnp.where(unseen, -jnp.inf, fresh * HEAD_DIM ** (-0.5))
+        stale = jnp.where(late, -jnp.inf, stale * HEAD_DIM ** (-0.5))
+        top = jnp.maximum(
+            jnp.max(fresh, axis=-1, keepdims=True), jnp.max(stale, axis=-1, keepdims=True)
+        )
+        fresh = jnp.exp(fresh - top)
+        stale = jnp.exp(stale - top)
+        total = jnp.sum(fresh, axis=-1, keepdims=True) + jnp.sum(stale, axis=-1, keepdims=True)
+        fresh = (fresh / total).astype(jnp.bfloat16)
+        stale = (stale / total).astype(jnp.bfloat16)
+        attended[:, part] = (
+            jnp.dot(fresh, values, preferred_element_type=jnp.float32)
+            + jnp.dot(stale, stale_ref[:, value_part], preferred_element_type=jnp.float32)
+        ).astype(jnp.bfloat16)
+
+
+def column_blocks(place, attended, out_ref, block_refs):
+    count = len(block_refs)
+    columns = out_ref.shape[1] // count
+    for k in range(count):
+        first = pl.multiple_of((place ^ k) * columns, columns)
+        block_refs[k][...] = jnp.dot(
+            attended[...], out_ref[:, pl.ds(first, columns)], preferred_element_type=jnp.float32
+        ).astype(jnp.bfloat16)
+
+
+def first_layer_kernel(count, place_ref, embed_ref, heads_ref, term_ref, stale_ref, out_ref, *refs):
+    latent_refs, refs = refs[:count], refs[count:]
+    block_refs, own_ref, latents, attended = refs[:count], *refs[count:]
+    place = place_ref[0]
+    rows_dev = latent_refs[0].shape[0]
+    for k in range(count):
+        first = pl.multiple_of((place ^ k) * rows_dev, rows_dev)
+        latents[pl.ds(first, rows_dev), :] = latent_refs[k][...]
+    embedded = jnp.dot(latents[...], embed_ref[...], preferred_element_type=jnp.float32)
+    embedded = embedded.astype(jnp.bfloat16).astype(jnp.float32)
+    norm = lax.rsqrt(jnp.mean(embedded * embedded, axis=-1, keepdims=True) + norm_eps)
+    projected = jnp.dot(latents[...], heads_ref[...], preferred_element_type=jnp.float32)
+    projected = (norm * projected + term_ref[:1]).astype(jnp.bfloat16)
+    attend(projected, stale_ref, attended)
+    column_blocks(place, attended, out_ref, block_refs)
+    columns = own_ref.shape[1]
+    first = pl.multiple_of(place * columns, columns)
+    own_ref[...] = jnp.dot(
+        latents[...], embed_ref[:, pl.ds(first, columns)], preferred_element_type=jnp.float32
+    ).astype(jnp.bfloat16)
+
+
+def first_layer(place, latent_pieces, w_embed, heads, term, stale, out):
+    count = len(latent_pieces)
+    rows = count * latent_pieces[0].shape[0]
+    lanes, depth = out.shape
+    block = jax.ShapeDtypeStruct((rows, depth // count), jnp.bfloat16)
+    return pl.pallas_call(
+        functools.partial(first_layer_kernel, count),
+        in_specs=[whole(pltpu.SMEM)] + [whole()] * (5 + count),
+        out_specs=[whole()] * (count + 1),
+        out_shape=[block] * (count + 1),
+        scratch_shapes=[
+            pltpu.VMEM((rows, w_embed.shape[0]), jnp.bfloat16),
+            pltpu.VMEM((rows, lanes), jnp.bfloat16),
+        ],
+        compiler_params=kernel_params(),
+    )(place, w_embed, heads, term, stale, out, *latent_pieces)
+
+
+def add_products(place, numbers, piece_refs, scale_ref, qkv_ref, sums_ref, squares):
+    columns = piece_refs[0].shape[1]
+    scaled = []
+    for k, piece_ref in zip(numbers, piece_refs):
+        first = pl.multiple_of((place ^ k) * columns, columns)
+        wide = piece_ref[...].astype(jnp.float32)
+        squares = squares + jnp.sum(wide * wide, axis=-1, keepdims=True)
+        scaled.append(
+            (first, (wide * scale_ref[:, pl.ds(first, columns)]).astype(jnp.bfloat16))
+        )
+    for i in range(qkv_ref.shape[0] // 256):
+        part = slice(i * 256, (i + 1) * 256)
+        total = sums_ref[:, part]
+        for first, piece in scaled:
+            total = total + lax.dot_general(
+                piece, qkv_ref[part, pl.ds(first, columns)], NT, preferred_element_type=jnp.float32
+            )
+        sums_ref[:, part] = total
+    return squares
+
+
+def sums_kernel(numbers, place_ref, scale_ref, qkv_ref, sums_in, squares_in, *refs):
+    piece_refs, sums_ref, squares_ref = refs[: len(numbers)], *refs[len(numbers) :]
+    sums_ref[...] = sums_in[...]
+    squares_ref[...] = add_products(
+        place_ref[0], numbers, piece_refs, scale_ref, qkv_ref, sums_ref, squares_in[...]
+    )
+
+
+def product_sums(place, numbers, pieces, scale_row, qkv, sums, squares):
+    return pl.pallas_call(
+        functools.partial(sums_kernel, numbers),
+        in_specs=[whole(pltpu.SMEM)] + [whole()] * (4 + len(numbers)),
+        out_specs=[whole()] * 2,
+        out_shape=[
+            jax.ShapeDtypeStruct(sums.shape, sums.dtype),
+            jax.ShapeDtypeStruct(squares.shape, squares.dtype),
+        ],
+        compiler_params=kernel_params(),
+    )(place, scale_row, qkv, sums, squares, *pieces)
+
+
+def later_layer_kernel(
+    count, numbers, last, place_ref, scale_ref, qkv_ref, term_ref, stale_ref, out_ref, sums_in, squares_in, *refs
+):
+    piece_refs, refs = refs[:count], refs[count:]
+    block_refs, own_ref, sums, attended, partial_out = refs[:count], *refs[count:]
+    place = place_ref[0]
+    sums[...] = sums_in[...]
+    squares = add_products(
+        place,
+        numbers,
+        [piece_refs[k] for k in numbers],
+        scale_ref,
+        qkv_ref,
+        sums,
+        squares_in[...],
+    )
+    norm = lax.rsqrt(squares / scale_ref.shape[1] + norm_eps)
+    projected = (norm * sums[...] + term_ref[:1]).astype(jnp.bfloat16)
+    attend(projected, stale_ref, attended)
+    if not last:
+        column_blocks(place, attended, out_ref, block_refs)
+        own_ref[...] = piece_refs[0][...]
+        return
+    partial_out[...] = jnp.dot(
+        attended[...], out_ref[...], preferred_element_type=jnp.float32
+    ).astype(jnp.bfloat16)
+    rows_dev = own_ref.shape[0]
+    columns = piece_refs[0].shape[1]
+    own_rows = pl.ds(pl.multiple_of(place * rows_dev, rows_dev), rows_dev)
+    for k in range(count):
+        first = pl.multiple_of((place ^ k) * rows_dev, rows_dev)
+        block_refs[k][...] = partial_out[pl.ds(first, rows_dev), :]
+        first = pl.multiple_of((place ^ k) * columns, columns)
+        own_ref[:, pl.ds(first, columns)] = piece_refs[k][own_rows, :]
+
+
+def later_layer(place, numbers, last, pieces, scale_row, qkv, term, stale, out, sums, squares):
+    count = len(pieces)
+    rows, columns = pieces[0].shape
+    lanes, depth = out.shape
+    shape = (rows // count, depth) if last else (rows, columns)
+    block = jax.ShapeDtypeStruct(shape, jnp.bfloat16)
+    return pl.pallas_call(
+        functools.partial(later_layer_kernel, count, numbers, last),
+        in_specs=[whole(pltpu.SMEM)] + [whole()] * (7 + count),
+        out_specs=[whole()] * (count + 1),
+        out_shape=[block] * (count + 1),
+        scratch_shapes=[
+            pltpu.VMEM(sums.shape, jnp.float32),
+            pltpu.VMEM((rows, lanes), jnp.bfloat16),
+            pltpu.VMEM((rows, depth), jnp.bfloat16),
+        ],
+        compiler_params=kernel_params(),
+    )(place, scale_row, qkv, term, stale, out, sums, squares, *pieces)
+
+
+def shards(
+    latent,
+    w_embed,
+    w_qkv,
+    w_out,
+    mod_table,
+    cond_mod,
+    stale_kv,
+    w_final,
+    w_conv,
+    patch_order,
+    timestep,
+    slab_rows,
+):
+    seq_count = lax.axis_size("seq")
+    segment_count = lax.axis_size("segment")
+    seq_index = lax.axis_index("seq")
+    segment_index = lax.axis_index("segment")
+    branch_index = lax.axis_index("cfg")
+    group_heads = HEADS // seq_count
+    lanes = group_heads * HEAD_DIM
+    rows_dev = MICRO * TOK_DEV
+    rows = seq_count * rows_dev
+    patch_rows = seq_count * TOK_DEV
+    table_row = lax.dynamic_index_in_dim(mod_table, timestep[0], 0, keepdims=False).astype(
+        jnp.float32
+    )
+    modulation = table_row + cond_mod[0, 0]
+    shift_row = modulation[0]
+    scale_row = 1.0 + modulation[1]
+    gate_row = modulation[2]
+    flipped = patch_order[0] == 1
+
+    def micro_ordered(value):
+        return jnp.where(flipped, value[::-1], value)
+
+    def within(k):
+        return [(i, i ^ k) for i in range(seq_count)]
+
+    def seq_ordered(pieces):
+        stacked = jnp.stack(pieces)
+        return jnp.take(stacked, jnp.arange(seq_count) ^ seq_index, axis=0)
+
+    place = seq_index.astype(jnp.int32)[None]
+    own_latent = micro_ordered(latent).astype(jnp.bfloat16).reshape(rows_dev, -1)
+    latent_pieces = [own_latent] + [
+        lax.ppermute(own_latent, "seq", within(k)) for k in range(1, seq_count)
+    ]
+    head_embed, shift_term, qkv, out = prepared(
+        w_embed, shift_row[None], scale_row[None], w_qkv[0], w_out[0]
+    )
+    stale = jnp.where(flipped, stale_kv[0, 0, 0, 0], stale_kv[0, 0, 0, 1])
+    *blocks, own = first_layer(
+        place, latent_pieces, w_embed, head_embed, shift_term, stale, out
+    )
+    columns = D // seq_count
+    own_gate = lax.dynamic_slice_in_dim(gate_row, seq_index * columns, columns, 0)
+    for step in range(1, segment_count):
+        mixed = blocks[0].astype(jnp.float32)
+        for k in range(1, seq_count):
+            mixed = mixed + lax.ppermute(blocks[k], "seq", within(k)).astype(jnp.float32)
+        block = (own.astype(jnp.float32) + own_gate * mixed).astype(jnp.bfloat16)
+        pieces = []
+        for k in range(seq_count):
+            pairs = [
+                (i * segment_count + step - 1, (i ^ k) * segment_count + step)
+                for i in range(seq_count)
+            ]
+            pieces.append(lax.ppermute(block, ("seq", "segment"), pairs))
+        sums = jnp.zeros((rows, qkv.shape[0]), jnp.float32)
+        squares = jnp.zeros((rows, 1), jnp.float32)
+        numbers = tuple(range(seq_count))
+        half = seq_count // 2
+        for some in (numbers[:half], numbers[half:-1]):
+            if some:
+                sums, squares = product_sums(
+                    place, some, [pieces[k] for k in some], scale_row[None], qkv, sums, squares
+                )
+        *blocks, own = later_layer(
+            place,
+            numbers[-1:],
+            step + 1 == segment_count,
+            pieces,
+            scale_row[None],
+            qkv,
+            shift_term,
+            stale,
+            out,
+            sums,
+            squares,
+        )
+
+    mixed = blocks[0].astype(jnp.float32)
+    for k in range(1, seq_count):
+        mixed = mixed + lax.ppermute(blocks[k], "seq", within(k)).astype(jnp.float32)
+    final = (own.astype(jnp.float32) + gate_row * mixed).astype(jnp.bfloat16)
+    predicted = jnp.dot(
+        rms_scaled(final).astype(jnp.bfloat16), w_final, preferred_element_type=jnp.float32
+    )
+    term = jnp.where(branch_index == 0, 1.0 - guide_scale, guide_scale) * predicted
+    velocity_own = term + swapped(term, "cfg", 0)
+    hop = [(segment_count - 1, i) for i in range(segment_count - 1)]
+    for pair in hop:
+        moved = lax.ppermute(velocity_own, "segment", [pair])
+        velocity_own = jnp.where(segment_index == pair[1], moved, velocity_own)
+    velocity_own = micro_ordered(velocity_own.reshape(MICRO, TOK_DEV, -1))
+    stepped_own = (latent - velocity_own / SCHED_STEPS).astype(jnp.bfloat16)
+    stepped = seq_ordered(
+        [stepped_own]
+        + [lax.ppermute(stepped_own, "seq", within(k)) for k in range(1, seq_count)]
+    )
+    stepped = jnp.transpose(stepped, (1, 0, 2, 3))
+    decoded = decoder_input(stepped, w_conv, slab_rows, seq_index, seq_count)
+    return (velocity_own, decoded)
+
+
+def decoder_input(stepped, w_conv, slab_rows, seq_index, seq_count):
     token_rows = MICRO * seq_count * TOK_DEV // (FRAMES * (LAT_W // 2))
     image_rows = 2 * token_rows
     slab_most = 2 * image_rows // seq_count
@@ -171,7 +548,6 @@
     image = (
         jnp.transpose(image, (0, 1, 3, 2, 4, 5))
         .reshape(FRAMES, image_rows, LAT_W, LAT_CH)
-        .astype(jnp.bfloat16)
     )
     padded = jnp.concatenate([image[:1], image[:1], image], 0)
     padded = jnp.pad(padded, ((0, 0), (1, 1 + slab_most), (1, 1), (0, 0)))
@@ -196,7 +572,7 @@
     features = features.reshape(FRAMES, slab_most, LAT_W, w_conv.shape[2])
     row_valid = jnp.arange(slab_most)[None, :, None, None] < slab_count
     decoded = jnp.where(row_valid, features, jnp.zeros_like(features))
-    return (velocity_own, decoded[None])
+    return decoded[None]
 
 
 def solution(mesh):
@@ -218,4 +594,6 @@
         P(None, ("groups", "seq"), None),
         P(("groups", "seq"), None, None, None, ("segment", "cfg")),
     )
-    return jax.shard_map(shards, mesh=mesh, in_specs=in_specs, out_specs=out_specs, check_vma=False)
+    whole_groups = HEADS % mesh.shape["seq"] == 0 and mesh.shape["seq"] <= 8
+    program = shards if whole_groups else cycled_shards
+    return jax.shard_map(program, mesh=mesh, in_specs=in_specs, out_specs=out_specs, check_vma=False)

time: 168 us -> 102 us (0.61)
  matrix products: 43.2 us -> 0.44 us
  blocking collectives: 36.4 us -> 0 us
  Pallas kernels: 0 us -> 20.3 us
  local copies, waits for them, and re-layouts: 5.78 us -> 23.2 us
  waiting for transfers between devices: 34.5 us -> 17.8 us
  between operations: 9.58 us -> 4.47 us
    dot_general x17 -> x2, matrix products: 43.2 us -> 0.44 us  [the longest x1 0.26 us: shards(): jnp.dot(rms_scaled(final).astype(jnp.bfloat16), w_final, preferred_elemen...]
    all_to_all x6 -> x0, waiting for transfers between devices: 34.5 us -> none  [the longest x3 18.6 us: shards(): lax.all_to_all(partial_out.astype(jnp.bfloat16), 'seq', split_axis=0, con...]
    all_gather x2 -> x0, blocking collectives: 26.2 us -> none  [the longest x1 13.1 us: shards(): lax.all_gather(velocity_own, 'seq', axis=1, tiled=True)]
    all_to_all x6 -> x0, starting transfers between devices: 23.6 us -> none  [the longest x3 13.2 us: shards(): lax.all_to_all(outgoing.reshape(share_rows, D), 'seq', split_axis=0, conc...]
    ppermute x2 -> x18, starting transfers between devices: 7.49 us -> 29.5 us  [the longest x4 9.32 us: shards(): pieces.append(lax.ppermute(block, ('seq', 'segment'), pairs))]
    unnamed x17 -> x34, local copies, waits for them, and re-layouts: 0.97 us -> 21.9 us
    pallas_call x0 -> x5, Pallas kernels: none -> 20.3 us  [the longest x1 9.71 us: prepared(): pl.pallas_call(prepare_kernel, in_specs=[whole(), whole(), whole(), whole...]
    ppermute x2 -> x18, waiting for transfers between devices: 0.01 us -> 17.8 us  [the longest x6 11.9 us: shards(): lax.ppermute(blocks[k], 'seq', within(k)).astype(jnp.float32)]
  transfers between devices with their start and end apart: 8 -> 18, of which waited for: 6 -> 7; matrix products, arithmetic and copies ran while one was open for 2% -> 3% of each run, Pallas kernels for 0% -> 13%
where the time goes in v2:
time: 102 us
  starting transfers between devices  29.5 us (29%)
  local copies, waits for them, and re-layouts  23.2 us (23%)
  Pallas kernels  20.3 us (20%)
  waiting for transfers between devices  17.8 us (17%)
  other arithmetic  5.8 us (6%)
  between operations  4.47 us (4%)
    unnamed x34, local copies, waits for them, and re-layouts  21.9 us
    ppermute x6, waiting for transfers between devices, shards(): lax.ppermute(blocks[k], 'seq', within(k)).astype(jnp.float32)  11.9 us
    pallas_call x1, Pallas kernels, prepared(): pl.pallas_call(prepare_kernel, in_specs=[whole(), whole(), whole(), whole...  9.71 us
    ppermute x4, starting transfers between devices, shards(): pieces.append(lax.ppermute(block, ('seq', 'segment'), pairs))  9.32 us
    ppermute x6, starting transfers between devices, shards(): lax.ppermute(blocks[k], 'seq', within(k)).astype(jnp.float32)  8.92 us
    ppermute x3, starting transfers between devices, shards(): lax.ppermute(own_latent, 'seq', within(k))  5.62 us
    ppermute x3, starting transfers between devices, shards(): lax.ppermute(stepped_own, 'seq', within(k))  4.39 us
    ppermute x1, waiting for transfers between devices, shards(): moved = lax.ppermute(velocity_own, 'segment', [pair])  4.22 us
  transfers between devices with their start and end apart: 18, of which 7 were waited for; matrix products, arithmetic and copies ran while one was open for 3% of the time, Pallas kernels for 13%

profile of v2, /device:TPU:0, one launch (start us, length us, event | category | flops | bytes accessed | tf_op | source)
XLA Modules:
  0.0 101.6 jit_solution(11070430297167116024)
XLA Ops:
  2.2 3.0 %collective-permute-start = (bf16[16,64]{1,0:T(8,128)(2,1)S(1)}, bf16[16,64]{1,0:T(8,128)(2,1)S(1)}, u32[]{:S(2)}, u32[]{:S(2)}) collective-permute-start(bf16[16,64]{1,0:T(8,128)(2,1)S(1)} %fusion.20.refs_0_), channel_id=1, source_target_pairs={{0,4},{4,0},{8,12},{12,8},{1,5},{5,1},{9,13},{13,9},{2,6},{6,2},{1... | collective-permute-start | bytes 6152 | tf_op jit(solution)/shard_map/ppermute | solution.py:473
  5.2 2.6 %collective-permute-start.1 = (bf16[16,64]{1,0:T(8,128)(2,1)S(1)}, bf16[16,64]{1,0:T(8,128)(2,1)S(1)}, u32[]{:S(2)}, u32[]{:S(2)}) collective-permute-start(bf16[16,64]{1,0:T(8,128)(2,1)S(1)} %fusion.20.refs_0_), channel_id=1, source_target_pairs={{0,8},{4,12},{8,0},{12,4},{1,9},{5,13},{9,1},{13,5},{2,10},{6,14},... | collective-permute-start | bytes 6152 | tf_op jit(solution)/shard_map/ppermute | solution.py:473
  10.3 2.3 %copy-done.6 = bf16[1,768,3072]{2,1,0:T(8,128)(2,1)S(1)} copy-done((bf16[1,768,3072]{2,1,0:T(8,128)(2,1)S(1)}, bf16[1,768,3072]{2,1,0:T(8,128)(2,1)}, u32[]{:S(2)}) %copy-start.6) | copy-done | bytes 4718616
  13.7 9.7 %shard_map.131 = (bf16[64,2304]{1,0:T(8,128)(2,1)S(1)}, f32[16,2304]{1,0:T(8,128)S(1)}, bf16[2304,3072]{1,0:T(8,128)(2,1)S(1)}, bf16[768,3072]{1,0:T(8,128)(2,1)S(1)}) custom-call(bf16[64,3072]{1,0:T(8,128)(2,1)S(1)} %copy-done.7, f32[1,3072]{1,0:T(1,128)S(1)} %get-tuple-element.72.shift_ref, f32[1,3072]{1,0:T(1,128)S(1)} %get-tuple-element.73.scale_ref, ...), custom_call_target="tpu_custom_call" | custom-call | flops 905969664 | bytes 18874368 | tf_op jit(solution)/shard_map/pallas_call | solution.py:219
  23.4 5.0 %copy-done.1 = bf16[2304,3072]{1,0:T(8,128)(2,1)} copy-done((bf16[2304,3072]{1,0:T(8,128)(2,1)}, bf16[2304,3072]{1,0:T(8,128)(2,1)S(1)}, u32[]{:S(2)}) %copy-start.1) | copy-done | bytes 14155800
  28.4 2.1 %copy-done.3 = bf16[768,3072]{1,0:T(8,128)(2,1)} copy-done((bf16[768,3072]{1,0:T(8,128)(2,1)}, bf16[768,3072]{1,0:T(8,128)(2,1)S(1)}, u32[]{:S(2)}) %copy-start.3) | copy-done | bytes 4718616
  30.6 2.3 %copy-done.4 = bf16[768,3072]{1,0:T(8,128)(2,1)S(1)} copy-done((bf16[768,3072]{1,0:T(8,128)(2,1)S(1)}, bf16[768,3072]{1,0:T(8,128)(2,1)}, u32[]{:S(2)}) %copy-start.4) | copy-done | bytes 4718616
  33.0 3.2 %shard_map.132 = (bf16[64,768]{1,0:T(8,128)(2,1)S(1)}, bf16[64,768]{1,0:T(8,128)(2,1)S(1)}, bf16[64,768]{1,0:T(8,128)(2,1)S(1)}, bf16[64,768]{1,0:T(8,128)(2,1)S(1)}, bf16[64,768]{1,0:T(8,128)(2,1)S(1)}) custom-call(s32[1]{0:T(128)} %bitcast.1.place_ref, bf16[64,3072]{1,0:T(8,128)(2,1)S(1)} %copy-done.8, bf16[64,2304]{1,0:T(8,128)(2,1)S(1)} %get-tuple-element.23.heads_ref, ...), custom_call_target="tpu_custom_call" | custom-call | tf_op jit(solution)/shard_map/pallas_call | solution.py:316
  37.2 3.5 %collective-permute-start.4 = (bf16[64,768]{1,0:T(8,128)(2,1)S(1)}, bf16[64,768]{1,0:T(8,128)(2,1)S(1)}, u32[]{:S(2)}, u32[]{:S(2)}) collective-permute-start(bf16[64,768]{1,0:T(8,128)(2,1)S(1)} %get-tuple-element.27), channel_id=1, source_target_pairs={{0,8},{4,12},{8,0},{12,4},{1,9},{5,13},{9,1},{13,5},{2,10},{6,14},... | collective-permute-start | bytes 294920 | tf_op jit(solution)/shard_map/ppermute | solution.py:487
  41.7 5.8 %collective-permute-done.4 = bf16[64,768]{1,0:T(8,128)(2,1)S(1)} collective-permute-done((bf16[64,768]{1,0:T(8,128)(2,1)S(1)}, bf16[64,768]{1,0:T(8,128)(2,1)S(1)}, u32[]{:S(2)}, u32[]{:S(2)}) %collective-permute-start.4) | collective-permute-done | bytes 98336 | tf_op jit(solution)/shard_map/ppermute | solution.py:487
  47.7 3.4 %collective-permute-start.6 = (bf16[64,768]{1,0:T(8,128)(2,1)S(1)}, bf16[64,768]{1,0:T(8,128)(2,1)S(1)}, u32[]{:S(2)}, u32[]{:S(2)}) collective-permute-start(bf16[64,768]{1,0:T(8,128)(2,1)S(1)} %add_convert_fusion.1), channel_id=1, source_target_pairs={{0,2},{4,6},{8,10},{12,14},{1,3},{5,7},{9,11},{13,15},{16,18},{20,... | collective-permute-start | bytes 294920 | tf_op jit(solution)/shard_map/ppermute | solution.py:495
  51.1 2.3 %collective-permute-start.7 = (bf16[64,768]{1,0:T(8,128)(2,1)S(1)}, bf16[64,768]{1,0:T(8,128)(2,1)S(1)}, u32[]{:S(2)}, u32[]{:S(2)}) collective-permute-start(bf16[64,768]{1,0:T(8,128)(2,1)S(1)} %add_convert_fusion.1), channel_id=1, source_target_pairs={{0,6},{4,2},{8,14},{12,10},{1,7},{5,3},{9,15},{13,11},{16,22},{20,... | collective-permute-start | bytes 294920 | tf_op jit(solution)/shard_map/ppermute | solution.py:495
  53.4 2.3 %collective-permute-start.8 = (bf16[64,768]{1,0:T(8,128)(2,1)S(1)}, bf16[64,768]{1,0:T(8,128)(2,1)S(1)}, u32[]{:S(2)}, u32[]{:S(2)}) collective-permute-start(bf16[64,768]{1,0:T(8,128)(2,1)S(1)} %add_convert_fusion.1), channel_id=1, source_target_pairs={{0,10},{4,14},{8,2},{12,6},{1,11},{5,15},{9,3},{13,7},{16,26},{20,... | collective-permute-start | bytes 294920 | tf_op jit(solution)/shard_map/ppermute | solution.py:495
  55.7 1.3 %collective-permute-start.9 = (bf16[64,768]{1,0:T(8,128)(2,1)S(1)}, bf16[64,768]{1,0:T(8,128)(2,1)S(1)}, u32[]{:S(2)}, u32[]{:S(2)}) collective-permute-start(bf16[64,768]{1,0:T(8,128)(2,1)S(1)} %add_convert_fusion.1), channel_id=1, source_target_pairs={{0,14},{4,10},{8,6},{12,2},{1,15},{5,11},{9,7},{13,3},{16,30},{20,... | collective-permute-start | bytes 294920 | tf_op jit(solution)/shard_map/ppermute | solution.py:495
  57.8 5.0 %copy-done.2 = bf16[2304,3072]{1,0:T(8,128)(2,1)S(1)} copy-done((bf16[2304,3072]{1,0:T(8,128)(2,1)S(1)}, bf16[2304,3072]{1,0:T(8,128)(2,1)}, u32[]{:S(2)}) %copy-start.2) | copy-done | bytes 14155800
  62.8 2.3 %shard_map.133 = (f32[64,2304]{1,0:T(8,128)S(1)}, f32[64,1]{1,0:T(8,128)S(1)}) custom-call(s32[1]{0:T(128)} %bitcast.1.place_ref, f32[1,3072]{1,0:T(1,128)S(1)} %get-tuple-element.73.scale_ref, bf16[2304,3072]{1,0:T(8,128)(2,1)S(1)} %copy-done.2, f32[64,2304]{1,0:T(8,128)S(1)} %broadcast_in_dim.46.sums_in, f32[64,1]{1,0:T(8,128)S(1)} %broadcast_in_dim.47.squares_in, ...), custom_call_target="tpu_custom_call" | custom-call | tf_op jit(solution)/shard_map/pallas_call | solution.py:359
  68.1 2.3 %copy-done.5 = bf16[768,3072]{1,0:T(8,128)(2,1)S(1)} copy-done((bf16[768,3072]{1,0:T(8,128)(2,1)S(1)}, bf16[768,3072]{1,0:T(8,128)(2,1)}, u32[]{:S(2)}) %copy-start.5) | copy-done | bytes 4718616
  70.4 3.9 %shard_map.135 = (bf16[16,3072]{1,0:T(8,128)(2,1)S(1)}, bf16[16,3072]{1,0:T(8,128)(2,1)S(1)}, bf16[16,3072]{1,0:T(8,128)(2,1)S(1)}, bf16[16,3072]{1,0:T(8,128)(2,1)S(1)}, bf16[16,3072]{1,0:T(8,128)(2,1)S(1)}) custom-call(s32[1]{0:T(128)} %bitcast.1.place_ref, f32[1,3072]{1,0:T(1,128)S(1)} %get-tuple-element.73.scale_ref, bf16[2304,3072]{1,0:T(8,128)(2,1)S(1)} %bitcast.43, ...), custom_call_target="tpu_custom_call" | custom-call | tf_op jit(solution)/shard_map/pallas_call | solution.py:413
  75.0 1.5 %collective-permute-start.11 = (bf16[16,3072]{1,0:T(8,128)(2,1)S(1)}, bf16[16,3072]{1,0:T(8,128)(2,1)S(1)}, u32[]{:S(2)}, u32[]{:S(2)}) collective-permute-start(bf16[16,3072]{1,0:T(8,128)(2,1)S(1)} %get-tuple-element.36), channel_id=1, source_target_pairs={{0,8},{4,12},{8,0},{12,4},{1,9},{5,13},{9,1},{13,5},{2,10},{6,14},... | collective-permute-start | bytes 294920 | tf_op jit(solution)/shard_map/ppermute | solution.py:521
  76.5 2.4 %collective-permute-start.12 = (bf16[16,3072]{1,0:T(8,128)(2,1)S(1)}, bf16[16,3072]{1,0:T(8,128)(2,1)S(1)}, u32[]{:S(2)}, u32[]{:S(2)}) collective-permute-start(bf16[16,3072]{1,0:T(8,128)(2,1)S(1)} %get-tuple-element.37), channel_id=1, source_target_pairs={{0,12},{4,8},{8,4},{12,0},{1,13},{5,9},{9,5},{13,1},{2,14},{6,10},... | collective-permute-start | bytes 294920 | tf_op jit(solution)/shard_map/ppermute | solution.py:521
  79.2 4.6 %collective-permute-done.11 = bf16[16,3072]{1,0:T(8,128)(2,1)S(1)} collective-permute-done((bf16[16,3072]{1,0:T(8,128)(2,1)S(1)}, bf16[16,3072]{1,0:T(8,128)(2,1)S(1)}, u32[]{:S(2)}, u32[]{:S(2)}) %collective-permute-start.11) | collective-permute-done | bytes 98336 | tf_op jit(solution)/shard_map/ppermute | solution.py:521
  86.8 4.2 %collective-permute-done.14 = f32[16,64]{1,0:T(8,128)S(1)} collective-permute-done((f32[16,64]{1,0:T(8,128)S(1)}, f32[16,64]{1,0:T(8,128)S(1)}, u32[]{:S(2)}, u32[]{:S(2)}) %collective-permute-start.14) | collective-permute-done | bytes 4128 | tf_op jit(solution)/shard_map/ppermute | solution.py:530
  91.7 1.6 %collective-permute-start.15 = (bf16[2,8,64]{2,1,0:T(8,128)(2,1)S(1)}, bf16[2,8,64]{2,1,0:T(8,128)(2,1)S(1)}, u32[]{:S(2)}, u32[]{:S(2)}) collective-permute-start(bf16[2,8,64]{2,1,0:T(8,128)(2,1)S(1)} %get-tuple-element.40), channel_id=1, source_target_pairs={{0,4},{4,0},{8,12},{12,8},{1,5},{5,1},{9,13},{13,9},{2,6},{6,2},{1... | collective-permute-start | bytes 6152 | tf_op jit(solution)/shard_map/ppermute | solution.py:536
  93.8 2.3 %collective-permute-start.17 = (bf16[2,8,64]{2,1,0:T(8,128)(2,1)S(1)}, bf16[2,8,64]{2,1,0:T(8,128)(2,1)S(1)}, u32[]{:S(2)}, u32[]{:S(2)}) collective-permute-start(bf16[2,8,64]{2,1,0:T(8,128)(2,1)S(1)} %get-tuple-element.40), channel_id=1, source_target_pairs={{0,12},{4,8},{8,4},{12,0},{1,13},{5,9},{9,5},{13,1},{2,14},{6,10},... | collective-permute-start | bytes 6152 | tf_op jit(solution)/shard_map/ppermute | solution.py:536
  (87 shorter events, 18.0 us)
Async XLA Ops:
  0.6 7.8 %copy-start = (bf16[50,3,3072]{2,0,1:T(8,128)(2,1)S(1)}, bf16[50,3,3072]{2,0,1:T(8,128)(2,1)}, u32[]{:S(2)}) copy-start(bf16[50,3,3072]{2,0,1:T(8,128)(2,1)} %param.16) | copy-start | bytes 2764804
  0.6 30.0 %copy-start.8 = (bf16[64,3072]{1,0:T(8,128)(2,1)S(1)}, bf16[64,3072]{1,0:T(8,128)(2,1)}, u32[]{:S(2)}) copy-start(bf16[64,3072]{1,0:T(8,128)(2,1)} %embed_ref.3) | copy-start | bytes 1179652
  0.7 56.4 %copy-start.12 = (s32[4]{0:T(128)S(1)}, s32[4]{0:T(128)}, u32[]{:S(2)}) copy-start(s32[4]{0:T(128)} %param.23) | copy-start | bytes 52
  2.2 28.4 %collective-permute-start = (bf16[16,64]{1,0:T(8,128)(2,1)S(1)}, bf16[16,64]{1,0:T(8,128)(2,1)S(1)}, u32[]{:S(2)}, u32[]{:S(2)}) collective-permute-start(bf16[16,64]{1,0:T(8,128)(2,1)S(1)} %fusion.20.refs_0_), channel_id=1, source_target_pairs={{0,4},{4,0},{8,12},{12,8},{1,5},{5,1},{9,13},{13,9},{2,6},{6,2},{1... | collective-permute-start | bytes 6152 | tf_op jit(solution)/shard_map/ppermute | solution.py:473
  5.2 25.4 %collective-permute-start.1 = (bf16[16,64]{1,0:T(8,128)(2,1)S(1)}, bf16[16,64]{1,0:T(8,128)(2,1)S(1)}, u32[]{:S(2)}, u32[]{:S(2)}) collective-permute-start(bf16[16,64]{1,0:T(8,128)(2,1)S(1)} %fusion.20.refs_0_), channel_id=1, source_target_pairs={{0,8},{4,12},{8,0},{12,4},{1,9},{5,13},{9,1},{13,5},{2,10},{6,14},... | collective-permute-start | bytes 6152 | tf_op jit(solution)/shard_map/ppermute | solution.py:473
  7.8 22.8 %collective-permute-start.2 = (bf16[16,64]{1,0:T(8,128)(2,1)S(1)}, bf16[16,64]{1,0:T(8,128)(2,1)S(1)}, u32[]{:S(2)}, u32[]{:S(2)}) collective-permute-start(bf16[16,64]{1,0:T(8,128)(2,1)S(1)} %fusion.20.refs_0_), channel_id=1, source_target_pairs={{0,12},{4,8},{8,4},{12,0},{1,13},{5,9},{9,5},{13,1},{2,14},{6,10},... | collective-permute-start | bytes 6152 | tf_op jit(solution)/shard_map/ppermute | solution.py:473
  36.2 5.6 %collective-permute-start.3 = (bf16[64,768]{1,0:T(8,128)(2,1)S(1)}, bf16[64,768]{1,0:T(8,128)(2,1)S(1)}, u32[]{:S(2)}, u32[]{:S(2)}) collective-permute-start(bf16[64,768]{1,0:T(8,128)(2,1)S(1)} %get-tuple-element.26), channel_id=1, source_target_pairs={{0,4},{4,0},{8,12},{12,8},{1,5},{5,1},{9,13},{13,9},{2,6},{6,2},{1... | collective-permute-start | bytes 294920 | tf_op jit(solution)/shard_map/ppermute | solution.py:487
  37.2 10.4 %collective-permute-start.4 = (bf16[64,768]{1,0:T(8,128)(2,1)S(1)}, bf16[64,768]{1,0:T(8,128)(2,1)S(1)}, u32[]{:S(2)}, u32[]{:S(2)}) collective-permute-start(bf16[64,768]{1,0:T(8,128)(2,1)S(1)} %get-tuple-element.27), channel_id=1, source_target_pairs={{0,8},{4,12},{8,0},{12,4},{1,9},{5,13},{9,1},{13,5},{2,10},{6,14},... | collective-permute-start | bytes 294920 | tf_op jit(solution)/shard_map/ppermute | solution.py:487
  40.6 6.9 %collective-permute-start.5 = (bf16[64,768]{1,0:T(8,128)(2,1)S(1)}, bf16[64,768]{1,0:T(8,128)(2,1)S(1)}, u32[]{:S(2)}, u32[]{:S(2)}) collective-permute-start(bf16[64,768]{1,0:T(8,128)(2,1)S(1)} %get-tuple-element.28), channel_id=1, source_target_pairs={{0,12},{4,8},{8,4},{12,0},{1,13},{5,9},{9,5},{13,1},{2,14},{6,10},... | collective-permute-start | bytes 294920 | tf_op jit(solution)/shard_map/ppermute | solution.py:487
  47.7 10.1 %collective-permute-start.6 = (bf16[64,768]{1,0:T(8,128)(2,1)S(1)}, bf16[64,768]{1,0:T(8,128)(2,1)S(1)}, u32[]{:S(2)}, u32[]{:S(2)}) collective-permute-start(bf16[64,768]{1,0:T(8,128)(2,1)S(1)} %add_convert_fusion.1), channel_id=1, source_target_pairs={{0,2},{4,6},{8,10},{12,14},{1,3},{5,7},{9,11},{13,15},{16,18},{20,... | collective-permute-start | bytes 294920 | tf_op jit(solution)/shard_map/ppermute | solution.py:495
  51.1 6.7 %collective-permute-start.7 = (bf16[64,768]{1,0:T(8,128)(2,1)S(1)}, bf16[64,768]{1,0:T(8,128)(2,1)S(1)}, u32[]{:S(2)}, u32[]{:S(2)}) collective-permute-start(bf16[64,768]{1,0:T(8,128)(2,1)S(1)} %add_convert_fusion.1), channel_id=1, source_target_pairs={{0,6},{4,2},{8,14},{12,10},{1,7},{5,3},{9,15},{13,11},{16,22},{20,... | collective-permute-start | bytes 294920 | tf_op jit(solution)/shard_map/ppermute | solution.py:495
  53.4 11.7 %collective-permute-start.8 = (bf16[64,768]{1,0:T(8,128)(2,1)S(1)}, bf16[64,768]{1,0:T(8,128)(2,1)S(1)}, u32[]{:S(2)}, u32[]{:S(2)}) collective-permute-start(bf16[64,768]{1,0:T(8,128)(2,1)S(1)} %add_convert_fusion.1), channel_id=1, source_target_pairs={{0,10},{4,14},{8,2},{12,6},{1,11},{5,15},{9,3},{13,7},{16,26},{20,... | collective-permute-start | bytes 294920 | tf_op jit(solution)/shard_map/ppermute | solution.py:495
  55.7 10.7 %collective-permute-start.9 = (bf16[64,768]{1,0:T(8,128)(2,1)S(1)}, bf16[64,768]{1,0:T(8,128)(2,1)S(1)}, u32[]{:S(2)}, u32[]{:S(2)}) collective-permute-start(bf16[64,768]{1,0:T(8,128)(2,1)S(1)} %add_convert_fusion.1), channel_id=1, source_target_pairs={{0,14},{4,10},{8,6},{12,2},{1,15},{5,11},{9,7},{13,3},{16,30},{20,... | collective-permute-start | bytes 294920 | tf_op jit(solution)/shard_map/ppermute | solution.py:495
  65.1 19.0 %copy-start.9 = (bf16[3072,64]{0,1:T(8,128)(2,1)S(1)}, bf16[3072,64]{0,1:T(8,128)(2,1)}, u32[]{:S(2)}) copy-start(bf16[3072,64]{0,1:T(8,128)(2,1)} %param.19) | copy-start | bytes 1179652
  65.1 25.9 %copy-start.11 = (f32[2,8,64]{2,1,0:T(8,128)S(1)}, f32[2,8,64]{2,1,0:T(8,128)}, u32[]{:S(2)}) copy-start(f32[2,8,64]{2,1,0:T(8,128)} %param.12) | copy-start | bytes 12292
  65.1 35.6 %copy-start.10 = (bf16[27,16,128]{2,1,0:T(8,128)(2,1)S(1)}, bf16[27,16,128]{2,1,0:T(8,128)(2,1)}, u32[]{:S(2)}) copy-start(bf16[27,16,128]{2,1,0:T(8,128)(2,1)} %param.20) | copy-start | bytes 331780
  74.4 4.9 %collective-permute-start.10 = (bf16[16,3072]{1,0:T(8,128)(2,1)S(1)}, bf16[16,3072]{1,0:T(8,128)(2,1)S(1)}, u32[]{:S(2)}, u32[]{:S(2)}) collective-permute-start(bf16[16,3072]{1,0:T(8,128)(2,1)S(1)} %get-tuple-element.35), channel_id=1, source_target_pairs={{0,4},{4,0},{8,12},{12,8},{1,5},{5,1},{9,13},{13,9},{2,6},{6,2},{1... | collective-permute-start | bytes 294920 | tf_op jit(solution)/shard_map/ppermute | solution.py:521
  75.0 8.9 %collective-permute-start.11 = (bf16[16,3072]{1,0:T(8,128)(2,1)S(1)}, bf16[16,3072]{1,0:T(8,128)(2,1)S(1)}, u32[]{:S(2)}, u32[]{:S(2)}) collective-permute-start(bf16[16,3072]{1,0:T(8,128)(2,1)S(1)} %get-tuple-element.36), channel_id=1, source_target_pairs={{0,8},{4,12},{8,0},{12,4},{1,9},{5,13},{9,1},{13,5},{2,10},{6,14},... | collective-permute-start | bytes 294920 | tf_op jit(solution)/shard_map/ppermute | solution.py:521
  76.5 7.4 %collective-permute-start.12 = (bf16[16,3072]{1,0:T(8,128)(2,1)S(1)}, bf16[16,3072]{1,0:T(8,128)(2,1)S(1)}, u32[]{:S(2)}, u32[]{:S(2)}) collective-permute-start(bf16[16,3072]{1,0:T(8,128)(2,1)S(1)} %get-tuple-element.37), channel_id=1, source_target_pairs={{0,12},{4,8},{8,4},{12,0},{1,13},{5,9},{9,5},{13,1},{2,14},{6,10},... | collective-permute-start | bytes 294920 | tf_op jit(solution)/shard_map/ppermute | solution.py:521
  84.3 1.2 %collective-permute-start.13 = (f32[16,64]{1,0:T(8,128)S(1)}, f32[16,64]{1,0:T(8,128)S(1)}, u32[]{:S(2)}, u32[]{:S(2)}) collective-permute-start(f32[16,64]{1,0:T(8,128)S(1)} %convolution_multiply_fusion), channel_id=1, source_target_pairs={{0,1},{1,0},{2,3},{3,2},{4,5},{5,4},{6,7},{7,6},{8,9},{9,8},{10,11... | collective-permute-start | bytes 12296 | tf_op jit(solution)/shard_map/ppermute | solution.py:26
  85.5 5.5 %collective-permute-start.14 = (f32[16,64]{1,0:T(8,128)S(1)}, f32[16,64]{1,0:T(8,128)S(1)}, u32[]{:S(2)}, u32[]{:S(2)}) collective-permute-start(f32[16,64]{1,0:T(8,128)S(1)} %add.86), channel_id=1, source_target_pairs={{2,0},{3,1},{6,4},{7,5},{10,8},{11,9},{14,12},{15,13},{18,16},{19,... | collective-permute-start | bytes 12296 | tf_op jit(solution)/shard_map/ppermute | solution.py:530
  91.7 7.0 %collective-permute-start.15 = (bf16[2,8,64]{2,1,0:T(8,128)(2,1)S(1)}, bf16[2,8,64]{2,1,0:T(8,128)(2,1)S(1)}, u32[]{:S(2)}, u32[]{:S(2)}) collective-permute-start(bf16[2,8,64]{2,1,0:T(8,128)(2,1)S(1)} %get-tuple-element.40), channel_id=1, source_target_pairs={{0,4},{4,0},{8,12},{12,8},{1,5},{5,1},{9,13},{13,9},{2,6},{6,2},{1... | collective-permute-start | bytes 6152 | tf_op jit(solution)/shard_map/ppermute | solution.py:536
  93.3 5.4 %collective-permute-start.16 = (bf16[2,8,64]{2,1,0:T(8,128)(2,1)S(1)}, bf16[2,8,64]{2,1,0:T(8,128)(2,1)S(1)}, u32[]{:S(2)}, u32[]{:S(2)}) collective-permute-start(bf16[2,8,64]{2,1,0:T(8,128)(2,1)S(1)} %get-tuple-element.40), channel_id=1, source_target_pairs={{0,8},{4,12},{8,0},{12,4},{1,9},{5,13},{9,1},{13,5},{2,10},{6,14},... | collective-permute-start | bytes 6152 | tf_op jit(solution)/shard_map/ppermute | solution.py:536
  93.8 5.4 %collective-permute-start.17 = (bf16[2,8,64]{2,1,0:T(8,128)(2,1)S(1)}, bf16[2,8,64]{2,1,0:T(8,128)(2,1)S(1)}, u32[]{:S(2)}, u32[]{:S(2)}) collective-permute-start(bf16[2,8,64]{2,1,0:T(8,128)(2,1)S(1)} %get-tuple-element.40), channel_id=1, source_target_pairs={{0,12},{4,8},{8,4},{12,0},{1,13},{5,9},{9,5},{13,1},{2,14},{6,10},... | collective-permute-start | bytes 6152 | tf_op jit(solution)/shard_map/ppermute | solution.py:536
  (11 other events, 35.0 us)

commit v3 on v2

--- a/solution.py
+++ b/solution.py
@@ -172,80 +172,109 @@
     return (velocity_own, decoded)
 
 
-VMEM_LIMIT = 24 * 2**20
 NT = (((1,), (1,)), ((), ()))
 
 
-def kernel_params():
-    return pltpu.CompilerParams(vmem_limit_bytes=VMEM_LIMIT)
+def kernel_params(mebibytes=8):
+    return pltpu.CompilerParams(vmem_limit_bytes=mebibytes * 2**20)
 
 
 def whole(space=pltpu.VMEM):
     return pl.BlockSpec(memory_space=space)
 
 
+def in_order(copies, ahead):
+    for copy in copies[:ahead]:
+        copy.start()
+
+    def landed():
+        for i, copy in enumerate(copies):
+            copy.wait()
+            if i + ahead < len(copies):
+                copies[i + ahead].start()
+            yield i
+
+    return landed()
+
+
 def prepare_kernel(
-    embed_ref, shift_ref, scale_ref, qkv_hbm, out_hbm, heads_ref, term_ref, qkv_ref, out_ref, lhs, sems
+    timestep_ref, table_hbm, cond_hbm, embed_hbm, qkv_hbm, rows_ref, heads_ref, term_ref, table, cond, embed, qkv, lhs, sems
 ):
-    tiles = sems.shape[0] - 1
-    tile = qkv_ref.shape[0] // tiles
-
-    def qkv_copy(i):
+    tiles, tile = qkv.shape[:2]
+    small = [
+        pltpu.make_async_copy(source, target, sems.at[tiles + i])
+        for i, (source, target) in enumerate(
+            ((table_hbm, table), (cond_hbm, cond), (embed_hbm, embed))
+        )
+    ]
+    for copy in small:
+        copy.start()
+    landed = in_order(
+        [
+            pltpu.make_async_copy(qkv_hbm.at[pl.ds(i * tile, tile)], qkv.at[i], sems.at[i])
+            for i in range(tiles)
+        ],
+        4,
+    )
+    for copy in small:
+        copy.wait()
+    steps = table.shape[1]
+    chosen = lax.broadcasted_iota(jnp.int32, (16, steps), 1) == timestep_ref[0]
+    chosen = jnp.where(chosen, 1.0, 0.0).astype(jnp.bfloat16)
+    for j in range(3):
+        row = jnp.dot(chosen, table[j], preferred_element_type=jnp.float32)[:1]
+        rows_ref[j : j + 1, :] = row + cond[j] + (1.0 if j == 1 else 0.0)
+    count = embed.shape[0]
+    lhs[:count] = (embed[...].astype(jnp.float32) * rows_ref[1:2]).astype(jnp.bfloat16)
+    lhs[count:] = jnp.broadcast_to(rows_ref[0:1], (16, lhs.shape[1])).astype(jnp.bfloat16)
+    for i in landed:
         part = pl.ds(i * tile, tile)
-        return pltpu.make_async_copy(qkv_hbm.at[part], qkv_ref.at[part], sems.at[i])
-
-    out_copy = pltpu.make_async_copy(out_hbm, out_ref, sems.at[tiles])
-    for i in range(tiles):
-        qkv_copy(i).start()
-    out_copy.start()
-    count = embed_ref.shape[0]
-    lhs[:count] = (embed_ref[...].astype(jnp.float32) * scale_ref[...]).astype(jnp.bfloat16)
-    lhs[count:] = jnp.broadcast_to(shift_ref[...], (16, lhs.shape[1])).astype(jnp.bfloat16)
-    for i in range(tiles):
-        qkv_copy(i).wait()
-        part = pl.ds(i * tile, tile)
-        product = lax.dot_general(
-            lhs[...], qkv_ref[part, :], NT, preferred_element_type=jnp.float32
-        )
+        product = lax.dot_general(lhs[...], qkv[i], NT, preferred_element_type=jnp.float32)
         heads_ref[:, part] = product[:count].astype(jnp.bfloat16)
         term_ref[:, part] = product[count:]
-    out_copy.wait()
-
-
-def prepared(w_embed, shift_row, scale_row, qkv, out):
+
+
+def in_hbm(*values):
+    return [pltpu.with_memory_space_constraint(value, pltpu.HBM) for value in values]
+
+
+def prepared(timestep, table, cond, w_embed, qkv):
     count, depth = w_embed.shape
     lanes = qkv.shape[0]
     tiles = lanes // 256
     return pl.pallas_call(
         prepare_kernel,
-        in_specs=[whole(), whole(), whole(), whole(pltpu.HBM), whole(pltpu.HBM)],
-        out_specs=[whole()] * 4,
+        in_specs=[whole(pltpu.SMEM)] + [whole(pltpu.HBM)] * 4,
+        out_specs=[whole()] * 3,
         out_shape=[
+            jax.ShapeDtypeStruct((3, depth), jnp.float32),
             jax.ShapeDtypeStruct((count, lanes), jnp.bfloat16),
             jax.ShapeDtypeStruct((16, lanes), jnp.float32),
-            pltpu.VMEM(qkv.shape, qkv.dtype),
-            pltpu.VMEM(out.shape, out.dtype),
         ],
         scratch_shapes=[
+            pltpu.VMEM(table.shape, table.dtype),
+            pltpu.VMEM(cond.shape, cond.dtype),
+            pltpu.VMEM(w_embed.shape, w_embed.dtype),
+            pltpu.VMEM((tiles, 256, depth), qkv.dtype),
             pltpu.VMEM((count + 16, depth), jnp.bfloat16),
-            pltpu.SemaphoreType.DMA((tiles + 1,)),
+            pltpu.SemaphoreType.DMA((tiles + 3,)),
         ],
         cost_estimate=pl.CostEstimate(
-            flops=2 * count * depth * lanes,
-            bytes_accessed=2 * (qkv.size + out.size),
-            transcendentals=0,
+            flops=2 * count * depth * lanes, bytes_accessed=2 * qkv.size, transcendentals=0
         ),
-        compiler_params=kernel_params(),
-    )(w_embed, shift_row, scale_row, qkv, out)
-
-
-def attend(projected, stale_ref, attended):
+        compiler_params=kernel_params(24),
+    )(timestep, *in_hbm(table, cond, w_embed, qkv))
+
+
+def attend(projected, order_ref, stale_ref, attended):
     rows = projected.shape[0]
-    patch_rows = stale_ref.shape[0]
+    patch_rows = stale_ref.shape[1]
     lanes = attended.shape[1]
+    kept = order_ref[1]
 
     def micro_of(shape, dim):
-        return lax.broadcasted_iota(jnp.int32, shape, dim) // TOK_DEV % MICRO
+        patch = lax.broadcasted_iota(jnp.int32, shape, dim) // TOK_DEV % MICRO
+        return jnp.where(patch == kept, 1, 0)
 
     unseen = micro_of((rows, rows), 0) < micro_of((rows, rows), 1)
     late = micro_of((rows, patch_rows), 0) > 0
@@ -258,7 +287,7 @@
         value_part = slice(lanes + head * HEAD_DIM, lanes + (head + 1) * HEAD_DIM)
         fresh = lax.dot_general(queries, keys, NT, preferred_element_type=jnp.float32)
         stale = lax.dot_general(
-            queries, stale_ref[:, part], NT, preferred_element_type=jnp.float32
+            queries, stale_ref[kept, :, part], NT, preferred_element_type=jnp.float32
         )
         fresh = jnp.where(unseen, -jnp.inf, fresh * HEAD_DIM ** (-0.5))
         stale = jnp.where(late, -jnp.inf, stale * HEAD_DIM ** (-0.5))
@@ -272,7 +301,7 @@
         stale = (stale / total).astype(jnp.bfloat16)
         attended[:, part] = (
             jnp.dot(fresh, values, preferred_element_type=jnp.float32)
-            + jnp.dot(stale, stale_ref[:, value_part], preferred_element_type=jnp.float32)
+            + jnp.dot(stale, stale_ref[kept, :, value_part], preferred_element_type=jnp.float32)
         ).astype(jnp.bfloat16)
 
 
@@ -286,107 +315,186 @@
         ).astype(jnp.bfloat16)
 
 
-def first_layer_kernel(count, place_ref, embed_ref, heads_ref, term_ref, stale_ref, out_ref, *refs):
+def first_layer_kernel(
+    count, order_ref, embed_ref, heads_ref, term_ref, stale_ref, out_hbm, *refs
+):
     latent_refs, refs = refs[:count], refs[count:]
-    block_refs, own_ref, latents, attended = refs[:count], *refs[count:]
-    place = place_ref[0]
-    rows_dev = latent_refs[0].shape[0]
+    block_refs, own_ref, latents, attended, out_ref, sem = refs[:count], *refs[count:]
+    out_copy = pltpu.make_async_copy(out_hbm, out_ref, sem)
+    out_copy.start()
+    place = lax.axis_index("seq")
+    rows_dev = MICRO * TOK_DEV
     for k in range(count):
         first = pl.multiple_of((place ^ k) * rows_dev, rows_dev)
-        latents[pl.ds(first, rows_dev), :] = latent_refs[k][...]
+        latents[pl.ds(first, rows_dev), :] = (
+            latent_refs[k][...].reshape(rows_dev, latents.shape[1]).astype(jnp.bfloat16)
+        )
     embedded = jnp.dot(latents[...], embed_ref[...], preferred_element_type=jnp.float32)
     embedded = embedded.astype(jnp.bfloat16).astype(jnp.float32)
     norm = lax.rsqrt(jnp.mean(embedded * embedded, axis=-1, keepdims=True) + norm_eps)
     projected = jnp.dot(latents[...], heads_ref[...], preferred_element_type=jnp.float32)
     projected = (norm * projected + term_ref[:1]).astype(jnp.bfloat16)
-    attend(projected, stale_ref, attended)
-    column_blocks(place, attended, out_ref, block_refs)
+    attend(projected, order_ref, stale_ref, attended)
     columns = own_ref.shape[1]
     first = pl.multiple_of(place * columns, columns)
     own_ref[...] = jnp.dot(
         latents[...], embed_ref[:, pl.ds(first, columns)], preferred_element_type=jnp.float32
     ).astype(jnp.bfloat16)
-
-
-def first_layer(place, latent_pieces, w_embed, heads, term, stale, out):
+    out_copy.wait()
+    column_blocks(place, attended, out_ref, block_refs)
+
+
+def first_layer(patch_order, latent_pieces, w_embed, heads, term, stale, out):
     count = len(latent_pieces)
-    rows = count * latent_pieces[0].shape[0]
+    rows = count * MICRO * TOK_DEV
     lanes, depth = out.shape
     block = jax.ShapeDtypeStruct((rows, depth // count), jnp.bfloat16)
     return pl.pallas_call(
         functools.partial(first_layer_kernel, count),
-        in_specs=[whole(pltpu.SMEM)] + [whole()] * (5 + count),
+        in_specs=[whole(pltpu.SMEM)] + [whole()] * 4 + [whole(pltpu.HBM)] + [whole()] * count,
         out_specs=[whole()] * (count + 1),
         out_shape=[block] * (count + 1),
         scratch_shapes=[
             pltpu.VMEM((rows, w_embed.shape[0]), jnp.bfloat16),
             pltpu.VMEM((rows, lanes), jnp.bfloat16),
+            pltpu.VMEM(out.shape, out.dtype),
+            pltpu.SemaphoreType.DMA,
+        ],
+        compiler_params=kernel_params(12),
+    )(
+        patch_order,
+        w_embed,
+        heads,
+        term,
+        stale,
+        *in_hbm(out),
+        *latent_pieces,
+    )
+
+
+def fetch_kernel(qkv_hbm, out_hbm, after_ref, *refs):
+    block_refs, out_ref, done_ref, sems = refs[:-3], *refs[-3:]
+    count = len(block_refs)
+    place = lax.axis_index("seq")
+    copies = []
+    for k, block_ref in enumerate(block_refs):
+        columns = block_ref.shape[1]
+        first = pl.multiple_of((place ^ k) * columns, columns)
+        copies.append(
+            pltpu.make_async_copy(qkv_hbm.at[:, pl.ds(first, columns)], block_ref, sems.at[k])
+        )
+    copies.append(pltpu.make_async_copy(out_hbm, out_ref, sems.at[count]))
+    for _ in in_order(copies, len(copies)):
+        pass
+    done_ref[...] = jnp.zeros_like(done_ref)
+
+
+def fetched(count, qkv, out, after):
+    lanes, depth = qkv.shape
+    return pl.pallas_call(
+        fetch_kernel,
+        in_specs=[whole(pltpu.HBM)] * 2 + [whole(pl.ANY)],
+        out_specs=[whole()] * (count + 2),
+        out_shape=[pltpu.VMEM((lanes, depth // count), qkv.dtype)] * count
+        + [pltpu.VMEM(out.shape, out.dtype), jax.ShapeDtypeStruct((8, 128), jnp.float32)],
+        scratch_shapes=[pltpu.SemaphoreType.DMA((count + 1,))],
+        cost_estimate=pl.CostEstimate(
+            flops=0, bytes_accessed=2 * (qkv.size + out.size), transcendentals=0
+        ),
+        compiler_params=kernel_params(),
+    )(*in_hbm(qkv, out), after)
+
+
+def block_sum_kernel(rows_ref, own_ref, done_ref, *refs):
+    part_refs, block_ref = refs[:-1], refs[-1]
+    columns = own_ref.shape[1]
+    first = pl.multiple_of(lax.axis_index("seq") * columns, columns)
+    mixed = part_refs[0][...].astype(jnp.float32)
+    for part_ref in part_refs[1:]:
+        mixed = mixed + part_ref[...].astype(jnp.float32)
+    gate = rows_ref[2:3, pl.ds(first, columns)]
+    block_ref[...] = (own_ref[...].astype(jnp.float32) + gate * mixed).astype(jnp.bfloat16)
+
+
+def block_sum(mod_rows, own, done, parts):
+    return pl.pallas_call(
+        block_sum_kernel,
+        in_specs=[whole()] * (3 + len(parts)),
+        out_specs=whole(),
+        out_shape=jax.ShapeDtypeStruct(own.shape, own.dtype),
+        compiler_params=kernel_params(),
+    )(mod_rows, own, done, *parts)
+
+
+def scaled_piece(place, k, piece_ref, rows_ref):
+    columns = piece_ref.shape[1]
+    first = pl.multiple_of((place ^ k) * columns, columns)
+    wide = piece_ref[...].astype(jnp.float32)
+    scaled = (wide * rows_ref[1:2, pl.ds(first, columns)]).astype(jnp.bfloat16)
+    return scaled, jnp.sum(wide * wide, axis=-1, keepdims=True)
+
+
+TILE = 256
+
+
+def sums_kernel(numbers, rows_ref, *refs):
+    count = len(numbers)
+    piece_refs, weight_refs = refs[:count], refs[count : 2 * count]
+    earlier, (sums_ref, squares_ref) = refs[2 * count : -2], refs[-2:]
+    place = lax.axis_index("seq")
+    squares = earlier[1][...] if earlier else 0.0
+    scaled = []
+    for k, piece_ref in zip(numbers, piece_refs):
+        piece, square = scaled_piece(place, k, piece_ref, rows_ref)
+        scaled.append(piece)
+        squares = squares + square
+    squares_ref[...] = squares
+    for i in range(0, sums_ref.shape[1], TILE):
+        lane = slice(i, i + TILE)
+        total = earlier[0][:, lane] if earlier else 0.0
+        for piece, weight_ref in zip(scaled, weight_refs):
+            total = total + lax.dot_general(
+                piece, weight_ref[lane, :], NT, preferred_element_type=jnp.float32
+            )
+        sums_ref[:, lane] = total
+
+
+def in_vmem(*values):
+    return [pltpu.with_memory_space_constraint(value, pltpu.VMEM) for value in values]
+
+
+def product_sums(numbers, pieces, mod_rows, weights, earlier):
+    rows, columns = pieces[0].shape
+    lanes = weights[0].shape[0]
+    return pl.pallas_call(
+        functools.partial(sums_kernel, numbers),
+        in_specs=[whole()] * (1 + 2 * len(numbers) + len(earlier)),
+        out_specs=[whole()] * 2,
+        out_shape=[
+            jax.ShapeDtypeStruct((rows, lanes), jnp.float32),
+            jax.ShapeDtypeStruct((rows, 1), jnp.float32),
         ],
         compiler_params=kernel_params(),
-    )(place, w_embed, heads, term, stale, out, *latent_pieces)
-
-
-def add_products(place, numbers, piece_refs, scale_ref, qkv_ref, sums_ref, squares):
-    columns = piece_refs[0].shape[1]
-    scaled = []
-    for k, piece_ref in zip(numbers, piece_refs):
-        first = pl.multiple_of((place ^ k) * columns, columns)
-        wide = piece_ref[...].astype(jnp.float32)
-        squares = squares + jnp.sum(wide * wide, axis=-1, keepdims=True)
-        scaled.append(
-            (first, (wide * scale_ref[:, pl.ds(first, columns)]).astype(jnp.bfloat16))
-        )
-    for i in range(qkv_ref.shape[0] // 256):
-        part = slice(i * 256, (i + 1) * 256)
-        total = sums_ref[:, part]
-        for first, piece in scaled:
-            total = total + lax.dot_general(
-                piece, qkv_ref[part, pl.ds(first, columns)], NT, preferred_element_type=jnp.float32
-            )
-        sums_ref[:, part] = total
-    return squares
-
-
-def sums_kernel(numbers, place_ref, scale_ref, qkv_ref, sums_in, squares_in, *refs):
-    piece_refs, sums_ref, squares_ref = refs[: len(numbers)], *refs[len(numbers) :]
-    sums_ref[...] = sums_in[...]
-    squares_ref[...] = add_products(
-        place_ref[0], numbers, piece_refs, scale_ref, qkv_ref, sums_ref, squares_in[...]
-    )
-
-
-def product_sums(place, numbers, pieces, scale_row, qkv, sums, squares):
-    return pl.pallas_call(
-        functools.partial(sums_kernel, numbers),
-        in_specs=[whole(pltpu.SMEM)] + [whole()] * (4 + len(numbers)),
-        out_specs=[whole()] * 2,
-        out_shape=[
-            jax.ShapeDtypeStruct(sums.shape, sums.dtype),
-            jax.ShapeDtypeStruct(squares.shape, squares.dtype),
-        ],
-        compiler_params=kernel_params(),
-    )(place, scale_row, qkv, sums, squares, *pieces)
+    )(mod_rows, *pieces, *in_vmem(*weights), *earlier)
 
 
 def later_layer_kernel(
-    count, numbers, last, place_ref, scale_ref, qkv_ref, term_ref, stale_ref, out_ref, sums_in, squares_in, *refs
+    count, last, order_ref, rows_ref, qkv_ref, out_ref, term_ref, stale_ref, sums_ref, squares_ref, *refs
 ):
     piece_refs, refs = refs[:count], refs[count:]
     block_refs, own_ref, sums, attended, partial_out = refs[:count], *refs[count:]
-    place = place_ref[0]
-    sums[...] = sums_in[...]
-    squares = add_products(
-        place,
-        numbers,
-        [piece_refs[k] for k in numbers],
-        scale_ref,
-        qkv_ref,
-        sums,
-        squares_in[...],
-    )
-    norm = lax.rsqrt(squares / scale_ref.shape[1] + norm_eps)
-    projected = (norm * sums[...] + term_ref[:1]).astype(jnp.bfloat16)
-    attend(projected, stale_ref, attended)
+    place = lax.axis_index("seq")
+    scaled, squares = scaled_piece(place, count - 1, piece_refs[-1], rows_ref)
+    norm = lax.rsqrt((squares_ref[...] + squares) / rows_ref.shape[1] + norm_eps)
+    for i in range(0, sums.shape[1], TILE):
+        lane = slice(i, i + TILE)
+        product = lax.dot_general(
+            scaled, qkv_ref[lane, :], NT, preferred_element_type=jnp.float32
+        )
+        sums[:, lane] = (norm * (product + sums_ref[:, lane]) + term_ref[:1, lane]).astype(
+            jnp.bfloat16
+        )
+    attend(sums, order_ref, stale_ref, attended)
     if not last:
         column_blocks(place, attended, out_ref, block_refs)
         own_ref[...] = piece_refs[0][...]
@@ -404,24 +512,24 @@
         own_ref[:, pl.ds(first, columns)] = piece_refs[k][own_rows, :]
 
 
-def later_layer(place, numbers, last, pieces, scale_row, qkv, term, stale, out, sums, squares):
+def later_layer(last, patch_order, pieces, mod_rows, qkv_block, out, term, stale, sums, squares):
     count = len(pieces)
     rows, columns = pieces[0].shape
     lanes, depth = out.shape
     shape = (rows // count, depth) if last else (rows, columns)
     block = jax.ShapeDtypeStruct(shape, jnp.bfloat16)
     return pl.pallas_call(
-        functools.partial(later_layer_kernel, count, numbers, last),
+        functools.partial(later_layer_kernel, count, last),
         in_specs=[whole(pltpu.SMEM)] + [whole()] * (7 + count),
         out_specs=[whole()] * (count + 1),
         out_shape=[block] * (count + 1),
         scratch_shapes=[
-            pltpu.VMEM(sums.shape, jnp.float32),
+            pltpu.VMEM(sums.shape, jnp.bfloat16),
             pltpu.VMEM((rows, lanes), jnp.bfloat16),
             pltpu.VMEM((rows, depth), jnp.bfloat16),
         ],
         compiler_params=kernel_params(),
-    )(place, scale_row, qkv, term, stale, out, sums, squares, *pieces)
+    )(patch_order, mod_rows, *in_vmem(qkv_block, out), term, stale, sums, squares, *pieces)
 
 
 def shards(
@@ -443,98 +551,83 @@
     seq_index = lax.axis_index("seq")
     segment_index = lax.axis_index("segment")
     branch_index = lax.axis_index("cfg")
-    group_heads = HEADS // seq_count
-    lanes = group_heads * HEAD_DIM
     rows_dev = MICRO * TOK_DEV
-    rows = seq_count * rows_dev
-    patch_rows = seq_count * TOK_DEV
-    table_row = lax.dynamic_index_in_dim(mod_table, timestep[0], 0, keepdims=False).astype(
-        jnp.float32
-    )
-    modulation = table_row + cond_mod[0, 0]
-    shift_row = modulation[0]
-    scale_row = 1.0 + modulation[1]
-    gate_row = modulation[2]
-    flipped = patch_order[0] == 1
-
-    def micro_ordered(value):
-        return jnp.where(flipped, value[::-1], value)
 
     def within(k):
         return [(i, i ^ k) for i in range(seq_count)]
 
-    def seq_ordered(pieces):
-        stacked = jnp.stack(pieces)
-        return jnp.take(stacked, jnp.arange(seq_count) ^ seq_index, axis=0)
-
-    place = seq_index.astype(jnp.int32)[None]
-    own_latent = micro_ordered(latent).astype(jnp.bfloat16).reshape(rows_dev, -1)
-    latent_pieces = [own_latent] + [
-        lax.ppermute(own_latent, "seq", within(k)) for k in range(1, seq_count)
-    ]
-    head_embed, shift_term, qkv, out = prepared(
-        w_embed, shift_row[None], scale_row[None], w_qkv[0], w_out[0]
-    )
-    stale = jnp.where(flipped, stale_kv[0, 0, 0, 0], stale_kv[0, 0, 0, 1])
+    def spread(value):
+        return [value] + [lax.ppermute(value, "seq", within(k)) for k in range(1, seq_count)]
+
+    def returned(values):
+        return values[:1] + [
+            lax.ppermute(values[k], "seq", within(k)) for k in range(1, seq_count)
+        ]
+
+    latent_pieces = spread(latent)
+    mod_rows, head_embed, shift_term = prepared(
+        timestep, jnp.transpose(mod_table, (1, 0, 2)), jnp.transpose(cond_mod[0], (1, 0, 2)), w_embed, w_qkv[0]
+    )
+    stale = stale_kv[0, 0, 0]
     *blocks, own = first_layer(
-        place, latent_pieces, w_embed, head_embed, shift_term, stale, out
-    )
-    columns = D // seq_count
-    own_gate = lax.dynamic_slice_in_dim(gate_row, seq_index * columns, columns, 0)
+        patch_order, latent_pieces, w_embed, head_embed, shift_term, stale, w_out[0]
+    )
+    numbers = tuple(range(seq_count))
+    *qkv_blocks, out, done = fetched(seq_count, w_qkv[0], w_out[0], own)
     for step in range(1, segment_count):
-        mixed = blocks[0].astype(jnp.float32)
-        for k in range(1, seq_count):
-            mixed = mixed + lax.ppermute(blocks[k], "seq", within(k)).astype(jnp.float32)
-        block = (own.astype(jnp.float32) + own_gate * mixed).astype(jnp.bfloat16)
+        block = block_sum(mod_rows, own, done, returned(blocks))
         pieces = []
-        for k in range(seq_count):
+        for k in numbers:
             pairs = [
                 (i * segment_count + step - 1, (i ^ k) * segment_count + step)
                 for i in range(seq_count)
             ]
             pieces.append(lax.ppermute(block, ("seq", "segment"), pairs))
-        sums = jnp.zeros((rows, qkv.shape[0]), jnp.float32)
-        squares = jnp.zeros((rows, 1), jnp.float32)
-        numbers = tuple(range(seq_count))
-        half = seq_count // 2
+        half = (seq_count + 1) // 2
+        sums = ()
         for some in (numbers[:half], numbers[half:-1]):
             if some:
-                sums, squares = product_sums(
-                    place, some, [pieces[k] for k in some], scale_row[None], qkv, sums, squares
+                sums = product_sums(
+                    some,
+                    [pieces[k] for k in some],
+                    mod_rows,
+                    [qkv_blocks[k] for k in some],
+                    sums,
                 )
         *blocks, own = later_layer(
-            place,
-            numbers[-1:],
             step + 1 == segment_count,
+            patch_order,
             pieces,
-            scale_row[None],
-            qkv,
+            mod_rows,
+            qkv_blocks[-1],
+            out,
             shift_term,
             stale,
-            out,
-            sums,
-            squares,
-        )
-
-    mixed = blocks[0].astype(jnp.float32)
-    for k in range(1, seq_count):
-        mixed = mixed + lax.ppermute(blocks[k], "seq", within(k)).astype(jnp.float32)
-    final = (own.astype(jnp.float32) + gate_row * mixed).astype(jnp.bfloat16)
+            *sums,
+        )
+
+    blocks, latent_pieces, slab_rows, w_conv, w_final = lax.optimization_barrier(
+        (blocks, latent_pieces, slab_rows, w_conv, w_final)
+    )
+    mixed = sum(part.astype(jnp.float32) for part in returned(blocks))
+    final = (own.astype(jnp.float32) + mod_rows[2] * mixed).astype(jnp.bfloat16)
     predicted = jnp.dot(
         rms_scaled(final).astype(jnp.bfloat16), w_final, preferred_element_type=jnp.float32
     )
     term = jnp.where(branch_index == 0, 1.0 - guide_scale, guide_scale) * predicted
-    velocity_own = term + swapped(term, "cfg", 0)
-    hop = [(segment_count - 1, i) for i in range(segment_count - 1)]
-    for pair in hop:
-        moved = lax.ppermute(velocity_own, "segment", [pair])
-        velocity_own = jnp.where(segment_index == pair[1], moved, velocity_own)
-    velocity_own = micro_ordered(velocity_own.reshape(MICRO, TOK_DEV, -1))
-    stepped_own = (latent - velocity_own / SCHED_STEPS).astype(jnp.bfloat16)
-    stepped = seq_ordered(
-        [stepped_own]
-        + [lax.ppermute(stepped_own, "seq", within(k)) for k in range(1, seq_count)]
-    )
+    peers = ("seq", "segment", "cfg")
+    sizes = tuple(lax.axis_size(axis) for axis in peers)
+    terms = lax.all_to_all(
+        jnp.broadcast_to(term, sizes + term.shape).reshape(-1, term.shape[1]),
+        peers,
+        split_axis=0,
+        concat_axis=0,
+        tiled=True,
+    ).reshape(sizes + (MICRO, TOK_DEV, -1))
+    velocity = terms[:, -1, 0] + terms[:, -1, 1]
+    velocity_own = lax.dynamic_index_in_dim(velocity, seq_index, 0, keepdims=False)
+    latents = jnp.take(jnp.stack(latent_pieces), jnp.arange(seq_count) ^ seq_index, axis=0)
+    stepped = (latents - velocity / SCHED_STEPS).astype(jnp.bfloat16)
     stepped = jnp.transpose(stepped, (1, 0, 2, 3))
     decoded = decoder_input(stepped, w_conv, slab_rows, seq_index, seq_count)
     return (velocity_own, decoded)
@@ -594,6 +687,6 @@
         P(None, ("groups", "seq"), None),
         P(("groups", "seq"), None, None, None, ("segment", "cfg")),
     )
-    whole_groups = HEADS % mesh.shape["seq"] == 0 and mesh.shape["seq"] <= 8
+    whole_groups = 2 <= mesh.shape["seq"] <= 8
     program = shards if whole_groups else cycled_shards
     return jax.shard_map(program, mesh=mesh, in_specs=in_specs, out_specs=out_specs, check_vma=False)

time: 102 us -> 80.7 us (0.79)
  local copies, waits for them, and re-layouts: 23.2 us -> 3.23 us
  Pallas kernels: 20.3 us -> 28.8 us
  waiting for transfers between devices: 17.8 us -> 9.82 us
  other arithmetic: 5.8 us -> 3.39 us
  starting transfers between devices: 29.5 us -> 31.1 us
    unnamed x34 -> x16, local copies, waits for them, and re-layouts: 21.9 us -> 0.88 us
    ppermute x14 -> x9, waiting for transfers between devices: 17.8 us -> 6.73 us  [the longest x6 6.72 us: returned(): lax.ppermute(values[k], 'seq', within(k))]
    pallas_call x4 -> x6, Pallas kernels: 17.1 us -> 24.9 us  [the longest x1 10.4 us: prepared(): pl.pallas_call(prepare_kernel, in_specs=[whole(pltpu.SMEM)] + [whole(pltp...]
    all_to_all x0 -> x1, starting transfers between devices: none -> 5.66 us  [shards(): lax.all_to_all(jnp.broadcast_to(term, sizes + term.shape).reshape(-1, ter...]
    ppermute x14 -> x9, starting transfers between devices: 20.2 us -> 15.2 us  [the longest x6 9.55 us: returned(): lax.ppermute(values[k], 'seq', within(k))]
    all_to_all x0 -> x1, waiting for transfers between devices: none -> 3.09 us  [shards(): lax.all_to_all(jnp.broadcast_to(term, sizes + term.shape).reshape(-1, ter...]
    select_n x3 -> x1, other arithmetic: 1.04 us -> 0.01 us  [shards(): jnp.take(jnp.stack(latent_pieces), jnp.arange(seq_count) ^ seq_index, axi...]
  transfers between devices with their start and end apart: 18 -> 14, of which waited for: 7 -> 4; matrix products, arithmetic and copies ran while one was open for 3% -> 2% of each run, Pallas kernels for 13% -> 25%
where the time goes in v3:
time: 80.7 us; the launch traced here: 80.4 us
  starting transfers between devices  31.1 us (39%)
  Pallas kernels  28.8 us (36%)
  waiting for transfers between devices  9.82 us (12%)
  between operations  3.62 us (4%)
  other arithmetic  3.39 us (4%)
  local copies, waits for them, and re-layouts  3.23 us (4%)
    pallas_call x1, Pallas kernels, prepared(): pl.pallas_call(prepare_kernel, in_specs=[whole(pltpu.SMEM)] + [whole(pltp...  10.4 us
    ppermute x4, starting transfers between devices, shards(): pieces.append(lax.ppermute(block, ('seq', 'segment'), pairs))  10.2 us
    ppermute x6, starting transfers between devices, returned(): lax.ppermute(values[k], 'seq', within(k))  9.55 us
    ppermute x6, waiting for transfers between devices, returned(): lax.ppermute(values[k], 'seq', within(k))  6.72 us
    pallas_call x1, Pallas kernels, fetched(): pl.pallas_call(fetch_kernel, in_specs=[whole(pltpu.HBM)] * 2 + [whole(pl....  6.56 us
    ppermute x3, starting transfers between devices, spread(): lax.ppermute(value, 'seq', within(k))  5.68 us
    all_to_all x1, starting transfers between devices, shards(): lax.all_to_all(jnp.broadcast_to(term, sizes + term.shape).reshape(-1, ter...  5.66 us
    pallas_call x1, Pallas kernels, later_layer(): pl.pallas_call(functools.partial(later_layer_kernel, count, last), in_spe...  4.44 us
  transfers between devices with their start and end apart: 14, of which 4 were waited for; matrix products, arithmetic and copies ran while one was open for 2% of the time, Pallas kernels for 25%

profile of v3, /device:TPU:0, one launch (start us, length us, event | category | flops | bytes accessed | tf_op | source)
XLA Modules:
  0.0 80.4 jit_solution(2748785620864382809)
XLA Ops:
  0.6 3.1 %collective-permute-start = (f32[2,8,64]{2,1,0:T(8,128)}, f32[2,8,64]{2,1,0:T(8,128)S(1)}, u32[]{:S(2)}, u32[]{:S(2)}) collective-permute-start(f32[2,8,64]{2,1,0:T(8,128)} %refs_0_.1), channel_id=1, source_target_pairs={{0,4},{4,0},{8,12},{12,8},{1,5},{5,1},{9,13},{13,9},{2,6},{6,2},{1... | collective-permute-start | bytes 12296 | tf_op jit(solution)/shard_map/ppermute | solution.py:560
  3.7 2.6 %collective-permute-start.1 = (f32[2,8,64]{2,1,0:T(8,128)}, f32[2,8,64]{2,1,0:T(8,128)S(1)}, u32[]{:S(2)}, u32[]{:S(2)}) collective-permute-start(f32[2,8,64]{2,1,0:T(8,128)} %refs_0_.1), channel_id=1, source_target_pairs={{0,8},{4,12},{8,0},{12,4},{1,9},{5,13},{9,1},{13,5},{2,10},{6,14},... | collective-permute-start | bytes 12296 | tf_op jit(solution)/shard_map/ppermute | solution.py:560
  7.1 10.4 %shard_map.131 = (f32[3,3072]{1,0:T(4,128)S(1)}, bf16[64,2304]{1,0:T(8,128)(2,1)S(1)}, f32[16,2304]{1,0:T(8,128)S(1)}) custom-call(s32[1]{0:T(128)S(6)} %copy.21.timestep_ref, bf16[3,50,3072]{2,1,0:T(8,128)(2,1)} %bitcast.54, f32[3,1,3072]{2,1,0:T(1,128)} %bitcast.64, bf16[64,3072]{1,0:T(8,128)(2,1)} %embed_ref.1, bf16[2304,3072]{1,0:T(8,128)(2,1)} %bitcast.50), custom_call_target="tpu_custom_call" | custom-call | flops 905969664 | bytes 14155776 | tf_op jit(solution)/shard_map/pallas_call | solution.py:245
  17.7 3.9 %shard_map.132 = (bf16[64,768]{1,0:T(8,128)(2,1)S(1)}, bf16[64,768]{1,0:T(8,128)(2,1)S(1)}, bf16[64,768]{1,0:T(8,128)(2,1)S(1)}, bf16[64,768]{1,0:T(8,128)(2,1)S(1)}, bf16[64,768]{1,0:T(8,128)(2,1)S(1)}) custom-call(s32[2]{0:T(128)S(1)} %copy-done.4, bf16[64,3072]{1,0:T(8,128)(2,1)S(1)} %copy-done.1, bf16[64,2304]{1,0:T(8,128)(2,1)S(1)} %get-tuple-element.37.heads_ref, ...), custom_call_target="tpu_custom_call" | custom-call | tf_op jit(solution)/shard_map/pallas_call | solution.py:352
  21.6 1.0 %collective-permute-start.3 = (bf16[64,768]{1,0:T(8,128)(2,1)S(1)}, bf16[64,768]{1,0:T(8,128)(2,1)S(1)}, u32[]{:S(2)}, u32[]{:S(2)}) collective-permute-start(bf16[64,768]{1,0:T(8,128)(2,1)S(1)} %get-tuple-element.44), channel_id=1, source_target_pairs={{0,4},{4,0},{8,12},{12,8},{1,5},{5,1},{9,13},{13,9},{2,6},{6,2},{1... | collective-permute-start | bytes 294920 | tf_op jit(solution)/shard_map/ppermute | solution.py:564
  22.5 3.5 %collective-permute-start.4 = (bf16[64,768]{1,0:T(8,128)(2,1)S(1)}, bf16[64,768]{1,0:T(8,128)(2,1)S(1)}, u32[]{:S(2)}, u32[]{:S(2)}) collective-permute-start(bf16[64,768]{1,0:T(8,128)(2,1)S(1)} %get-tuple-element.45), channel_id=1, source_target_pairs={{0,8},{4,12},{8,0},{12,4},{1,9},{5,13},{9,1},{13,5},{2,10},{6,14},... | collective-permute-start | bytes 294920 | tf_op jit(solution)/shard_map/ppermute | solution.py:564
  26.0 6.6 %shard_map.133 = (bf16[2304,768]{1,0:T(8,128)(2,1)S(1)}, bf16[2304,768]{1,0:T(8,128)(2,1)S(1)}, bf16[2304,768]{1,0:T(8,128)(2,1)S(1)}, bf16[2304,768]{1,0:T(8,12...) custom-call(bf16[2304,3072]{1,0:T(8,128)(2,1)} %bitcast.51, bf16[768,3072]{1,0:T(8,128)(2,1)} %bitcast.53, ...), custom_call_target="tpu_custom_call" | custom-call | bytes 18874368 | tf_op jit(solution)/shard_map/pallas_call | solution.py:394
  33.0 3.4 %collective-permute-start.7 = (bf16[64,768]{1,0:T(8,128)(2,1)S(1)}, bf16[64,768]{1,0:T(8,128)(2,1)S(1)}, u32[]{:S(2)}, u32[]{:S(2)}) collective-permute-start(bf16[64,768]{1,0:T(8,128)(2,1)S(1)} %shard_map.134), channel_id=1, source_target_pairs={{0,2},{4,6},{8,10},{12,14},{1,3},{5,7},{9,11},{13,15},{16,18},{20,... | collective-permute-start | bytes 294920 | tf_op jit(solution)/shard_map/ppermute | solution.py:585
  36.4 2.3 %collective-permute-start.8 = (bf16[64,768]{1,0:T(8,128)(2,1)S(1)}, bf16[64,768]{1,0:T(8,128)(2,1)S(1)}, u32[]{:S(2)}, u32[]{:S(2)}) collective-permute-start(bf16[64,768]{1,0:T(8,128)(2,1)S(1)} %shard_map.134), channel_id=1, source_target_pairs={{0,6},{4,2},{8,14},{12,10},{1,7},{5,3},{9,15},{13,11},{16,22},{20,... | collective-permute-start | bytes 294920 | tf_op jit(solution)/shard_map/ppermute | solution.py:585
  38.8 2.3 %collective-permute-start.6 = (bf16[64,768]{1,0:T(8,128)(2,1)S(1)}, bf16[64,768]{1,0:T(8,128)(2,1)S(1)}, u32[]{:S(2)}, u32[]{:S(2)}) collective-permute-start(bf16[64,768]{1,0:T(8,128)(2,1)S(1)} %shard_map.134), channel_id=1, source_target_pairs={{0,10},{4,14},{8,2},{12,6},{1,11},{5,15},{9,3},{13,7},{16,26},{20,... | collective-permute-start | bytes 294920 | tf_op jit(solution)/shard_map/ppermute | solution.py:585
  41.1 2.2 %collective-permute-start.9 = (bf16[64,768]{1,0:T(8,128)(2,1)S(1)}, bf16[64,768]{1,0:T(8,128)(2,1)S(1)}, u32[]{:S(2)}, u32[]{:S(2)}) collective-permute-start(bf16[64,768]{1,0:T(8,128)(2,1)S(1)} %shard_map.134), channel_id=1, source_target_pairs={{0,14},{4,10},{8,6},{12,2},{1,15},{5,11},{9,7},{13,3},{16,30},{20,... | collective-permute-start | bytes 294920 | tf_op jit(solution)/shard_map/ppermute | solution.py:585
  43.3 2.2 %shard_map.135 = (f32[64,2304]{1,0:T(8,128)S(1)}, f32[64,1]{1,0:T(8,128)S(1)}) custom-call(f32[3,3072]{1,0:T(4,128)S(1)} %get-tuple-element.36.rows_ref, bf16[64,768]{1,0:T(8,128)(2,1)S(1)} %collective-permute-done.7.refs_0_, bf16[64,768]{1,0:T(8,128)(2,1)S(1)} %collective-permute-done.8.refs_1_, bf16[2304,768]{1,0:T(8,128)(2,1)S(1)} %get-tuple-element.48.refs_2_, ...), custom_call_target="tpu_custom_call" | custom-call | tf_op jit(solution)/shard_map/pallas_call | solution.py:469
  45.5 1.2 %shard_map.136 = (f32[64,2304]{1,0:T(8,128)S(1)}, f32[64,1]{1,0:T(8,128)S(1)}) custom-call(f32[3,3072]{1,0:T(4,128)S(1)} %get-tuple-element.36.rows_ref, bf16[64,768]{1,0:T(8,128)(2,1)S(1)} %collective-permute-done.6.refs_0_.refs_2_, bf16[2304,768]{1,0:T(8,128)(2,1)S(1)} %get-tuple-element.47.refs_1_, f32[64,2304]{1,0:T(8,128)S(1)} %get-tuple-element.50.refs_2_, ...), custom_call_target="tpu_custom_call" | custom-call | tf_op jit(solution)/shard_map/pallas_call | solution.py:469
  46.8 4.4 %shard_map.137 = (bf16[16,3072]{1,0:T(8,128)(2,1)S(1)}, bf16[16,3072]{1,0:T(8,128)(2,1)S(1)}, bf16[16,3072]{1,0:T(8,128)(2,1)S(1)}, bf16[16,3072]{1,0:T(8,128)(2,1)S(1)}, bf16[16,3072]{1,0:T(8,128)(2,1)S(1)}) custom-call(s32[2]{0:T(128)S(1)} %copy-done.4, f32[3,3072]{1,0:T(4,128)S(1)} %get-tuple-element.36.rows_ref, ...), custom_call_target="tpu_custom_call" | custom-call | tf_op jit(solution)/shard_map/pallas_call | solution.py:521
  51.2 2.7 %collective-permute-start.10 = (bf16[16,3072]{1,0:T(8,128)(2,1)S(1)}, bf16[16,3072]{1,0:T(8,128)(2,1)S(1)}, u32[]{:S(2)}, u32[]{:S(2)}) collective-permute-start(bf16[16,3072]{1,0:T(8,128)(2,1)S(1)} %get-tuple-element.60), channel_id=1, source_target_pairs={{0,4},{4,0},{8,12},{12,8},{1,5},{5,1},{9,13},{13,9},{2,6},{6,2},{1... | collective-permute-start | bytes 294920 | tf_op jit(solution)/shard_map/ppermute | solution.py:564
  54.0 2.4 %collective-permute-start.12 = (bf16[16,3072]{1,0:T(8,128)(2,1)S(1)}, bf16[16,3072]{1,0:T(8,128)(2,1)S(1)}, u32[]{:S(2)}, u32[]{:S(2)}) collective-permute-start(bf16[16,3072]{1,0:T(8,128)(2,1)S(1)} %get-tuple-element.62), channel_id=1, source_target_pairs={{0,12},{4,8},{8,4},{12,0},{1,13},{5,9},{9,5},{13,1},{2,14},{6,10},... | collective-permute-start | bytes 294920 | tf_op jit(solution)/shard_map/ppermute | solution.py:564
  56.7 6.0 %collective-permute-done.11 = bf16[16,3072]{1,0:T(8,128)(2,1)S(1)} collective-permute-done((bf16[16,3072]{1,0:T(8,128)(2,1)S(1)}, bf16[16,3072]{1,0:T(8,128)(2,1)S(1)}, u32[]{:S(2)}, u32[]{:S(2)}) %collective-permute-start.11) | collective-permute-done | bytes 98336 | tf_op jit(solution)/shard_map/ppermute | solution.py:564
  63.2 0.8 reshape.91
  64.0 5.7 %all-to-all-start = ((f32[16,1,1024]{2,1,0:T(1,128)}), f32[16,1,1024]{2,1,0:T(1,128)S(1)}, u32[]{:S(2)}, u32[]{:S(2)}) async-start(f32[16,1,1024]{2,1,0:T(1,128)} %reshape.91), calls=%async_computation | async-start | bytes 131072 | tf_op jit(solution)/shard_map/all_to_all | solution.py:620
  69.7 0.6 fusion.22
  72.8 0.7 iota_compare_fusion.4
  73.5 3.1 %all-to-all-done = f32[16,1,1024]{2,1,0:T(1,128)S(1)} async-done(((f32[16,1,1024]{2,1,0:T(1,128)}), f32[16,1,1024]{2,1,0:T(1,128)S(1)}, u32[]{:S(2)}, u32[]{:S(2)}) %all-to-all-start) | async-done | bytes 65568 | tf_op jit(solution)/shard_map/all_to_all | solution.py:620
  77.1 0.8 reduce
  79.1 0.7 broadcast_select_fusion
  (55 shorter events, 4.4 us)
Async XLA Ops:
  0.6 62.3 %copy-start = (bf16[3072,64]{0,1:T(8,128)(2,1)S(1)}, bf16[3072,64]{0,1:T(8,128)(2,1)}, u32[]{:S(2)}) copy-start(bf16[3072,64]{0,1:T(8,128)(2,1)} %param.19) | copy-start | bytes 1179652
  0.6 16.9 %collective-permute-start = (f32[2,8,64]{2,1,0:T(8,128)}, f32[2,8,64]{2,1,0:T(8,128)S(1)}, u32[]{:S(2)}, u32[]{:S(2)}) collective-permute-start(f32[2,8,64]{2,1,0:T(8,128)} %refs_0_.1), channel_id=1, source_target_pairs={{0,4},{4,0},{8,12},{12,8},{1,5},{5,1},{9,13},{13,9},{2,6},{6,2},{1... | collective-permute-start | bytes 12296 | tf_op jit(solution)/shard_map/ppermute | solution.py:560
  3.7 13.9 %collective-permute-start.1 = (f32[2,8,64]{2,1,0:T(8,128)}, f32[2,8,64]{2,1,0:T(8,128)S(1)}, u32[]{:S(2)}, u32[]{:S(2)}) collective-permute-start(f32[2,8,64]{2,1,0:T(8,128)} %refs_0_.1), channel_id=1, source_target_pairs={{0,8},{4,12},{8,0},{12,4},{1,9},{5,13},{9,1},{13,5},{2,10},{6,14},... | collective-permute-start | bytes 12296 | tf_op jit(solution)/shard_map/ppermute | solution.py:560
  6.3 11.3 %collective-permute-start.2 = (f32[2,8,64]{2,1,0:T(8,128)}, f32[2,8,64]{2,1,0:T(8,128)S(1)}, u32[]{:S(2)}, u32[]{:S(2)}) collective-permute-start(f32[2,8,64]{2,1,0:T(8,128)} %refs_0_.1), channel_id=1, source_target_pairs={{0,12},{4,8},{8,4},{12,0},{1,13},{5,9},{9,5},{13,1},{2,14},{6,10},... | collective-permute-start | bytes 12296 | tf_op jit(solution)/shard_map/ppermute | solution.py:560
  7.1 10.5 %copy-start.1 = (bf16[64,3072]{1,0:T(8,128)(2,1)S(1)}, bf16[64,3072]{1,0:T(8,128)(2,1)}, u32[]{:S(2)}) copy-start(bf16[64,3072]{1,0:T(8,128)(2,1)} %embed_ref.1) | copy-start | bytes 1179652
  7.1 10.5 %copy-start.2 = (bf16[1,1,1,2,32,1536]{5,4,3,2,1,0:T(8,128)(2,1)S(1)}, bf16[1,1,1,2,32,1536]{5,4,3,2,1,0:T(8,128)(2,1)}, u32[]{:S(2)}) copy-start(bf16[1,1,1,2,32,1536]{5,4,3,2,1,0:T(8,128)(2,1)} %param.18) | copy-start | bytes 589828
  7.1 10.5 %copy-start.3 = (f32[2,8,64]{2,1,0:T(8,128)S(1)}, f32[2,8,64]{2,1,0:T(8,128)}, u32[]{:S(2)}) copy-start(f32[2,8,64]{2,1,0:T(8,128)} %refs_0_.1) | copy-start | bytes 12292
  7.1 10.5 %copy-start.4 = (s32[2]{0:T(128)S(1)}, s32[2]{0:T(128)}, u32[]{:S(2)}) copy-start(s32[2]{0:T(128)} %order_ref.3) | copy-start | bytes 28
  21.6 11.0 %collective-permute-start.3 = (bf16[64,768]{1,0:T(8,128)(2,1)S(1)}, bf16[64,768]{1,0:T(8,128)(2,1)S(1)}, u32[]{:S(2)}, u32[]{:S(2)}) collective-permute-start(bf16[64,768]{1,0:T(8,128)(2,1)S(1)} %get-tuple-element.44), channel_id=1, source_target_pairs={{0,4},{4,0},{8,12},{12,8},{1,5},{5,1},{9,13},{13,9},{2,6},{6,2},{1... | collective-permute-start | bytes 294920 | tf_op jit(solution)/shard_map/ppermute | solution.py:564
  22.5 10.4 %collective-permute-start.4 = (bf16[64,768]{1,0:T(8,128)(2,1)S(1)}, bf16[64,768]{1,0:T(8,128)(2,1)S(1)}, u32[]{:S(2)}, u32[]{:S(2)}) collective-permute-start(bf16[64,768]{1,0:T(8,128)(2,1)S(1)} %get-tuple-element.45), channel_id=1, source_target_pairs={{0,8},{4,12},{8,0},{12,4},{1,9},{5,13},{9,1},{13,5},{2,10},{6,14},... | collective-permute-start | bytes 294920 | tf_op jit(solution)/shard_map/ppermute | solution.py:564
  26.0 6.9 %collective-permute-start.5 = (bf16[64,768]{1,0:T(8,128)(2,1)S(1)}, bf16[64,768]{1,0:T(8,128)(2,1)S(1)}, u32[]{:S(2)}, u32[]{:S(2)}) collective-permute-start(bf16[64,768]{1,0:T(8,128)(2,1)S(1)} %get-tuple-element.46), channel_id=1, source_target_pairs={{0,12},{4,8},{8,4},{12,0},{1,13},{5,9},{9,5},{13,1},{2,14},{6,10},... | collective-permute-start | bytes 294920 | tf_op jit(solution)/shard_map/ppermute | solution.py:564
  33.0 10.2 %collective-permute-start.7 = (bf16[64,768]{1,0:T(8,128)(2,1)S(1)}, bf16[64,768]{1,0:T(8,128)(2,1)S(1)}, u32[]{:S(2)}, u32[]{:S(2)}) collective-permute-start(bf16[64,768]{1,0:T(8,128)(2,1)S(1)} %shard_map.134), channel_id=1, source_target_pairs={{0,2},{4,6},{8,10},{12,14},{1,3},{5,7},{9,11},{13,15},{16,18},{20,... | collective-permute-start | bytes 294920 | tf_op jit(solution)/shard_map/ppermute | solution.py:585
  36.4 6.8 %collective-permute-start.8 = (bf16[64,768]{1,0:T(8,128)(2,1)S(1)}, bf16[64,768]{1,0:T(8,128)(2,1)S(1)}, u32[]{:S(2)}, u32[]{:S(2)}) collective-permute-start(bf16[64,768]{1,0:T(8,128)(2,1)S(1)} %shard_map.134), channel_id=1, source_target_pairs={{0,6},{4,2},{8,14},{12,10},{1,7},{5,3},{9,15},{13,11},{16,22},{20,... | collective-permute-start | bytes 294920 | tf_op jit(solution)/shard_map/ppermute | solution.py:585
  38.8 6.7 %collective-permute-start.6 = (bf16[64,768]{1,0:T(8,128)(2,1)S(1)}, bf16[64,768]{1,0:T(8,128)(2,1)S(1)}, u32[]{:S(2)}, u32[]{:S(2)}) collective-permute-start(bf16[64,768]{1,0:T(8,128)(2,1)S(1)} %shard_map.134), channel_id=1, source_target_pairs={{0,10},{4,14},{8,2},{12,6},{1,11},{5,15},{9,3},{13,7},{16,26},{20,... | collective-permute-start | bytes 294920 | tf_op jit(solution)/shard_map/ppermute | solution.py:585
  41.1 5.7 %collective-permute-start.9 = (bf16[64,768]{1,0:T(8,128)(2,1)S(1)}, bf16[64,768]{1,0:T(8,128)(2,1)S(1)}, u32[]{:S(2)}, u32[]{:S(2)}) collective-permute-start(bf16[64,768]{1,0:T(8,128)(2,1)S(1)} %shard_map.134), channel_id=1, source_target_pairs={{0,14},{4,10},{8,6},{12,2},{1,15},{5,11},{9,7},{13,3},{16,30},{20,... | collective-permute-start | bytes 294920 | tf_op jit(solution)/shard_map/ppermute | solution.py:585
  46.8 22.9 %copy-start.6 = (s32[4]{0:T(128)S(1)}, s32[4]{0:T(128)}, u32[]{:S(2)}) copy-start(s32[4]{0:T(128)} %param.23) | copy-start | bytes 52
  51.2 27.7 %copy-start.5 = (bf16[27,16,128]{2,1,0:T(8,128)(2,1)S(1)}, bf16[27,16,128]{2,1,0:T(8,128)(2,1)}, u32[]{:S(2)}) copy-start(bf16[27,16,128]{2,1,0:T(8,128)(2,1)} %param.20) | copy-start | bytes 331780
  51.2 5.5 %collective-permute-start.10 = (bf16[16,3072]{1,0:T(8,128)(2,1)S(1)}, bf16[16,3072]{1,0:T(8,128)(2,1)S(1)}, u32[]{:S(2)}, u32[]{:S(2)}) collective-permute-start(bf16[16,3072]{1,0:T(8,128)(2,1)S(1)} %get-tuple-element.60), channel_id=1, source_target_pairs={{0,4},{4,0},{8,12},{12,8},{1,5},{5,1},{9,13},{13,9},{2,6},{6,2},{1... | collective-permute-start | bytes 294920 | tf_op jit(solution)/shard_map/ppermute | solution.py:564
  53.9 8.8 %collective-permute-start.11 = (bf16[16,3072]{1,0:T(8,128)(2,1)S(1)}, bf16[16,3072]{1,0:T(8,128)(2,1)S(1)}, u32[]{:S(2)}, u32[]{:S(2)}) collective-permute-start(bf16[16,3072]{1,0:T(8,128)(2,1)S(1)} %get-tuple-element.61), channel_id=1, source_target_pairs={{0,8},{4,12},{8,0},{12,4},{1,9},{5,13},{9,1},{13,5},{2,10},{6,14},... | collective-permute-start | bytes 294920 | tf_op jit(solution)/shard_map/ppermute | solution.py:564
  54.0 8.7 %collective-permute-start.12 = (bf16[16,3072]{1,0:T(8,128)(2,1)S(1)}, bf16[16,3072]{1,0:T(8,128)(2,1)S(1)}, u32[]{:S(2)}, u32[]{:S(2)}) collective-permute-start(bf16[16,3072]{1,0:T(8,128)(2,1)S(1)} %get-tuple-element.62), channel_id=1, source_target_pairs={{0,12},{4,8},{8,4},{12,0},{1,13},{5,9},{9,5},{13,1},{2,14},{6,10},... | collective-permute-start | bytes 294920 | tf_op jit(solution)/shard_map/ppermute | solution.py:564
  64.0 12.6 %all-to-all-start = ((f32[16,1,1024]{2,1,0:T(1,128)}), f32[16,1,1024]{2,1,0:T(1,128)S(1)}, u32[]{:S(2)}, u32[]{:S(2)}) async-start(f32[16,1,1024]{2,1,0:T(1,128)} %reshape.91), calls=%async_computation | async-start | bytes 131072 | tf_op jit(solution)/shard_map/all_to_all | solution.py:620

commit v4 on v3

--- a/solution.py
+++ b/solution.py
@@ -198,11 +198,11 @@
 
 
 def prepare_kernel(
-    timestep_ref, table_hbm, cond_hbm, embed_hbm, qkv_hbm, rows_ref, heads_ref, term_ref, table, cond, embed, qkv, lhs, sems
+    timestep_ref, table_hbm, cond_hbm, embed_hbm, qkv_hbm, rows_ref, heads_ref, term_ref, table, cond, embed, qkv, sums, sems
 ):
-    tiles, tile = qkv.shape[:2]
+    blocks, lanes, width = qkv.shape
     small = [
-        pltpu.make_async_copy(source, target, sems.at[tiles + i])
+        pltpu.make_async_copy(source, target, sems.at[blocks + i])
         for i, (source, target) in enumerate(
             ((table_hbm, table), (cond_hbm, cond), (embed_hbm, embed))
         )
@@ -211,8 +211,10 @@
         copy.start()
     landed = in_order(
         [
-            pltpu.make_async_copy(qkv_hbm.at[pl.ds(i * tile, tile)], qkv.at[i], sems.at[i])
-            for i in range(tiles)
+            pltpu.make_async_copy(
+                qkv_hbm.at[:, pl.ds(i * width, width)], qkv.at[i], sems.at[i]
+            )
+            for i in range(blocks)
         ],
         4,
     )
@@ -225,13 +227,23 @@
         row = jnp.dot(chosen, table[j], preferred_element_type=jnp.float32)[:1]
         rows_ref[j : j + 1, :] = row + cond[j] + (1.0 if j == 1 else 0.0)
     count = embed.shape[0]
-    lhs[:count] = (embed[...].astype(jnp.float32) * rows_ref[1:2]).astype(jnp.bfloat16)
-    lhs[count:] = jnp.broadcast_to(rows_ref[0:1], (16, lhs.shape[1])).astype(jnp.bfloat16)
     for i in landed:
-        part = pl.ds(i * tile, tile)
-        product = lax.dot_general(lhs[...], qkv[i], NT, preferred_element_type=jnp.float32)
-        heads_ref[:, part] = product[:count].astype(jnp.bfloat16)
-        term_ref[:, part] = product[count:]
+        part = slice(i * width, (i + 1) * width)
+        scaled = (embed[:, part].astype(jnp.float32) * rows_ref[1:2, part]).astype(jnp.bfloat16)
+        shift = jnp.broadcast_to(rows_ref[0:1, part], (16, width)).astype(jnp.bfloat16)
+        lhs = jnp.concatenate([scaled, shift], axis=0)
+        for j in range(0, lanes, TILE):
+            lane = slice(j, j + TILE)
+            product = lax.dot_general(
+                lhs, qkv[i, lane, :], NT, preferred_element_type=jnp.float32
+            )
+            if i:
+                product = product + sums[:, lane]
+            if i + 1 < blocks:
+                sums[:, lane] = product
+            else:
+                heads_ref[:, lane] = product[:count].astype(jnp.bfloat16)
+                term_ref[:, lane] = product[count:]
 
 
 def in_hbm(*values):
@@ -241,7 +253,7 @@
 def prepared(timestep, table, cond, w_embed, qkv):
     count, depth = w_embed.shape
     lanes = qkv.shape[0]
-    tiles = lanes // 256
+    blocks = 6
     return pl.pallas_call(
         prepare_kernel,
         in_specs=[whole(pltpu.SMEM)] + [whole(pltpu.HBM)] * 4,
@@ -255,9 +267,9 @@
             pltpu.VMEM(table.shape, table.dtype),
             pltpu.VMEM(cond.shape, cond.dtype),
             pltpu.VMEM(w_embed.shape, w_embed.dtype),
-            pltpu.VMEM((tiles, 256, depth), qkv.dtype),
-            pltpu.VMEM((count + 16, depth), jnp.bfloat16),
-            pltpu.SemaphoreType.DMA((tiles + 3,)),
+            pltpu.VMEM((blocks, lanes, depth // blocks), qkv.dtype),
+            pltpu.VMEM((count + 16, lanes), jnp.float32),
+            pltpu.SemaphoreType.DMA((blocks + 3,)),
         ],
         cost_estimate=pl.CostEstimate(
             flops=2 * count * depth * lanes, bytes_accessed=2 * qkv.size, transcendentals=0
@@ -579,8 +591,9 @@
         pieces = []
         for k in numbers:
             pairs = [
-                (i * segment_count + step - 1, (i ^ k) * segment_count + step)
+                (i * segment_count + j, (i ^ k) * segment_count + (j + 1) % segment_count)
                 for i in range(seq_count)
+                for j in range(segment_count)
             ]
             pieces.append(lax.ppermute(block, ("seq", "segment"), pairs))
         half = (seq_count + 1) // 2

time: 80.7 us -> 75.1 us (0.931)
  starting transfers between devices: 31.1 us -> 26.1 us
  Pallas kernels: 28.8 us -> 25.7 us
  waiting for transfers between devices: 9.82 us -> 12.5 us
    ppermute x4, waiting for transfers between devices: 0.01 us -> 3.65 us  [shards(): pieces.append(lax.ppermute(block, ('seq', 'segment'), pairs))]
    ppermute x4, starting transfers between devices: 10.2 us -> 6.81 us  [shards(): pieces.append(lax.ppermute(block, ('seq', 'segment'), pairs))]
    pallas_call x1, Pallas kernels: 10.4 us -> 7.3 us  [prepared(): pl.pallas_call(prepare_kernel, in_specs=[whole(pltpu.SMEM)] + [whole(pltp...]
    ppermute x6, waiting for transfers between devices: 6.72 us -> 5.73 us  [returned(): lax.ppermute(values[k], 'seq', within(k))]
    all_to_all x1, starting transfers between devices: 5.66 us -> 4.7 us  [shards(): lax.all_to_all(jnp.broadcast_to(term, sizes + term.shape).reshape(-1, ter...]
  transfers between devices with their start and end apart: 14 -> 14, of which waited for: 4 -> 8; matrix products, arithmetic and copies ran while one was open for 2% -> 3% of each run, Pallas kernels for 25% -> 23%
where the time goes in v4:
time: 75.1 us; the launch traced here: 74.9 us
  starting transfers between devices  26.1 us (35%)
  Pallas kernels  25.7 us (34%)
  waiting for transfers between devices  12.5 us (17%)
  between operations  3.55 us (5%)
  other arithmetic  3.39 us (5%)
  local copies, waits for them, and re-layouts  3.22 us (4%)
    ppermute x6, starting transfers between devices, returned(): lax.ppermute(values[k], 'seq', within(k))  8.9 us
    pallas_call x1, Pallas kernels, prepared(): pl.pallas_call(prepare_kernel, in_specs=[whole(pltpu.SMEM)] + [whole(pltp...  7.3 us
    ppermute x4, starting transfers between devices, shards(): pieces.append(lax.ppermute(block, ('seq', 'segment'), pairs))  6.81 us
    pallas_call x1, Pallas kernels, fetched(): pl.pallas_call(fetch_kernel, in_specs=[whole(pltpu.HBM)] * 2 + [whole(pl....  6.56 us
    ppermute x6, waiting for transfers between devices, returned(): lax.ppermute(values[k], 'seq', within(k))  5.73 us
    ppermute x3, starting transfers between devices, spread(): lax.ppermute(value, 'seq', within(k))  5.68 us
    all_to_all x1, starting transfers between devices, shards(): lax.all_to_all(jnp.broadcast_to(term, sizes + term.shape).reshape(-1, ter...  4.7 us
    pallas_call x1, Pallas kernels, later_layer(): pl.pallas_call(functools.partial(later_layer_kernel, count, last), in_spe...  4.43 us
  transfers between devices with their start and end apart: 14, of which 8 were waited for; matrix products, arithmetic and copies ran while one was open for 3% of the time, Pallas kernels for 23%

profile of v4, /device:TPU:0, one launch (start us, length us, event | category | flops | bytes accessed | tf_op | source)
XLA Modules:
  0.0 74.9 jit_solution(2576048950356466218)
XLA Ops:
  0.6 3.1 %collective-permute-start = (f32[2,8,64]{2,1,0:T(8,128)}, f32[2,8,64]{2,1,0:T(8,128)S(1)}, u32[]{:S(2)}, u32[]{:S(2)}) collective-permute-start(f32[2,8,64]{2,1,0:T(8,128)} %refs_0_.1), channel_id=1, source_target_pairs={{0,4},{4,0},{8,12},{12,8},{1,5},{5,1},{9,13},{13,9},{2,6},{6,2},{1... | collective-permute-start | bytes 12296 | tf_op jit(solution)/shard_map/ppermute | solution.py:572
  3.7 2.6 %collective-permute-start.1 = (f32[2,8,64]{2,1,0:T(8,128)}, f32[2,8,64]{2,1,0:T(8,128)S(1)}, u32[]{:S(2)}, u32[]{:S(2)}) collective-permute-start(f32[2,8,64]{2,1,0:T(8,128)} %refs_0_.1), channel_id=1, source_target_pairs={{0,8},{4,12},{8,0},{12,4},{1,9},{5,13},{9,1},{13,5},{2,10},{6,14},... | collective-permute-start | bytes 12296 | tf_op jit(solution)/shard_map/ppermute | solution.py:572
  7.1 7.3 %shard_map.131 = (f32[3,3072]{1,0:T(4,128)S(1)}, bf16[64,2304]{1,0:T(8,128)(2,1)S(1)}, f32[16,2304]{1,0:T(8,128)S(1)}) custom-call(s32[1]{0:T(128)S(6)} %copy.21.timestep_ref, bf16[3,50,3072]{2,1,0:T(8,128)(2,1)} %bitcast.54, f32[3,1,3072]{2,1,0:T(1,128)} %bitcast.64, bf16[64,3072]{1,0:T(8,128)(2,1)} %embed_ref.1, bf16[2304,3072]{1,0:T(8,128)(2,1)} %bitcast.50), custom_call_target="tpu_custom_call" | custom-call | flops 905969664 | bytes 14155776 | tf_op jit(solution)/shard_map/pallas_call | solution.py:257
  14.5 3.9 %shard_map.132 = (bf16[64,768]{1,0:T(8,128)(2,1)S(1)}, bf16[64,768]{1,0:T(8,128)(2,1)S(1)}, bf16[64,768]{1,0:T(8,128)(2,1)S(1)}, bf16[64,768]{1,0:T(8,128)(2,1)S(1)}, bf16[64,768]{1,0:T(8,128)(2,1)S(1)}) custom-call(s32[2]{0:T(128)S(1)} %copy-done.4, bf16[64,3072]{1,0:T(8,128)(2,1)S(1)} %copy-done.1, bf16[64,2304]{1,0:T(8,128)(2,1)S(1)} %get-tuple-element.37.heads_ref, ...), custom_call_target="tpu_custom_call" | custom-call | tf_op jit(solution)/shard_map/pallas_call | solution.py:364
  18.4 1.0 %collective-permute-start.3 = (bf16[64,768]{1,0:T(8,128)(2,1)S(1)}, bf16[64,768]{1,0:T(8,128)(2,1)S(1)}, u32[]{:S(2)}, u32[]{:S(2)}) collective-permute-start(bf16[64,768]{1,0:T(8,128)(2,1)S(1)} %get-tuple-element.44), channel_id=1, source_target_pairs={{0,4},{4,0},{8,12},{12,8},{1,5},{5,1},{9,13},{13,9},{2,6},{6,2},{1... | collective-permute-start | bytes 294920 | tf_op jit(solution)/shard_map/ppermute | solution.py:576
  19.4 3.5 %collective-permute-start.4 = (bf16[64,768]{1,0:T(8,128)(2,1)S(1)}, bf16[64,768]{1,0:T(8,128)(2,1)S(1)}, u32[]{:S(2)}, u32[]{:S(2)}) collective-permute-start(bf16[64,768]{1,0:T(8,128)(2,1)S(1)} %get-tuple-element.45), channel_id=1, source_target_pairs={{0,8},{4,12},{8,0},{12,4},{1,9},{5,13},{9,1},{13,5},{2,10},{6,14},... | collective-permute-start | bytes 294920 | tf_op jit(solution)/shard_map/ppermute | solution.py:576
  22.9 6.6 %shard_map.133 = (bf16[2304,768]{1,0:T(8,128)(2,1)S(1)}, bf16[2304,768]{1,0:T(8,128)(2,1)S(1)}, bf16[2304,768]{1,0:T(8,128)(2,1)S(1)}, bf16[2304,768]{1,0:T(8,12...) custom-call(bf16[2304,3072]{1,0:T(8,128)(2,1)} %bitcast.51, bf16[768,3072]{1,0:T(8,128)(2,1)} %bitcast.53, ...), custom_call_target="tpu_custom_call" | custom-call | bytes 18874368 | tf_op jit(solution)/shard_map/pallas_call | solution.py:406
  29.9 1.6 %collective-permute-start.7 = (bf16[64,768]{1,0:T(8,128)(2,1)S(1)}, bf16[64,768]{1,0:T(8,128)(2,1)S(1)}, u32[]{:S(2)}, u32[]{:S(2)}) collective-permute-start(bf16[64,768]{1,0:T(8,128)(2,1)S(1)} %shard_map.134), channel_id=1, source_target_pairs={{0,2},{2,0},{4,6},{6,4},{8,10},{10,8},{12,14},{14,12},{1,3},{3,1},... | collective-permute-start | bytes 294920 | tf_op jit(solution)/shard_map/ppermute | solution.py:598
  31.5 1.6 %collective-permute-start.8 = (bf16[64,768]{1,0:T(8,128)(2,1)S(1)}, bf16[64,768]{1,0:T(8,128)(2,1)S(1)}, u32[]{:S(2)}, u32[]{:S(2)}) collective-permute-start(bf16[64,768]{1,0:T(8,128)(2,1)S(1)} %shard_map.134), channel_id=1, source_target_pairs={{0,6},{2,4},{4,2},{6,0},{8,14},{10,12},{12,10},{14,8},{1,7},{3,5},... | collective-permute-start | bytes 294920 | tf_op jit(solution)/shard_map/ppermute | solution.py:598
  33.0 3.4 %collective-permute-start.6 = (bf16[64,768]{1,0:T(8,128)(2,1)S(1)}, bf16[64,768]{1,0:T(8,128)(2,1)S(1)}, u32[]{:S(2)}, u32[]{:S(2)}) collective-permute-start(bf16[64,768]{1,0:T(8,128)(2,1)S(1)} %shard_map.134), channel_id=1, source_target_pairs={{0,10},{2,8},{4,14},{6,12},{8,2},{10,0},{12,6},{14,4},{1,11},{3,9}... | collective-permute-start | bytes 294920 | tf_op jit(solution)/shard_map/ppermute | solution.py:598
  36.7 0.8 %collective-permute-done.8.refs_1_ = bf16[64,768]{1,0:T(8,128)(2,1)S(1)} collective-permute-done((bf16[64,768]{1,0:T(8,128)(2,1)S(1)}, bf16[64,768]{1,0:T(8,128)(2,1)S(1)}, u32[]{:S(2)}, u32[]{:S(2)}) %collective-permute-start.8) | collective-permute-done | bytes 98336 | tf_op jit(solution)/shard_map/ppermute | solution.py:598
  37.5 2.2 %shard_map.135 = (f32[64,2304]{1,0:T(8,128)S(1)}, f32[64,1]{1,0:T(8,128)S(1)}) custom-call(f32[3,3072]{1,0:T(4,128)S(1)} %get-tuple-element.36.rows_ref, bf16[64,768]{1,0:T(8,128)(2,1)S(1)} %collective-permute-done.7.refs_0_, bf16[64,768]{1,0:T(8,128)(2,1)S(1)} %collective-permute-done.8.refs_1_, bf16[2304,768]{1,0:T(8,128)(2,1)S(1)} %get-tuple-element.48.refs_2_, ...), custom_call_target="tpu_custom_call" | custom-call | tf_op jit(solution)/shard_map/pallas_call | solution.py:481
  39.7 2.2 %collective-permute-done.6.refs_0_.refs_2_ = bf16[64,768]{1,0:T(8,128)(2,1)S(1)} collective-permute-done((bf16[64,768]{1,0:T(8,128)(2,1)S(1)}, bf16[64,768]{1,0:T(8,128)(2,1)S(1)}, u32[]{:S(2)}, u32[]{:S(2)}) %collective-permute-start.6) | collective-permute-done | bytes 98336 | tf_op jit(solution)/shard_map/ppermute | solution.py:598
  41.9 1.2 %shard_map.136 = (f32[64,2304]{1,0:T(8,128)S(1)}, f32[64,1]{1,0:T(8,128)S(1)}) custom-call(f32[3,3072]{1,0:T(4,128)S(1)} %get-tuple-element.36.rows_ref, bf16[64,768]{1,0:T(8,128)(2,1)S(1)} %collective-permute-done.6.refs_0_.refs_2_, bf16[2304,768]{1,0:T(8,128)(2,1)S(1)} %get-tuple-element.47.refs_1_, f32[64,2304]{1,0:T(8,128)S(1)} %get-tuple-element.50.refs_2_, ...), custom_call_target="tpu_custom_call" | custom-call | tf_op jit(solution)/shard_map/pallas_call | solution.py:481
  43.8 4.4 %shard_map.137 = (bf16[16,3072]{1,0:T(8,128)(2,1)S(1)}, bf16[16,3072]{1,0:T(8,128)(2,1)S(1)}, bf16[16,3072]{1,0:T(8,128)(2,1)S(1)}, bf16[16,3072]{1,0:T(8,128)(2,1)S(1)}, bf16[16,3072]{1,0:T(8,128)(2,1)S(1)}) custom-call(s32[2]{0:T(128)S(1)} %copy-done.4, f32[3,3072]{1,0:T(4,128)S(1)} %get-tuple-element.36.rows_ref, ...), custom_call_target="tpu_custom_call" | custom-call | tf_op jit(solution)/shard_map/pallas_call | solution.py:533
  48.3 0.8 %collective-permute-start.10 = (bf16[16,3072]{1,0:T(8,128)(2,1)S(1)}, bf16[16,3072]{1,0:T(8,128)(2,1)S(1)}, u32[]{:S(2)}, u32[]{:S(2)}) collective-permute-start(bf16[16,3072]{1,0:T(8,128)(2,1)S(1)} %get-tuple-element.60), channel_id=1, source_target_pairs={{0,4},{4,0},{8,12},{12,8},{1,5},{5,1},{9,13},{13,9},{2,6},{6,2},{1... | collective-permute-start | bytes 294920 | tf_op jit(solution)/shard_map/ppermute | solution.py:576
  49.1 2.5 %collective-permute-start.11 = (bf16[16,3072]{1,0:T(8,128)(2,1)S(1)}, bf16[16,3072]{1,0:T(8,128)(2,1)S(1)}, u32[]{:S(2)}, u32[]{:S(2)}) collective-permute-start(bf16[16,3072]{1,0:T(8,128)(2,1)S(1)} %get-tuple-element.61), channel_id=1, source_target_pairs={{0,8},{4,12},{8,0},{12,4},{1,9},{5,13},{9,1},{13,5},{2,10},{6,14},... | collective-permute-start | bytes 294920 | tf_op jit(solution)/shard_map/ppermute | solution.py:576
  51.6 1.1 %collective-permute-start.12 = (bf16[16,3072]{1,0:T(8,128)(2,1)S(1)}, bf16[16,3072]{1,0:T(8,128)(2,1)S(1)}, u32[]{:S(2)}, u32[]{:S(2)}) collective-permute-start(bf16[16,3072]{1,0:T(8,128)(2,1)S(1)} %get-tuple-element.62), channel_id=1, source_target_pairs={{0,12},{4,8},{8,4},{12,0},{1,13},{5,9},{9,5},{13,1},{2,14},{6,10},... | collective-permute-start | bytes 294920 | tf_op jit(solution)/shard_map/ppermute | solution.py:576
  52.7 0.8 %collective-permute-done.10 = bf16[16,3072]{1,0:T(8,128)(2,1)S(1)} collective-permute-done((bf16[16,3072]{1,0:T(8,128)(2,1)S(1)}, bf16[16,3072]{1,0:T(8,128)(2,1)S(1)}, u32[]{:S(2)}, u32[]{:S(2)}) %collective-permute-start.10) | collective-permute-done | bytes 98336 | tf_op jit(solution)/shard_map/ppermute | solution.py:576
  53.6 3.2 %collective-permute-done.11 = bf16[16,3072]{1,0:T(8,128)(2,1)S(1)} collective-permute-done((bf16[16,3072]{1,0:T(8,128)(2,1)S(1)}, bf16[16,3072]{1,0:T(8,128)(2,1)S(1)}, u32[]{:S(2)}, u32[]{:S(2)}) %collective-permute-start.11) | collective-permute-done | bytes 98336 | tf_op jit(solution)/shard_map/ppermute | solution.py:576
  56.8 1.3 %collective-permute-done.12 = bf16[16,3072]{1,0:T(8,128)(2,1)S(1)} collective-permute-done((bf16[16,3072]{1,0:T(8,128)(2,1)S(1)}, bf16[16,3072]{1,0:T(8,128)(2,1)S(1)}, u32[]{:S(2)}, u32[]{:S(2)}) %collective-permute-start.12) | collective-permute-done | bytes 98336 | tf_op jit(solution)/shard_map/ppermute | solution.py:576
  59.4 4.7 %all-to-all-start = ((f32[16,1,1024]{2,1,0:T(1,128)}), f32[16,1,1024]{2,1,0:T(1,128)S(1)}, u32[]{:S(2)}, u32[]{:S(2)}) async-start(f32[16,1,1024]{2,1,0:T(1,128)} %reshape.91), calls=%async_computation | async-start | bytes 131072 | tf_op jit(solution)/shard_map/all_to_all | solution.py:633
  67.9 3.1 %all-to-all-done = f32[16,1,1024]{2,1,0:T(1,128)S(1)} async-done(((f32[16,1,1024]{2,1,0:T(1,128)}), f32[16,1,1024]{2,1,0:T(1,128)S(1)}, u32[]{:S(2)}, u32[]{:S(2)}) %all-to-all-start) | async-done | bytes 65568 | tf_op jit(solution)/shard_map/all_to_all | solution.py:633
  71.5 0.8 %reduce = f32[16,1024]{1,0:T(8,128)S(1)} reduce(f32[16,1,1024]{2,1,0:T(1,128)S(1)} %all-to-all-done, f32[]{:T(128)} %broadcast.130), dimensions={1}, to_apply=%all_to_all.7.reduce_sub_computation | reduce | bytes 131076 | tf_op jit(solution)/shard_map/all_to_all | solution.py:633
  (55 shorter events, 7.7 us)
Async XLA Ops:
  0.6 57.7 %copy-start = (bf16[3072,64]{0,1:T(8,128)(2,1)S(1)}, bf16[3072,64]{0,1:T(8,128)(2,1)}, u32[]{:S(2)}) copy-start(bf16[3072,64]{0,1:T(8,128)(2,1)} %param.19) | copy-start | bytes 1179652
  0.6 13.8 %collective-permute-start = (f32[2,8,64]{2,1,0:T(8,128)}, f32[2,8,64]{2,1,0:T(8,128)S(1)}, u32[]{:S(2)}, u32[]{:S(2)}) collective-permute-start(f32[2,8,64]{2,1,0:T(8,128)} %refs_0_.1), channel_id=1, source_target_pairs={{0,4},{4,0},{8,12},{12,8},{1,5},{5,1},{9,13},{13,9},{2,6},{6,2},{1... | collective-permute-start | bytes 12296 | tf_op jit(solution)/shard_map/ppermute | solution.py:572
  3.7 10.7 %collective-permute-start.1 = (f32[2,8,64]{2,1,0:T(8,128)}, f32[2,8,64]{2,1,0:T(8,128)S(1)}, u32[]{:S(2)}, u32[]{:S(2)}) collective-permute-start(f32[2,8,64]{2,1,0:T(8,128)} %refs_0_.1), channel_id=1, source_target_pairs={{0,8},{4,12},{8,0},{12,4},{1,9},{5,13},{9,1},{13,5},{2,10},{6,14},... | collective-permute-start | bytes 12296 | tf_op jit(solution)/shard_map/ppermute | solution.py:572
  6.3 8.2 %collective-permute-start.2 = (f32[2,8,64]{2,1,0:T(8,128)}, f32[2,8,64]{2,1,0:T(8,128)S(1)}, u32[]{:S(2)}, u32[]{:S(2)}) collective-permute-start(f32[2,8,64]{2,1,0:T(8,128)} %refs_0_.1), channel_id=1, source_target_pairs={{0,12},{4,8},{8,4},{12,0},{1,13},{5,9},{9,5},{13,1},{2,14},{6,10},... | collective-permute-start | bytes 12296 | tf_op jit(solution)/shard_map/ppermute | solution.py:572
  7.1 7.4 %copy-start.1 = (bf16[64,3072]{1,0:T(8,128)(2,1)S(1)}, bf16[64,3072]{1,0:T(8,128)(2,1)}, u32[]{:S(2)}) copy-start(bf16[64,3072]{1,0:T(8,128)(2,1)} %embed_ref.1) | copy-start | bytes 1179652
  7.1 7.4 %copy-start.2 = (bf16[1,1,1,2,32,1536]{5,4,3,2,1,0:T(8,128)(2,1)S(1)}, bf16[1,1,1,2,32,1536]{5,4,3,2,1,0:T(8,128)(2,1)}, u32[]{:S(2)}) copy-start(bf16[1,1,1,2,32,1536]{5,4,3,2,1,0:T(8,128)(2,1)} %param.18) | copy-start | bytes 589828
  7.1 7.4 %copy-start.3 = (f32[2,8,64]{2,1,0:T(8,128)S(1)}, f32[2,8,64]{2,1,0:T(8,128)}, u32[]{:S(2)}) copy-start(f32[2,8,64]{2,1,0:T(8,128)} %refs_0_.1) | copy-start | bytes 12292
  7.1 7.4 %copy-start.4 = (s32[2]{0:T(128)S(1)}, s32[2]{0:T(128)}, u32[]{:S(2)}) copy-start(s32[2]{0:T(128)} %order_ref.3) | copy-start | bytes 28
  18.4 11.0 %collective-permute-start.3 = (bf16[64,768]{1,0:T(8,128)(2,1)S(1)}, bf16[64,768]{1,0:T(8,128)(2,1)S(1)}, u32[]{:S(2)}, u32[]{:S(2)}) collective-permute-start(bf16[64,768]{1,0:T(8,128)(2,1)S(1)} %get-tuple-element.44), channel_id=1, source_target_pairs={{0,4},{4,0},{8,12},{12,8},{1,5},{5,1},{9,13},{13,9},{2,6},{6,2},{1... | collective-permute-start | bytes 294920 | tf_op jit(solution)/shard_map/ppermute | solution.py:576
  19.4 10.4 %collective-permute-start.4 = (bf16[64,768]{1,0:T(8,128)(2,1)S(1)}, bf16[64,768]{1,0:T(8,128)(2,1)S(1)}, u32[]{:S(2)}, u32[]{:S(2)}) collective-permute-start(bf16[64,768]{1,0:T(8,128)(2,1)S(1)} %get-tuple-element.45), channel_id=1, source_target_pairs={{0,8},{4,12},{8,0},{12,4},{1,9},{5,13},{9,1},{13,5},{2,10},{6,14},... | collective-permute-start | bytes 294920 | tf_op jit(solution)/shard_map/ppermute | solution.py:576
  22.9 6.9 %collective-permute-start.5 = (bf16[64,768]{1,0:T(8,128)(2,1)S(1)}, bf16[64,768]{1,0:T(8,128)(2,1)S(1)}, u32[]{:S(2)}, u32[]{:S(2)}) collective-permute-start(bf16[64,768]{1,0:T(8,128)(2,1)S(1)} %get-tuple-element.46), channel_id=1, source_target_pairs={{0,12},{4,8},{8,4},{12,0},{1,13},{5,9},{9,5},{13,1},{2,14},{6,10},... | collective-permute-start | bytes 294920 | tf_op jit(solution)/shard_map/ppermute | solution.py:576
  29.9 6.8 %collective-permute-start.7 = (bf16[64,768]{1,0:T(8,128)(2,1)S(1)}, bf16[64,768]{1,0:T(8,128)(2,1)S(1)}, u32[]{:S(2)}, u32[]{:S(2)}) collective-permute-start(bf16[64,768]{1,0:T(8,128)(2,1)S(1)} %shard_map.134), channel_id=1, source_target_pairs={{0,2},{2,0},{4,6},{6,4},{8,10},{10,8},{12,14},{14,12},{1,3},{3,1},... | collective-permute-start | bytes 294920 | tf_op jit(solution)/shard_map/ppermute | solution.py:598
  31.5 6.0 %collective-permute-start.8 = (bf16[64,768]{1,0:T(8,128)(2,1)S(1)}, bf16[64,768]{1,0:T(8,128)(2,1)S(1)}, u32[]{:S(2)}, u32[]{:S(2)}) collective-permute-start(bf16[64,768]{1,0:T(8,128)(2,1)S(1)} %shard_map.134), channel_id=1, source_target_pairs={{0,6},{2,4},{4,2},{6,0},{8,14},{10,12},{12,10},{14,8},{1,7},{3,5},... | collective-permute-start | bytes 294920 | tf_op jit(solution)/shard_map/ppermute | solution.py:598
  33.0 8.9 %collective-permute-start.6 = (bf16[64,768]{1,0:T(8,128)(2,1)S(1)}, bf16[64,768]{1,0:T(8,128)(2,1)S(1)}, u32[]{:S(2)}, u32[]{:S(2)}) collective-permute-start(bf16[64,768]{1,0:T(8,128)(2,1)S(1)} %shard_map.134), channel_id=1, source_target_pairs={{0,10},{2,8},{4,14},{6,12},{8,2},{10,0},{12,6},{14,4},{1,11},{3,9}... | collective-permute-start | bytes 294920 | tf_op jit(solution)/shard_map/ppermute | solution.py:598
  36.4 7.4 %collective-permute-start.9 = (bf16[64,768]{1,0:T(8,128)(2,1)S(1)}, bf16[64,768]{1,0:T(8,128)(2,1)S(1)}, u32[]{:S(2)}, u32[]{:S(2)}) collective-permute-start(bf16[64,768]{1,0:T(8,128)(2,1)S(1)} %shard_map.134), channel_id=1, source_target_pairs={{0,14},{2,12},{4,10},{6,8},{8,6},{10,4},{12,2},{14,0},{1,15},{3,13... | collective-permute-start | bytes 294920 | tf_op jit(solution)/shard_map/ppermute | solution.py:598
  43.8 20.3 %copy-start.6 = (s32[4]{0:T(128)S(1)}, s32[4]{0:T(128)}, u32[]{:S(2)}) copy-start(s32[4]{0:T(128)} %param.23) | copy-start | bytes 52
  48.3 25.1 %copy-start.5 = (bf16[27,16,128]{2,1,0:T(8,128)(2,1)S(1)}, bf16[27,16,128]{2,1,0:T(8,128)(2,1)}, u32[]{:S(2)}) copy-start(bf16[27,16,128]{2,1,0:T(8,128)(2,1)} %param.20) | copy-start | bytes 331780
  48.3 5.3 %collective-permute-start.10 = (bf16[16,3072]{1,0:T(8,128)(2,1)S(1)}, bf16[16,3072]{1,0:T(8,128)(2,1)S(1)}, u32[]{:S(2)}, u32[]{:S(2)}) collective-permute-start(bf16[16,3072]{1,0:T(8,128)(2,1)S(1)} %get-tuple-element.60), channel_id=1, source_target_pairs={{0,4},{4,0},{8,12},{12,8},{1,5},{5,1},{9,13},{13,9},{2,6},{6,2},{1... | collective-permute-start | bytes 294920 | tf_op jit(solution)/shard_map/ppermute | solution.py:576
  49.1 7.7 %collective-permute-start.11 = (bf16[16,3072]{1,0:T(8,128)(2,1)S(1)}, bf16[16,3072]{1,0:T(8,128)(2,1)S(1)}, u32[]{:S(2)}, u32[]{:S(2)}) collective-permute-start(bf16[16,3072]{1,0:T(8,128)(2,1)S(1)} %get-tuple-element.61), channel_id=1, source_target_pairs={{0,8},{4,12},{8,0},{12,4},{1,9},{5,13},{9,1},{13,5},{2,10},{6,14},... | collective-permute-start | bytes 294920 | tf_op jit(solution)/shard_map/ppermute | solution.py:576
  51.6 6.5 %collective-permute-start.12 = (bf16[16,3072]{1,0:T(8,128)(2,1)S(1)}, bf16[16,3072]{1,0:T(8,128)(2,1)S(1)}, u32[]{:S(2)}, u32[]{:S(2)}) collective-permute-start(bf16[16,3072]{1,0:T(8,128)(2,1)S(1)} %get-tuple-element.62), channel_id=1, source_target_pairs={{0,12},{4,8},{8,4},{12,0},{1,13},{5,9},{9,5},{13,1},{2,14},{6,10},... | collective-permute-start | bytes 294920 | tf_op jit(solution)/shard_map/ppermute | solution.py:576
  59.4 11.6 %all-to-all-start = ((f32[16,1,1024]{2,1,0:T(1,128)}), f32[16,1,1024]{2,1,0:T(1,128)S(1)}, u32[]{:S(2)}, u32[]{:S(2)}) async-start(f32[16,1,1024]{2,1,0:T(1,128)} %reshape.91), calls=%async_computation | async-start | bytes 131072 | tf_op jit(solution)/shard_map/all_to_all | solution.py:633

commit v5 on v4

--- a/solution.py
+++ b/solution.py
@@ -278,42 +278,52 @@
     )(timestep, *in_hbm(table, cond, w_embed, qkv))
 
 
-def attend(projected, order_ref, stale_ref, attended):
+def span_of(rows, patch_rows):
+    return -(-(rows + patch_rows) // 128) * 128
+
+
+def attention_scratch(rows, patch_rows, lanes):
+    shape = (lanes // HEAD_DIM, span_of(rows, patch_rows), HEAD_DIM)
+    return [pltpu.VMEM((rows, lanes), jnp.bfloat16)] + [pltpu.VMEM(shape, jnp.bfloat16)] * 2
+
+
+def attend(projected, order_ref, stale_ref, attended, keys, values):
     rows = projected.shape[0]
     patch_rows = stale_ref.shape[1]
-    lanes = attended.shape[1]
+    heads, span, _ = keys.shape
     kept = order_ref[1]
-
-    def micro_of(shape, dim):
-        patch = lax.broadcasted_iota(jnp.int32, shape, dim) // TOK_DEV % MICRO
-        return jnp.where(patch == kept, 1, 0)
-
-    unseen = micro_of((rows, rows), 0) < micro_of((rows, rows), 1)
-    late = micro_of((rows, patch_rows), 0) > 0
-    for head in range(lanes // HEAD_DIM):
+    filled = rows + patch_rows
+
+    def micro_of(index):
+        return jnp.where(index // TOK_DEV % MICRO == kept, 1, 0)
+
+    query = micro_of(lax.broadcasted_iota(jnp.int32, (rows, span), 0))
+    column = lax.broadcasted_iota(jnp.int32, (rows, span), 1)
+    fresh_seen = (column < rows) & (query >= micro_of(column))
+    stale_seen = (column >= rows) & (column < filled) & (query == 0)
+    seen = fresh_seen | stale_seen
+    scores = []
+    for head in range(heads):
         first = 3 * HEAD_DIM * head
+        for j, buffer in enumerate((keys, values)):
+            lane = first + (j + 1) * HEAD_DIM
+            stale_lane = (j * heads + head) * HEAD_DIM
+            buffer[head, :rows] = projected[:, lane : lane + HEAD_DIM]
+            buffer[head, rows:filled] = stale_ref[kept, :, stale_lane : stale_lane + HEAD_DIM]
+            if filled < span:
+                buffer[head, filled:] = jnp.zeros((span - filled, HEAD_DIM), jnp.bfloat16)
         queries = projected[:, first : first + HEAD_DIM]
-        keys = projected[:, first + HEAD_DIM : first + 2 * HEAD_DIM]
-        values = projected[:, first + 2 * HEAD_DIM : first + 3 * HEAD_DIM]
-        part = slice(head * HEAD_DIM, (head + 1) * HEAD_DIM)
-        value_part = slice(lanes + head * HEAD_DIM, lanes + (head + 1) * HEAD_DIM)
-        fresh = lax.dot_general(queries, keys, NT, preferred_element_type=jnp.float32)
-        stale = lax.dot_general(
-            queries, stale_ref[kept, :, part], NT, preferred_element_type=jnp.float32
-        )
-        fresh = jnp.where(unseen, -jnp.inf, fresh * HEAD_DIM ** (-0.5))
-        stale = jnp.where(late, -jnp.inf, stale * HEAD_DIM ** (-0.5))
-        top = jnp.maximum(
-            jnp.max(fresh, axis=-1, keepdims=True), jnp.max(stale, axis=-1, keepdims=True)
-        )
-        fresh = jnp.exp(fresh - top)
-        stale = jnp.exp(stale - top)
-        total = jnp.sum(fresh, axis=-1, keepdims=True) + jnp.sum(stale, axis=-1, keepdims=True)
-        fresh = (fresh / total).astype(jnp.bfloat16)
-        stale = (stale / total).astype(jnp.bfloat16)
-        attended[:, part] = (
-            jnp.dot(fresh, values, preferred_element_type=jnp.float32)
-            + jnp.dot(stale, stale_ref[kept, :, value_part], preferred_element_type=jnp.float32)
+        scores.append(
+            lax.dot_general(queries, keys[head], NT, preferred_element_type=jnp.float32)
+        )
+    scores = [jnp.where(seen, score * HEAD_DIM ** (-0.5), -jnp.inf) for score in scores]
+    tops = [jnp.max(score, axis=-1, keepdims=True) for score in scores]
+    weights = [jnp.exp(score - top) for score, top in zip(scores, tops)]
+    totals = [jnp.sum(weight, axis=-1, keepdims=True) for weight in weights]
+    for head in range(heads):
+        probs = (weights[head] / totals[head]).astype(jnp.bfloat16)
+        attended[:, head * HEAD_DIM : (head + 1) * HEAD_DIM] = jnp.dot(
+            probs, values[head], preferred_element_type=jnp.float32
         ).astype(jnp.bfloat16)
 
 
@@ -331,7 +341,7 @@
     count, order_ref, embed_ref, heads_ref, term_ref, stale_ref, out_hbm, *refs
 ):
     latent_refs, refs = refs[:count], refs[count:]
-    block_refs, own_ref, latents, attended, out_ref, sem = refs[:count], *refs[count:]
+    block_refs, own_ref, latents, attended, keys, values, out_ref, sem = refs[:count], *refs[count:]
     out_copy = pltpu.make_async_copy(out_hbm, out_ref, sem)
     out_copy.start()
     place = lax.axis_index("seq")
@@ -346,7 +356,7 @@
     norm = lax.rsqrt(jnp.mean(embedded * embedded, axis=-1, keepdims=True) + norm_eps)
     projected = jnp.dot(latents[...], heads_ref[...], preferred_element_type=jnp.float32)
     projected = (norm * projected + term_ref[:1]).astype(jnp.bfloat16)
-    attend(projected, order_ref, stale_ref, attended)
+    attend(projected, order_ref, stale_ref, attended, keys, values)
     columns = own_ref.shape[1]
     first = pl.multiple_of(place * columns, columns)
     own_ref[...] = jnp.dot(
@@ -368,7 +378,7 @@
         out_shape=[block] * (count + 1),
         scratch_shapes=[
             pltpu.VMEM((rows, w_embed.shape[0]), jnp.bfloat16),
-            pltpu.VMEM((rows, lanes), jnp.bfloat16),
+            *attention_scratch(rows, stale.shape[1], lanes),
             pltpu.VMEM(out.shape, out.dtype),
             pltpu.SemaphoreType.DMA,
         ],
@@ -494,7 +504,7 @@
     count, last, order_ref, rows_ref, qkv_ref, out_ref, term_ref, stale_ref, sums_ref, squares_ref, *refs
 ):
     piece_refs, refs = refs[:count], refs[count:]
-    block_refs, own_ref, sums, attended, partial_out = refs[:count], *refs[count:]
+    block_refs, own_ref, sums, attended, keys, values, partial_out = refs[:count], *refs[count:]
     place = lax.axis_index("seq")
     scaled, squares = scaled_piece(place, count - 1, piece_refs[-1], rows_ref)
     norm = lax.rsqrt((squares_ref[...] + squares) / rows_ref.shape[1] + norm_eps)
@@ -506,7 +516,7 @@
         sums[:, lane] = (norm * (product + sums_ref[:, lane]) + term_ref[:1, lane]).astype(
             jnp.bfloat16
         )
-    attend(sums, order_ref, stale_ref, attended)
+    attend(sums, order_ref, stale_ref, attended, keys, values)
     if not last:
         column_blocks(place, attended, out_ref, block_refs)
         own_ref[...] = piece_refs[0][...]
@@ -537,11 +547,182 @@
         out_shape=[block] * (count + 1),
         scratch_shapes=[
             pltpu.VMEM(sums.shape, jnp.bfloat16),
-            pltpu.VMEM((rows, lanes), jnp.bfloat16),
+            *attention_scratch(rows, stale.shape[1], lanes),
             pltpu.VMEM((rows, depth), jnp.bfloat16),
         ],
         compiler_params=kernel_params(),
     )(patch_order, mod_rows, *in_vmem(qkv_block, out), term, stale, sums, squares, *pieces)
+
+
+def term_kernel(rows_ref, own_ref, final_ref, *refs):
+    part_refs, term_ref = refs[:-1], refs[-1]
+    mixed = part_refs[0][...].astype(jnp.float32)
+    for part_ref in part_refs[1:]:
+        mixed = mixed + part_ref[...].astype(jnp.float32)
+    hidden = (own_ref[...].astype(jnp.float32) + rows_ref[2:3] * mixed).astype(jnp.bfloat16)
+    predicted = lax.dot_general(
+        rms_scaled(hidden).astype(jnp.bfloat16),
+        final_ref[...],
+        NT,
+        preferred_element_type=jnp.float32,
+    )
+    weight = jnp.where(lax.axis_index("cfg") == 0, 1.0 - guide_scale, guide_scale)
+    patches = [predicted[i * TOK_DEV : (i + 1) * TOK_DEV] for i in range(MICRO)]
+    term = weight * jnp.concatenate(patches, axis=1)
+    term_ref[...] = jnp.broadcast_to(term, term_ref.shape)
+
+
+def velocity_terms(peers, mod_rows, own, final, parts):
+    shape = (peers, TOK_DEV, MICRO * final.shape[0])
+    return pl.pallas_call(
+        term_kernel,
+        in_specs=[whole()] * (3 + len(parts)),
+        out_specs=whole(),
+        out_shape=jax.ShapeDtypeStruct(shape, jnp.float32),
+        compiler_params=kernel_params(),
+    )(mod_rows, own, final, *parts)
+
+
+TAPS = 27
+TAP_GROUP = 4
+HALF = LAT_W // 2
+
+
+def window_kernel(sizes, slab_ref, conv_ref, chosen_ref, weights_ref):
+    seq_count, slab_most, token_rows = sizes
+    place = lax.axis_index("seq")
+    rows = seq_count * MICRO * TOK_DEV
+    start = 0
+    for j in range(seq_count - 1):
+        start = start + jnp.where(j < place, slab_ref[j], 0)
+    shape = (chosen_ref.shape[0], 2 * rows)
+    target = lax.broadcasted_iota(jnp.int32, shape, 0)
+    column = lax.broadcasted_iota(jnp.int32, shape, 1)
+    across = target % HALF
+    down = target // HALF % slab_most
+    frame = target // (HALF * slab_most)
+    kept = down < slab_ref[place]
+    patch_rows = seq_count * TOK_DEV
+    for tap in range(TAPS):
+        time, row_shift, token_shift = tap // 9, tap // 3 % 3, tap % 3
+        source_frame = jnp.maximum(frame + (time - 2), 0)
+        row = start + down + (row_shift - 1)
+        token = across + (token_shift - 1)
+        inside = kept & (row >= 0) & (row < 2 * token_rows) & (token >= 0) & (token < HALF)
+        row = jnp.maximum(row, 0)
+        index = (source_frame * token_rows + row // 2) * HALF + jnp.maximum(token, 0)
+        patch = index // patch_rows
+        slot = index % patch_rows
+        source = (slot // TOK_DEV * MICRO + patch) * TOK_DEV + slot % TOK_DEV + row % 2 * rows
+        chosen_ref[:, tap * 2 * rows : (tap + 1) * 2 * rows] = jnp.where(
+            inside & (column == source), 1.0, 0.0
+        ).astype(jnp.bfloat16)
+    chosen_ref[:, TAPS * 2 * rows :] = jnp.zeros(
+        (shape[0], chosen_ref.shape[1] - TAPS * 2 * rows), jnp.bfloat16
+    )
+    weights_ref[...] = jnp.zeros_like(weights_ref)
+    channels = conv_ref.shape[2]
+    for tap in range(TAPS):
+        for source in range(2):
+            for side in range(2):
+                shift = 2 * (tap % 3 - 1) + source - side + 1
+                if 0 <= shift < 3:
+                    first = (tap * 2 + source) * LAT_CH
+                    weights_ref[first : first + LAT_CH, side * channels : (side + 1) * channels] = (
+                        conv_ref[tap // 3 * 3 + shift]
+                    )
+
+
+def window_parts(seq_count, slab_most, token_rows, slab_rows, w_conv):
+    rows = seq_count * MICRO * TOK_DEV
+    groups = -(-TAPS // TAP_GROUP)
+    return pl.pallas_call(
+        functools.partial(window_kernel, (seq_count, slab_most, token_rows)),
+        in_specs=[whole(pltpu.SMEM), whole()],
+        out_specs=[whole()] * 2,
+        out_shape=[
+            jax.ShapeDtypeStruct(
+                (FRAMES * slab_most * HALF, groups * TAP_GROUP * 2 * rows), jnp.bfloat16
+            ),
+            jax.ShapeDtypeStruct(
+                (groups * TAP_GROUP * 2 * LAT_CH, 2 * w_conv.shape[2]), jnp.bfloat16
+            ),
+        ],
+        compiler_params=kernel_params(),
+    )(slab_rows, w_conv)
+
+
+def decode_kernel(segment_count, terms_ref, chosen_ref, weights_ref, *refs):
+    latent_refs, refs = refs[:-7], refs[-7:]
+    velocity_ref, decoded_ref, latents, tokens, halves, columns, features = refs
+    place = lax.axis_index("seq")
+    count = len(latent_refs)
+    for k in range(count):
+        latents[place ^ k] = latent_refs[k][...]
+
+    def velocity_of(z):
+        first = (z * segment_count + segment_count - 1) * 2
+        both = terms_ref[first] + terms_ref[first + 1]
+        width = both.shape[1] // MICRO
+        return [both[:, i * width : (i + 1) * width] for i in range(MICRO)]
+
+    for i, value in enumerate(velocity_of(place)):
+        velocity_ref[i] = value
+    for z in range(count):
+        stepped = [
+            latents[z, i] - value / SCHED_STEPS for i, value in enumerate(velocity_of(z))
+        ]
+        tokens[z * MICRO * TOK_DEV : (z + 1) * MICRO * TOK_DEV] = jnp.concatenate(
+            stepped, axis=0
+        ).astype(jnp.bfloat16)
+    rows, width = tokens.shape
+    half = width // 2
+    halves[...] = jnp.zeros_like(halves)
+    for j in range(TAP_GROUP):
+        for side in range(2):
+            first = (j * 2 + side) * rows
+            halves[first : first + rows, j * half : (j + 1) * half] = tokens[
+                :, side * half : (side + 1) * half
+            ]
+    depth, group_width = halves.shape
+    for group in range(chosen_ref.shape[1] // depth):
+        columns[:, group * group_width : (group + 1) * group_width] = jnp.dot(
+            chosen_ref[:, group * depth : (group + 1) * depth],
+            halves[...],
+            preferred_element_type=jnp.float32,
+        ).astype(jnp.bfloat16)
+    result = jnp.dot(columns[...], weights_ref[...], preferred_element_type=jnp.float32)
+    channels = features.shape[1]
+    for side in range(2):
+        features[pl.ds(side, result.shape[0], stride=2), :] = result[
+            :, side * channels : (side + 1) * channels
+        ]
+    decoded_ref[...] = features[...].astype(jnp.bfloat16)
+
+
+def decoded_slab(segment_count, terms, chosen, weights, latent_pieces):
+    count = len(latent_pieces)
+    rows = count * MICRO * TOK_DEV
+    width = latent_pieces[0].shape[-1]
+    targets = chosen.shape[0]
+    channels = weights.shape[1] // 2
+    return pl.pallas_call(
+        functools.partial(decode_kernel, segment_count),
+        in_specs=[whole()] * (3 + count),
+        out_specs=[whole()] * 2,
+        out_shape=[
+            jax.ShapeDtypeStruct(latent_pieces[0].shape, jnp.float32),
+            jax.ShapeDtypeStruct((2 * targets, channels), jnp.bfloat16),
+        ],
+        scratch_shapes=[
+            pltpu.VMEM((count,) + latent_pieces[0].shape, jnp.float32),
+            pltpu.VMEM((rows, width), jnp.bfloat16),
+            pltpu.VMEM((TAP_GROUP * 2 * rows, TAP_GROUP * width // 2), jnp.bfloat16),
+            pltpu.VMEM((targets, weights.shape[0]), jnp.bfloat16),
+            pltpu.VMEM((2 * targets, channels), jnp.float32),
+        ],
+        compiler_params=kernel_params(),
+    )(terms, chosen, weights, *latent_pieces)
 
 
 def shards(
@@ -560,10 +741,6 @@
 ):
     seq_count = lax.axis_size("seq")
     segment_count = lax.axis_size("segment")
-    seq_index = lax.axis_index("seq")
-    segment_index = lax.axis_index("segment")
-    branch_index = lax.axis_index("cfg")
-    rows_dev = MICRO * TOK_DEV
 
     def within(k):
         return [(i, i ^ k) for i in range(seq_count)]
@@ -619,31 +796,16 @@
             *sums,
         )
 
-    blocks, latent_pieces, slab_rows, w_conv, w_final = lax.optimization_barrier(
-        (blocks, latent_pieces, slab_rows, w_conv, w_final)
-    )
-    mixed = sum(part.astype(jnp.float32) for part in returned(blocks))
-    final = (own.astype(jnp.float32) + mod_rows[2] * mixed).astype(jnp.bfloat16)
-    predicted = jnp.dot(
-        rms_scaled(final).astype(jnp.bfloat16), w_final, preferred_element_type=jnp.float32
-    )
-    term = jnp.where(branch_index == 0, 1.0 - guide_scale, guide_scale) * predicted
+    blocks, slab_rows, w_conv = lax.optimization_barrier((blocks, slab_rows, w_conv))
+    token_rows = MICRO * seq_count * TOK_DEV // (FRAMES * HALF)
+    slab_most = 4 * token_rows // seq_count
+    chosen, weights = window_parts(seq_count, slab_most, token_rows, slab_rows, w_conv)
     peers = ("seq", "segment", "cfg")
-    sizes = tuple(lax.axis_size(axis) for axis in peers)
-    terms = lax.all_to_all(
-        jnp.broadcast_to(term, sizes + term.shape).reshape(-1, term.shape[1]),
-        peers,
-        split_axis=0,
-        concat_axis=0,
-        tiled=True,
-    ).reshape(sizes + (MICRO, TOK_DEV, -1))
-    velocity = terms[:, -1, 0] + terms[:, -1, 1]
-    velocity_own = lax.dynamic_index_in_dim(velocity, seq_index, 0, keepdims=False)
-    latents = jnp.take(jnp.stack(latent_pieces), jnp.arange(seq_count) ^ seq_index, axis=0)
-    stepped = (latents - velocity / SCHED_STEPS).astype(jnp.bfloat16)
-    stepped = jnp.transpose(stepped, (1, 0, 2, 3))
-    decoded = decoder_input(stepped, w_conv, slab_rows, seq_index, seq_count)
-    return (velocity_own, decoded)
+    peer_count = seq_count * segment_count * lax.axis_size("cfg")
+    terms = velocity_terms(peer_count, mod_rows, own, w_final.T, returned(blocks))
+    terms = lax.all_to_all(terms, peers, split_axis=0, concat_axis=0, tiled=True)
+    velocity, decoded = decoded_slab(segment_count, terms, chosen, weights, latent_pieces)
+    return (velocity, decoded.reshape(1, FRAMES, slab_most, LAT_W, w_conv.shape[2]))
 
 
 def decoder_input(stepped, w_conv, slab_rows, seq_index, seq_count):

time: 75.1 us -> 71.1 us (0.947)
  Pallas kernels: 25.7 us -> 29.1 us
  other arithmetic: 3.39 us -> 0 us
  local copies, waits for them, and re-layouts: 3.22 us -> 0.03 us
  between operations: 3.55 us -> 1.46 us
  waiting for transfers between devices: 12.5 us -> 14.2 us
    pallas_call x0 -> x3, Pallas kernels: none -> 4.38 us  [the longest x1 2.08 us: window_parts(): pl.pallas_call(functools.partial(window_kernel, (seq_count, slab_most, to...]
    all_to_all x1, waiting for transfers between devices: 3.09 us -> 4.79 us  [shards(): lax.all_to_all(terms, peers, split_axis=0, concat_axis=0, tiled=True)]
    pallas_call x1, Pallas kernels: 4.43 us -> 3.16 us  [later_layer(): pl.pallas_call(functools.partial(later_layer_kernel, count, last), in_spe...]
    unnamed x16 -> x14, local copies, waits for them, and re-layouts: 0.88 us -> 0.03 us
    reduce_sum x2 -> x0, other arithmetic: 0.83 us -> none  [the longest x1 0.64 us: decoder_input(): slab_count = jnp.sum(jnp.where(positions == seq_index, slab_rows, 0))]
    all_to_all x1 -> x0, other arithmetic: 0.8 us -> none  [shards(): lax.all_to_all(jnp.broadcast_to(term, sizes + term.shape).reshape(-1, ter...]
  transfers between devices with their start and end apart: 14 -> 14, of which waited for: 8 -> 8; matrix products, arithmetic and copies ran while one was open for 3% -> 0% of each run, Pallas kernels for 23% -> 27%
where the time goes in v5:
time: 71.1 us; the launch traced here: 70.8 us
  Pallas kernels  29.1 us (41%)
  starting transfers between devices  26 us (37%)
  waiting for transfers between devices  14.2 us (20%)
  between operations  1.46 us (2%)
    ppermute x6, starting transfers between devices, returned(): lax.ppermute(values[k], 'seq', within(k))  8.91 us
    pallas_call x1, Pallas kernels, prepared(): pl.pallas_call(prepare_kernel, in_specs=[whole(pltpu.SMEM)] + [whole(pltp...  7.29 us
    ppermute x4, starting transfers between devices, shards(): pieces.append(lax.ppermute(block, ('seq', 'segment'), pairs))  6.81 us
    pallas_call x1, Pallas kernels, fetched(): pl.pallas_call(fetch_kernel, in_specs=[whole(pltpu.HBM)] * 2 + [whole(pl....  6.55 us
    ppermute x6, waiting for transfers between devices, returned(): lax.ppermute(values[k], 'seq', within(k))  5.8 us
    ppermute x3, starting transfers between devices, spread(): lax.ppermute(value, 'seq', within(k))  5.68 us
    all_to_all x1, waiting for transfers between devices, shards(): lax.all_to_all(terms, peers, split_axis=0, concat_axis=0, tiled=True)  4.79 us
    all_to_all x1, starting transfers between devices, shards(): lax.all_to_all(terms, peers, split_axis=0, concat_axis=0, tiled=True)  4.65 us
  transfers between devices with their start and end apart: 14, of which 8 were waited for; matrix products, arithmetic and copies ran while one was open for 0% of the time, Pallas kernels for 27%

profile of v5, /device:TPU:0, one launch (start us, length us, event | category | flops | bytes accessed | tf_op | source)
XLA Modules:
  0.0 70.8 jit_solution(11028901534514720361)
XLA Ops:
  0.6 3.1 %collective-permute-start = (f32[2,8,64]{2,1,0:T(8,128)}, f32[2,8,64]{2,1,0:T(8,128)S(1)}, u32[]{:S(2)}, u32[]{:S(2)}) collective-permute-start(f32[2,8,64]{2,1,0:T(8,128)} %refs_0_.3), channel_id=1, source_target_pairs={{0,4},{4,0},{8,12},{12,8},{1,5},{5,1},{9,13},{13,9},{2,6},{6,2},{1... | collective-permute-start | bytes 12296 | tf_op jit(solution)/shard_map/ppermute | solution.py:749
  3.7 2.6 %collective-permute-start.1 = (f32[2,8,64]{2,1,0:T(8,128)}, f32[2,8,64]{2,1,0:T(8,128)S(1)}, u32[]{:S(2)}, u32[]{:S(2)}) collective-permute-start(f32[2,8,64]{2,1,0:T(8,128)} %refs_0_.3), channel_id=1, source_target_pairs={{0,8},{4,12},{8,0},{12,4},{1,9},{5,13},{9,1},{13,5},{2,10},{6,14},... | collective-permute-start | bytes 12296 | tf_op jit(solution)/shard_map/ppermute | solution.py:749
  7.0 7.3 %shard_map.131 = (f32[3,3072]{1,0:T(4,128)S(1)}, bf16[64,2304]{1,0:T(8,128)(2,1)S(1)}, f32[16,2304]{1,0:T(8,128)S(1)}) custom-call(s32[1]{0:T(128)S(6)} %copy.14.timestep_ref, bf16[3,50,3072]{2,1,0:T(8,128)(2,1)} %bitcast.14, f32[3,1,3072]{2,1,0:T(1,128)} %bitcast.15, bf16[64,3072]{1,0:T(8,128)(2,1)} %embed_ref.1, bf16[2304,3072]{1,0:T(8,128)(2,1)} %bitcast.10), custom_call_target="tpu_custom_call" | custom-call | flops 905969664 | bytes 14155776 | tf_op jit(solution)/shard_map/pallas_call | solution.py:257
  14.4 4.2 %shard_map.132 = (bf16[64,768]{1,0:T(8,128)(2,1)S(1)}, bf16[64,768]{1,0:T(8,128)(2,1)S(1)}, bf16[64,768]{1,0:T(8,128)(2,1)S(1)}, bf16[64,768]{1,0:T(8,128)(2,1)S(1)}, bf16[64,768]{1,0:T(8,128)(2,1)S(1)}) custom-call(s32[2]{0:T(128)S(1)} %copy-done.5, bf16[64,3072]{1,0:T(8,128)(2,1)S(1)} %copy-done, bf16[64,2304]{1,0:T(8,128)(2,1)S(1)} %get-tuple-element.36.heads_ref, ...), custom_call_target="tpu_custom_call" | custom-call | tf_op jit(solution)/shard_map/pallas_call | solution.py:374
  18.6 1.0 %collective-permute-start.3 = (bf16[64,768]{1,0:T(8,128)(2,1)S(1)}, bf16[64,768]{1,0:T(8,128)(2,1)S(1)}, u32[]{:S(2)}, u32[]{:S(2)}) collective-permute-start(bf16[64,768]{1,0:T(8,128)(2,1)S(1)} %get-tuple-element.43), channel_id=1, source_target_pairs={{0,4},{4,0},{8,12},{12,8},{1,5},{5,1},{9,13},{13,9},{2,6},{6,2},{1... | collective-permute-start | bytes 294920 | tf_op jit(solution)/shard_map/ppermute | solution.py:753
  19.5 3.5 %collective-permute-start.4 = (bf16[64,768]{1,0:T(8,128)(2,1)S(1)}, bf16[64,768]{1,0:T(8,128)(2,1)S(1)}, u32[]{:S(2)}, u32[]{:S(2)}) collective-permute-start(bf16[64,768]{1,0:T(8,128)(2,1)S(1)} %get-tuple-element.44), channel_id=1, source_target_pairs={{0,8},{4,12},{8,0},{12,4},{1,9},{5,13},{9,1},{13,5},{2,10},{6,14},... | collective-permute-start | bytes 294920 | tf_op jit(solution)/shard_map/ppermute | solution.py:753
  23.0 6.5 %shard_map.133 = (bf16[2304,768]{1,0:T(8,128)(2,1)S(1)}, bf16[2304,768]{1,0:T(8,128)(2,1)S(1)}, bf16[2304,768]{1,0:T(8,128)(2,1)S(1)}, bf16[2304,768]{1,0:T(8,12...) custom-call(bf16[2304,3072]{1,0:T(8,128)(2,1)} %bitcast.11, bf16[768,3072]{1,0:T(8,128)(2,1)} %bitcast.13, ...), custom_call_target="tpu_custom_call" | custom-call | bytes 18874368 | tf_op jit(solution)/shard_map/pallas_call | solution.py:416
  30.0 1.6 %collective-permute-start.7 = (bf16[64,768]{1,0:T(8,128)(2,1)S(1)}, bf16[64,768]{1,0:T(8,128)(2,1)S(1)}, u32[]{:S(2)}, u32[]{:S(2)}) collective-permute-start(bf16[64,768]{1,0:T(8,128)(2,1)S(1)} %shard_map.134), channel_id=1, source_target_pairs={{0,2},{2,0},{4,6},{6,4},{8,10},{10,8},{12,14},{14,12},{1,3},{3,1},... | collective-permute-start | bytes 294920 | tf_op jit(solution)/shard_map/ppermute | solution.py:775
  31.6 1.6 %collective-permute-start.8 = (bf16[64,768]{1,0:T(8,128)(2,1)S(1)}, bf16[64,768]{1,0:T(8,128)(2,1)S(1)}, u32[]{:S(2)}, u32[]{:S(2)}) collective-permute-start(bf16[64,768]{1,0:T(8,128)(2,1)S(1)} %shard_map.134), channel_id=1, source_target_pairs={{0,6},{2,4},{4,2},{6,0},{8,14},{10,12},{12,10},{14,8},{1,7},{3,5},... | collective-permute-start | bytes 294920 | tf_op jit(solution)/shard_map/ppermute | solution.py:775
  33.2 3.4 %collective-permute-start.6 = (bf16[64,768]{1,0:T(8,128)(2,1)S(1)}, bf16[64,768]{1,0:T(8,128)(2,1)S(1)}, u32[]{:S(2)}, u32[]{:S(2)}) collective-permute-start(bf16[64,768]{1,0:T(8,128)(2,1)S(1)} %shard_map.134), channel_id=1, source_target_pairs={{0,10},{2,8},{4,14},{6,12},{8,2},{10,0},{12,6},{14,4},{1,11},{3,9}... | collective-permute-start | bytes 294920 | tf_op jit(solution)/shard_map/ppermute | solution.py:775
  37.6 2.2 %shard_map.135 = (f32[64,2304]{1,0:T(8,128)S(1)}, f32[64,1]{1,0:T(8,128)S(1)}) custom-call(f32[3,3072]{1,0:T(4,128)S(1)} %get-tuple-element.35.rows_ref, bf16[64,768]{1,0:T(8,128)(2,1)S(1)} %collective-permute-done.7.refs_0_, bf16[64,768]{1,0:T(8,128)(2,1)S(1)} %collective-permute-done.8.refs_1_, bf16[2304,768]{1,0:T(8,128)(2,1)S(1)} %get-tuple-element.47.refs_2_, ...), custom_call_target="tpu_custom_call" | custom-call | tf_op jit(solution)/shard_map/pallas_call | solution.py:491
  39.9 2.2 %collective-permute-done.6.refs_0_.refs_2_ = bf16[64,768]{1,0:T(8,128)(2,1)S(1)} collective-permute-done((bf16[64,768]{1,0:T(8,128)(2,1)S(1)}, bf16[64,768]{1,0:T(8,128)(2,1)S(1)}, u32[]{:S(2)}, u32[]{:S(2)}) %collective-permute-start.6) | collective-permute-done | bytes 98336 | tf_op jit(solution)/shard_map/ppermute | solution.py:775
  42.1 1.2 %shard_map.136 = (f32[64,2304]{1,0:T(8,128)S(1)}, f32[64,1]{1,0:T(8,128)S(1)}) custom-call(f32[3,3072]{1,0:T(4,128)S(1)} %get-tuple-element.35.rows_ref, bf16[64,768]{1,0:T(8,128)(2,1)S(1)} %collective-permute-done.6.refs_0_.refs_2_, bf16[2304,768]{1,0:T(8,128)(2,1)S(1)} %get-tuple-element.46.refs_1_, f32[64,2304]{1,0:T(8,128)S(1)} %get-tuple-element.49.refs_2_, ...), custom_call_target="tpu_custom_call" | custom-call | tf_op jit(solution)/shard_map/pallas_call | solution.py:491
  43.9 3.2 %shard_map.137 = (bf16[16,3072]{1,0:T(8,128)(2,1)S(1)}, bf16[16,3072]{1,0:T(8,128)(2,1)S(1)}, bf16[16,3072]{1,0:T(8,128)(2,1)S(1)}, bf16[16,3072]{1,0:T(8,128)(2,1)S(1)}, bf16[16,3072]{1,0:T(8,128)(2,1)S(1)}) custom-call(s32[2]{0:T(128)S(1)} %copy-done.5, f32[3,3072]{1,0:T(4,128)S(1)} %get-tuple-element.35.rows_ref, ...), custom_call_target="tpu_custom_call" | custom-call | tf_op jit(solution)/shard_map/pallas_call | solution.py:543
  47.1 0.9 %collective-permute-start.10 = (bf16[16,3072]{1,0:T(8,128)(2,1)S(1)}, bf16[16,3072]{1,0:T(8,128)(2,1)S(1)}, u32[]{:S(2)}, u32[]{:S(2)}) collective-permute-start(bf16[16,3072]{1,0:T(8,128)(2,1)S(1)} %get-tuple-element.59), channel_id=1, source_target_pairs={{0,4},{4,0},{8,12},{12,8},{1,5},{5,1},{9,13},{13,9},{2,6},{6,2},{1... | collective-permute-start | bytes 294920 | tf_op jit(solution)/shard_map/ppermute | solution.py:753
  48.0 2.5 %collective-permute-start.11 = (bf16[16,3072]{1,0:T(8,128)(2,1)S(1)}, bf16[16,3072]{1,0:T(8,128)(2,1)S(1)}, u32[]{:S(2)}, u32[]{:S(2)}) collective-permute-start(bf16[16,3072]{1,0:T(8,128)(2,1)S(1)} %get-tuple-element.60), channel_id=1, source_target_pairs={{0,8},{4,12},{8,0},{12,4},{1,9},{5,13},{9,1},{13,5},{2,10},{6,14},... | collective-permute-start | bytes 294920 | tf_op jit(solution)/shard_map/ppermute | solution.py:753
  50.5 1.1 %collective-permute-start.12 = (bf16[16,3072]{1,0:T(8,128)(2,1)S(1)}, bf16[16,3072]{1,0:T(8,128)(2,1)S(1)}, u32[]{:S(2)}, u32[]{:S(2)}) collective-permute-start(bf16[16,3072]{1,0:T(8,128)(2,1)S(1)} %get-tuple-element.61), channel_id=1, source_target_pairs={{0,12},{4,8},{8,4},{12,0},{1,13},{5,9},{9,5},{13,1},{2,14},{6,10},... | collective-permute-start | bytes 294920 | tf_op jit(solution)/shard_map/ppermute | solution.py:753
  52.4 3.3 %collective-permute-done.11.refs_2_ = bf16[16,3072]{1,0:T(8,128)(2,1)S(1)} collective-permute-done((bf16[16,3072]{1,0:T(8,128)(2,1)S(1)}, bf16[16,3072]{1,0:T(8,128)(2,1)S(1)}, u32[]{:S(2)}, u32[]{:S(2)}) %collective-permute-start.11) | collective-permute-done | bytes 98336 | tf_op jit(solution)/shard_map/ppermute | solution.py:753
  55.7 1.3 %collective-permute-done.12.refs_3_ = bf16[16,3072]{1,0:T(8,128)(2,1)S(1)} collective-permute-done((bf16[16,3072]{1,0:T(8,128)(2,1)S(1)}, bf16[16,3072]{1,0:T(8,128)(2,1)S(1)}, u32[]{:S(2)}, u32[]{:S(2)}) %collective-permute-start.12) | collective-permute-done | bytes 98336 | tf_op jit(solution)/shard_map/ppermute | solution.py:753
  57.0 1.1 %shard_map.138 = f32[16,8,128]{2,1,0:T(8,128)} custom-call(f32[3,3072]{1,0:T(4,128)S(1)} %get-tuple-element.35.rows_ref, bf16[16,3072]{1,0:T(8,128)(2,1)S(1)} %get-tuple-element.53.own_ref, bf16[64,3072]{1,0:T(8,128)(2,1)S(1)} %bitcast.9, bf16[16,3072]{1,0:T(8,128)(2,1)S(1)} %get-tuple-element.58.refs_0_, ...), custom_call_target="tpu_custom_call" | custom-call | tf_op jit(solution)/shard_map/pallas_call | solution.py:577
  58.1 4.6 %all-to-all-start = ((f32[16,8,128]{2,1,0:T(8,128)}), f32[16,8,128]{2,1,0:T(8,128)S(1)}, u32[]{:S(2)}, u32[]{:S(2)}) async-start(f32[16,8,128]{2,1,0:T(8,128)} %shard_map.138), calls=%async_computation | async-start | bytes 131072 | tf_op jit(solution)/shard_map/all_to_all | solution.py:806
  62.7 2.1 %shard_map.139 = (bf16[64,3584]{1,0:T(8,128)(2,1)S(1)}, bf16[896,256]{1,0:T(8,128)(2,1)S(1)}) custom-call(s32[4]{0:T(128)S(1)} %copy-done.6, bf16[27,16,128]{2,1,0:T(8,128)(2,1)S(1)} %copy-done.3), custom_call_target="tpu_custom_call" | custom-call | tf_op jit(solution)/shard_map/pallas_call | solution.py:639
  64.8 4.8 %all-to-all-done.terms_ref = f32[16,8,128]{2,1,0:T(8,128)S(1)} async-done(((f32[16,8,128]{2,1,0:T(8,128)}), f32[16,8,128]{2,1,0:T(8,128)S(1)}, u32[]{:S(2)}, u32[]{:S(2)}) %all-to-all-start) | async-done | bytes 65568 | tf_op jit(solution)/shard_map/all_to_all | solution.py:806
  69.6 1.2 %shard_map.140 = (f32[2,8,64]{2,1,0:T(8,128)}, bf16[128,128]{1,0:T(8,128)(2,1)}) custom-call(f32[16,8,128]{2,1,0:T(8,128)S(1)} %all-to-all-done.terms_ref, bf16[64,3584]{1,0:T(8,128)(2,1)S(1)} %get-tuple-element.64.chosen_ref, bf16[896,256]{1,0:T(8,128)(2,1)S(1)} %get-tuple-element.65.weights_ref, f32[2,8,64]{2,1,0:T(8,128)S(1)} %copy-done.4, ...), custom_call_target="tpu_custom_call" | custom-call | tf_op jit(solution)/shard_map/pallas_call | solution.py:709
  (28 shorter events, 3.1 us)
Async XLA Ops:
  0.6 13.7 %collective-permute-start = (f32[2,8,64]{2,1,0:T(8,128)}, f32[2,8,64]{2,1,0:T(8,128)S(1)}, u32[]{:S(2)}, u32[]{:S(2)}) collective-permute-start(f32[2,8,64]{2,1,0:T(8,128)} %refs_0_.3), channel_id=1, source_target_pairs={{0,4},{4,0},{8,12},{12,8},{1,5},{5,1},{9,13},{13,9},{2,6},{6,2},{1... | collective-permute-start | bytes 12296 | tf_op jit(solution)/shard_map/ppermute | solution.py:749
  3.7 10.6 %collective-permute-start.1 = (f32[2,8,64]{2,1,0:T(8,128)}, f32[2,8,64]{2,1,0:T(8,128)S(1)}, u32[]{:S(2)}, u32[]{:S(2)}) collective-permute-start(f32[2,8,64]{2,1,0:T(8,128)} %refs_0_.3), channel_id=1, source_target_pairs={{0,8},{4,12},{8,0},{12,4},{1,9},{5,13},{9,1},{13,5},{2,10},{6,14},... | collective-permute-start | bytes 12296 | tf_op jit(solution)/shard_map/ppermute | solution.py:749
  6.3 8.0 %collective-permute-start.2 = (f32[2,8,64]{2,1,0:T(8,128)}, f32[2,8,64]{2,1,0:T(8,128)S(1)}, u32[]{:S(2)}, u32[]{:S(2)}) collective-permute-start(f32[2,8,64]{2,1,0:T(8,128)} %refs_0_.3), channel_id=1, source_target_pairs={{0,12},{4,8},{8,4},{12,0},{1,13},{5,9},{9,5},{13,1},{2,14},{6,10},... | collective-permute-start | bytes 12296 | tf_op jit(solution)/shard_map/ppermute | solution.py:749
  7.0 7.4 %copy-start = (bf16[64,3072]{1,0:T(8,128)(2,1)S(1)}, bf16[64,3072]{1,0:T(8,128)(2,1)}, u32[]{:S(2)}) copy-start(bf16[64,3072]{1,0:T(8,128)(2,1)} %embed_ref.1) | copy-start | bytes 1179652
  7.0 7.4 %copy-start.1 = (bf16[1,1,1,2,32,1536]{5,4,3,2,1,0:T(8,128)(2,1)S(1)}, bf16[1,1,1,2,32,1536]{5,4,3,2,1,0:T(8,128)(2,1)}, u32[]{:S(2)}) copy-start(bf16[1,1,1,2,32,1536]{5,4,3,2,1,0:T(8,128)(2,1)} %param.18) | copy-start | bytes 589828
  7.0 7.4 %copy-start.4 = (f32[2,8,64]{2,1,0:T(8,128)S(1)}, f32[2,8,64]{2,1,0:T(8,128)}, u32[]{:S(2)}) copy-start(f32[2,8,64]{2,1,0:T(8,128)} %refs_0_.3) | copy-start | bytes 12292
  7.0 7.4 %copy-start.5 = (s32[2]{0:T(128)S(1)}, s32[2]{0:T(128)}, u32[]{:S(2)}) copy-start(s32[2]{0:T(128)} %order_ref.3) | copy-start | bytes 28
  18.6 11.0 %collective-permute-start.3 = (bf16[64,768]{1,0:T(8,128)(2,1)S(1)}, bf16[64,768]{1,0:T(8,128)(2,1)S(1)}, u32[]{:S(2)}, u32[]{:S(2)}) collective-permute-start(bf16[64,768]{1,0:T(8,128)(2,1)S(1)} %get-tuple-element.43), channel_id=1, source_target_pairs={{0,4},{4,0},{8,12},{12,8},{1,5},{5,1},{9,13},{13,9},{2,6},{6,2},{1... | collective-permute-start | bytes 294920 | tf_op jit(solution)/shard_map/ppermute | solution.py:753
  19.5 10.4 %collective-permute-start.4 = (bf16[64,768]{1,0:T(8,128)(2,1)S(1)}, bf16[64,768]{1,0:T(8,128)(2,1)S(1)}, u32[]{:S(2)}, u32[]{:S(2)}) collective-permute-start(bf16[64,768]{1,0:T(8,128)(2,1)S(1)} %get-tuple-element.44), channel_id=1, source_target_pairs={{0,8},{4,12},{8,0},{12,4},{1,9},{5,13},{9,1},{13,5},{2,10},{6,14},... | collective-permute-start | bytes 294920 | tf_op jit(solution)/shard_map/ppermute | solution.py:753
  23.0 6.9 %collective-permute-start.5 = (bf16[64,768]{1,0:T(8,128)(2,1)S(1)}, bf16[64,768]{1,0:T(8,128)(2,1)S(1)}, u32[]{:S(2)}, u32[]{:S(2)}) collective-permute-start(bf16[64,768]{1,0:T(8,128)(2,1)S(1)} %get-tuple-element.45), channel_id=1, source_target_pairs={{0,12},{4,8},{8,4},{12,0},{1,13},{5,9},{9,5},{13,1},{2,14},{6,10},... | collective-permute-start | bytes 294920 | tf_op jit(solution)/shard_map/ppermute | solution.py:753
  30.0 6.8 %collective-permute-start.7 = (bf16[64,768]{1,0:T(8,128)(2,1)S(1)}, bf16[64,768]{1,0:T(8,128)(2,1)S(1)}, u32[]{:S(2)}, u32[]{:S(2)}) collective-permute-start(bf16[64,768]{1,0:T(8,128)(2,1)S(1)} %shard_map.134), channel_id=1, source_target_pairs={{0,2},{2,0},{4,6},{6,4},{8,10},{10,8},{12,14},{14,12},{1,3},{3,1},... | collective-permute-start | bytes 294920 | tf_op jit(solution)/shard_map/ppermute | solution.py:775
  31.6 6.0 %collective-permute-start.8 = (bf16[64,768]{1,0:T(8,128)(2,1)S(1)}, bf16[64,768]{1,0:T(8,128)(2,1)S(1)}, u32[]{:S(2)}, u32[]{:S(2)}) collective-permute-start(bf16[64,768]{1,0:T(8,128)(2,1)S(1)} %shard_map.134), channel_id=1, source_target_pairs={{0,6},{2,4},{4,2},{6,0},{8,14},{10,12},{12,10},{14,8},{1,7},{3,5},... | collective-permute-start | bytes 294920 | tf_op jit(solution)/shard_map/ppermute | solution.py:775
  33.2 8.9 %collective-permute-start.6 = (bf16[64,768]{1,0:T(8,128)(2,1)S(1)}, bf16[64,768]{1,0:T(8,128)(2,1)S(1)}, u32[]{:S(2)}, u32[]{:S(2)}) collective-permute-start(bf16[64,768]{1,0:T(8,128)(2,1)S(1)} %shard_map.134), channel_id=1, source_target_pairs={{0,10},{2,8},{4,14},{6,12},{8,2},{10,0},{12,6},{14,4},{1,11},{3,9}... | collective-permute-start | bytes 294920 | tf_op jit(solution)/shard_map/ppermute | solution.py:775
  36.5 7.4 %collective-permute-start.9 = (bf16[64,768]{1,0:T(8,128)(2,1)S(1)}, bf16[64,768]{1,0:T(8,128)(2,1)S(1)}, u32[]{:S(2)}, u32[]{:S(2)}) collective-permute-start(bf16[64,768]{1,0:T(8,128)(2,1)S(1)} %shard_map.134), channel_id=1, source_target_pairs={{0,14},{2,12},{4,10},{6,8},{8,6},{10,4},{12,2},{14,0},{1,15},{3,13... | collective-permute-start | bytes 294920 | tf_op jit(solution)/shard_map/ppermute | solution.py:775
  43.9 13.1 %copy-start.2 = (bf16[3072,64]{0,1:T(8,128)(2,1)S(1)}, bf16[3072,64]{0,1:T(8,128)(2,1)}, u32[]{:S(2)}) copy-start(bf16[3072,64]{0,1:T(8,128)(2,1)} %param.19) | copy-start | bytes 1179652
  43.9 18.8 %copy-start.3 = (bf16[27,16,128]{2,1,0:T(8,128)(2,1)S(1)}, bf16[27,16,128]{2,1,0:T(8,128)(2,1)}, u32[]{:S(2)}) copy-start(bf16[27,16,128]{2,1,0:T(8,128)(2,1)} %conv_ref) | copy-start | bytes 331780
  43.9 18.8 %copy-start.6 = (s32[4]{0:T(128)S(1)}, s32[4]{0:T(128)}, u32[]{:S(2)}) copy-start(s32[4]{0:T(128)} %slab_ref) | copy-start | bytes 52
  47.1 5.3 %collective-permute-start.10 = (bf16[16,3072]{1,0:T(8,128)(2,1)S(1)}, bf16[16,3072]{1,0:T(8,128)(2,1)S(1)}, u32[]{:S(2)}, u32[]{:S(2)}) collective-permute-start(bf16[16,3072]{1,0:T(8,128)(2,1)S(1)} %get-tuple-element.59), channel_id=1, source_target_pairs={{0,4},{4,0},{8,12},{12,8},{1,5},{5,1},{9,13},{13,9},{2,6},{6,2},{1... | collective-permute-start | bytes 294920 | tf_op jit(solution)/shard_map/ppermute | solution.py:753
  48.0 7.7 %collective-permute-start.11 = (bf16[16,3072]{1,0:T(8,128)(2,1)S(1)}, bf16[16,3072]{1,0:T(8,128)(2,1)S(1)}, u32[]{:S(2)}, u32[]{:S(2)}) collective-permute-start(bf16[16,3072]{1,0:T(8,128)(2,1)S(1)} %get-tuple-element.60), channel_id=1, source_target_pairs={{0,8},{4,12},{8,0},{12,4},{1,9},{5,13},{9,1},{13,5},{2,10},{6,14},... | collective-permute-start | bytes 294920 | tf_op jit(solution)/shard_map/ppermute | solution.py:753
  50.5 6.5 %collective-permute-start.12 = (bf16[16,3072]{1,0:T(8,128)(2,1)S(1)}, bf16[16,3072]{1,0:T(8,128)(2,1)S(1)}, u32[]{:S(2)}, u32[]{:S(2)}) collective-permute-start(bf16[16,3072]{1,0:T(8,128)(2,1)S(1)} %get-tuple-element.61), channel_id=1, source_target_pairs={{0,12},{4,8},{8,4},{12,0},{1,13},{5,9},{9,5},{13,1},{2,14},{6,10},... | collective-permute-start | bytes 294920 | tf_op jit(solution)/shard_map/ppermute | solution.py:753
  58.1 11.6 %all-to-all-start = ((f32[16,8,128]{2,1,0:T(8,128)}), f32[16,8,128]{2,1,0:T(8,128)S(1)}, u32[]{:S(2)}, u32[]{:S(2)}) async-start(f32[16,8,128]{2,1,0:T(8,128)} %shard_map.138), calls=%async_computation | async-start | bytes 131072 | tf_op jit(solution)/shard_map/all_to_all | solution.py:806

commit v6 on v5

--- a/solution.py
+++ b/solution.py
@@ -173,6 +173,9 @@
 
 
 NT = (((1,), (1,)), ((), ()))
+TILE = 256
+PART = 768
+AHEAD = 4
 
 
 def kernel_params(mebibytes=8):
@@ -197,29 +200,21 @@
     return landed()
 
 
-def prepare_kernel(
-    timestep_ref, table_hbm, cond_hbm, embed_hbm, qkv_hbm, rows_ref, heads_ref, term_ref, table, cond, embed, qkv, sums, sems
+def in_hbm(*values):
+    return [pltpu.with_memory_space_constraint(value, pltpu.HBM) for value in values]
+
+
+def modulation_kernel(
+    timestep_ref, table_hbm, cond_hbm, embed_hbm, rows_ref, lhs_ref, table, cond, embed, sems
 ):
-    blocks, lanes, width = qkv.shape
-    small = [
-        pltpu.make_async_copy(source, target, sems.at[blocks + i])
+    copies = [
+        pltpu.make_async_copy(source, target, sems.at[i])
         for i, (source, target) in enumerate(
             ((table_hbm, table), (cond_hbm, cond), (embed_hbm, embed))
         )
     ]
-    for copy in small:
-        copy.start()
-    landed = in_order(
-        [
-            pltpu.make_async_copy(
-                qkv_hbm.at[:, pl.ds(i * width, width)], qkv.at[i], sems.at[i]
-            )
-            for i in range(blocks)
-        ],
-        4,
-    )
-    for copy in small:
-        copy.wait()
+    for _ in in_order(copies, 3):
+        pass
     steps = table.shape[1]
     chosen = lax.broadcasted_iota(jnp.int32, (16, steps), 1) == timestep_ref[0]
     chosen = jnp.where(chosen, 1.0, 0.0).astype(jnp.bfloat16)
@@ -227,55 +222,62 @@
         row = jnp.dot(chosen, table[j], preferred_element_type=jnp.float32)[:1]
         rows_ref[j : j + 1, :] = row + cond[j] + (1.0 if j == 1 else 0.0)
     count = embed.shape[0]
-    for i in landed:
-        part = slice(i * width, (i + 1) * width)
-        scaled = (embed[:, part].astype(jnp.float32) * rows_ref[1:2, part]).astype(jnp.bfloat16)
-        shift = jnp.broadcast_to(rows_ref[0:1, part], (16, width)).astype(jnp.bfloat16)
-        lhs = jnp.concatenate([scaled, shift], axis=0)
-        for j in range(0, lanes, TILE):
-            lane = slice(j, j + TILE)
-            product = lax.dot_general(
-                lhs, qkv[i, lane, :], NT, preferred_element_type=jnp.float32
-            )
-            if i:
-                product = product + sums[:, lane]
-            if i + 1 < blocks:
-                sums[:, lane] = product
-            else:
-                heads_ref[:, lane] = product[:count].astype(jnp.bfloat16)
-                term_ref[:, lane] = product[count:]
-
-
-def in_hbm(*values):
-    return [pltpu.with_memory_space_constraint(value, pltpu.HBM) for value in values]
-
-
-def prepared(timestep, table, cond, w_embed, qkv):
+    lhs_ref[:count] = (embed[...].astype(jnp.float32) * rows_ref[1:2]).astype(jnp.bfloat16)
+    lhs_ref[count:] = jnp.broadcast_to(rows_ref[0:1], (16, lhs_ref.shape[1])).astype(jnp.bfloat16)
+
+
+def modulated(timestep, table, cond, w_embed):
     count, depth = w_embed.shape
-    lanes = qkv.shape[0]
-    blocks = 6
     return pl.pallas_call(
-        prepare_kernel,
-        in_specs=[whole(pltpu.SMEM)] + [whole(pltpu.HBM)] * 4,
-        out_specs=[whole()] * 3,
+        modulation_kernel,
+        in_specs=[whole(pltpu.SMEM)] + [whole(pltpu.HBM)] * 3,
+        out_specs=[whole()] * 2,
         out_shape=[
             jax.ShapeDtypeStruct((3, depth), jnp.float32),
-            jax.ShapeDtypeStruct((count, lanes), jnp.bfloat16),
-            jax.ShapeDtypeStruct((16, lanes), jnp.float32),
+            jax.ShapeDtypeStruct((count + 16, depth), jnp.bfloat16),
         ],
         scratch_shapes=[
             pltpu.VMEM(table.shape, table.dtype),
             pltpu.VMEM(cond.shape, cond.dtype),
             pltpu.VMEM(w_embed.shape, w_embed.dtype),
-            pltpu.VMEM((blocks, lanes, depth // blocks), qkv.dtype),
-            pltpu.VMEM((count + 16, lanes), jnp.float32),
-            pltpu.SemaphoreType.DMA((blocks + 3,)),
+            pltpu.SemaphoreType.DMA((3,)),
         ],
         cost_estimate=pl.CostEstimate(
-            flops=2 * count * depth * lanes, bytes_accessed=2 * qkv.size, transcendentals=0
+            flops=10**10, bytes_accessed=2 * (table.size + w_embed.size), transcendentals=0
         ),
-        compiler_params=kernel_params(24),
-    )(timestep, *in_hbm(table, cond, w_embed, qkv))
+        compiler_params=kernel_params(),
+    )(timestep, *in_hbm(table, cond, w_embed))
+
+
+def prepare_kernel(lhs_ref, qkv_ref, out_hbm, heads_ref, term_ref, out_ref, sem):
+    out_copy = pltpu.make_async_copy(out_hbm, out_ref, sem)
+    out_copy.start()
+    count = heads_ref.shape[0]
+    for j in range(0, qkv_ref.shape[0], PART):
+        lane = slice(j, j + PART)
+        product = lax.dot_general(
+            lhs_ref[...], qkv_ref[lane, :], NT, preferred_element_type=jnp.float32
+        )
+        heads_ref[:, lane] = product[:count].astype(jnp.bfloat16)
+        term_ref[:, lane] = product[count:]
+    out_copy.wait()
+
+
+def prepared(lhs, qkv, out):
+    rows, depth = lhs.shape
+    lanes = qkv.shape[0]
+    return pl.pallas_call(
+        prepare_kernel,
+        in_specs=[whole()] * 2 + [whole(pltpu.HBM)],
+        out_specs=[whole()] * 3,
+        out_shape=[
+            jax.ShapeDtypeStruct((rows - 16, lanes), jnp.bfloat16),
+            jax.ShapeDtypeStruct((16, lanes), jnp.float32),
+            pltpu.VMEM(out.shape, out.dtype),
+        ],
+        scratch_shapes=[pltpu.SemaphoreType.DMA],
+        compiler_params=kernel_params(),
+    )(lhs, qkv, *in_hbm(out))
 
 
 def span_of(rows, patch_rows):
@@ -338,12 +340,10 @@
 
 
 def first_layer_kernel(
-    count, order_ref, embed_ref, heads_ref, term_ref, stale_ref, out_hbm, *refs
+    count, order_ref, embed_ref, heads_ref, term_ref, stale_ref, out_ref, *refs
 ):
     latent_refs, refs = refs[:count], refs[count:]
-    block_refs, own_ref, latents, attended, keys, values, out_ref, sem = refs[:count], *refs[count:]
-    out_copy = pltpu.make_async_copy(out_hbm, out_ref, sem)
-    out_copy.start()
+    block_refs, (own_ref, latents, attended, keys, values) = refs[:count], refs[count:]
     place = lax.axis_index("seq")
     rows_dev = MICRO * TOK_DEV
     for k in range(count):
@@ -362,72 +362,28 @@
     own_ref[...] = jnp.dot(
         latents[...], embed_ref[:, pl.ds(first, columns)], preferred_element_type=jnp.float32
     ).astype(jnp.bfloat16)
-    out_copy.wait()
     column_blocks(place, attended, out_ref, block_refs)
 
 
-def first_layer(patch_order, latent_pieces, w_embed, heads, term, stale, out):
-    count = len(latent_pieces)
+def first_layer(patch_order, latents, w_embed, heads, term, stale, out):
+    count = len(latents)
     rows = count * MICRO * TOK_DEV
     lanes, depth = out.shape
     block = jax.ShapeDtypeStruct((rows, depth // count), jnp.bfloat16)
     return pl.pallas_call(
         functools.partial(first_layer_kernel, count),
-        in_specs=[whole(pltpu.SMEM)] + [whole()] * 4 + [whole(pltpu.HBM)] + [whole()] * count,
+        in_specs=[whole(pltpu.SMEM)] + [whole()] * (5 + count),
         out_specs=[whole()] * (count + 1),
         out_shape=[block] * (count + 1),
         scratch_shapes=[
             pltpu.VMEM((rows, w_embed.shape[0]), jnp.bfloat16),
             *attention_scratch(rows, stale.shape[1], lanes),
-            pltpu.VMEM(out.shape, out.dtype),
-            pltpu.SemaphoreType.DMA,
         ],
-        compiler_params=kernel_params(12),
-    )(
-        patch_order,
-        w_embed,
-        heads,
-        term,
-        stale,
-        *in_hbm(out),
-        *latent_pieces,
-    )
-
-
-def fetch_kernel(qkv_hbm, out_hbm, after_ref, *refs):
-    block_refs, out_ref, done_ref, sems = refs[:-3], *refs[-3:]
-    count = len(block_refs)
-    place = lax.axis_index("seq")
-    copies = []
-    for k, block_ref in enumerate(block_refs):
-        columns = block_ref.shape[1]
-        first = pl.multiple_of((place ^ k) * columns, columns)
-        copies.append(
-            pltpu.make_async_copy(qkv_hbm.at[:, pl.ds(first, columns)], block_ref, sems.at[k])
-        )
-    copies.append(pltpu.make_async_copy(out_hbm, out_ref, sems.at[count]))
-    for _ in in_order(copies, len(copies)):
-        pass
-    done_ref[...] = jnp.zeros_like(done_ref)
-
-
-def fetched(count, qkv, out, after):
-    lanes, depth = qkv.shape
-    return pl.pallas_call(
-        fetch_kernel,
-        in_specs=[whole(pltpu.HBM)] * 2 + [whole(pl.ANY)],
-        out_specs=[whole()] * (count + 2),
-        out_shape=[pltpu.VMEM((lanes, depth // count), qkv.dtype)] * count
-        + [pltpu.VMEM(out.shape, out.dtype), jax.ShapeDtypeStruct((8, 128), jnp.float32)],
-        scratch_shapes=[pltpu.SemaphoreType.DMA((count + 1,))],
-        cost_estimate=pl.CostEstimate(
-            flops=0, bytes_accessed=2 * (qkv.size + out.size), transcendentals=0
-        ),
         compiler_params=kernel_params(),
-    )(*in_hbm(qkv, out), after)
-
-
-def block_sum_kernel(rows_ref, own_ref, done_ref, *refs):
+    )(patch_order, w_embed, heads, term, stale, out, *latents)
+
+
+def block_sum_kernel(rows_ref, own_ref, *refs):
     part_refs, block_ref = refs[:-1], refs[-1]
     columns = own_ref.shape[1]
     first = pl.multiple_of(lax.axis_index("seq") * columns, columns)
@@ -438,14 +394,14 @@
     block_ref[...] = (own_ref[...].astype(jnp.float32) + gate * mixed).astype(jnp.bfloat16)
 
 
-def block_sum(mod_rows, own, done, parts):
+def block_sum(mod_rows, own, parts):
     return pl.pallas_call(
         block_sum_kernel,
-        in_specs=[whole()] * (3 + len(parts)),
+        in_specs=[whole()] * (2 + len(parts)),
         out_specs=whole(),
         out_shape=jax.ShapeDtypeStruct(own.shape, own.dtype),
         compiler_params=kernel_params(),
-    )(mod_rows, own, done, *parts)
+    )(mod_rows, own, *parts)
 
 
 def scaled_piece(place, k, piece_ref, rows_ref):
@@ -456,48 +412,41 @@
     return scaled, jnp.sum(wide * wide, axis=-1, keepdims=True)
 
 
-TILE = 256
-
-
-def sums_kernel(numbers, rows_ref, *refs):
+def sums_kernel(numbers, rows_ref, qkv_ref, *refs):
     count = len(numbers)
-    piece_refs, weight_refs = refs[:count], refs[count : 2 * count]
-    earlier, (sums_ref, squares_ref) = refs[2 * count : -2], refs[-2:]
+    piece_refs, earlier, (sums_ref, squares_ref) = refs[:count], refs[count:-2], refs[-2:]
     place = lax.axis_index("seq")
+    columns = piece_refs[0].shape[1]
     squares = earlier[1][...] if earlier else 0.0
     scaled = []
     for k, piece_ref in zip(numbers, piece_refs):
         piece, square = scaled_piece(place, k, piece_ref, rows_ref)
-        scaled.append(piece)
+        scaled.append((piece, pl.ds(pl.multiple_of((place ^ k) * columns, columns), columns)))
         squares = squares + square
     squares_ref[...] = squares
     for i in range(0, sums_ref.shape[1], TILE):
         lane = slice(i, i + TILE)
         total = earlier[0][:, lane] if earlier else 0.0
-        for piece, weight_ref in zip(scaled, weight_refs):
+        for piece, part in scaled:
             total = total + lax.dot_general(
-                piece, weight_ref[lane, :], NT, preferred_element_type=jnp.float32
+                piece, qkv_ref[lane, part], NT, preferred_element_type=jnp.float32
             )
         sums_ref[:, lane] = total
 
 
-def in_vmem(*values):
-    return [pltpu.with_memory_space_constraint(value, pltpu.VMEM) for value in values]
-
-
-def product_sums(numbers, pieces, mod_rows, weights, earlier):
-    rows, columns = pieces[0].shape
-    lanes = weights[0].shape[0]
+def product_sums(numbers, pieces, mod_rows, qkv, earlier):
+    rows = pieces[0].shape[0]
+    lanes = qkv.shape[0]
     return pl.pallas_call(
         functools.partial(sums_kernel, numbers),
-        in_specs=[whole()] * (1 + 2 * len(numbers) + len(earlier)),
+        in_specs=[whole()] * (2 + len(numbers) + len(earlier)),
         out_specs=[whole()] * 2,
         out_shape=[
             jax.ShapeDtypeStruct((rows, lanes), jnp.float32),
             jax.ShapeDtypeStruct((rows, 1), jnp.float32),
         ],
         compiler_params=kernel_params(),
-    )(mod_rows, *pieces, *in_vmem(*weights), *earlier)
+    )(mod_rows, qkv, *pieces, *earlier)
 
 
 def later_layer_kernel(
@@ -508,10 +457,12 @@
     place = lax.axis_index("seq")
     scaled, squares = scaled_piece(place, count - 1, piece_refs[-1], rows_ref)
     norm = lax.rsqrt((squares_ref[...] + squares) / rows_ref.shape[1] + norm_eps)
+    columns = piece_refs[-1].shape[1]
+    part = pl.ds(pl.multiple_of((place ^ (count - 1)) * columns, columns), columns)
     for i in range(0, sums.shape[1], TILE):
         lane = slice(i, i + TILE)
         product = lax.dot_general(
-            scaled, qkv_ref[lane, :], NT, preferred_element_type=jnp.float32
+            scaled, qkv_ref[lane, part], NT, preferred_element_type=jnp.float32
         )
         sums[:, lane] = (norm * (product + sums_ref[:, lane]) + term_ref[:1, lane]).astype(
             jnp.bfloat16
@@ -534,7 +485,7 @@
         own_ref[:, pl.ds(first, columns)] = piece_refs[k][own_rows, :]
 
 
-def later_layer(last, patch_order, pieces, mod_rows, qkv_block, out, term, stale, sums, squares):
+def later_layer(last, patch_order, pieces, mod_rows, qkv, out, term, stale, sums, squares):
     count = len(pieces)
     rows, columns = pieces[0].shape
     lanes, depth = out.shape
@@ -551,7 +502,7 @@
             pltpu.VMEM((rows, depth), jnp.bfloat16),
         ],
         compiler_params=kernel_params(),
-    )(patch_order, mod_rows, *in_vmem(qkv_block, out), term, stale, sums, squares, *pieces)
+    )(patch_order, mod_rows, qkv, out, term, stale, sums, squares, *pieces)
 
 
 def term_kernel(rows_ref, own_ref, final_ref, *refs):
@@ -652,11 +603,12 @@
     )(slab_rows, w_conv)
 
 
-def decode_kernel(segment_count, terms_ref, chosen_ref, weights_ref, *refs):
-    latent_refs, refs = refs[:-7], refs[-7:]
+def decode_kernel(
+    segment_count, count, terms_ref, chosen_ref, weights_ref, *refs
+):
+    latent_refs, refs = refs[:count], refs[count:]
     velocity_ref, decoded_ref, latents, tokens, halves, columns, features = refs
     place = lax.axis_index("seq")
-    count = len(latent_refs)
     for k in range(count):
         latents[place ^ k] = latent_refs[k][...]
 
@@ -700,29 +652,29 @@
     decoded_ref[...] = features[...].astype(jnp.bfloat16)
 
 
-def decoded_slab(segment_count, terms, chosen, weights, latent_pieces):
-    count = len(latent_pieces)
+def decoded_slab(segment_count, terms, chosen, weights, latents):
+    count = len(latents)
     rows = count * MICRO * TOK_DEV
-    width = latent_pieces[0].shape[-1]
+    width = latents[0].shape[-1]
     targets = chosen.shape[0]
     channels = weights.shape[1] // 2
     return pl.pallas_call(
-        functools.partial(decode_kernel, segment_count),
+        functools.partial(decode_kernel, segment_count, count),
         in_specs=[whole()] * (3 + count),
         out_specs=[whole()] * 2,
         out_shape=[
-            jax.ShapeDtypeStruct(latent_pieces[0].shape, jnp.float32),
+            jax.ShapeDtypeStruct(latents[0].shape, jnp.float32),
             jax.ShapeDtypeStruct((2 * targets, channels), jnp.bfloat16),
         ],
         scratch_shapes=[
-            pltpu.VMEM((count,) + latent_pieces[0].shape, jnp.float32),
+            pltpu.VMEM((count,) + latents[0].shape, jnp.float32),
             pltpu.VMEM((rows, width), jnp.bfloat16),
             pltpu.VMEM((TAP_GROUP * 2 * rows, TAP_GROUP * width // 2), jnp.bfloat16),
             pltpu.VMEM((targets, weights.shape[0]), jnp.bfloat16),
             pltpu.VMEM((2 * targets, channels), jnp.float32),
         ],
         compiler_params=kernel_params(),
-    )(terms, chosen, weights, *latent_pieces)
+    )(terms, chosen, weights, *latents)
 
 
 def shards(
@@ -745,35 +697,35 @@
     def within(k):
         return [(i, i ^ k) for i in range(seq_count)]
 
-    def spread(value):
-        return [value] + [lax.ppermute(value, "seq", within(k)) for k in range(1, seq_count)]
-
     def returned(values):
-        return values[:1] + [
-            lax.ppermute(values[k], "seq", within(k)) for k in range(1, seq_count)
-        ]
-
-    latent_pieces = spread(latent)
-    mod_rows, head_embed, shift_term = prepared(
-        timestep, jnp.transpose(mod_table, (1, 0, 2)), jnp.transpose(cond_mod[0], (1, 0, 2)), w_embed, w_qkv[0]
-    )
+        far_first = [lax.ppermute(values[k], "seq", within(k)) for k in range(seq_count - 1, 0, -1)]
+        return values[:1] + far_first[::-1]
+
+    numbers = tuple(range(seq_count))
+    half = (seq_count + 1) // 2
+    mod_rows, lhs = modulated(
+        timestep,
+        jnp.transpose(mod_table, (1, 0, 2)),
+        jnp.transpose(cond_mod[0], (1, 0, 2)),
+        w_embed,
+    )
+    latent, mod_rows = lax.optimization_barrier((latent, mod_rows))
+    latents = returned([latent] * seq_count)
+    head_embed, shift_term, out = prepared(lhs, w_qkv[0], w_out[0])
     stale = stale_kv[0, 0, 0]
     *blocks, own = first_layer(
-        patch_order, latent_pieces, w_embed, head_embed, shift_term, stale, w_out[0]
-    )
-    numbers = tuple(range(seq_count))
-    *qkv_blocks, out, done = fetched(seq_count, w_qkv[0], w_out[0], own)
+        patch_order, latents, w_embed, head_embed, shift_term, stale, out
+    )
     for step in range(1, segment_count):
-        block = block_sum(mod_rows, own, done, returned(blocks))
+        block = block_sum(mod_rows, own, returned(blocks))
         pieces = []
-        for k in numbers:
+        for k in numbers[::-1]:
             pairs = [
                 (i * segment_count + j, (i ^ k) * segment_count + (j + 1) % segment_count)
                 for i in range(seq_count)
                 for j in range(segment_count)
             ]
-            pieces.append(lax.ppermute(block, ("seq", "segment"), pairs))
-        half = (seq_count + 1) // 2
+            pieces.insert(0, lax.ppermute(block, ("seq", "segment"), pairs))
         sums = ()
         for some in (numbers[:half], numbers[half:-1]):
             if some:
@@ -781,7 +733,7 @@
                     some,
                     [pieces[k] for k in some],
                     mod_rows,
-                    [qkv_blocks[k] for k in some],
+                    w_qkv[0],
                     sums,
                 )
         *blocks, own = later_layer(
@@ -789,7 +741,7 @@
             patch_order,
             pieces,
             mod_rows,
-            qkv_blocks[-1],
+            w_qkv[0],
             out,
             shift_term,
             stale,
@@ -804,7 +756,7 @@
     peer_count = seq_count * segment_count * lax.axis_size("cfg")
     terms = velocity_terms(peer_count, mod_rows, own, w_final.T, returned(blocks))
     terms = lax.all_to_all(terms, peers, split_axis=0, concat_axis=0, tiled=True)
-    velocity, decoded = decoded_slab(segment_count, terms, chosen, weights, latent_pieces)
+    velocity, decoded = decoded_slab(segment_count, terms, chosen, weights, latents)
     return (velocity, decoded.reshape(1, FRAMES, slab_most, LAT_W, w_conv.shape[2]))
 
 

time: 71.1 us -> 67.1 us (0.944)
  Pallas kernels: 29.1 us -> 19.7 us
  waiting for transfers between devices: 14.2 us -> 20.3 us
    pallas_call x4, Pallas kernels: 15.2 us -> 7.52 us  [the longest x1 4.4 us: prepared(): pl.pallas_call(prepare_kernel, in_specs=[whole()] * 2 + [whole(pltpu.HBM)...]
    ppermute x6 -> x9, waiting for transfers between devices: 5.8 us -> 12.9 us  [returned(): lax.ppermute(values[k], 'seq', within(k))]
    ppermute x6 -> x9, starting transfers between devices: 8.91 us -> 14.7 us  [returned(): lax.ppermute(values[k], 'seq', within(k))]
    ppermute x7 -> x4, starting transfers between devices: 12.5 us -> 6.81 us  [shards(): pieces.insert(0, lax.ppermute(block, ('seq', 'segment'), pairs))]
    pallas_call x1, Pallas kernels: 4.18 us -> 2.31 us  [first_layer(): pl.pallas_call(functools.partial(first_layer_kernel, count), in_specs=[wh...]
    ppermute x7 -> x4, waiting for transfers between devices: 3.65 us -> 2.65 us  [shards(): pieces.insert(0, lax.ppermute(block, ('seq', 'segment'), pairs))]
    all_to_all x1, starting transfers between devices: 4.65 us -> 3.84 us  [shards(): lax.all_to_all(terms, peers, split_axis=0, concat_axis=0, tiled=True)]
  transfers between devices with their start and end apart: 14 -> 14, of which waited for: 8 -> 8; matrix products, arithmetic and copies ran while one was open for 0% -> 0% of each run, Pallas kernels for 27% -> 15%
where the time goes in v6:
time: 67.1 us; the launch traced here: 66.9 us
  starting transfers between devices  25.3 us (38%)
  waiting for transfers between devices  20.3 us (30%)
  Pallas kernels  19.7 us (29%)
  between operations  1.52 us (2%)
    ppermute x9, starting transfers between devices, returned(): lax.ppermute(values[k], 'seq', within(k))  14.7 us
    ppermute x9, waiting for transfers between devices, returned(): lax.ppermute(values[k], 'seq', within(k))  12.9 us
    ppermute x4, starting transfers between devices, shards(): pieces.insert(0, lax.ppermute(block, ('seq', 'segment'), pairs))  6.81 us
    all_to_all x1, waiting for transfers between devices, shards(): lax.all_to_all(terms, peers, split_axis=0, concat_axis=0, tiled=True)  4.79 us
    pallas_call x1, Pallas kernels, prepared(): pl.pallas_call(prepare_kernel, in_specs=[whole()] * 2 + [whole(pltpu.HBM)...  4.4 us
    all_to_all x1, starting transfers between devices, shards(): lax.all_to_all(terms, peers, split_axis=0, concat_axis=0, tiled=True)  3.84 us
    pallas_call x2, Pallas kernels, product_sums(): pl.pallas_call(functools.partial(sums_kernel, numbers), in_specs=[whole()...  3.48 us
    pallas_call x1, Pallas kernels, later_layer(): pl.pallas_call(functools.partial(later_layer_kernel, count, last), in_spe...  3.19 us
  transfers between devices with their start and end apart: 14, of which 8 were waited for; matrix products, arithmetic and copies ran while one was open for 0% of the time, Pallas kernels for 15%

profile of v6, /device:TPU:0, one launch (start us, length us, event | category | flops | bytes accessed | tf_op | source)
XLA Modules:
  0.0 66.9 jit_solution(16613675982555279349)
XLA Ops:
  1.3 1.8 %shard_map.131 = (f32[3,3072]{1,0:T(4,128)S(1)}, bf16[80,3072]{1,0:T(8,128)(2,1)S(1)}) custom-call(s32[1]{0:T(128)S(6)} %copy.14.timestep_ref, bf16[3,50,3072]{2,1,0:T(8,128)(2,1)} %bitcast.17, f32[3,1,3072]{2,1,0:T(1,128)} %bitcast.18, bf16[64,3072]{1,0:T(8,128)(2,1)} %embed_ref.1), custom_call_target="tpu_custom_call" | custom-call | flops 10000000000 | bytes 1314816 | tf_op jit(solution)/shard_map/pallas_call | solution.py:231
  3.1 5.1 %collective-permute-start.2 = (f32[2,8,64]{2,1,0:T(8,128)S(1)}, f32[2,8,64]{2,1,0:T(8,128)S(1)}, u32[]{:S(2)}, u32[]{:S(2)}) collective-permute-start(f32[2,8,64]{2,1,0:T(8,128)S(1)} %copy-done.4), channel_id=1, source_target_pairs={{0,12},{4,8},{8,4},{12,0},{1,13},{5,9},{9,5},{13,1},{2,14},{6,10},... | collective-permute-start | bytes 12296 | tf_op jit(solution)/shard_map/ppermute | solution.py:701
  9.0 4.4 %shard_map.132 = (bf16[64,2304]{1,0:T(8,128)(2,1)S(1)}, f32[16,2304]{1,0:T(8,128)S(1)}, bf16[768,3072]{1,0:T(8,128)(2,1)S(1)}) custom-call(bf16[80,3072]{1,0:T(8,128)(2,1)S(1)} %get-tuple-element.35.lhs_ref, bf16[2304,3072]{1,0:T(8,128)(2,1)S(1)} %bitcast.9, bf16[768,3072]{1,0:T(8,128)(2,1)} %bitcast.16), custom_call_target="tpu_custom_call" | custom-call | tf_op jit(solution)/shard_map/pallas_call | solution.py:269
  13.4 2.3 %shard_map.133 = (bf16[64,768]{1,0:T(8,128)(2,1)S(1)}, bf16[64,768]{1,0:T(8,128)(2,1)S(1)}, bf16[64,768]{1,0:T(8,128)(2,1)S(1)}, bf16[64,768]{1,0:T(8,128)(2,1)S(1)}, bf16[64,768]{1,0:T(8,128)(2,1)S(1)}) custom-call(s32[2]{0:T(128)S(1)} %copy-done.5, bf16[64,3072]{1,0:T(8,128)(2,1)S(1)} %copy-done.1, bf16[64,2304]{1,0:T(8,128)(2,1)S(1)} %get-tuple-element.38.heads_ref, ...), custom_call_target="tpu_custom_call" | custom-call | tf_op jit(solution)/shard_map/pallas_call | solution.py:373
  15.8 1.4 %collective-permute-start.3 = (bf16[64,768]{1,0:T(8,128)(2,1)S(1)}, bf16[64,768]{1,0:T(8,128)(2,1)S(1)}, u32[]{:S(2)}, u32[]{:S(2)}) collective-permute-start(bf16[64,768]{1,0:T(8,128)(2,1)S(1)} %get-tuple-element.42), channel_id=1, source_target_pairs={{0,4},{4,0},{8,12},{12,8},{1,5},{5,1},{9,13},{13,9},{2,6},{6,2},{1... | collective-permute-start | bytes 294920 | tf_op jit(solution)/shard_map/ppermute | solution.py:701
  17.2 2.9 %collective-permute-start.4 = (bf16[64,768]{1,0:T(8,128)(2,1)S(1)}, bf16[64,768]{1,0:T(8,128)(2,1)S(1)}, u32[]{:S(2)}, u32[]{:S(2)}) collective-permute-start(bf16[64,768]{1,0:T(8,128)(2,1)S(1)} %get-tuple-element.43), channel_id=1, source_target_pairs={{0,8},{4,12},{8,0},{12,4},{1,9},{5,13},{9,1},{13,5},{2,10},{6,14},... | collective-permute-start | bytes 294920 | tf_op jit(solution)/shard_map/ppermute | solution.py:701
  20.2 1.3 %collective-permute-done.3.refs_1_ = bf16[64,768]{1,0:T(8,128)(2,1)S(1)} collective-permute-done((bf16[64,768]{1,0:T(8,128)(2,1)S(1)}, bf16[64,768]{1,0:T(8,128)(2,1)S(1)}, u32[]{:S(2)}, u32[]{:S(2)}) %collective-permute-start.3) | collective-permute-done | bytes 98336 | tf_op jit(solution)/shard_map/ppermute | solution.py:701
  21.5 5.6 %collective-permute-done.4.refs_2_ = bf16[64,768]{1,0:T(8,128)(2,1)S(1)} collective-permute-done((bf16[64,768]{1,0:T(8,128)(2,1)S(1)}, bf16[64,768]{1,0:T(8,128)(2,1)S(1)}, u32[]{:S(2)}, u32[]{:S(2)}) %collective-permute-start.4) | collective-permute-done | bytes 98336 | tf_op jit(solution)/shard_map/ppermute | solution.py:701
  27.2 2.6 %collective-permute-start.8 = (bf16[64,768]{1,0:T(8,128)(2,1)S(1)}, bf16[64,768]{1,0:T(8,128)(2,1)S(1)}, u32[]{:S(2)}, u32[]{:S(2)}) collective-permute-start(bf16[64,768]{1,0:T(8,128)(2,1)S(1)} %shard_map.134), channel_id=1, source_target_pairs={{0,6},{2,4},{4,2},{6,0},{8,14},{10,12},{12,10},{14,8},{1,7},{3,5},... | collective-permute-start | bytes 294920 | tf_op jit(solution)/shard_map/ppermute | solution.py:728
  30.3 2.4 %collective-permute-start.6 = (bf16[64,768]{1,0:T(8,128)(2,1)S(1)}, bf16[64,768]{1,0:T(8,128)(2,1)S(1)}, u32[]{:S(2)}, u32[]{:S(2)}) collective-permute-start(bf16[64,768]{1,0:T(8,128)(2,1)S(1)} %shard_map.134), channel_id=1, source_target_pairs={{0,10},{2,8},{4,14},{6,12},{8,2},{10,0},{12,6},{14,4},{1,11},{3,9}... | collective-permute-start | bytes 294920 | tf_op jit(solution)/shard_map/ppermute | solution.py:728
  32.7 1.3 %collective-permute-start.9 = (bf16[64,768]{1,0:T(8,128)(2,1)S(1)}, bf16[64,768]{1,0:T(8,128)(2,1)S(1)}, u32[]{:S(2)}, u32[]{:S(2)}) collective-permute-start(bf16[64,768]{1,0:T(8,128)(2,1)S(1)} %shard_map.134), channel_id=1, source_target_pairs={{0,14},{2,12},{4,10},{6,8},{8,6},{10,4},{12,2},{14,0},{1,15},{3,13... | collective-permute-start | bytes 294920 | tf_op jit(solution)/shard_map/ppermute | solution.py:728
  34.0 2.5 %collective-permute-done.7.refs_0_ = bf16[64,768]{1,0:T(8,128)(2,1)S(1)} collective-permute-done((bf16[64,768]{1,0:T(8,128)(2,1)S(1)}, bf16[64,768]{1,0:T(8,128)(2,1)S(1)}, u32[]{:S(2)}, u32[]{:S(2)}) %collective-permute-start.7) | collective-permute-done | bytes 98336 | tf_op jit(solution)/shard_map/ppermute | solution.py:728
  36.5 2.3 %shard_map.135 = (f32[64,2304]{1,0:T(8,128)S(1)}, f32[64,1]{1,0:T(8,128)S(1)}) custom-call(f32[3,3072]{1,0:T(4,128)S(1)} %get-tuple-element.34.rows_ref, bf16[2304,3072]{1,0:T(8,128)(2,1)S(1)} %bitcast.10, bf16[64,768]{1,0:T(8,128)(2,1)S(1)} %collective-permute-done.7.refs_0_, bf16[64,768]{1,0:T(8,128)(2,1)S(1)} %collective-permute-done.8.refs_1_), custom_call_target="tpu_custom_call" | custom-call | tf_op jit(solution)/shard_map/pallas_call | solution.py:440
  38.9 1.2 %shard_map.136 = (f32[64,2304]{1,0:T(8,128)S(1)}, f32[64,1]{1,0:T(8,128)S(1)}) custom-call(f32[3,3072]{1,0:T(4,128)S(1)} %get-tuple-element.34.rows_ref, bf16[2304,3072]{1,0:T(8,128)(2,1)S(1)} %bitcast.11, bf16[64,768]{1,0:T(8,128)(2,1)S(1)} %collective-permute-done.6.refs_0_.refs_2_, f32[64,2304]{1,0:T(8,128)S(1)} %get-tuple-element.45.refs_1_, ...), custom_call_target="tpu_custom_call" | custom-call | tf_op jit(solution)/shard_map/pallas_call | solution.py:440
  40.2 3.2 %shard_map.137 = (bf16[16,3072]{1,0:T(8,128)(2,1)S(1)}, bf16[16,3072]{1,0:T(8,128)(2,1)S(1)}, bf16[16,3072]{1,0:T(8,128)(2,1)S(1)}, bf16[16,3072]{1,0:T(8,128)(2,1)S(1)}, bf16[16,3072]{1,0:T(8,128)(2,1)S(1)}) custom-call(s32[2]{0:T(128)S(1)} %copy-done.5, f32[3,3072]{1,0:T(4,128)S(1)} %get-tuple-element.34.rows_ref, bf16[2304,3072]{1,0:T(8,128)(2,1)S(1)} %bitcast.12, ...), custom_call_target="tpu_custom_call" | custom-call | tf_op jit(solution)/shard_map/pallas_call | solution.py:494
  43.4 1.5 %collective-permute-start.10 = (bf16[16,3072]{1,0:T(8,128)(2,1)S(1)}, bf16[16,3072]{1,0:T(8,128)(2,1)S(1)}, u32[]{:S(2)}, u32[]{:S(2)}) collective-permute-start(bf16[16,3072]{1,0:T(8,128)(2,1)S(1)} %get-tuple-element.55), channel_id=1, source_target_pairs={{0,4},{4,0},{8,12},{12,8},{1,5},{5,1},{9,13},{13,9},{2,6},{6,2},{1... | collective-permute-start | bytes 294920 | tf_op jit(solution)/shard_map/ppermute | solution.py:701
  44.9 2.4 %collective-permute-start.11 = (bf16[16,3072]{1,0:T(8,128)(2,1)S(1)}, bf16[16,3072]{1,0:T(8,128)(2,1)S(1)}, u32[]{:S(2)}, u32[]{:S(2)}) collective-permute-start(bf16[16,3072]{1,0:T(8,128)(2,1)S(1)} %get-tuple-element.56), channel_id=1, source_target_pairs={{0,8},{4,12},{8,0},{12,4},{1,9},{5,13},{9,1},{13,5},{2,10},{6,14},... | collective-permute-start | bytes 294920 | tf_op jit(solution)/shard_map/ppermute | solution.py:701
  48.1 4.5 %collective-permute-done.11.refs_2_ = bf16[16,3072]{1,0:T(8,128)(2,1)S(1)} collective-permute-done((bf16[16,3072]{1,0:T(8,128)(2,1)S(1)}, bf16[16,3072]{1,0:T(8,128)(2,1)S(1)}, u32[]{:S(2)}, u32[]{:S(2)}) %collective-permute-start.11) | collective-permute-done | bytes 98336 | tf_op jit(solution)/shard_map/ppermute | solution.py:701
  52.6 1.2 %collective-permute-done.12.refs_3_ = bf16[16,3072]{1,0:T(8,128)(2,1)S(1)} collective-permute-done((bf16[16,3072]{1,0:T(8,128)(2,1)S(1)}, bf16[16,3072]{1,0:T(8,128)(2,1)S(1)}, u32[]{:S(2)}, u32[]{:S(2)}) %collective-permute-start.12) | collective-permute-done | bytes 98336 | tf_op jit(solution)/shard_map/ppermute | solution.py:701
  53.8 1.1 %shard_map.138 = f32[16,8,128]{2,1,0:T(8,128)} custom-call(f32[3,3072]{1,0:T(4,128)S(1)} %get-tuple-element.34.rows_ref, bf16[16,3072]{1,0:T(8,128)(2,1)S(1)} %get-tuple-element.49.own_ref, bf16[64,3072]{1,0:T(8,128)(2,1)S(1)} %bitcast.15, bf16[16,3072]{1,0:T(8,128)(2,1)S(1)} %get-tuple-element.54.refs_0_, ...), custom_call_target="tpu_custom_call" | custom-call | tf_op jit(solution)/shard_map/pallas_call | solution.py:528
  54.9 3.8 %all-to-all-start = ((f32[16,8,128]{2,1,0:T(8,128)}), f32[16,8,128]{2,1,0:T(8,128)S(1)}, u32[]{:S(2)}, u32[]{:S(2)}) async-start(f32[16,8,128]{2,1,0:T(8,128)} %shard_map.138), calls=%async_computation | async-start | bytes 131072 | tf_op jit(solution)/shard_map/all_to_all | solution.py:758
  58.7 2.1 %shard_map.139 = (bf16[64,3584]{1,0:T(8,128)(2,1)S(1)}, bf16[896,256]{1,0:T(8,128)(2,1)S(1)}) custom-call(s32[4]{0:T(128)S(1)} %copy-done.6, bf16[27,16,128]{2,1,0:T(8,128)(2,1)S(1)} %copy-done.3), custom_call_target="tpu_custom_call" | custom-call | tf_op jit(solution)/shard_map/pallas_call | solution.py:590
  60.8 4.8 %all-to-all-done.terms_ref = f32[16,8,128]{2,1,0:T(8,128)S(1)} async-done(((f32[16,8,128]{2,1,0:T(8,128)}), f32[16,8,128]{2,1,0:T(8,128)S(1)}, u32[]{:S(2)}, u32[]{:S(2)}) %all-to-all-start) | async-done | bytes 65568 | tf_op jit(solution)/shard_map/all_to_all | solution.py:758
  65.6 1.2 %shard_map.140 = (f32[2,8,64]{2,1,0:T(8,128)}, bf16[128,128]{1,0:T(8,128)(2,1)}) custom-call(f32[16,8,128]{2,1,0:T(8,128)S(1)} %all-to-all-done.terms_ref, bf16[64,3584]{1,0:T(8,128)(2,1)S(1)} %get-tuple-element.60.chosen_ref, bf16[896,256]{1,0:T(8,128)(2,1)S(1)} %get-tuple-element.61.weights_ref, f32[2,8,64]{2,1,0:T(8,128)S(1)} %copy-done.4, ...), custom_call_target="tpu_custom_call" | custom-call | tf_op jit(solution)/shard_map/pallas_call | solution.py:661
  (37 shorter events, 2.4 us)
Async XLA Ops:
  1.3 7.6 %slice-start = ((s8[14155776]{0:T(1024)(128)(4,1)}), s8[4194304]{0:T(1024)(128)(4,1)S(1)}, s32[]{:S(2)}) async-start(s8[14155776]{0:T(1024)(128)(4,1)} %bitcast.7), calls=%async_computation.1 | async-start | bytes 8388608
  1.3 7.6 %slice-start.1 = ((s8[14155776]{0:T(1024)(128)(4,1)}), s8[4194304]{0:T(1024)(128)(4,1)S(1)}, s32[]{:S(2)}) async-start(s8[14155776]{0:T(1024)(128)(4,1)} %bitcast.7), calls=%async_computation.2 | async-start | bytes 8388608
  1.3 7.6 %slice-start.2 = ((s8[14155776]{0:T(1024)(128)(4,1)}), s8[4194304]{0:T(1024)(128)(4,1)S(1)}, s32[]{:S(2)}) async-start(s8[14155776]{0:T(1024)(128)(4,1)} %bitcast.7), calls=%async_computation.3 | async-start | bytes 8388608
  1.3 7.6 %slice-start.3 = ((s8[14155776]{0:T(1024)(128)(4,1)}), s8[1572864]{0:T(1024)(128)(4,1)S(1)}, s32[]{:S(2)}) async-start(s8[14155776]{0:T(1024)(128)(4,1)} %bitcast.7), calls=%async_computation.4 | async-start | bytes 3145728
  3.1 10.2 %collective-permute-start.2 = (f32[2,8,64]{2,1,0:T(8,128)S(1)}, f32[2,8,64]{2,1,0:T(8,128)S(1)}, u32[]{:S(2)}, u32[]{:S(2)}) collective-permute-start(f32[2,8,64]{2,1,0:T(8,128)S(1)} %copy-done.4), channel_id=1, source_target_pairs={{0,12},{4,8},{8,4},{12,0},{1,13},{5,9},{9,5},{13,1},{2,14},{6,10},... | collective-permute-start | bytes 12296 | tf_op jit(solution)/shard_map/ppermute | solution.py:701
  8.3 5.1 %collective-permute-start.1 = (f32[2,8,64]{2,1,0:T(8,128)S(1)}, f32[2,8,64]{2,1,0:T(8,128)S(1)}, u32[]{:S(2)}, u32[]{:S(2)}) collective-permute-start(f32[2,8,64]{2,1,0:T(8,128)S(1)} %copy-done.4), channel_id=1, source_target_pairs={{0,8},{4,12},{8,0},{12,4},{1,9},{5,13},{9,1},{13,5},{2,10},{6,14},... | collective-permute-start | bytes 12296 | tf_op jit(solution)/shard_map/ppermute | solution.py:701
  8.3 5.1 %collective-permute-start = (f32[2,8,64]{2,1,0:T(8,128)S(1)}, f32[2,8,64]{2,1,0:T(8,128)S(1)}, u32[]{:S(2)}, u32[]{:S(2)}) collective-permute-start(f32[2,8,64]{2,1,0:T(8,128)S(1)} %copy-done.4), channel_id=1, source_target_pairs={{0,4},{4,0},{8,12},{12,8},{1,5},{5,1},{9,13},{13,9},{2,6},{6,2},{1... | collective-permute-start | bytes 12296 | tf_op jit(solution)/shard_map/ppermute | solution.py:701
  8.9 4.5 %copy-start = (bf16[1,1,1,2,32,1536]{5,4,3,2,1,0:T(8,128)(2,1)S(1)}, bf16[1,1,1,2,32,1536]{5,4,3,2,1,0:T(8,128)(2,1)}, u32[]{:S(2)}) copy-start(bf16[1,1,1,2,32,1536]{5,4,3,2,1,0:T(8,128)(2,1)} %param.18) | copy-start | bytes 589828
  8.9 4.5 %copy-start.1 = (bf16[64,3072]{1,0:T(8,128)(2,1)S(1)}, bf16[64,3072]{1,0:T(8,128)(2,1)}, u32[]{:S(2)}) copy-start(bf16[64,3072]{1,0:T(8,128)(2,1)} %embed_ref.1) | copy-start | bytes 1179652
  9.0 4.5 %copy-start.5 = (s32[2]{0:T(128)S(1)}, s32[2]{0:T(128)}, u32[]{:S(2)}) copy-start(s32[2]{0:T(128)} %order_ref.3) | copy-start | bytes 28
  15.8 5.7 %collective-permute-start.3 = (bf16[64,768]{1,0:T(8,128)(2,1)S(1)}, bf16[64,768]{1,0:T(8,128)(2,1)S(1)}, u32[]{:S(2)}, u32[]{:S(2)}) collective-permute-start(bf16[64,768]{1,0:T(8,128)(2,1)S(1)} %get-tuple-element.42), channel_id=1, source_target_pairs={{0,4},{4,0},{8,12},{12,8},{1,5},{5,1},{9,13},{13,9},{2,6},{6,2},{1... | collective-permute-start | bytes 294920 | tf_op jit(solution)/shard_map/ppermute | solution.py:701
  17.2 9.9 %collective-permute-start.4 = (bf16[64,768]{1,0:T(8,128)(2,1)S(1)}, bf16[64,768]{1,0:T(8,128)(2,1)S(1)}, u32[]{:S(2)}, u32[]{:S(2)}) collective-permute-start(bf16[64,768]{1,0:T(8,128)(2,1)S(1)} %get-tuple-element.43), channel_id=1, source_target_pairs={{0,8},{4,12},{8,0},{12,4},{1,9},{5,13},{9,1},{13,5},{2,10},{6,14},... | collective-permute-start | bytes 294920 | tf_op jit(solution)/shard_map/ppermute | solution.py:701
  20.1 7.0 %collective-permute-start.5 = (bf16[64,768]{1,0:T(8,128)(2,1)S(1)}, bf16[64,768]{1,0:T(8,128)(2,1)S(1)}, u32[]{:S(2)}, u32[]{:S(2)}) collective-permute-start(bf16[64,768]{1,0:T(8,128)(2,1)S(1)} %get-tuple-element.44), channel_id=1, source_target_pairs={{0,12},{4,8},{8,4},{12,0},{1,13},{5,9},{9,5},{13,1},{2,14},{6,10},... | collective-permute-start | bytes 294920 | tf_op jit(solution)/shard_map/ppermute | solution.py:701
  27.2 6.8 %collective-permute-start.8 = (bf16[64,768]{1,0:T(8,128)(2,1)S(1)}, bf16[64,768]{1,0:T(8,128)(2,1)S(1)}, u32[]{:S(2)}, u32[]{:S(2)}) collective-permute-start(bf16[64,768]{1,0:T(8,128)(2,1)S(1)} %shard_map.134), channel_id=1, source_target_pairs={{0,6},{2,4},{4,2},{6,0},{8,14},{10,12},{12,10},{14,8},{1,7},{3,5},... | collective-permute-start | bytes 294920 | tf_op jit(solution)/shard_map/ppermute | solution.py:728
  29.8 6.7 %collective-permute-start.7 = (bf16[64,768]{1,0:T(8,128)(2,1)S(1)}, bf16[64,768]{1,0:T(8,128)(2,1)S(1)}, u32[]{:S(2)}, u32[]{:S(2)}) collective-permute-start(bf16[64,768]{1,0:T(8,128)(2,1)S(1)} %shard_map.134), channel_id=1, source_target_pairs={{0,2},{2,0},{4,6},{6,4},{8,10},{10,8},{12,14},{14,12},{1,3},{3,1},... | collective-permute-start | bytes 294920 | tf_op jit(solution)/shard_map/ppermute | solution.py:728
  30.3 8.6 %collective-permute-start.6 = (bf16[64,768]{1,0:T(8,128)(2,1)S(1)}, bf16[64,768]{1,0:T(8,128)(2,1)S(1)}, u32[]{:S(2)}, u32[]{:S(2)}) collective-permute-start(bf16[64,768]{1,0:T(8,128)(2,1)S(1)} %shard_map.134), channel_id=1, source_target_pairs={{0,10},{2,8},{4,14},{6,12},{8,2},{10,0},{12,6},{14,4},{1,11},{3,9}... | collective-permute-start | bytes 294920 | tf_op jit(solution)/shard_map/ppermute | solution.py:728
  32.7 7.5 %collective-permute-start.9 = (bf16[64,768]{1,0:T(8,128)(2,1)S(1)}, bf16[64,768]{1,0:T(8,128)(2,1)S(1)}, u32[]{:S(2)}, u32[]{:S(2)}) collective-permute-start(bf16[64,768]{1,0:T(8,128)(2,1)S(1)} %shard_map.134), channel_id=1, source_target_pairs={{0,14},{2,12},{4,10},{6,8},{8,6},{10,4},{12,2},{14,0},{1,15},{3,13... | collective-permute-start | bytes 294920 | tf_op jit(solution)/shard_map/ppermute | solution.py:728
  40.2 13.7 %copy-start.2 = (bf16[3072,64]{0,1:T(8,128)(2,1)S(1)}, bf16[3072,64]{0,1:T(8,128)(2,1)}, u32[]{:S(2)}) copy-start(bf16[3072,64]{0,1:T(8,128)(2,1)} %param.19) | copy-start | bytes 1179652
  40.2 18.6 %copy-start.3 = (bf16[27,16,128]{2,1,0:T(8,128)(2,1)S(1)}, bf16[27,16,128]{2,1,0:T(8,128)(2,1)}, u32[]{:S(2)}) copy-start(bf16[27,16,128]{2,1,0:T(8,128)(2,1)} %conv_ref) | copy-start | bytes 331780
  40.2 18.6 %copy-start.6 = (s32[4]{0:T(128)S(1)}, s32[4]{0:T(128)}, u32[]{:S(2)}) copy-start(s32[4]{0:T(128)} %slab_ref) | copy-start | bytes 52
  43.4 4.7 %collective-permute-start.10 = (bf16[16,3072]{1,0:T(8,128)(2,1)S(1)}, bf16[16,3072]{1,0:T(8,128)(2,1)S(1)}, u32[]{:S(2)}, u32[]{:S(2)}) collective-permute-start(bf16[16,3072]{1,0:T(8,128)(2,1)S(1)} %get-tuple-element.55), channel_id=1, source_target_pairs={{0,4},{4,0},{8,12},{12,8},{1,5},{5,1},{9,13},{13,9},{2,6},{6,2},{1... | collective-permute-start | bytes 294920 | tf_op jit(solution)/shard_map/ppermute | solution.py:701
  44.9 7.7 %collective-permute-start.11 = (bf16[16,3072]{1,0:T(8,128)(2,1)S(1)}, bf16[16,3072]{1,0:T(8,128)(2,1)S(1)}, u32[]{:S(2)}, u32[]{:S(2)}) collective-permute-start(bf16[16,3072]{1,0:T(8,128)(2,1)S(1)} %get-tuple-element.56), channel_id=1, source_target_pairs={{0,8},{4,12},{8,0},{12,4},{1,9},{5,13},{9,1},{13,5},{2,10},{6,14},... | collective-permute-start | bytes 294920 | tf_op jit(solution)/shard_map/ppermute | solution.py:701
  47.3 6.5 %collective-permute-start.12 = (bf16[16,3072]{1,0:T(8,128)(2,1)S(1)}, bf16[16,3072]{1,0:T(8,128)(2,1)S(1)}, u32[]{:S(2)}, u32[]{:S(2)}) collective-permute-start(bf16[16,3072]{1,0:T(8,128)(2,1)S(1)} %get-tuple-element.57), channel_id=1, source_target_pairs={{0,12},{4,8},{8,4},{12,0},{1,13},{5,9},{9,5},{13,1},{2,14},{6,10},... | collective-permute-start | bytes 294920 | tf_op jit(solution)/shard_map/ppermute | solution.py:701
  54.9 10.7 %all-to-all-start = ((f32[16,8,128]{2,1,0:T(8,128)}), f32[16,8,128]{2,1,0:T(8,128)S(1)}, u32[]{:S(2)}, u32[]{:S(2)}) async-start(f32[16,8,128]{2,1,0:T(8,128)} %shard_map.138), calls=%async_computation | async-start | bytes 131072 | tf_op jit(solution)/shard_map/all_to_all | solution.py:758
  (1 other events, 1.9 us)

commit v7 on v6

--- a/solution.py
+++ b/solution.py
@@ -204,80 +204,64 @@
     return [pltpu.with_memory_space_constraint(value, pltpu.HBM) for value in values]
 
 
-def modulation_kernel(
-    timestep_ref, table_hbm, cond_hbm, embed_hbm, rows_ref, lhs_ref, table, cond, embed, sems
+def stage_kernel(latent_ref, staged_ref):
+    staged_ref[...] = latent_ref[...]
+
+
+def staged(latent):
+    return pl.pallas_call(
+        stage_kernel,
+        in_specs=[whole()],
+        out_specs=whole(),
+        out_shape=jax.ShapeDtypeStruct(latent.shape, latent.dtype),
+        cost_estimate=pl.CostEstimate(flops=10**10, bytes_accessed=0, transcendentals=0),
+        compiler_params=kernel_params(),
+    )(latent)
+
+
+def prepare_kernel(
+    timestep_ref, table_ref, cond_ref, embed_ref, qkv_ref, out_hbm, rows_ref, heads_ref, term_ref, out_ref, lhs, sem
 ):
-    copies = [
-        pltpu.make_async_copy(source, target, sems.at[i])
-        for i, (source, target) in enumerate(
-            ((table_hbm, table), (cond_hbm, cond), (embed_hbm, embed))
-        )
-    ]
-    for _ in in_order(copies, 3):
-        pass
-    steps = table.shape[1]
+    out_copy = pltpu.make_async_copy(out_hbm, out_ref, sem)
+    out_copy.start()
+    steps = table_ref.shape[1]
     chosen = lax.broadcasted_iota(jnp.int32, (16, steps), 1) == timestep_ref[0]
     chosen = jnp.where(chosen, 1.0, 0.0).astype(jnp.bfloat16)
     for j in range(3):
-        row = jnp.dot(chosen, table[j], preferred_element_type=jnp.float32)[:1]
-        rows_ref[j : j + 1, :] = row + cond[j] + (1.0 if j == 1 else 0.0)
-    count = embed.shape[0]
-    lhs_ref[:count] = (embed[...].astype(jnp.float32) * rows_ref[1:2]).astype(jnp.bfloat16)
-    lhs_ref[count:] = jnp.broadcast_to(rows_ref[0:1], (16, lhs_ref.shape[1])).astype(jnp.bfloat16)
-
-
-def modulated(timestep, table, cond, w_embed):
-    count, depth = w_embed.shape
-    return pl.pallas_call(
-        modulation_kernel,
-        in_specs=[whole(pltpu.SMEM)] + [whole(pltpu.HBM)] * 3,
-        out_specs=[whole()] * 2,
-        out_shape=[
-            jax.ShapeDtypeStruct((3, depth), jnp.float32),
-            jax.ShapeDtypeStruct((count + 16, depth), jnp.bfloat16),
-        ],
-        scratch_shapes=[
-            pltpu.VMEM(table.shape, table.dtype),
-            pltpu.VMEM(cond.shape, cond.dtype),
-            pltpu.VMEM(w_embed.shape, w_embed.dtype),
-            pltpu.SemaphoreType.DMA((3,)),
-        ],
-        cost_estimate=pl.CostEstimate(
-            flops=10**10, bytes_accessed=2 * (table.size + w_embed.size), transcendentals=0
-        ),
-        compiler_params=kernel_params(),
-    )(timestep, *in_hbm(table, cond, w_embed))
-
-
-def prepare_kernel(lhs_ref, qkv_ref, out_hbm, heads_ref, term_ref, out_ref, sem):
-    out_copy = pltpu.make_async_copy(out_hbm, out_ref, sem)
-    out_copy.start()
-    count = heads_ref.shape[0]
+        row = jnp.dot(chosen, table_ref[j], preferred_element_type=jnp.float32)[:1]
+        rows_ref[j : j + 1, :] = row + cond_ref[j] + (1.0 if j == 1 else 0.0)
+    count = embed_ref.shape[0]
+    lhs[:count] = (embed_ref[...].astype(jnp.float32) * rows_ref[1:2]).astype(jnp.bfloat16)
+    lhs[count:] = jnp.broadcast_to(rows_ref[0:1], (16, lhs.shape[1])).astype(jnp.bfloat16)
     for j in range(0, qkv_ref.shape[0], PART):
         lane = slice(j, j + PART)
         product = lax.dot_general(
-            lhs_ref[...], qkv_ref[lane, :], NT, preferred_element_type=jnp.float32
+            lhs[...], qkv_ref[lane, :], NT, preferred_element_type=jnp.float32
         )
         heads_ref[:, lane] = product[:count].astype(jnp.bfloat16)
         term_ref[:, lane] = product[count:]
     out_copy.wait()
 
 
-def prepared(lhs, qkv, out):
-    rows, depth = lhs.shape
+def prepared(timestep, table, cond, w_embed, qkv, out):
+    count, depth = w_embed.shape
     lanes = qkv.shape[0]
     return pl.pallas_call(
         prepare_kernel,
-        in_specs=[whole()] * 2 + [whole(pltpu.HBM)],
-        out_specs=[whole()] * 3,
+        in_specs=[whole(pltpu.SMEM)] + [whole()] * 4 + [whole(pltpu.HBM)],
+        out_specs=[whole()] * 4,
         out_shape=[
-            jax.ShapeDtypeStruct((rows - 16, lanes), jnp.bfloat16),
+            jax.ShapeDtypeStruct((3, depth), jnp.float32),
+            jax.ShapeDtypeStruct((count, lanes), jnp.bfloat16),
             jax.ShapeDtypeStruct((16, lanes), jnp.float32),
             pltpu.VMEM(out.shape, out.dtype),
         ],
-        scratch_shapes=[pltpu.SemaphoreType.DMA],
-        compiler_params=kernel_params(),
-    )(lhs, qkv, *in_hbm(out))
+        scratch_shapes=[
+            pltpu.VMEM((count + 16, depth), jnp.bfloat16),
+            pltpu.SemaphoreType.DMA,
+        ],
+        compiler_params=kernel_params(),
+    )(timestep, table, cond, w_embed, qkv, *in_hbm(out))
 
 
 def span_of(rows, patch_rows):
@@ -383,7 +367,29 @@
     )(patch_order, w_embed, heads, term, stale, out, *latents)
 
 
-def block_sum_kernel(rows_ref, own_ref, *refs):
+def turn_kernel(after_ref, qkv_ref, turned_ref, done_ref):
+    lanes, depth = qkv_ref.shape
+    for i in range(0, lanes, TILE):
+        for j in range(0, depth, TILE):
+            turned_ref[j : j + TILE, i : i + TILE] = qkv_ref[i : i + TILE, j : j + TILE].T
+    done_ref[...] = jnp.zeros_like(done_ref)
+
+
+def turned(qkv, after):
+    return pl.pallas_call(
+        turn_kernel,
+        in_specs=[whole(pl.ANY), whole()],
+        out_specs=[whole()] * 2,
+        out_shape=[
+            pltpu.VMEM(qkv.shape[::-1], qkv.dtype),
+            jax.ShapeDtypeStruct((8, 128), jnp.float32),
+        ],
+        cost_estimate=pl.CostEstimate(flops=5 * 10**9, bytes_accessed=0, transcendentals=0),
+        compiler_params=kernel_params(),
+    )(after, qkv)
+
+
+def block_sum_kernel(rows_ref, own_ref, done_ref, *refs):
     part_refs, block_ref = refs[:-1], refs[-1]
     columns = own_ref.shape[1]
     first = pl.multiple_of(lax.axis_index("seq") * columns, columns)
@@ -394,14 +400,14 @@
     block_ref[...] = (own_ref[...].astype(jnp.float32) + gate * mixed).astype(jnp.bfloat16)
 
 
-def block_sum(mod_rows, own, parts):
+def block_sum(mod_rows, own, done, parts):
     return pl.pallas_call(
         block_sum_kernel,
-        in_specs=[whole()] * (2 + len(parts)),
+        in_specs=[whole()] * (3 + len(parts)),
         out_specs=whole(),
         out_shape=jax.ShapeDtypeStruct(own.shape, own.dtype),
         compiler_params=kernel_params(),
-    )(mod_rows, own, *parts)
+    )(mod_rows, own, done, *parts)
 
 
 def scaled_piece(place, k, piece_ref, rows_ref):
@@ -412,7 +418,7 @@
     return scaled, jnp.sum(wide * wide, axis=-1, keepdims=True)
 
 
-def sums_kernel(numbers, rows_ref, qkv_ref, *refs):
+def sums_kernel(numbers, rows_ref, turned_ref, *refs):
     count = len(numbers)
     piece_refs, earlier, (sums_ref, squares_ref) = refs[:count], refs[count:-2], refs[-2:]
     place = lax.axis_index("seq")
@@ -424,19 +430,19 @@
         scaled.append((piece, pl.ds(pl.multiple_of((place ^ k) * columns, columns), columns)))
         squares = squares + square
     squares_ref[...] = squares
-    for i in range(0, sums_ref.shape[1], TILE):
-        lane = slice(i, i + TILE)
+    for i in range(0, sums_ref.shape[1], PART):
+        lane = slice(i, i + PART)
         total = earlier[0][:, lane] if earlier else 0.0
         for piece, part in scaled:
-            total = total + lax.dot_general(
-                piece, qkv_ref[lane, part], NT, preferred_element_type=jnp.float32
+            total = total + jnp.dot(
+                piece, turned_ref[part, lane], preferred_element_type=jnp.float32
             )
         sums_ref[:, lane] = total
 
 
 def product_sums(numbers, pieces, mod_rows, qkv, earlier):
     rows = pieces[0].shape[0]
-    lanes = qkv.shape[0]
+    lanes = qkv.shape[1]
     return pl.pallas_call(
         functools.partial(sums_kernel, numbers),
         in_specs=[whole()] * (2 + len(numbers) + len(earlier)),
@@ -459,11 +465,9 @@
     norm = lax.rsqrt((squares_ref[...] + squares) / rows_ref.shape[1] + norm_eps)
     columns = piece_refs[-1].shape[1]
     part = pl.ds(pl.multiple_of((place ^ (count - 1)) * columns, columns), columns)
-    for i in range(0, sums.shape[1], TILE):
-        lane = slice(i, i + TILE)
-        product = lax.dot_general(
-            scaled, qkv_ref[lane, part], NT, preferred_element_type=jnp.float32
-        )
+    for i in range(0, sums.shape[1], PART):
+        lane = slice(i, i + PART)
+        product = jnp.dot(scaled, qkv_ref[part, lane], preferred_element_type=jnp.float32)
         sums[:, lane] = (norm * (product + sums_ref[:, lane]) + term_ref[:1, lane]).astype(
             jnp.bfloat16
         )
@@ -512,11 +516,11 @@
         mixed = mixed + part_ref[...].astype(jnp.float32)
     hidden = (own_ref[...].astype(jnp.float32) + rows_ref[2:3] * mixed).astype(jnp.bfloat16)
     predicted = lax.dot_general(
-        rms_scaled(hidden).astype(jnp.bfloat16),
-        final_ref[...],
-        NT,
-        preferred_element_type=jnp.float32,
-    )
+        hidden, final_ref[...], NT, preferred_element_type=jnp.float32
+    )
+    wide = hidden.astype(jnp.float32)
+    norm = lax.rsqrt(jnp.mean(wide * wide, axis=-1, keepdims=True) + norm_eps)
+    predicted = norm * predicted
     weight = jnp.where(lax.axis_index("cfg") == 0, 1.0 - guide_scale, guide_scale)
     patches = [predicted[i * TOK_DEV : (i + 1) * TOK_DEV] for i in range(MICRO)]
     term = weight * jnp.concatenate(patches, axis=1)
@@ -703,21 +707,22 @@
 
     numbers = tuple(range(seq_count))
     half = (seq_count + 1) // 2
-    mod_rows, lhs = modulated(
+    latents = returned([staged(latent)] * seq_count)
+    mod_rows, head_embed, shift_term, out = prepared(
         timestep,
         jnp.transpose(mod_table, (1, 0, 2)),
         jnp.transpose(cond_mod[0], (1, 0, 2)),
         w_embed,
-    )
-    latent, mod_rows = lax.optimization_barrier((latent, mod_rows))
-    latents = returned([latent] * seq_count)
-    head_embed, shift_term, out = prepared(lhs, w_qkv[0], w_out[0])
+        w_qkv[0],
+        w_out[0],
+    )
     stale = stale_kv[0, 0, 0]
     *blocks, own = first_layer(
         patch_order, latents, w_embed, head_embed, shift_term, stale, out
     )
+    qkv, done = turned(w_qkv[0], own)
     for step in range(1, segment_count):
-        block = block_sum(mod_rows, own, returned(blocks))
+        block = block_sum(mod_rows, own, done, returned(blocks))
         pieces = []
         for k in numbers[::-1]:
             pairs = [
@@ -733,7 +738,7 @@
                     some,
                     [pieces[k] for k in some],
                     mod_rows,
-                    w_qkv[0],
+                    qkv,
                     sums,
                 )
         *blocks, own = later_layer(
@@ -741,7 +746,7 @@
             patch_order,
             pieces,
             mod_rows,
-            w_qkv[0],
+            qkv,
             out,
             shift_term,
             stale,

time: 67.1 us -> 66.4 us (0.990)
  waiting for transfers between devices: 20.3 us -> 18.7 us
  local copies, waits for them, and re-layouts: 0.06 us -> 0.88 us
    ppermute x9, waiting for transfers between devices: 12.9 us -> 9.9 us  [returned(): lax.ppermute(values[k], 'seq', within(k))]
    pallas_call x3 -> x4, Pallas kernels: 6.28 us -> 8.35 us  [the longest x1 4.59 us: prepared(): pl.pallas_call(prepare_kernel, in_specs=[whole(pltpu.SMEM)] + [whole()] *...]
    pallas_call x2, Pallas kernels: 3.48 us -> 2.09 us  [product_sums(): pl.pallas_call(functools.partial(sums_kernel, numbers), in_specs=[whole()...]
    ppermute x4, waiting for transfers between devices: 2.65 us -> 3.98 us  [shards(): pieces.insert(0, lax.ppermute(block, ('seq', 'segment'), pairs))]
    unnamed x22 -> x20, local copies, waits for them, and re-layouts: 0.06 us -> 0.88 us
  transfers between devices with their start and end apart: 14 -> 14, of which waited for: 8 -> 7; matrix products, arithmetic and copies ran while one was open for 0% -> 0% of each run, Pallas kernels for 15% -> 19%
where the time goes in v7:
time: 66.4 us; the launch traced here: 66.2 us
  starting transfers between devices  25.4 us (38%)
  Pallas kernels  19.7 us (30%)
  waiting for transfers between devices  18.7 us (28%)
  between operations  1.5 us (2%)
  local copies, waits for them, and re-layouts  0.88 us (1%)
    ppermute x9, starting transfers between devices, returned(): lax.ppermute(values[k], 'seq', within(k))  14.6 us
    ppermute x9, waiting for transfers between devices, returned(): lax.ppermute(values[k], 'seq', within(k))  9.9 us
    ppermute x4, starting transfers between devices, shards(): pieces.insert(0, lax.ppermute(block, ('seq', 'segment'), pairs))  6.81 us
    all_to_all x1, waiting for transfers between devices, shards(): lax.all_to_all(terms, peers, split_axis=0, concat_axis=0, tiled=True)  4.79 us
    pallas_call x1, Pallas kernels, prepared(): pl.pallas_call(prepare_kernel, in_specs=[whole(pltpu.SMEM)] + [whole()] *...  4.59 us
    all_to_all x1, starting transfers between devices, shards(): lax.all_to_all(terms, peers, split_axis=0, concat_axis=0, tiled=True)  4.01 us
    ppermute x4, waiting for transfers between devices, shards(): pieces.insert(0, lax.ppermute(block, ('seq', 'segment'), pairs))  3.98 us
    pallas_call x1, Pallas kernels, turned(): pl.pallas_call(turn_kernel, in_specs=[whole(pl.ANY), whole()], out_specs=...  3.69 us
  transfers between devices with their start and end apart: 14, of which 7 were waited for; matrix products, arithmetic and copies ran while one was open for 0% of the time, Pallas kernels for 19%

profile of v7, /device:TPU:0, one launch (start us, length us, event | category | flops | bytes accessed | tf_op | source)
XLA Modules:
  0.0 66.2 jit_solution(12145170797902279744)
XLA Ops:
  0.7 0.8 %copy-done.9 = f32[2,8,64]{2,1,0:T(8,128)S(1)} copy-done((f32[2,8,64]{2,1,0:T(8,128)S(1)}, f32[2,8,64]{2,1,0:T(8,128)}, u32[]{:S(2)}) %copy-start.9) | copy-done | bytes 4120
  1.5 5.0 %collective-permute-start.2 = (f32[2,8,64]{2,1,0:T(8,128)S(1)}, f32[2,8,64]{2,1,0:T(8,128)S(1)}, u32[]{:S(2)}, u32[]{:S(2)}) collective-permute-start(f32[2,8,64]{2,1,0:T(8,128)S(1)} %shard_map.132.refs_0_), channel_id=1, source_target_pairs={{0,12},{4,8},{8,4},{12,0},{1,13},{5,9},{9,5},{13,1},{2,14},{6,10},... | collective-permute-start | bytes 12296 | tf_op jit(solution)/shard_map/ppermute | solution.py:705
  7.9 4.6 %shard_map.131 = (f32[3,3072]{1,0:T(4,128)S(1)}, bf16[64,2304]{1,0:T(8,128)(2,1)S(1)}, f32[16,2304]{1,0:T(8,128)S(1)}, bf16[768,3072]{1,0:T(8,128)(2,1)S(1)}) custom-call(s32[1]{0:T(128)S(6)} %copy.14.timestep_ref, bf16[3,50,3072]{2,1,0:T(8,128)(2,1)S(1)} %bitcast.9, f32[3,1,3072]{2,1,0:T(1,128)S(1)} %bitcast.13, bf16[64,3072]{1,0:T(8,128)(2,1)S(1)} %copy-done.1, ...), custom_call_target="tpu_custom_call" | custom-call | tf_op jit(solution)/shard_map/pallas_call | solution.py:249
  12.6 2.3 %shard_map.133 = (bf16[64,768]{1,0:T(8,128)(2,1)S(1)}, bf16[64,768]{1,0:T(8,128)(2,1)S(1)}, bf16[64,768]{1,0:T(8,128)(2,1)S(1)}, bf16[64,768]{1,0:T(8,128)(2,1)S(1)}, bf16[64,768]{1,0:T(8,128)(2,1)S(1)}) custom-call(s32[2]{0:T(128)S(1)} %copy-done.7, bf16[64,3072]{1,0:T(8,128)(2,1)S(1)} %copy-done.1, bf16[64,2304]{1,0:T(8,128)(2,1)S(1)} %get-tuple-element.33.heads_ref, ...), custom_call_target="tpu_custom_call" | custom-call | tf_op jit(solution)/shard_map/pallas_call | solution.py:357
  14.9 1.5 %collective-permute-start.3 = (bf16[64,768]{1,0:T(8,128)(2,1)S(1)}, bf16[64,768]{1,0:T(8,128)(2,1)S(1)}, u32[]{:S(2)}, u32[]{:S(2)}) collective-permute-start(bf16[64,768]{1,0:T(8,128)(2,1)S(1)} %get-tuple-element.40), channel_id=1, source_target_pairs={{0,4},{4,0},{8,12},{12,8},{1,5},{5,1},{9,13},{13,9},{2,6},{6,2},{1... | collective-permute-start | bytes 294920 | tf_op jit(solution)/shard_map/ppermute | solution.py:705
  16.3 2.9 %collective-permute-start.4 = (bf16[64,768]{1,0:T(8,128)(2,1)S(1)}, bf16[64,768]{1,0:T(8,128)(2,1)S(1)}, u32[]{:S(2)}, u32[]{:S(2)}) collective-permute-start(bf16[64,768]{1,0:T(8,128)(2,1)S(1)} %get-tuple-element.41), channel_id=1, source_target_pairs={{0,8},{4,12},{8,0},{12,4},{1,9},{5,13},{9,1},{13,5},{2,10},{6,14},... | collective-permute-start | bytes 294920 | tf_op jit(solution)/shard_map/ppermute | solution.py:705
  19.3 3.7 %shard_map.134 = (bf16[3072,2304]{1,0:T(8,128)(2,1)S(1)}, f32[8,128]{1,0:T(8,128)S(1)}) custom-call(bf16[64,768]{1,0:T(8,128)(2,1)S(1)} %get-tuple-element.36.after_ref.own_ref, bf16[2304,3072]{1,0:T(8,128)(2,1)S(1)} %bitcast.8), custom_call_target="tpu_custom_call" | custom-call | flops 5000000000 | tf_op jit(solution)/shard_map/pallas_call | solution.py:379
  23.0 3.6 %collective-permute-done.4.refs_2_ = bf16[64,768]{1,0:T(8,128)(2,1)S(1)} collective-permute-done((bf16[64,768]{1,0:T(8,128)(2,1)S(1)}, bf16[64,768]{1,0:T(8,128)(2,1)S(1)}, u32[]{:S(2)}, u32[]{:S(2)}) %collective-permute-start.4) | collective-permute-done | bytes 98336 | tf_op jit(solution)/shard_map/ppermute | solution.py:705
  26.7 2.6 %collective-permute-start.8 = (bf16[64,768]{1,0:T(8,128)(2,1)S(1)}, bf16[64,768]{1,0:T(8,128)(2,1)S(1)}, u32[]{:S(2)}, u32[]{:S(2)}) collective-permute-start(bf16[64,768]{1,0:T(8,128)(2,1)S(1)} %shard_map.135), channel_id=1, source_target_pairs={{0,6},{2,4},{4,2},{6,0},{8,14},{10,12},{12,10},{14,8},{1,7},{3,5},... | collective-permute-start | bytes 294920 | tf_op jit(solution)/shard_map/ppermute | solution.py:733
  29.8 2.4 %collective-permute-start.6 = (bf16[64,768]{1,0:T(8,128)(2,1)S(1)}, bf16[64,768]{1,0:T(8,128)(2,1)S(1)}, u32[]{:S(2)}, u32[]{:S(2)}) collective-permute-start(bf16[64,768]{1,0:T(8,128)(2,1)S(1)} %shard_map.135), channel_id=1, source_target_pairs={{0,10},{2,8},{4,14},{6,12},{8,2},{10,0},{12,6},{14,4},{1,11},{3,9}... | collective-permute-start | bytes 294920 | tf_op jit(solution)/shard_map/ppermute | solution.py:733
  32.2 1.3 %collective-permute-start.9 = (bf16[64,768]{1,0:T(8,128)(2,1)S(1)}, bf16[64,768]{1,0:T(8,128)(2,1)S(1)}, u32[]{:S(2)}, u32[]{:S(2)}) collective-permute-start(bf16[64,768]{1,0:T(8,128)(2,1)S(1)} %shard_map.135), channel_id=1, source_target_pairs={{0,14},{2,12},{4,10},{6,8},{8,6},{10,4},{12,2},{14,0},{1,15},{3,13... | collective-permute-start | bytes 294920 | tf_op jit(solution)/shard_map/ppermute | solution.py:733
  33.5 2.5 %collective-permute-done.7.refs_0_ = bf16[64,768]{1,0:T(8,128)(2,1)S(1)} collective-permute-done((bf16[64,768]{1,0:T(8,128)(2,1)S(1)}, bf16[64,768]{1,0:T(8,128)(2,1)S(1)}, u32[]{:S(2)}, u32[]{:S(2)}) %collective-permute-start.7) | collective-permute-done | bytes 98336 | tf_op jit(solution)/shard_map/ppermute | solution.py:733
  36.0 1.3 %shard_map.136 = (f32[64,2304]{1,0:T(8,128)S(1)}, f32[64,1]{1,0:T(8,128)S(1)}) custom-call(f32[3,3072]{1,0:T(4,128)S(1)} %get-tuple-element.32.rows_ref, bf16[3072,2304]{1,0:T(8,128)(2,1)S(1)} %get-tuple-element.37.turned_ref.qkv_ref, bf16[64,768]{1,0:T(8,128)(2,1)S(1)} %collective-permute-done.7.refs_0_, bf16[64,768]{1,0:T(8,128)(2,1)S(1)} %collective-permute-done.8.refs_1_), custom_call_target="tpu_custom_call" | custom-call | tf_op jit(solution)/shard_map/pallas_call | solution.py:446
  37.3 1.2 %collective-permute-done.6.refs_0_.refs_2_ = bf16[64,768]{1,0:T(8,128)(2,1)S(1)} collective-permute-done((bf16[64,768]{1,0:T(8,128)(2,1)S(1)}, bf16[64,768]{1,0:T(8,128)(2,1)S(1)}, u32[]{:S(2)}, u32[]{:S(2)}) %collective-permute-start.6) | collective-permute-done | bytes 98336 | tf_op jit(solution)/shard_map/ppermute | solution.py:733
  38.6 0.7 %shard_map.137 = (f32[64,2304]{1,0:T(8,128)S(1)}, f32[64,1]{1,0:T(8,128)S(1)}) custom-call(f32[3,3072]{1,0:T(4,128)S(1)} %get-tuple-element.32.rows_ref, bf16[3072,2304]{1,0:T(8,128)(2,1)S(1)} %get-tuple-element.37.turned_ref.qkv_ref, bf16[64,768]{1,0:T(8,128)(2,1)S(1)} %collective-permute-done.6.refs_0_.refs_2_, f32[64,2304]{1,0:T(8,128)S(1)} %get-tuple-element.43.refs_1_, ...), custom_call_target="tpu_custom_call" | custom-call | tf_op jit(solution)/shard_map/pallas_call | solution.py:446
  39.6 2.7 %shard_map.138 = (bf16[16,3072]{1,0:T(8,128)(2,1)S(1)}, bf16[16,3072]{1,0:T(8,128)(2,1)S(1)}, bf16[16,3072]{1,0:T(8,128)(2,1)S(1)}, bf16[16,3072]{1,0:T(8,128)(2,1)S(1)}, bf16[16,3072]{1,0:T(8,128)(2,1)S(1)}) custom-call(s32[2]{0:T(128)S(1)} %copy-done.7, f32[3,3072]{1,0:T(4,128)S(1)} %get-tuple-element.32.rows_ref, ...), custom_call_target="tpu_custom_call" | custom-call | tf_op jit(solution)/shard_map/pallas_call | solution.py:498
  42.3 1.7 %collective-permute-start.10 = (bf16[16,3072]{1,0:T(8,128)(2,1)S(1)}, bf16[16,3072]{1,0:T(8,128)(2,1)S(1)}, u32[]{:S(2)}, u32[]{:S(2)}) collective-permute-start(bf16[16,3072]{1,0:T(8,128)(2,1)S(1)} %get-tuple-element.53), channel_id=1, source_target_pairs={{0,4},{4,0},{8,12},{12,8},{1,5},{5,1},{9,13},{13,9},{2,6},{6,2},{1... | collective-permute-start | bytes 294920 | tf_op jit(solution)/shard_map/ppermute | solution.py:705
  44.0 2.2 %collective-permute-start.11 = (bf16[16,3072]{1,0:T(8,128)(2,1)S(1)}, bf16[16,3072]{1,0:T(8,128)(2,1)S(1)}, u32[]{:S(2)}, u32[]{:S(2)}) collective-permute-start(bf16[16,3072]{1,0:T(8,128)(2,1)S(1)} %get-tuple-element.54), channel_id=1, source_target_pairs={{0,8},{4,12},{8,0},{12,4},{1,9},{5,13},{9,1},{13,5},{2,10},{6,14},... | collective-permute-start | bytes 294920 | tf_op jit(solution)/shard_map/ppermute | solution.py:705
  47.1 6.0 %collective-permute-done.11.refs_2_ = bf16[16,3072]{1,0:T(8,128)(2,1)S(1)} collective-permute-done((bf16[16,3072]{1,0:T(8,128)(2,1)S(1)}, bf16[16,3072]{1,0:T(8,128)(2,1)S(1)}, u32[]{:S(2)}, u32[]{:S(2)}) %collective-permute-start.11) | collective-permute-done | bytes 98336 | tf_op jit(solution)/shard_map/ppermute | solution.py:705
  53.1 0.9 %shard_map.139 = f32[16,8,128]{2,1,0:T(8,128)} custom-call(f32[3,3072]{1,0:T(4,128)S(1)} %get-tuple-element.32.rows_ref, bf16[16,3072]{1,0:T(8,128)(2,1)S(1)} %get-tuple-element.47.own_ref, bf16[64,3072]{1,0:T(8,128)(2,1)S(1)} %bitcast.12, bf16[16,3072]{1,0:T(8,128)(2,1)S(1)} %get-tuple-element.52.refs_0_, ...), custom_call_target="tpu_custom_call" | custom-call | tf_op jit(solution)/shard_map/pallas_call | solution.py:532
  54.0 4.0 %all-to-all-start = ((f32[16,8,128]{2,1,0:T(8,128)}), f32[16,8,128]{2,1,0:T(8,128)S(1)}, u32[]{:S(2)}, u32[]{:S(2)}) async-start(f32[16,8,128]{2,1,0:T(8,128)} %shard_map.139), calls=%async_computation | async-start | bytes 131072 | tf_op jit(solution)/shard_map/all_to_all | solution.py:763
  58.0 2.1 %shard_map.140 = (bf16[64,3584]{1,0:T(8,128)(2,1)S(1)}, bf16[896,256]{1,0:T(8,128)(2,1)S(1)}) custom-call(s32[4]{0:T(128)S(1)} %copy-done.8, bf16[27,16,128]{2,1,0:T(8,128)(2,1)S(1)} %copy-done.5), custom_call_target="tpu_custom_call" | custom-call | tf_op jit(solution)/shard_map/pallas_call | solution.py:594
  60.1 4.8 %all-to-all-done.terms_ref = f32[16,8,128]{2,1,0:T(8,128)S(1)} async-done(((f32[16,8,128]{2,1,0:T(8,128)}), f32[16,8,128]{2,1,0:T(8,128)S(1)}, u32[]{:S(2)}, u32[]{:S(2)}) %all-to-all-start) | async-done | bytes 65568 | tf_op jit(solution)/shard_map/all_to_all | solution.py:763
  64.9 1.2 %shard_map.141 = (f32[2,8,64]{2,1,0:T(8,128)}, bf16[128,128]{1,0:T(8,128)(2,1)}) custom-call(f32[16,8,128]{2,1,0:T(8,128)S(1)} %all-to-all-done.terms_ref, bf16[64,3584]{1,0:T(8,128)(2,1)S(1)} %get-tuple-element.58.chosen_ref, bf16[896,256]{1,0:T(8,128)(2,1)S(1)} %get-tuple-element.59.weights_ref, f32[2,8,64]{2,1,0:T(8,128)S(1)} %shard_map.132.refs_0_, ...), custom_call_target="tpu_custom_call" | custom-call | tf_op jit(solution)/shard_map/pallas_call | solution.py:665
  (35 shorter events, 2.5 us)
Async XLA Ops:
  0.6 7.2 %copy-start.1 = (bf16[64,3072]{1,0:T(8,128)(2,1)S(1)}, bf16[64,3072]{1,0:T(8,128)(2,1)}, u32[]{:S(2)}) copy-start(bf16[64,3072]{1,0:T(8,128)(2,1)} %embed_ref.3) | copy-start | bytes 1179652
  0.6 7.2 %copy-start.6 = (f32[1,1,3,3072]{3,1,2,0:T(1,128)S(1)}, f32[1,1,3,3072]{3,1,2,0:T(1,128)}, u32[]{:S(2)}) copy-start(f32[1,1,3,3072]{3,1,2,0:T(1,128)} %param.17) | copy-start | bytes 110596
  0.7 7.2 %copy-start.2 = (bf16[50,3,3072]{2,0,1:T(8,128)(2,1)S(1)}, bf16[50,3,3072]{2,0,1:T(8,128)(2,1)}, u32[]{:S(2)}) copy-start(bf16[50,3,3072]{2,0,1:T(8,128)(2,1)} %param.16) | copy-start | bytes 2764804
  0.7 7.2 %copy-start = (bf16[1,2304,3072]{2,1,0:T(8,128)(2,1)S(1)}, bf16[1,2304,3072]{2,1,0:T(8,128)(2,1)}, u32[]{:S(2)}) copy-start(bf16[1,2304,3072]{2,1,0:T(8,128)(2,1)} %param.14) | copy-start | bytes 42467332
  0.7 0.8 %copy-start.9 = (f32[2,8,64]{2,1,0:T(8,128)S(1)}, f32[2,8,64]{2,1,0:T(8,128)}, u32[]{:S(2)}) copy-start(f32[2,8,64]{2,1,0:T(8,128)} %latent_ref.1) | copy-start | bytes 12292
  1.5 11.0 %copy-start.3 = (bf16[1,1,1,2,32,1536]{5,4,3,2,1,0:T(8,128)(2,1)S(1)}, bf16[1,1,1,2,32,1536]{5,4,3,2,1,0:T(8,128)(2,1)}, u32[]{:S(2)}) copy-start(bf16[1,1,1,2,32,1536]{5,4,3,2,1,0:T(8,128)(2,1)} %param.18) | copy-start | bytes 589828
  1.5 11.0 %copy-start.7 = (s32[2]{0:T(128)S(1)}, s32[2]{0:T(128)}, u32[]{:S(2)}) copy-start(s32[2]{0:T(128)} %order_ref.3) | copy-start | bytes 28
  1.5 11.0 %collective-permute-start.2 = (f32[2,8,64]{2,1,0:T(8,128)S(1)}, f32[2,8,64]{2,1,0:T(8,128)S(1)}, u32[]{:S(2)}, u32[]{:S(2)}) collective-permute-start(f32[2,8,64]{2,1,0:T(8,128)S(1)} %shard_map.132.refs_0_), channel_id=1, source_target_pairs={{0,12},{4,8},{8,4},{12,0},{1,13},{5,9},{9,5},{13,1},{2,14},{6,10},... | collective-permute-start | bytes 12296 | tf_op jit(solution)/shard_map/ppermute | solution.py:705
  6.6 5.9 %collective-permute-start.1 = (f32[2,8,64]{2,1,0:T(8,128)S(1)}, f32[2,8,64]{2,1,0:T(8,128)S(1)}, u32[]{:S(2)}, u32[]{:S(2)}) collective-permute-start(f32[2,8,64]{2,1,0:T(8,128)S(1)} %shard_map.132.refs_0_), channel_id=1, source_target_pairs={{0,8},{4,12},{8,0},{12,4},{1,9},{5,13},{9,1},{13,5},{2,10},{6,14},... | collective-permute-start | bytes 12296 | tf_op jit(solution)/shard_map/ppermute | solution.py:705
  6.6 5.9 %collective-permute-start = (f32[2,8,64]{2,1,0:T(8,128)S(1)}, f32[2,8,64]{2,1,0:T(8,128)S(1)}, u32[]{:S(2)}, u32[]{:S(2)}) collective-permute-start(f32[2,8,64]{2,1,0:T(8,128)S(1)} %shard_map.132.refs_0_), channel_id=1, source_target_pairs={{0,4},{4,0},{8,12},{12,8},{1,5},{5,1},{9,13},{13,9},{2,6},{6,2},{1... | collective-permute-start | bytes 12296 | tf_op jit(solution)/shard_map/ppermute | solution.py:705
  14.9 8.1 %collective-permute-start.3 = (bf16[64,768]{1,0:T(8,128)(2,1)S(1)}, bf16[64,768]{1,0:T(8,128)(2,1)S(1)}, u32[]{:S(2)}, u32[]{:S(2)}) collective-permute-start(bf16[64,768]{1,0:T(8,128)(2,1)S(1)} %get-tuple-element.40), channel_id=1, source_target_pairs={{0,4},{4,0},{8,12},{12,8},{1,5},{5,1},{9,13},{13,9},{2,6},{6,2},{1... | collective-permute-start | bytes 294920 | tf_op jit(solution)/shard_map/ppermute | solution.py:705
  16.3 10.3 %collective-permute-start.4 = (bf16[64,768]{1,0:T(8,128)(2,1)S(1)}, bf16[64,768]{1,0:T(8,128)(2,1)S(1)}, u32[]{:S(2)}, u32[]{:S(2)}) collective-permute-start(bf16[64,768]{1,0:T(8,128)(2,1)S(1)} %get-tuple-element.41), channel_id=1, source_target_pairs={{0,8},{4,12},{8,0},{12,4},{1,9},{5,13},{9,1},{13,5},{2,10},{6,14},... | collective-permute-start | bytes 294920 | tf_op jit(solution)/shard_map/ppermute | solution.py:705
  19.3 7.4 %collective-permute-start.5 = (bf16[64,768]{1,0:T(8,128)(2,1)S(1)}, bf16[64,768]{1,0:T(8,128)(2,1)S(1)}, u32[]{:S(2)}, u32[]{:S(2)}) collective-permute-start(bf16[64,768]{1,0:T(8,128)(2,1)S(1)} %get-tuple-element.42), channel_id=1, source_target_pairs={{0,12},{4,8},{8,4},{12,0},{1,13},{5,9},{9,5},{13,1},{2,14},{6,10},... | collective-permute-start | bytes 294920 | tf_op jit(solution)/shard_map/ppermute | solution.py:705
  26.7 6.8 %collective-permute-start.8 = (bf16[64,768]{1,0:T(8,128)(2,1)S(1)}, bf16[64,768]{1,0:T(8,128)(2,1)S(1)}, u32[]{:S(2)}, u32[]{:S(2)}) collective-permute-start(bf16[64,768]{1,0:T(8,128)(2,1)S(1)} %shard_map.135), channel_id=1, source_target_pairs={{0,6},{2,4},{4,2},{6,0},{8,14},{10,12},{12,10},{14,8},{1,7},{3,5},... | collective-permute-start | bytes 294920 | tf_op jit(solution)/shard_map/ppermute | solution.py:733
  29.3 6.7 %collective-permute-start.7 = (bf16[64,768]{1,0:T(8,128)(2,1)S(1)}, bf16[64,768]{1,0:T(8,128)(2,1)S(1)}, u32[]{:S(2)}, u32[]{:S(2)}) collective-permute-start(bf16[64,768]{1,0:T(8,128)(2,1)S(1)} %shard_map.135), channel_id=1, source_target_pairs={{0,2},{2,0},{4,6},{6,4},{8,10},{10,8},{12,14},{14,12},{1,3},{3,1},... | collective-permute-start | bytes 294920 | tf_op jit(solution)/shard_map/ppermute | solution.py:733
  29.8 8.7 %collective-permute-start.6 = (bf16[64,768]{1,0:T(8,128)(2,1)S(1)}, bf16[64,768]{1,0:T(8,128)(2,1)S(1)}, u32[]{:S(2)}, u32[]{:S(2)}) collective-permute-start(bf16[64,768]{1,0:T(8,128)(2,1)S(1)} %shard_map.135), channel_id=1, source_target_pairs={{0,10},{2,8},{4,14},{6,12},{8,2},{10,0},{12,6},{14,4},{1,11},{3,9}... | collective-permute-start | bytes 294920 | tf_op jit(solution)/shard_map/ppermute | solution.py:733
  32.2 7.4 %collective-permute-start.9 = (bf16[64,768]{1,0:T(8,128)(2,1)S(1)}, bf16[64,768]{1,0:T(8,128)(2,1)S(1)}, u32[]{:S(2)}, u32[]{:S(2)}) collective-permute-start(bf16[64,768]{1,0:T(8,128)(2,1)S(1)} %shard_map.135), channel_id=1, source_target_pairs={{0,14},{2,12},{4,10},{6,8},{8,6},{10,4},{12,2},{14,0},{1,15},{3,13... | collective-permute-start | bytes 294920 | tf_op jit(solution)/shard_map/ppermute | solution.py:733
  38.6 14.5 %copy-start.4 = (bf16[3072,64]{0,1:T(8,128)(2,1)S(1)}, bf16[3072,64]{0,1:T(8,128)(2,1)}, u32[]{:S(2)}) copy-start(bf16[3072,64]{0,1:T(8,128)(2,1)} %param.19) | copy-start | bytes 1179652
  39.3 18.7 %copy-start.5 = (bf16[27,16,128]{2,1,0:T(8,128)(2,1)S(1)}, bf16[27,16,128]{2,1,0:T(8,128)(2,1)}, u32[]{:S(2)}) copy-start(bf16[27,16,128]{2,1,0:T(8,128)(2,1)} %conv_ref) | copy-start | bytes 331780
  39.3 18.7 %copy-start.8 = (s32[4]{0:T(128)S(1)}, s32[4]{0:T(128)}, u32[]{:S(2)}) copy-start(s32[4]{0:T(128)} %slab_ref) | copy-start | bytes 52
  42.3 4.7 %collective-permute-start.10 = (bf16[16,3072]{1,0:T(8,128)(2,1)S(1)}, bf16[16,3072]{1,0:T(8,128)(2,1)S(1)}, u32[]{:S(2)}, u32[]{:S(2)}) collective-permute-start(bf16[16,3072]{1,0:T(8,128)(2,1)S(1)} %get-tuple-element.53), channel_id=1, source_target_pairs={{0,4},{4,0},{8,12},{12,8},{1,5},{5,1},{9,13},{13,9},{2,6},{6,2},{1... | collective-permute-start | bytes 294920 | tf_op jit(solution)/shard_map/ppermute | solution.py:705
  44.0 9.1 %collective-permute-start.11 = (bf16[16,3072]{1,0:T(8,128)(2,1)S(1)}, bf16[16,3072]{1,0:T(8,128)(2,1)S(1)}, u32[]{:S(2)}, u32[]{:S(2)}) collective-permute-start(bf16[16,3072]{1,0:T(8,128)(2,1)S(1)} %get-tuple-element.54), channel_id=1, source_target_pairs={{0,8},{4,12},{8,0},{12,4},{1,9},{5,13},{9,1},{13,5},{2,10},{6,14},... | collective-permute-start | bytes 294920 | tf_op jit(solution)/shard_map/ppermute | solution.py:705
  46.2 6.9 %collective-permute-start.12 = (bf16[16,3072]{1,0:T(8,128)(2,1)S(1)}, bf16[16,3072]{1,0:T(8,128)(2,1)S(1)}, u32[]{:S(2)}, u32[]{:S(2)}) collective-permute-start(bf16[16,3072]{1,0:T(8,128)(2,1)S(1)} %get-tuple-element.55), channel_id=1, source_target_pairs={{0,12},{4,8},{8,4},{12,0},{1,13},{5,9},{9,5},{13,1},{2,14},{6,10},... | collective-permute-start | bytes 294920 | tf_op jit(solution)/shard_map/ppermute | solution.py:705
  54.0 10.9 %all-to-all-start = ((f32[16,8,128]{2,1,0:T(8,128)}), f32[16,8,128]{2,1,0:T(8,128)S(1)}, u32[]{:S(2)}, u32[]{:S(2)}) async-start(f32[16,8,128]{2,1,0:T(8,128)} %shard_map.139), calls=%async_computation | async-start | bytes 131072 | tf_op jit(solution)/shard_map/all_to_all | solution.py:763

commit v8 on v7

--- a/solution.py
+++ b/solution.py
@@ -204,23 +204,26 @@
     return [pltpu.with_memory_space_constraint(value, pltpu.HBM) for value in values]
 
 
-def stage_kernel(latent_ref, staged_ref):
-    staged_ref[...] = latent_ref[...]
+def stage_kernel(latent_hbm, staged_ref, sem):
+    copy = pltpu.make_async_copy(latent_hbm, staged_ref, sem)
+    copy.start()
+    copy.wait()
 
 
 def staged(latent):
     return pl.pallas_call(
         stage_kernel,
-        in_specs=[whole()],
+        in_specs=[whole(pltpu.HBM)],
         out_specs=whole(),
-        out_shape=jax.ShapeDtypeStruct(latent.shape, latent.dtype),
+        out_shape=pltpu.VMEM(latent.shape, latent.dtype),
+        scratch_shapes=[pltpu.SemaphoreType.DMA],
         cost_estimate=pl.CostEstimate(flops=10**10, bytes_accessed=0, transcendentals=0),
         compiler_params=kernel_params(),
-    )(latent)
+    )(*in_hbm(latent))
 
 
 def prepare_kernel(
-    timestep_ref, table_ref, cond_ref, embed_ref, qkv_ref, out_hbm, rows_ref, heads_ref, term_ref, out_ref, lhs, sem
+    timestep_ref, table_ref, cond_ref, embed_ref, qkv_ref, out_hbm, rows_ref, heads_ref, out_ref, lhs, sem
 ):
     out_copy = pltpu.make_async_copy(out_hbm, out_ref, sem)
     out_copy.start()
@@ -231,15 +234,17 @@
         row = jnp.dot(chosen, table_ref[j], preferred_element_type=jnp.float32)[:1]
         rows_ref[j : j + 1, :] = row + cond_ref[j] + (1.0 if j == 1 else 0.0)
     count = embed_ref.shape[0]
+    spare, depth = lhs.shape[0] - count, lhs.shape[1]
     lhs[:count] = (embed_ref[...].astype(jnp.float32) * rows_ref[1:2]).astype(jnp.bfloat16)
-    lhs[count:] = jnp.broadcast_to(rows_ref[0:1], (16, lhs.shape[1])).astype(jnp.bfloat16)
+    lhs[count:] = jnp.broadcast_to(rows_ref[0:1], (spare, depth)).astype(jnp.bfloat16)
+    lane = lax.broadcasted_iota(jnp.int32, (PART, lhs.shape[0]), 1)
     for j in range(0, qkv_ref.shape[0], PART):
-        lane = slice(j, j + PART)
         product = lax.dot_general(
-            lhs[...], qkv_ref[lane, :], NT, preferred_element_type=jnp.float32
-        )
-        heads_ref[:, lane] = product[:count].astype(jnp.bfloat16)
-        term_ref[:, lane] = product[count:]
+            qkv_ref[j : j + PART, :], lhs[...], NT, preferred_element_type=jnp.float32
+        )
+        upper = product.astype(jnp.bfloat16).astype(jnp.float32)
+        value = jnp.where(lane == count + 1, product - upper, upper)
+        heads_ref[j : j + PART, :] = jnp.where(lane <= count + 2, value, 0.0).astype(jnp.bfloat16)
     out_copy.wait()
 
 
@@ -249,15 +254,14 @@
     return pl.pallas_call(
         prepare_kernel,
         in_specs=[whole(pltpu.SMEM)] + [whole()] * 4 + [whole(pltpu.HBM)],
-        out_specs=[whole()] * 4,
+        out_specs=[whole()] * 3,
         out_shape=[
             jax.ShapeDtypeStruct((3, depth), jnp.float32),
-            jax.ShapeDtypeStruct((count, lanes), jnp.bfloat16),
-            jax.ShapeDtypeStruct((16, lanes), jnp.float32),
+            jax.ShapeDtypeStruct((lanes, 2 * count), jnp.bfloat16),
             pltpu.VMEM(out.shape, out.dtype),
         ],
         scratch_shapes=[
-            pltpu.VMEM((count + 16, depth), jnp.bfloat16),
+            pltpu.VMEM((2 * count, depth), jnp.bfloat16),
             pltpu.SemaphoreType.DMA,
         ],
         compiler_params=kernel_params(),
@@ -324,72 +328,84 @@
 
 
 def first_layer_kernel(
-    count, order_ref, embed_ref, heads_ref, term_ref, stale_ref, out_ref, *refs
+    count, order_ref, embed_ref, heads_ref, stale_ref, out_ref, *refs
 ):
     latent_refs, refs = refs[:count], refs[count:]
     block_refs, (own_ref, latents, attended, keys, values) = refs[:count], refs[count:]
     place = lax.axis_index("seq")
     rows_dev = MICRO * TOK_DEV
+    width = embed_ref.shape[0]
     for k in range(count):
         first = pl.multiple_of((place ^ k) * rows_dev, rows_dev)
-        latents[pl.ds(first, rows_dev), :] = (
-            latent_refs[k][...].reshape(rows_dev, latents.shape[1]).astype(jnp.bfloat16)
-        )
-    embedded = jnp.dot(latents[...], embed_ref[...], preferred_element_type=jnp.float32)
+        latents[pl.ds(first, rows_dev), :width] = (
+            latent_refs[k][...].reshape(rows_dev, width).astype(jnp.bfloat16)
+        )
+    embedded = jnp.dot(latents[:, :width], embed_ref[...], preferred_element_type=jnp.float32)
     embedded = embedded.astype(jnp.bfloat16).astype(jnp.float32)
-    norm = lax.rsqrt(jnp.mean(embedded * embedded, axis=-1, keepdims=True) + norm_eps)
-    projected = jnp.dot(latents[...], heads_ref[...], preferred_element_type=jnp.float32)
-    projected = (norm * projected + term_ref[:1]).astype(jnp.bfloat16)
+    square = jnp.mean(embedded * embedded, axis=-1, keepdims=True) + norm_eps
+    norm = lax.rsqrt(square)
+    size = square * norm
+    upper = size.astype(jnp.bfloat16).astype(jnp.float32)
+    lane = lax.broadcasted_iota(jnp.int32, (latents.shape[0], width), 1)
+    spare = jnp.where(lane < 2, upper, jnp.where(lane == 2, size - upper, 0.0))
+    latents[:, width:] = spare.astype(jnp.bfloat16)
+    projected = lax.dot_general(
+        latents[...], heads_ref[...], NT, preferred_element_type=jnp.float32
+    )
+    projected = (norm * projected).astype(jnp.bfloat16)
     attend(projected, order_ref, stale_ref, attended, keys, values)
     columns = own_ref.shape[1]
     first = pl.multiple_of(place * columns, columns)
     own_ref[...] = jnp.dot(
-        latents[...], embed_ref[:, pl.ds(first, columns)], preferred_element_type=jnp.float32
+        latents[:, :width], embed_ref[:, pl.ds(first, columns)], preferred_element_type=jnp.float32
     ).astype(jnp.bfloat16)
     column_blocks(place, attended, out_ref, block_refs)
 
 
-def first_layer(patch_order, latents, w_embed, heads, term, stale, out):
+def first_layer(patch_order, latents, w_embed, heads, stale, out):
     count = len(latents)
     rows = count * MICRO * TOK_DEV
     lanes, depth = out.shape
     block = jax.ShapeDtypeStruct((rows, depth // count), jnp.bfloat16)
     return pl.pallas_call(
         functools.partial(first_layer_kernel, count),
-        in_specs=[whole(pltpu.SMEM)] + [whole()] * (5 + count),
+        in_specs=[whole(pltpu.SMEM)] + [whole()] * (4 + count),
         out_specs=[whole()] * (count + 1),
         out_shape=[block] * (count + 1),
         scratch_shapes=[
-            pltpu.VMEM((rows, w_embed.shape[0]), jnp.bfloat16),
+            pltpu.VMEM((rows, 2 * w_embed.shape[0]), jnp.bfloat16),
             *attention_scratch(rows, stale.shape[1], lanes),
         ],
         compiler_params=kernel_params(),
-    )(patch_order, w_embed, heads, term, stale, out, *latents)
-
-
-def turn_kernel(after_ref, qkv_ref, turned_ref, done_ref):
+    )(patch_order, w_embed, heads, stale, out, *latents)
+
+
+def turn_kernel(after_ref, qkv_ref, heads_ref, turned_ref, term_ref):
     lanes, depth = qkv_ref.shape
     for i in range(0, lanes, TILE):
         for j in range(0, depth, TILE):
             turned_ref[j : j + TILE, i : i + TILE] = qkv_ref[i : i + TILE, j : j + TILE].T
-    done_ref[...] = jnp.zeros_like(done_ref)
-
-
-def turned(qkv, after):
+    count = heads_ref.shape[1] // 2
+    for i in range(0, lanes, TILE):
+        across = heads_ref[i : i + TILE, :].astype(jnp.float32).T
+        term_ref[:, i : i + TILE] = across[count : count + 1] + across[count + 1 : count + 2]
+
+
+def turned(qkv, heads, after):
     return pl.pallas_call(
         turn_kernel,
-        in_specs=[whole(pl.ANY), whole()],
+        in_specs=[whole(pl.ANY)] + [whole()] * 2,
         out_specs=[whole()] * 2,
         out_shape=[
             pltpu.VMEM(qkv.shape[::-1], qkv.dtype),
-            jax.ShapeDtypeStruct((8, 128), jnp.float32),
+            jax.ShapeDtypeStruct((1, qkv.shape[0]), jnp.float32),
         ],
         cost_estimate=pl.CostEstimate(flops=5 * 10**9, bytes_accessed=0, transcendentals=0),
         compiler_params=kernel_params(),
-    )(after, qkv)
-
-
-def block_sum_kernel(rows_ref, own_ref, done_ref, *refs):
+    )(after, qkv, heads)
+
+
+def block_sum_kernel(rows_ref, own_ref, term_ref, *refs):
     part_refs, block_ref = refs[:-1], refs[-1]
     columns = own_ref.shape[1]
     first = pl.multiple_of(lax.axis_index("seq") * columns, columns)
@@ -400,14 +416,14 @@
     block_ref[...] = (own_ref[...].astype(jnp.float32) + gate * mixed).astype(jnp.bfloat16)
 
 
-def block_sum(mod_rows, own, done, parts):
+def block_sum(mod_rows, own, term, parts):
     return pl.pallas_call(
         block_sum_kernel,
         in_specs=[whole()] * (3 + len(parts)),
         out_specs=whole(),
         out_shape=jax.ShapeDtypeStruct(own.shape, own.dtype),
         compiler_params=kernel_params(),
-    )(mod_rows, own, done, *parts)
+    )(mod_rows, own, term, *parts)
 
 
 def scaled_piece(place, k, piece_ref, rows_ref):
@@ -708,7 +724,7 @@
     numbers = tuple(range(seq_count))
     half = (seq_count + 1) // 2
     latents = returned([staged(latent)] * seq_count)
-    mod_rows, head_embed, shift_term, out = prepared(
+    mod_rows, head_embed, out = prepared(
         timestep,
         jnp.transpose(mod_table, (1, 0, 2)),
         jnp.transpose(cond_mod[0], (1, 0, 2)),
@@ -718,11 +734,11 @@
     )
     stale = stale_kv[0, 0, 0]
     *blocks, own = first_layer(
-        patch_order, latents, w_embed, head_embed, shift_term, stale, out
-    )
-    qkv, done = turned(w_qkv[0], own)
+        patch_order, latents, w_embed, head_embed, stale, out
+    )
+    qkv, shift_term = turned(w_qkv[0], head_embed, own)
     for step in range(1, segment_count):
-        block = block_sum(mod_rows, own, done, returned(blocks))
+        block = block_sum(mod_rows, own, shift_term, returned(blocks))
         pieces = []
         for k in numbers[::-1]:
             pairs = [

time: 66.4 us -> 66 us (level)
  local copies, waits for them, and re-layouts: 0.88 us -> 0.05 us
    pallas_call x2, Pallas kernels: 3.69 us -> 4.7 us  [the longest x1 3.84 us: turned(): pl.pallas_call(turn_kernel, in_specs=[whole(pl.ANY)] + [whole()] * 2, out...]
    unnamed x20 -> x18, local copies, waits for them, and re-layouts: 0.88 us -> 0.05 us
  transfers between devices with their start and end apart: 14 -> 14, of which waited for: 7 -> 7; matrix products, arithmetic and copies ran while one was open for 0% -> 0% of each run, Pallas kernels for 19% -> 18%
where the time goes in v8:
time: 66 us; the launch traced here: 65.7 us
  starting transfers between devices  25.5 us (39%)
  Pallas kernels  20.3 us (31%)
  waiting for transfers between devices  18.3 us (28%)
  between operations  1.52 us (2%)
    ppermute x9, starting transfers between devices, returned(): lax.ppermute(values[k], 'seq', within(k))  14.7 us
    ppermute x9, waiting for transfers between devices, returned(): lax.ppermute(values[k], 'seq', within(k))  9.55 us
    ppermute x4, starting transfers between devices, shards(): pieces.insert(0, lax.ppermute(block, ('seq', 'segment'), pairs))  6.81 us
    all_to_all x1, waiting for transfers between devices, shards(): lax.all_to_all(terms, peers, split_axis=0, concat_axis=0, tiled=True)  4.79 us
    pallas_call x1, Pallas kernels, prepared(): pl.pallas_call(prepare_kernel, in_specs=[whole(pltpu.SMEM)] + [whole()] *...  4.05 us
    all_to_all x1, starting transfers between devices, shards(): lax.all_to_all(terms, peers, split_axis=0, concat_axis=0, tiled=True)  4.02 us
    ppermute x4, waiting for transfers between devices, shards(): pieces.insert(0, lax.ppermute(block, ('seq', 'segment'), pairs))  3.96 us
    pallas_call x1, Pallas kernels, turned(): pl.pallas_call(turn_kernel, in_specs=[whole(pl.ANY)] + [whole()] * 2, out...  3.84 us
  transfers between devices with their start and end apart: 14, of which 7 were waited for; matrix products, arithmetic and copies ran while one was open for 0% of the time, Pallas kernels for 18%

profile of v8, /device:TPU:0, one launch (start us, length us, event | category | flops | bytes accessed | tf_op | source)
XLA Modules:
  0.0 65.7 jit_solution(12729082135547396314)
XLA Ops:
  0.7 0.9 %shard_map.132.refs_0_ = f32[2,8,64]{2,1,0:T(8,128)S(1)} custom-call(f32[2,8,64]{2,1,0:T(8,128)} %latent_hbm.1), custom_call_target="tpu_custom_call" | custom-call | flops 10000000000 | tf_op jit(solution)/shard_map/pallas_call | solution.py:214
  1.6 5.1 %collective-permute-start.2 = (f32[2,8,64]{2,1,0:T(8,128)S(1)}, f32[2,8,64]{2,1,0:T(8,128)S(1)}, u32[]{:S(2)}, u32[]{:S(2)}) collective-permute-start(f32[2,8,64]{2,1,0:T(8,128)S(1)} %shard_map.132.refs_0_), channel_id=1, source_target_pairs={{0,12},{4,8},{8,4},{12,0},{1,13},{5,9},{9,5},{13,1},{2,14},{6,10},... | collective-permute-start | bytes 12296 | tf_op jit(solution)/shard_map/ppermute | solution.py:721
  8.0 4.1 %shard_map.131 = (f32[3,3072]{1,0:T(4,128)S(1)}, bf16[2304,128]{1,0:T(8,128)(2,1)S(1)}, bf16[768,3072]{1,0:T(8,128)(2,1)S(1)}) custom-call(s32[1]{0:T(128)S(6)} %copy.14.timestep_ref, bf16[3,50,3072]{2,1,0:T(8,128)(2,1)S(1)} %bitcast.9, f32[3,1,3072]{2,1,0:T(1,128)S(1)} %bitcast.13, bf16[64,3072]{1,0:T(8,128)(2,1)S(1)} %copy-done.1, ...), custom_call_target="tpu_custom_call" | custom-call | tf_op jit(solution)/shard_map/pallas_call | solution.py:254
  12.1 2.5 %shard_map.133 = (bf16[64,768]{1,0:T(8,128)(2,1)S(1)}, bf16[64,768]{1,0:T(8,128)(2,1)S(1)}, bf16[64,768]{1,0:T(8,128)(2,1)S(1)}, bf16[64,768]{1,0:T(8,128)(2,1)S(1)}, bf16[64,768]{1,0:T(8,128)(2,1)S(1)}) custom-call(s32[2]{0:T(128)S(1)} %copy-done.7, bf16[64,3072]{1,0:T(8,128)(2,1)S(1)} %copy-done.1, bf16[2304,128]{1,0:T(8,128)(2,1)S(1)} %get-tuple-element.32.heads_ref, ...), custom_call_target="tpu_custom_call" | custom-call | tf_op jit(solution)/shard_map/pallas_call | solution.py:370
  14.6 1.5 %collective-permute-start.3 = (bf16[64,768]{1,0:T(8,128)(2,1)S(1)}, bf16[64,768]{1,0:T(8,128)(2,1)S(1)}, u32[]{:S(2)}, u32[]{:S(2)}) collective-permute-start(bf16[64,768]{1,0:T(8,128)(2,1)S(1)} %get-tuple-element.38), channel_id=1, source_target_pairs={{0,4},{4,0},{8,12},{12,8},{1,5},{5,1},{9,13},{13,9},{2,6},{6,2},{1... | collective-permute-start | bytes 294920 | tf_op jit(solution)/shard_map/ppermute | solution.py:721
  16.1 2.9 %collective-permute-start.4 = (bf16[64,768]{1,0:T(8,128)(2,1)S(1)}, bf16[64,768]{1,0:T(8,128)(2,1)S(1)}, u32[]{:S(2)}, u32[]{:S(2)}) collective-permute-start(bf16[64,768]{1,0:T(8,128)(2,1)S(1)} %get-tuple-element.39), channel_id=1, source_target_pairs={{0,8},{4,12},{8,0},{12,4},{1,9},{5,13},{9,1},{13,5},{2,10},{6,14},... | collective-permute-start | bytes 294920 | tf_op jit(solution)/shard_map/ppermute | solution.py:721
  19.1 3.8 %shard_map.134 = (bf16[3072,2304]{1,0:T(8,128)(2,1)S(1)}, f32[1,2304]{1,0:T(1,128)S(1)}) custom-call(bf16[64,768]{1,0:T(8,128)(2,1)S(1)} %get-tuple-element.34.after_ref.own_ref, bf16[2304,3072]{1,0:T(8,128)(2,1)S(1)} %bitcast.8, bf16[2304,128]{1,0:T(8,128)(2,1)S(1)} %get-tuple-element.32.heads_ref), custom_call_target="tpu_custom_call" | custom-call | flops 5000000000 | tf_op jit(solution)/shard_map/pallas_call | solution.py:395
  22.9 3.3 %collective-permute-done.4.refs_2_ = bf16[64,768]{1,0:T(8,128)(2,1)S(1)} collective-permute-done((bf16[64,768]{1,0:T(8,128)(2,1)S(1)}, bf16[64,768]{1,0:T(8,128)(2,1)S(1)}, u32[]{:S(2)}, u32[]{:S(2)}) %collective-permute-start.4) | collective-permute-done | bytes 98336 | tf_op jit(solution)/shard_map/ppermute | solution.py:721
  26.3 2.6 %collective-permute-start.8 = (bf16[64,768]{1,0:T(8,128)(2,1)S(1)}, bf16[64,768]{1,0:T(8,128)(2,1)S(1)}, u32[]{:S(2)}, u32[]{:S(2)}) collective-permute-start(bf16[64,768]{1,0:T(8,128)(2,1)S(1)} %shard_map.135), channel_id=1, source_target_pairs={{0,6},{2,4},{4,2},{6,0},{8,14},{10,12},{12,10},{14,8},{1,7},{3,5},... | collective-permute-start | bytes 294920 | tf_op jit(solution)/shard_map/ppermute | solution.py:749
  29.5 2.4 %collective-permute-start.6 = (bf16[64,768]{1,0:T(8,128)(2,1)S(1)}, bf16[64,768]{1,0:T(8,128)(2,1)S(1)}, u32[]{:S(2)}, u32[]{:S(2)}) collective-permute-start(bf16[64,768]{1,0:T(8,128)(2,1)S(1)} %shard_map.135), channel_id=1, source_target_pairs={{0,10},{2,8},{4,14},{6,12},{8,2},{10,0},{12,6},{14,4},{1,11},{3,9}... | collective-permute-start | bytes 294920 | tf_op jit(solution)/shard_map/ppermute | solution.py:749
  31.8 1.3 %collective-permute-start.9 = (bf16[64,768]{1,0:T(8,128)(2,1)S(1)}, bf16[64,768]{1,0:T(8,128)(2,1)S(1)}, u32[]{:S(2)}, u32[]{:S(2)}) collective-permute-start(bf16[64,768]{1,0:T(8,128)(2,1)S(1)} %shard_map.135), channel_id=1, source_target_pairs={{0,14},{2,12},{4,10},{6,8},{8,6},{10,4},{12,2},{14,0},{1,15},{3,13... | collective-permute-start | bytes 294920 | tf_op jit(solution)/shard_map/ppermute | solution.py:749
  33.2 2.5 %collective-permute-done.7.refs_0_ = bf16[64,768]{1,0:T(8,128)(2,1)S(1)} collective-permute-done((bf16[64,768]{1,0:T(8,128)(2,1)S(1)}, bf16[64,768]{1,0:T(8,128)(2,1)S(1)}, u32[]{:S(2)}, u32[]{:S(2)}) %collective-permute-start.7) | collective-permute-done | bytes 98336 | tf_op jit(solution)/shard_map/ppermute | solution.py:749
  35.6 1.3 %shard_map.136 = (f32[64,2304]{1,0:T(8,128)S(1)}, f32[64,1]{1,0:T(8,128)S(1)}) custom-call(f32[3,3072]{1,0:T(4,128)S(1)} %get-tuple-element.31.rows_ref, bf16[3072,2304]{1,0:T(8,128)(2,1)S(1)} %get-tuple-element.35.turned_ref.qkv_ref, bf16[64,768]{1,0:T(8,128)(2,1)S(1)} %collective-permute-done.7.refs_0_, bf16[64,768]{1,0:T(8,128)(2,1)S(1)} %collective-permute-done.8.refs_1_), custom_call_target="tpu_custom_call" | custom-call | tf_op jit(solution)/shard_map/pallas_call | solution.py:462
  37.0 1.2 %collective-permute-done.6.refs_0_.refs_2_ = bf16[64,768]{1,0:T(8,128)(2,1)S(1)} collective-permute-done((bf16[64,768]{1,0:T(8,128)(2,1)S(1)}, bf16[64,768]{1,0:T(8,128)(2,1)S(1)}, u32[]{:S(2)}, u32[]{:S(2)}) %collective-permute-start.6) | collective-permute-done | bytes 98336 | tf_op jit(solution)/shard_map/ppermute | solution.py:749
  38.2 0.8 %shard_map.137 = (f32[64,2304]{1,0:T(8,128)S(1)}, f32[64,1]{1,0:T(8,128)S(1)}) custom-call(f32[3,3072]{1,0:T(4,128)S(1)} %get-tuple-element.31.rows_ref, bf16[3072,2304]{1,0:T(8,128)(2,1)S(1)} %get-tuple-element.35.turned_ref.qkv_ref, bf16[64,768]{1,0:T(8,128)(2,1)S(1)} %collective-permute-done.6.refs_0_.refs_2_, f32[64,2304]{1,0:T(8,128)S(1)} %get-tuple-element.41.refs_1_, ...), custom_call_target="tpu_custom_call" | custom-call | tf_op jit(solution)/shard_map/pallas_call | solution.py:462
  39.2 2.7 %shard_map.138 = (bf16[16,3072]{1,0:T(8,128)(2,1)S(1)}, bf16[16,3072]{1,0:T(8,128)(2,1)S(1)}, bf16[16,3072]{1,0:T(8,128)(2,1)S(1)}, bf16[16,3072]{1,0:T(8,128)(2,1)S(1)}, bf16[16,3072]{1,0:T(8,128)(2,1)S(1)}) custom-call(s32[2]{0:T(128)S(1)} %copy-done.7, f32[3,3072]{1,0:T(4,128)S(1)} %get-tuple-element.31.rows_ref, ...), custom_call_target="tpu_custom_call" | custom-call | tf_op jit(solution)/shard_map/pallas_call | solution.py:514
  41.9 1.7 %collective-permute-start.10 = (bf16[16,3072]{1,0:T(8,128)(2,1)S(1)}, bf16[16,3072]{1,0:T(8,128)(2,1)S(1)}, u32[]{:S(2)}, u32[]{:S(2)}) collective-permute-start(bf16[16,3072]{1,0:T(8,128)(2,1)S(1)} %get-tuple-element.51), channel_id=1, source_target_pairs={{0,4},{4,0},{8,12},{12,8},{1,5},{5,1},{9,13},{13,9},{2,6},{6,2},{1... | collective-permute-start | bytes 294920 | tf_op jit(solution)/shard_map/ppermute | solution.py:721
  43.6 2.1 %collective-permute-start.11 = (bf16[16,3072]{1,0:T(8,128)(2,1)S(1)}, bf16[16,3072]{1,0:T(8,128)(2,1)S(1)}, u32[]{:S(2)}, u32[]{:S(2)}) collective-permute-start(bf16[16,3072]{1,0:T(8,128)(2,1)S(1)} %get-tuple-element.52), channel_id=1, source_target_pairs={{0,8},{4,12},{8,0},{12,4},{1,9},{5,13},{9,1},{13,5},{2,10},{6,14},... | collective-permute-start | bytes 294920 | tf_op jit(solution)/shard_map/ppermute | solution.py:721
  46.6 6.0 %collective-permute-done.11.refs_2_ = bf16[16,3072]{1,0:T(8,128)(2,1)S(1)} collective-permute-done((bf16[16,3072]{1,0:T(8,128)(2,1)S(1)}, bf16[16,3072]{1,0:T(8,128)(2,1)S(1)}, u32[]{:S(2)}, u32[]{:S(2)}) %collective-permute-start.11) | collective-permute-done | bytes 98336 | tf_op jit(solution)/shard_map/ppermute | solution.py:721
  52.6 0.9 %shard_map.139 = f32[16,8,128]{2,1,0:T(8,128)} custom-call(f32[3,3072]{1,0:T(4,128)S(1)} %get-tuple-element.31.rows_ref, bf16[16,3072]{1,0:T(8,128)(2,1)S(1)} %get-tuple-element.45.own_ref, bf16[64,3072]{1,0:T(8,128)(2,1)S(1)} %bitcast.12, bf16[16,3072]{1,0:T(8,128)(2,1)S(1)} %get-tuple-element.50.refs_0_, ...), custom_call_target="tpu_custom_call" | custom-call | tf_op jit(solution)/shard_map/pallas_call | solution.py:548
  53.5 4.0 %all-to-all-start = ((f32[16,8,128]{2,1,0:T(8,128)}), f32[16,8,128]{2,1,0:T(8,128)S(1)}, u32[]{:S(2)}, u32[]{:S(2)}) async-start(f32[16,8,128]{2,1,0:T(8,128)} %shard_map.139), calls=%async_computation | async-start | bytes 131072 | tf_op jit(solution)/shard_map/all_to_all | solution.py:779
  57.6 2.1 %shard_map.140 = (bf16[64,3584]{1,0:T(8,128)(2,1)S(1)}, bf16[896,256]{1,0:T(8,128)(2,1)S(1)}) custom-call(s32[4]{0:T(128)S(1)} %copy-done.8, bf16[27,16,128]{2,1,0:T(8,128)(2,1)S(1)} %copy-done.5), custom_call_target="tpu_custom_call" | custom-call | tf_op jit(solution)/shard_map/pallas_call | solution.py:610
  59.6 4.8 %all-to-all-done.terms_ref = f32[16,8,128]{2,1,0:T(8,128)S(1)} async-done(((f32[16,8,128]{2,1,0:T(8,128)}), f32[16,8,128]{2,1,0:T(8,128)S(1)}, u32[]{:S(2)}, u32[]{:S(2)}) %all-to-all-start) | async-done | bytes 65568 | tf_op jit(solution)/shard_map/all_to_all | solution.py:779
  64.4 1.2 %shard_map.141 = (f32[2,8,64]{2,1,0:T(8,128)}, bf16[128,128]{1,0:T(8,128)(2,1)}) custom-call(f32[16,8,128]{2,1,0:T(8,128)S(1)} %all-to-all-done.terms_ref, bf16[64,3584]{1,0:T(8,128)(2,1)S(1)} %get-tuple-element.56.chosen_ref, bf16[896,256]{1,0:T(8,128)(2,1)S(1)} %get-tuple-element.57.weights_ref, f32[2,8,64]{2,1,0:T(8,128)S(1)} %shard_map.132.refs_0_, ...), custom_call_target="tpu_custom_call" | custom-call | tf_op jit(solution)/shard_map/pallas_call | solution.py:681
  (33 shorter events, 2.5 us)
Async XLA Ops:
  0.6 7.3 %copy-start.1 = (bf16[64,3072]{1,0:T(8,128)(2,1)S(1)}, bf16[64,3072]{1,0:T(8,128)(2,1)}, u32[]{:S(2)}) copy-start(bf16[64,3072]{1,0:T(8,128)(2,1)} %embed_ref.3) | copy-start | bytes 1179652
  0.6 7.3 %copy-start.6 = (f32[1,1,3,3072]{3,1,2,0:T(1,128)S(1)}, f32[1,1,3,3072]{3,1,2,0:T(1,128)}, u32[]{:S(2)}) copy-start(f32[1,1,3,3072]{3,1,2,0:T(1,128)} %param.17) | copy-start | bytes 110596
  0.7 7.3 %copy-start.2 = (bf16[50,3,3072]{2,0,1:T(8,128)(2,1)S(1)}, bf16[50,3,3072]{2,0,1:T(8,128)(2,1)}, u32[]{:S(2)}) copy-start(bf16[50,3,3072]{2,0,1:T(8,128)(2,1)} %param.16) | copy-start | bytes 2764804
  0.7 7.3 %copy-start = (bf16[1,2304,3072]{2,1,0:T(8,128)(2,1)S(1)}, bf16[1,2304,3072]{2,1,0:T(8,128)(2,1)}, u32[]{:S(2)}) copy-start(bf16[1,2304,3072]{2,1,0:T(8,128)(2,1)} %param.14) | copy-start | bytes 42467332
  1.5 10.6 %copy-start.3 = (bf16[1,1,1,2,32,1536]{5,4,3,2,1,0:T(8,128)(2,1)S(1)}, bf16[1,1,1,2,32,1536]{5,4,3,2,1,0:T(8,128)(2,1)}, u32[]{:S(2)}) copy-start(bf16[1,1,1,2,32,1536]{5,4,3,2,1,0:T(8,128)(2,1)} %param.18) | copy-start | bytes 589828
  1.5 10.6 %copy-start.7 = (s32[2]{0:T(128)S(1)}, s32[2]{0:T(128)}, u32[]{:S(2)}) copy-start(s32[2]{0:T(128)} %order_ref.3) | copy-start | bytes 28
  1.6 10.5 %collective-permute-start.2 = (f32[2,8,64]{2,1,0:T(8,128)S(1)}, f32[2,8,64]{2,1,0:T(8,128)S(1)}, u32[]{:S(2)}, u32[]{:S(2)}) collective-permute-start(f32[2,8,64]{2,1,0:T(8,128)S(1)} %shard_map.132.refs_0_), channel_id=1, source_target_pairs={{0,12},{4,8},{8,4},{12,0},{1,13},{5,9},{9,5},{13,1},{2,14},{6,10},... | collective-permute-start | bytes 12296 | tf_op jit(solution)/shard_map/ppermute | solution.py:721
  6.7 5.4 %collective-permute-start.1 = (f32[2,8,64]{2,1,0:T(8,128)S(1)}, f32[2,8,64]{2,1,0:T(8,128)S(1)}, u32[]{:S(2)}, u32[]{:S(2)}) collective-permute-start(f32[2,8,64]{2,1,0:T(8,128)S(1)} %shard_map.132.refs_0_), channel_id=1, source_target_pairs={{0,8},{4,12},{8,0},{12,4},{1,9},{5,13},{9,1},{13,5},{2,10},{6,14},... | collective-permute-start | bytes 12296 | tf_op jit(solution)/shard_map/ppermute | solution.py:721
  6.7 5.4 %collective-permute-start = (f32[2,8,64]{2,1,0:T(8,128)S(1)}, f32[2,8,64]{2,1,0:T(8,128)S(1)}, u32[]{:S(2)}, u32[]{:S(2)}) collective-permute-start(f32[2,8,64]{2,1,0:T(8,128)S(1)} %shard_map.132.refs_0_), channel_id=1, source_target_pairs={{0,4},{4,0},{8,12},{12,8},{1,5},{5,1},{9,13},{13,9},{2,6},{6,2},{1... | collective-permute-start | bytes 12296 | tf_op jit(solution)/shard_map/ppermute | solution.py:721
  14.6 8.3 %collective-permute-start.3 = (bf16[64,768]{1,0:T(8,128)(2,1)S(1)}, bf16[64,768]{1,0:T(8,128)(2,1)S(1)}, u32[]{:S(2)}, u32[]{:S(2)}) collective-permute-start(bf16[64,768]{1,0:T(8,128)(2,1)S(1)} %get-tuple-element.38), channel_id=1, source_target_pairs={{0,4},{4,0},{8,12},{12,8},{1,5},{5,1},{9,13},{13,9},{2,6},{6,2},{1... | collective-permute-start | bytes 294920 | tf_op jit(solution)/shard_map/ppermute | solution.py:721
  16.1 10.2 %collective-permute-start.4 = (bf16[64,768]{1,0:T(8,128)(2,1)S(1)}, bf16[64,768]{1,0:T(8,128)(2,1)S(1)}, u32[]{:S(2)}, u32[]{:S(2)}) collective-permute-start(bf16[64,768]{1,0:T(8,128)(2,1)S(1)} %get-tuple-element.39), channel_id=1, source_target_pairs={{0,8},{4,12},{8,0},{12,4},{1,9},{5,13},{9,1},{13,5},{2,10},{6,14},... | collective-permute-start | bytes 294920 | tf_op jit(solution)/shard_map/ppermute | solution.py:721
  19.0 7.3 %collective-permute-start.5 = (bf16[64,768]{1,0:T(8,128)(2,1)S(1)}, bf16[64,768]{1,0:T(8,128)(2,1)S(1)}, u32[]{:S(2)}, u32[]{:S(2)}) collective-permute-start(bf16[64,768]{1,0:T(8,128)(2,1)S(1)} %get-tuple-element.40), channel_id=1, source_target_pairs={{0,12},{4,8},{8,4},{12,0},{1,13},{5,9},{9,5},{13,1},{2,14},{6,10},... | collective-permute-start | bytes 294920 | tf_op jit(solution)/shard_map/ppermute | solution.py:721
  26.3 6.8 %collective-permute-start.8 = (bf16[64,768]{1,0:T(8,128)(2,1)S(1)}, bf16[64,768]{1,0:T(8,128)(2,1)S(1)}, u32[]{:S(2)}, u32[]{:S(2)}) collective-permute-start(bf16[64,768]{1,0:T(8,128)(2,1)S(1)} %shard_map.135), channel_id=1, source_target_pairs={{0,6},{2,4},{4,2},{6,0},{8,14},{10,12},{12,10},{14,8},{1,7},{3,5},... | collective-permute-start | bytes 294920 | tf_op jit(solution)/shard_map/ppermute | solution.py:749
  29.0 6.7 %collective-permute-start.7 = (bf16[64,768]{1,0:T(8,128)(2,1)S(1)}, bf16[64,768]{1,0:T(8,128)(2,1)S(1)}, u32[]{:S(2)}, u32[]{:S(2)}) collective-permute-start(bf16[64,768]{1,0:T(8,128)(2,1)S(1)} %shard_map.135), channel_id=1, source_target_pairs={{0,2},{2,0},{4,6},{6,4},{8,10},{10,8},{12,14},{14,12},{1,3},{3,1},... | collective-permute-start | bytes 294920 | tf_op jit(solution)/shard_map/ppermute | solution.py:749
  29.5 8.7 %collective-permute-start.6 = (bf16[64,768]{1,0:T(8,128)(2,1)S(1)}, bf16[64,768]{1,0:T(8,128)(2,1)S(1)}, u32[]{:S(2)}, u32[]{:S(2)}) collective-permute-start(bf16[64,768]{1,0:T(8,128)(2,1)S(1)} %shard_map.135), channel_id=1, source_target_pairs={{0,10},{2,8},{4,14},{6,12},{8,2},{10,0},{12,6},{14,4},{1,11},{3,9}... | collective-permute-start | bytes 294920 | tf_op jit(solution)/shard_map/ppermute | solution.py:749
  31.8 7.4 %collective-permute-start.9 = (bf16[64,768]{1,0:T(8,128)(2,1)S(1)}, bf16[64,768]{1,0:T(8,128)(2,1)S(1)}, u32[]{:S(2)}, u32[]{:S(2)}) collective-permute-start(bf16[64,768]{1,0:T(8,128)(2,1)S(1)} %shard_map.135), channel_id=1, source_target_pairs={{0,14},{2,12},{4,10},{6,8},{8,6},{10,4},{12,2},{14,0},{1,15},{3,13... | collective-permute-start | bytes 294920 | tf_op jit(solution)/shard_map/ppermute | solution.py:749
  38.2 14.4 %copy-start.4 = (bf16[3072,64]{0,1:T(8,128)(2,1)S(1)}, bf16[3072,64]{0,1:T(8,128)(2,1)}, u32[]{:S(2)}) copy-start(bf16[3072,64]{0,1:T(8,128)(2,1)} %param.19) | copy-start | bytes 1179652
  39.0 18.6 %copy-start.5 = (bf16[27,16,128]{2,1,0:T(8,128)(2,1)S(1)}, bf16[27,16,128]{2,1,0:T(8,128)(2,1)}, u32[]{:S(2)}) copy-start(bf16[27,16,128]{2,1,0:T(8,128)(2,1)} %conv_ref) | copy-start | bytes 331780
  39.0 18.6 %copy-start.8 = (s32[4]{0:T(128)S(1)}, s32[4]{0:T(128)}, u32[]{:S(2)}) copy-start(s32[4]{0:T(128)} %slab_ref) | copy-start | bytes 52
  41.9 4.7 %collective-permute-start.10 = (bf16[16,3072]{1,0:T(8,128)(2,1)S(1)}, bf16[16,3072]{1,0:T(8,128)(2,1)S(1)}, u32[]{:S(2)}, u32[]{:S(2)}) collective-permute-start(bf16[16,3072]{1,0:T(8,128)(2,1)S(1)} %get-tuple-element.51), channel_id=1, source_target_pairs={{0,4},{4,0},{8,12},{12,8},{1,5},{5,1},{9,13},{13,9},{2,6},{6,2},{1... | collective-permute-start | bytes 294920 | tf_op jit(solution)/shard_map/ppermute | solution.py:721
  43.6 9.0 %collective-permute-start.11 = (bf16[16,3072]{1,0:T(8,128)(2,1)S(1)}, bf16[16,3072]{1,0:T(8,128)(2,1)S(1)}, u32[]{:S(2)}, u32[]{:S(2)}) collective-permute-start(bf16[16,3072]{1,0:T(8,128)(2,1)S(1)} %get-tuple-element.52), channel_id=1, source_target_pairs={{0,8},{4,12},{8,0},{12,4},{1,9},{5,13},{9,1},{13,5},{2,10},{6,14},... | collective-permute-start | bytes 294920 | tf_op jit(solution)/shard_map/ppermute | solution.py:721
  45.8 6.8 %collective-permute-start.12 = (bf16[16,3072]{1,0:T(8,128)(2,1)S(1)}, bf16[16,3072]{1,0:T(8,128)(2,1)S(1)}, u32[]{:S(2)}, u32[]{:S(2)}) collective-permute-start(bf16[16,3072]{1,0:T(8,128)(2,1)S(1)} %get-tuple-element.53), channel_id=1, source_target_pairs={{0,12},{4,8},{8,4},{12,0},{1,13},{5,9},{9,5},{13,1},{2,14},{6,10},... | collective-permute-start | bytes 294920 | tf_op jit(solution)/shard_map/ppermute | solution.py:721
  53.5 10.9 %all-to-all-start = ((f32[16,8,128]{2,1,0:T(8,128)}), f32[16,8,128]{2,1,0:T(8,128)S(1)}, u32[]{:S(2)}, u32[]{:S(2)}) async-start(f32[16,8,128]{2,1,0:T(8,128)} %shard_map.139), calls=%async_computation | async-start | bytes 131072 | tf_op jit(solution)/shard_map/all_to_all | solution.py:779

commit v9 on v8

--- a/solution.py
+++ b/solution.py
@@ -328,7 +328,7 @@
 
 
 def first_layer_kernel(
-    count, order_ref, embed_ref, heads_ref, stale_ref, out_ref, *refs
+    count, order_ref, embed_ref, heads_ref, stale_ref, out_ref, near_ref, *refs
 ):
     latent_refs, refs = refs[:count], refs[count:]
     block_refs, (own_ref, latents, attended, keys, values) = refs[:count], refs[count:]
@@ -369,7 +369,7 @@
     block = jax.ShapeDtypeStruct((rows, depth // count), jnp.bfloat16)
     return pl.pallas_call(
         functools.partial(first_layer_kernel, count),
-        in_specs=[whole(pltpu.SMEM)] + [whole()] * (4 + count),
+        in_specs=[whole(pltpu.SMEM)] + [whole()] * (5 + count),
         out_specs=[whole()] * (count + 1),
         out_shape=[block] * (count + 1),
         scratch_shapes=[
@@ -377,7 +377,7 @@
             *attention_scratch(rows, stale.shape[1], lanes),
         ],
         compiler_params=kernel_params(),
-    )(patch_order, w_embed, heads, stale, out, *latents)
+    )(patch_order, w_embed, heads, stale, out, met(latents[1:2]), *latents)
 
 
 def turn_kernel(after_ref, qkv_ref, heads_ref, turned_ref, term_ref):
@@ -403,6 +403,20 @@
         cost_estimate=pl.CostEstimate(flops=5 * 10**9, bytes_accessed=0, transcendentals=0),
         compiler_params=kernel_params(),
     )(after, qkv, heads)
+
+
+def meet_kernel(*refs):
+    refs[-1][...] = jnp.zeros_like(refs[-1])
+
+
+def met(values):
+    return pl.pallas_call(
+        meet_kernel,
+        in_specs=[whole(pl.ANY)] * len(values),
+        out_specs=whole(),
+        out_shape=jax.ShapeDtypeStruct((8, 128), jnp.float32),
+        compiler_params=kernel_params(),
+    )(*values)
 
 
 def block_sum_kernel(rows_ref, own_ref, term_ref, *refs):
@@ -525,7 +539,7 @@
     )(patch_order, mod_rows, qkv, out, term, stale, sums, squares, *pieces)
 
 
-def term_kernel(rows_ref, own_ref, final_ref, *refs):
+def term_kernel(rows_ref, own_ref, final_ref, far_ref, *refs):
     part_refs, term_ref = refs[:-1], refs[-1]
     mixed = part_refs[0][...].astype(jnp.float32)
     for part_ref in part_refs[1:]:
@@ -547,11 +561,11 @@
     shape = (peers, TOK_DEV, MICRO * final.shape[0])
     return pl.pallas_call(
         term_kernel,
-        in_specs=[whole()] * (3 + len(parts)),
+        in_specs=[whole()] * (4 + len(parts)),
         out_specs=whole(),
         out_shape=jax.ShapeDtypeStruct(shape, jnp.float32),
         compiler_params=kernel_params(),
-    )(mod_rows, own, final, *parts)
+    )(mod_rows, own, final, met(parts[2:]), *parts)
 
 
 TAPS = 27

time: 66 us -> 64.9 us (0.983)
  starting transfers between devices: 25.5 us -> 24.4 us
  transfers between devices with their start and end apart: 14 -> 14, of which waited for: 7 -> 8; matrix products, arithmetic and copies ran while one was open for 0% -> 0% of each run, Pallas kernels for 18% -> 19%
where the time goes in v9:
time: 64.9 us; the launch traced here: 64.6 us
  starting transfers between devices  24.4 us (38%)
  Pallas kernels  20.3 us (31%)
  waiting for transfers between devices  18.3 us (28%)
  between operations  1.52 us (2%)
    ppermute x9, starting transfers between devices, returned(): lax.ppermute(values[k], 'seq', within(k))  14.1 us
    ppermute x9, waiting for transfers between devices, returned(): lax.ppermute(values[k], 'seq', within(k))  9.59 us
    ppermute x4, starting transfers between devices, shards(): pieces.insert(0, lax.ppermute(block, ('seq', 'segment'), pairs))  6.81 us
    all_to_all x1, waiting for transfers between devices, shards(): lax.all_to_all(terms, peers, split_axis=0, concat_axis=0, tiled=True)  4.75 us
    pallas_call x1, Pallas kernels, prepared(): pl.pallas_call(prepare_kernel, in_specs=[whole(pltpu.SMEM)] + [whole()] *...  4.05 us
    ppermute x4, waiting for transfers between devices, shards(): pieces.insert(0, lax.ppermute(block, ('seq', 'segment'), pairs))  3.96 us
    pallas_call x1, Pallas kernels, turned(): pl.pallas_call(turn_kernel, in_specs=[whole(pl.ANY)] + [whole()] * 2, out...  3.84 us
    all_to_all x1, starting transfers between devices, shards(): lax.all_to_all(terms, peers, split_axis=0, concat_axis=0, tiled=True)  3.5 us
  transfers between devices with their start and end apart: 14, of which 8 were waited for; matrix products, arithmetic and copies ran while one was open for 0% of the time, Pallas kernels for 19%

profile of v9, /device:TPU:0, one launch (start us, length us, event | category | flops | bytes accessed | tf_op | source)
XLA Modules:
  0.0 64.6 jit_solution(12437262657102011680)
XLA Ops:
  0.7 0.9 %shard_map.132.refs_0_ = f32[2,8,64]{2,1,0:T(8,128)S(1)} custom-call(f32[2,8,64]{2,1,0:T(8,128)} %latent_hbm.1), custom_call_target="tpu_custom_call" | custom-call | flops 10000000000 | tf_op jit(solution)/shard_map/pallas_call | solution.py:214
  1.6 3.1 %collective-permute-start = (f32[2,8,64]{2,1,0:T(8,128)S(1)}, f32[2,8,64]{2,1,0:T(8,128)S(1)}, u32[]{:S(2)}, u32[]{:S(2)}) collective-permute-start(f32[2,8,64]{2,1,0:T(8,128)S(1)} %shard_map.132.refs_0_), channel_id=1, source_target_pairs={{0,4},{4,0},{8,12},{12,8},{1,5},{5,1},{9,13},{13,9},{2,6},{6,2},{1... | collective-permute-start | bytes 12296 | tf_op jit(solution)/shard_map/ppermute | solution.py:735
  4.6 2.5 %collective-permute-start.2 = (f32[2,8,64]{2,1,0:T(8,128)S(1)}, f32[2,8,64]{2,1,0:T(8,128)S(1)}, u32[]{:S(2)}, u32[]{:S(2)}) collective-permute-start(f32[2,8,64]{2,1,0:T(8,128)S(1)} %shard_map.132.refs_0_), channel_id=1, source_target_pairs={{0,12},{4,8},{8,4},{12,0},{1,13},{5,9},{9,5},{13,1},{2,14},{6,10},... | collective-permute-start | bytes 12296 | tf_op jit(solution)/shard_map/ppermute | solution.py:735
  7.9 4.1 %shard_map.131 = (f32[3,3072]{1,0:T(4,128)S(1)}, bf16[2304,128]{1,0:T(8,128)(2,1)S(1)}, bf16[768,3072]{1,0:T(8,128)(2,1)S(1)}) custom-call(s32[1]{0:T(128)S(6)} %copy.14.timestep_ref, bf16[3,50,3072]{2,1,0:T(8,128)(2,1)S(1)} %bitcast.9, f32[3,1,3072]{2,1,0:T(1,128)S(1)} %bitcast.13, bf16[64,3072]{1,0:T(8,128)(2,1)S(1)} %copy-done.1, ...), custom_call_target="tpu_custom_call" | custom-call | tf_op jit(solution)/shard_map/pallas_call | solution.py:254
  12.1 2.5 %shard_map.134 = (bf16[64,768]{1,0:T(8,128)(2,1)S(1)}, bf16[64,768]{1,0:T(8,128)(2,1)S(1)}, bf16[64,768]{1,0:T(8,128)(2,1)S(1)}, bf16[64,768]{1,0:T(8,128)(2,1)S(1)}, bf16[64,768]{1,0:T(8,128)(2,1)S(1)}) custom-call(s32[2]{0:T(128)S(1)} %copy-done.7, bf16[64,3072]{1,0:T(8,128)(2,1)S(1)} %copy-done.1, bf16[2304,128]{1,0:T(8,128)(2,1)S(1)} %get-tuple-element.32.heads_ref, ...), custom_call_target="tpu_custom_call" | custom-call | tf_op jit(solution)/shard_map/pallas_call | solution.py:370
  14.6 1.9 %collective-permute-start.3 = (bf16[64,768]{1,0:T(8,128)(2,1)S(1)}, bf16[64,768]{1,0:T(8,128)(2,1)S(1)}, u32[]{:S(2)}, u32[]{:S(2)}) collective-permute-start(bf16[64,768]{1,0:T(8,128)(2,1)S(1)} %get-tuple-element.38), channel_id=1, source_target_pairs={{0,4},{4,0},{8,12},{12,8},{1,5},{5,1},{9,13},{13,9},{2,6},{6,2},{1... | collective-permute-start | bytes 294920 | tf_op jit(solution)/shard_map/ppermute | solution.py:735
  16.4 2.0 %collective-permute-start.4 = (bf16[64,768]{1,0:T(8,128)(2,1)S(1)}, bf16[64,768]{1,0:T(8,128)(2,1)S(1)}, u32[]{:S(2)}, u32[]{:S(2)}) collective-permute-start(bf16[64,768]{1,0:T(8,128)(2,1)S(1)} %get-tuple-element.39), channel_id=1, source_target_pairs={{0,8},{4,12},{8,0},{12,4},{1,9},{5,13},{9,1},{13,5},{2,10},{6,14},... | collective-permute-start | bytes 294920 | tf_op jit(solution)/shard_map/ppermute | solution.py:735
  19.0 3.8 %shard_map.135 = (bf16[3072,2304]{1,0:T(8,128)(2,1)S(1)}, f32[1,2304]{1,0:T(1,128)S(1)}) custom-call(bf16[64,768]{1,0:T(8,128)(2,1)S(1)} %get-tuple-element.34.after_ref.own_ref, bf16[2304,3072]{1,0:T(8,128)(2,1)S(1)} %bitcast.8, bf16[2304,128]{1,0:T(8,128)(2,1)S(1)} %get-tuple-element.32.heads_ref), custom_call_target="tpu_custom_call" | custom-call | flops 5000000000 | tf_op jit(solution)/shard_map/pallas_call | solution.py:395
  22.9 3.4 %collective-permute-done.4.refs_2_ = bf16[64,768]{1,0:T(8,128)(2,1)S(1)} collective-permute-done((bf16[64,768]{1,0:T(8,128)(2,1)S(1)}, bf16[64,768]{1,0:T(8,128)(2,1)S(1)}, u32[]{:S(2)}, u32[]{:S(2)}) %collective-permute-start.4) | collective-permute-done | bytes 98336 | tf_op jit(solution)/shard_map/ppermute | solution.py:735
  26.4 2.6 %collective-permute-start.8 = (bf16[64,768]{1,0:T(8,128)(2,1)S(1)}, bf16[64,768]{1,0:T(8,128)(2,1)S(1)}, u32[]{:S(2)}, u32[]{:S(2)}) collective-permute-start(bf16[64,768]{1,0:T(8,128)(2,1)S(1)} %shard_map.136), channel_id=1, source_target_pairs={{0,6},{2,4},{4,2},{6,0},{8,14},{10,12},{12,10},{14,8},{1,7},{3,5},... | collective-permute-start | bytes 294920 | tf_op jit(solution)/shard_map/ppermute | solution.py:763
  29.5 2.4 %collective-permute-start.6 = (bf16[64,768]{1,0:T(8,128)(2,1)S(1)}, bf16[64,768]{1,0:T(8,128)(2,1)S(1)}, u32[]{:S(2)}, u32[]{:S(2)}) collective-permute-start(bf16[64,768]{1,0:T(8,128)(2,1)S(1)} %shard_map.136), channel_id=1, source_target_pairs={{0,10},{2,8},{4,14},{6,12},{8,2},{10,0},{12,6},{14,4},{1,11},{3,9}... | collective-permute-start | bytes 294920 | tf_op jit(solution)/shard_map/ppermute | solution.py:763
  31.8 1.3 %collective-permute-start.9 = (bf16[64,768]{1,0:T(8,128)(2,1)S(1)}, bf16[64,768]{1,0:T(8,128)(2,1)S(1)}, u32[]{:S(2)}, u32[]{:S(2)}) collective-permute-start(bf16[64,768]{1,0:T(8,128)(2,1)S(1)} %shard_map.136), channel_id=1, source_target_pairs={{0,14},{2,12},{4,10},{6,8},{8,6},{10,4},{12,2},{14,0},{1,15},{3,13... | collective-permute-start | bytes 294920 | tf_op jit(solution)/shard_map/ppermute | solution.py:763
  33.2 2.5 %collective-permute-done.7.refs_0_ = bf16[64,768]{1,0:T(8,128)(2,1)S(1)} collective-permute-done((bf16[64,768]{1,0:T(8,128)(2,1)S(1)}, bf16[64,768]{1,0:T(8,128)(2,1)S(1)}, u32[]{:S(2)}, u32[]{:S(2)}) %collective-permute-start.7) | collective-permute-done | bytes 98336 | tf_op jit(solution)/shard_map/ppermute | solution.py:763
  35.6 1.3 %shard_map.137 = (f32[64,2304]{1,0:T(8,128)S(1)}, f32[64,1]{1,0:T(8,128)S(1)}) custom-call(f32[3,3072]{1,0:T(4,128)S(1)} %get-tuple-element.31.rows_ref, bf16[3072,2304]{1,0:T(8,128)(2,1)S(1)} %get-tuple-element.35.turned_ref.qkv_ref, bf16[64,768]{1,0:T(8,128)(2,1)S(1)} %collective-permute-done.7.refs_0_, bf16[64,768]{1,0:T(8,128)(2,1)S(1)} %collective-permute-done.8.refs_1_), custom_call_target="tpu_custom_call" | custom-call | tf_op jit(solution)/shard_map/pallas_call | solution.py:476
  37.0 1.2 %collective-permute-done.6.refs_0_.refs_2_ = bf16[64,768]{1,0:T(8,128)(2,1)S(1)} collective-permute-done((bf16[64,768]{1,0:T(8,128)(2,1)S(1)}, bf16[64,768]{1,0:T(8,128)(2,1)S(1)}, u32[]{:S(2)}, u32[]{:S(2)}) %collective-permute-start.6) | collective-permute-done | bytes 98336 | tf_op jit(solution)/shard_map/ppermute | solution.py:763
  39.3 2.7 %shard_map.139 = (bf16[16,3072]{1,0:T(8,128)(2,1)S(1)}, bf16[16,3072]{1,0:T(8,128)(2,1)S(1)}, bf16[16,3072]{1,0:T(8,128)(2,1)S(1)}, bf16[16,3072]{1,0:T(8,128)(2,1)S(1)}, bf16[16,3072]{1,0:T(8,128)(2,1)S(1)}) custom-call(s32[2]{0:T(128)S(1)} %copy-done.7, f32[3,3072]{1,0:T(4,128)S(1)} %get-tuple-element.31.rows_ref, ...), custom_call_target="tpu_custom_call" | custom-call | tf_op jit(solution)/shard_map/pallas_call | solution.py:528
  42.0 2.3 %collective-permute-start.10 = (bf16[16,3072]{1,0:T(8,128)(2,1)S(1)}, bf16[16,3072]{1,0:T(8,128)(2,1)S(1)}, u32[]{:S(2)}, u32[]{:S(2)}) collective-permute-start(bf16[16,3072]{1,0:T(8,128)(2,1)S(1)} %get-tuple-element.50), channel_id=1, source_target_pairs={{0,8},{4,12},{8,0},{12,4},{1,9},{5,13},{9,1},{13,5},{2,10},{6,14},... | collective-permute-start | bytes 294920 | tf_op jit(solution)/shard_map/ppermute | solution.py:735
  44.3 1.7 %collective-permute-start.11 = (bf16[16,3072]{1,0:T(8,128)(2,1)S(1)}, bf16[16,3072]{1,0:T(8,128)(2,1)S(1)}, u32[]{:S(2)}, u32[]{:S(2)}) collective-permute-start(bf16[16,3072]{1,0:T(8,128)(2,1)S(1)} %get-tuple-element.51), channel_id=1, source_target_pairs={{0,12},{4,8},{8,4},{12,0},{1,13},{5,9},{9,5},{13,1},{2,14},{6,10},... | collective-permute-start | bytes 294920 | tf_op jit(solution)/shard_map/ppermute | solution.py:735
  46.0 4.5 %collective-permute-done.10.refs_0_.refs_2_ = bf16[16,3072]{1,0:T(8,128)(2,1)S(1)} collective-permute-done((bf16[16,3072]{1,0:T(8,128)(2,1)S(1)}, bf16[16,3072]{1,0:T(8,128)(2,1)S(1)}, u32[]{:S(2)}, u32[]{:S(2)}) %collective-permute-start.10) | collective-permute-done | bytes 98336 | tf_op jit(solution)/shard_map/ppermute | solution.py:735
  52.1 0.9 %shard_map.141 = f32[16,8,128]{2,1,0:T(8,128)} custom-call(f32[3,3072]{1,0:T(4,128)S(1)} %get-tuple-element.31.rows_ref, bf16[16,3072]{1,0:T(8,128)(2,1)S(1)} %get-tuple-element.45.own_ref, bf16[64,3072]{1,0:T(8,128)(2,1)S(1)} %bitcast.12, f32[8,128]{1,0:T(8,128)S(1)} %shard_map.140.far_ref, bf16[16,3072]{1,0:T(8,128)(2,1)S(1)} %get-tuple-element.52.refs_0_, ...), custom_call_target="tpu_custom_call" | custom-call | tf_op jit(solution)/shard_map/pallas_call | solution.py:562
  53.0 3.5 %all-to-all-start = ((f32[16,8,128]{2,1,0:T(8,128)}), f32[16,8,128]{2,1,0:T(8,128)S(1)}, u32[]{:S(2)}, u32[]{:S(2)}) async-start(f32[16,8,128]{2,1,0:T(8,128)} %shard_map.141), calls=%async_computation | async-start | bytes 131072 | tf_op jit(solution)/shard_map/all_to_all | solution.py:793
  56.6 2.1 %shard_map.142 = (bf16[64,3584]{1,0:T(8,128)(2,1)S(1)}, bf16[896,256]{1,0:T(8,128)(2,1)S(1)}) custom-call(s32[4]{0:T(128)S(1)} %copy-done.8, bf16[27,16,128]{2,1,0:T(8,128)(2,1)S(1)} %copy-done.5), custom_call_target="tpu_custom_call" | custom-call | tf_op jit(solution)/shard_map/pallas_call | solution.py:624
  58.6 4.8 %all-to-all-done.terms_ref = f32[16,8,128]{2,1,0:T(8,128)S(1)} async-done(((f32[16,8,128]{2,1,0:T(8,128)}), f32[16,8,128]{2,1,0:T(8,128)S(1)}, u32[]{:S(2)}, u32[]{:S(2)}) %all-to-all-start) | async-done | bytes 65568 | tf_op jit(solution)/shard_map/all_to_all | solution.py:793
  63.4 1.2 %shard_map.143 = (f32[2,8,64]{2,1,0:T(8,128)}, bf16[128,128]{1,0:T(8,128)(2,1)}) custom-call(f32[16,8,128]{2,1,0:T(8,128)S(1)} %all-to-all-done.terms_ref, bf16[64,3584]{1,0:T(8,128)(2,1)S(1)} %get-tuple-element.56.chosen_ref, bf16[896,256]{1,0:T(8,128)(2,1)S(1)} %get-tuple-element.57.weights_ref, f32[2,8,64]{2,1,0:T(8,128)S(1)} %shard_map.132.refs_0_, ...), custom_call_target="tpu_custom_call" | custom-call | tf_op jit(solution)/shard_map/pallas_call | solution.py:695
  (35 shorter events, 4.1 us)
Async XLA Ops:
  0.6 7.3 %copy-start.1 = (bf16[64,3072]{1,0:T(8,128)(2,1)S(1)}, bf16[64,3072]{1,0:T(8,128)(2,1)}, u32[]{:S(2)}) copy-start(bf16[64,3072]{1,0:T(8,128)(2,1)} %embed_ref.3) | copy-start | bytes 1179652
  0.6 7.3 %copy-start.6 = (f32[1,1,3,3072]{3,1,2,0:T(1,128)S(1)}, f32[1,1,3,3072]{3,1,2,0:T(1,128)}, u32[]{:S(2)}) copy-start(f32[1,1,3,3072]{3,1,2,0:T(1,128)} %param.17) | copy-start | bytes 110596
  0.7 7.3 %copy-start.2 = (bf16[50,3,3072]{2,0,1:T(8,128)(2,1)S(1)}, bf16[50,3,3072]{2,0,1:T(8,128)(2,1)}, u32[]{:S(2)}) copy-start(bf16[50,3,3072]{2,0,1:T(8,128)(2,1)} %param.16) | copy-start | bytes 2764804
  0.7 7.3 %copy-start = (bf16[1,2304,3072]{2,1,0:T(8,128)(2,1)S(1)}, bf16[1,2304,3072]{2,1,0:T(8,128)(2,1)}, u32[]{:S(2)}) copy-start(bf16[1,2304,3072]{2,1,0:T(8,128)(2,1)} %param.14) | copy-start | bytes 42467332
  1.5 10.5 %copy-start.3 = (bf16[1,1,1,2,32,1536]{5,4,3,2,1,0:T(8,128)(2,1)S(1)}, bf16[1,1,1,2,32,1536]{5,4,3,2,1,0:T(8,128)(2,1)}, u32[]{:S(2)}) copy-start(bf16[1,1,1,2,32,1536]{5,4,3,2,1,0:T(8,128)(2,1)} %param.18) | copy-start | bytes 589828
  1.5 10.5 %copy-start.7 = (s32[2]{0:T(128)S(1)}, s32[2]{0:T(128)}, u32[]{:S(2)}) copy-start(s32[2]{0:T(128)} %order_ref.3) | copy-start | bytes 28
  1.6 10.4 %collective-permute-start = (f32[2,8,64]{2,1,0:T(8,128)S(1)}, f32[2,8,64]{2,1,0:T(8,128)S(1)}, u32[]{:S(2)}, u32[]{:S(2)}) collective-permute-start(f32[2,8,64]{2,1,0:T(8,128)S(1)} %shard_map.132.refs_0_), channel_id=1, source_target_pairs={{0,4},{4,0},{8,12},{12,8},{1,5},{5,1},{9,13},{13,9},{2,6},{6,2},{1... | collective-permute-start | bytes 12296 | tf_op jit(solution)/shard_map/ppermute | solution.py:735
  4.6 7.4 %collective-permute-start.2 = (f32[2,8,64]{2,1,0:T(8,128)S(1)}, f32[2,8,64]{2,1,0:T(8,128)S(1)}, u32[]{:S(2)}, u32[]{:S(2)}) collective-permute-start(f32[2,8,64]{2,1,0:T(8,128)S(1)} %shard_map.132.refs_0_), channel_id=1, source_target_pairs={{0,12},{4,8},{8,4},{12,0},{1,13},{5,9},{9,5},{13,1},{2,14},{6,10},... | collective-permute-start | bytes 12296 | tf_op jit(solution)/shard_map/ppermute | solution.py:735
  7.1 4.9 %collective-permute-start.1 = (f32[2,8,64]{2,1,0:T(8,128)S(1)}, f32[2,8,64]{2,1,0:T(8,128)S(1)}, u32[]{:S(2)}, u32[]{:S(2)}) collective-permute-start(f32[2,8,64]{2,1,0:T(8,128)S(1)} %shard_map.132.refs_0_), channel_id=1, source_target_pairs={{0,8},{4,12},{8,0},{12,4},{1,9},{5,13},{9,1},{13,5},{2,10},{6,14},... | collective-permute-start | bytes 12296 | tf_op jit(solution)/shard_map/ppermute | solution.py:735
  14.6 8.3 %collective-permute-start.3 = (bf16[64,768]{1,0:T(8,128)(2,1)S(1)}, bf16[64,768]{1,0:T(8,128)(2,1)S(1)}, u32[]{:S(2)}, u32[]{:S(2)}) collective-permute-start(bf16[64,768]{1,0:T(8,128)(2,1)S(1)} %get-tuple-element.38), channel_id=1, source_target_pairs={{0,4},{4,0},{8,12},{12,8},{1,5},{5,1},{9,13},{13,9},{2,6},{6,2},{1... | collective-permute-start | bytes 294920 | tf_op jit(solution)/shard_map/ppermute | solution.py:735
  16.4 9.9 %collective-permute-start.4 = (bf16[64,768]{1,0:T(8,128)(2,1)S(1)}, bf16[64,768]{1,0:T(8,128)(2,1)S(1)}, u32[]{:S(2)}, u32[]{:S(2)}) collective-permute-start(bf16[64,768]{1,0:T(8,128)(2,1)S(1)} %get-tuple-element.39), channel_id=1, source_target_pairs={{0,8},{4,12},{8,0},{12,4},{1,9},{5,13},{9,1},{13,5},{2,10},{6,14},... | collective-permute-start | bytes 294920 | tf_op jit(solution)/shard_map/ppermute | solution.py:735
  18.4 7.8 %collective-permute-start.5 = (bf16[64,768]{1,0:T(8,128)(2,1)S(1)}, bf16[64,768]{1,0:T(8,128)(2,1)S(1)}, u32[]{:S(2)}, u32[]{:S(2)}) collective-permute-start(bf16[64,768]{1,0:T(8,128)(2,1)S(1)} %get-tuple-element.40), channel_id=1, source_target_pairs={{0,12},{4,8},{8,4},{12,0},{1,13},{5,9},{9,5},{13,1},{2,14},{6,10},... | collective-permute-start | bytes 294920 | tf_op jit(solution)/shard_map/ppermute | solution.py:735
  26.4 6.8 %collective-permute-start.8 = (bf16[64,768]{1,0:T(8,128)(2,1)S(1)}, bf16[64,768]{1,0:T(8,128)(2,1)S(1)}, u32[]{:S(2)}, u32[]{:S(2)}) collective-permute-start(bf16[64,768]{1,0:T(8,128)(2,1)S(1)} %shard_map.136), channel_id=1, source_target_pairs={{0,6},{2,4},{4,2},{6,0},{8,14},{10,12},{12,10},{14,8},{1,7},{3,5},... | collective-permute-start | bytes 294920 | tf_op jit(solution)/shard_map/ppermute | solution.py:763
  29.0 6.7 %collective-permute-start.7 = (bf16[64,768]{1,0:T(8,128)(2,1)S(1)}, bf16[64,768]{1,0:T(8,128)(2,1)S(1)}, u32[]{:S(2)}, u32[]{:S(2)}) collective-permute-start(bf16[64,768]{1,0:T(8,128)(2,1)S(1)} %shard_map.136), channel_id=1, source_target_pairs={{0,2},{2,0},{4,6},{6,4},{8,10},{10,8},{12,14},{14,12},{1,3},{3,1},... | collective-permute-start | bytes 294920 | tf_op jit(solution)/shard_map/ppermute | solution.py:763
  29.5 8.7 %collective-permute-start.6 = (bf16[64,768]{1,0:T(8,128)(2,1)S(1)}, bf16[64,768]{1,0:T(8,128)(2,1)S(1)}, u32[]{:S(2)}, u32[]{:S(2)}) collective-permute-start(bf16[64,768]{1,0:T(8,128)(2,1)S(1)} %shard_map.136), channel_id=1, source_target_pairs={{0,10},{2,8},{4,14},{6,12},{8,2},{10,0},{12,6},{14,4},{1,11},{3,9}... | collective-permute-start | bytes 294920 | tf_op jit(solution)/shard_map/ppermute | solution.py:763
  31.8 7.4 %collective-permute-start.9 = (bf16[64,768]{1,0:T(8,128)(2,1)S(1)}, bf16[64,768]{1,0:T(8,128)(2,1)S(1)}, u32[]{:S(2)}, u32[]{:S(2)}) collective-permute-start(bf16[64,768]{1,0:T(8,128)(2,1)S(1)} %shard_map.136), channel_id=1, source_target_pairs={{0,14},{2,12},{4,10},{6,8},{8,6},{10,4},{12,2},{14,0},{1,15},{3,13... | collective-permute-start | bytes 294920 | tf_op jit(solution)/shard_map/ppermute | solution.py:763
  38.2 14.0 %copy-start.4 = (bf16[3072,64]{0,1:T(8,128)(2,1)S(1)}, bf16[3072,64]{0,1:T(8,128)(2,1)}, u32[]{:S(2)}) copy-start(bf16[3072,64]{0,1:T(8,128)(2,1)} %param.19) | copy-start | bytes 1179652
  38.9 17.6 %copy-start.5 = (bf16[27,16,128]{2,1,0:T(8,128)(2,1)S(1)}, bf16[27,16,128]{2,1,0:T(8,128)(2,1)}, u32[]{:S(2)}) copy-start(bf16[27,16,128]{2,1,0:T(8,128)(2,1)} %conv_ref) | copy-start | bytes 331780
  38.9 17.6 %copy-start.8 = (s32[4]{0:T(128)S(1)}, s32[4]{0:T(128)}, u32[]{:S(2)}) copy-start(s32[4]{0:T(128)} %slab_ref) | copy-start | bytes 52
  42.0 8.5 %collective-permute-start.10 = (bf16[16,3072]{1,0:T(8,128)(2,1)S(1)}, bf16[16,3072]{1,0:T(8,128)(2,1)S(1)}, u32[]{:S(2)}, u32[]{:S(2)}) collective-permute-start(bf16[16,3072]{1,0:T(8,128)(2,1)S(1)} %get-tuple-element.50), channel_id=1, source_target_pairs={{0,8},{4,12},{8,0},{12,4},{1,9},{5,13},{9,1},{13,5},{2,10},{6,14},... | collective-permute-start | bytes 294920 | tf_op jit(solution)/shard_map/ppermute | solution.py:735
  44.3 7.0 %collective-permute-start.11 = (bf16[16,3072]{1,0:T(8,128)(2,1)S(1)}, bf16[16,3072]{1,0:T(8,128)(2,1)S(1)}, u32[]{:S(2)}, u32[]{:S(2)}) collective-permute-start(bf16[16,3072]{1,0:T(8,128)(2,1)S(1)} %get-tuple-element.51), channel_id=1, source_target_pairs={{0,12},{4,8},{8,4},{12,0},{1,13},{5,9},{9,5},{13,1},{2,14},{6,10},... | collective-permute-start | bytes 294920 | tf_op jit(solution)/shard_map/ppermute | solution.py:735
  45.9 6.2 %collective-permute-start.12 = (bf16[16,3072]{1,0:T(8,128)(2,1)S(1)}, bf16[16,3072]{1,0:T(8,128)(2,1)S(1)}, u32[]{:S(2)}, u32[]{:S(2)}) collective-permute-start(bf16[16,3072]{1,0:T(8,128)(2,1)S(1)} %get-tuple-element.53), channel_id=1, source_target_pairs={{0,4},{4,0},{8,12},{12,8},{1,5},{5,1},{9,13},{13,9},{2,6},{6,2},{1... | collective-permute-start | bytes 294920 | tf_op jit(solution)/shard_map/ppermute | solution.py:735
  53.0 10.4 %all-to-all-start = ((f32[16,8,128]{2,1,0:T(8,128)}), f32[16,8,128]{2,1,0:T(8,128)S(1)}, u32[]{:S(2)}, u32[]{:S(2)}) async-start(f32[16,8,128]{2,1,0:T(8,128)} %shard_map.141), calls=%async_computation | async-start | bytes 131072 | tf_op jit(solution)/shard_map/all_to_all | solution.py:793

commit v10 on v9

--- a/solution.py
+++ b/solution.py
@@ -565,7 +565,7 @@
         out_specs=whole(),
         out_shape=jax.ShapeDtypeStruct(shape, jnp.float32),
         compiler_params=kernel_params(),
-    )(mod_rows, own, final, met(parts[2:]), *parts)
+    )(mod_rows, own, final, met(parts[3:]), *parts)
 
 
 TAPS = 27
@@ -762,7 +762,7 @@
             ]
             pieces.insert(0, lax.ppermute(block, ("seq", "segment"), pairs))
         sums = ()
-        for some in (numbers[:half], numbers[half:-1]):
+        for some in (numbers[:1], numbers[1:-1]):
             if some:
                 sums = product_sums(
                     some,

time: 64.9 us -> 64.1 us (0.988)
  waiting for transfers between devices: 18.3 us -> 17 us
    ppermute x9, waiting for transfers between devices: 9.59 us -> 8.32 us  [returned(): lax.ppermute(values[k], 'seq', within(k))]
  transfers between devices with their start and end apart: 14 -> 14, of which waited for: 8 -> 6; matrix products, arithmetic and copies ran while one was open for 0% -> 0% of each run, Pallas kernels for 19% -> 19%
where the time goes in v10:
time: 64.1 us; the launch traced here: 63.8 us
  starting transfers between devices  24.9 us (39%)
  Pallas kernels  20.4 us (32%)
  waiting for transfers between devices  17 us (27%)
  between operations  1.52 us (2%)
    ppermute x9, starting transfers between devices, returned(): lax.ppermute(values[k], 'seq', within(k))  14.6 us
    ppermute x9, waiting for transfers between devices, returned(): lax.ppermute(values[k], 'seq', within(k))  8.32 us
    ppermute x4, starting transfers between devices, shards(): pieces.insert(0, lax.ppermute(block, ('seq', 'segment'), pairs))  6.81 us
    all_to_all x1, waiting for transfers between devices, shards(): lax.all_to_all(terms, peers, split_axis=0, concat_axis=0, tiled=True)  4.75 us
    pallas_call x1, Pallas kernels, prepared(): pl.pallas_call(prepare_kernel, in_specs=[whole(pltpu.SMEM)] + [whole()] *...  4.05 us
    ppermute x4, waiting for transfers between devices, shards(): pieces.insert(0, lax.ppermute(block, ('seq', 'segment'), pairs))  3.94 us
    pallas_call x1, Pallas kernels, turned(): pl.pallas_call(turn_kernel, in_specs=[whole(pl.ANY)] + [whole()] * 2, out...  3.84 us
    all_to_all x1, starting transfers between devices, shards(): lax.all_to_all(terms, peers, split_axis=0, concat_axis=0, tiled=True)  3.5 us
  transfers between devices with their start and end apart: 14, of which 6 were waited for; matrix products, arithmetic and copies ran while one was open for 0% of the time, Pallas kernels for 19%

profile of v10, /device:TPU:0, one launch (start us, length us, event | category | flops | bytes accessed | tf_op | source)
XLA Modules:
  0.0 63.8 jit_solution(7493446078129857322)
XLA Ops:
  1.6 3.1 %collective-permute-start = (f32[2,8,64]{2,1,0:T(8,128)S(1)}, f32[2,8,64]{2,1,0:T(8,128)S(1)}, u32[]{:S(2)}, u32[]{:S(2)}) collective-permute-start(f32[2,8,64]{2,1,0:T(8,128)S(1)} %shard_map.132.refs_0_), channel_id=1, source_target_pairs={{0,4},{4,0},{8,12},{12,8},{1,5},{5,1},{9,13},{13,9},{2,6},{6,2},{1... | collective-permute-start | bytes 12296 | tf_op jit(solution)/shard_map/ppermute | solution.py:735
  4.6 2.5 %collective-permute-start.2 = (f32[2,8,64]{2,1,0:T(8,128)S(1)}, f32[2,8,64]{2,1,0:T(8,128)S(1)}, u32[]{:S(2)}, u32[]{:S(2)}) collective-permute-start(f32[2,8,64]{2,1,0:T(8,128)S(1)} %shard_map.132.refs_0_), channel_id=1, source_target_pairs={{0,12},{4,8},{8,4},{12,0},{1,13},{5,9},{9,5},{13,1},{2,14},{6,10},... | collective-permute-start | bytes 12296 | tf_op jit(solution)/shard_map/ppermute | solution.py:735
  7.9 4.1 %shard_map.131 = (f32[3,3072]{1,0:T(4,128)S(1)}, bf16[2304,128]{1,0:T(8,128)(2,1)S(1)}, bf16[768,3072]{1,0:T(8,128)(2,1)S(1)}) custom-call(s32[1]{0:T(128)S(6)} %copy.14.timestep_ref, bf16[3,50,3072]{2,1,0:T(8,128)(2,1)S(1)} %bitcast.9, f32[3,1,3072]{2,1,0:T(1,128)S(1)} %bitcast.13, bf16[64,3072]{1,0:T(8,128)(2,1)S(1)} %copy-done.1, ...), custom_call_target="tpu_custom_call" | custom-call | tf_op jit(solution)/shard_map/pallas_call | solution.py:254
  12.1 2.5 %shard_map.134 = (bf16[64,768]{1,0:T(8,128)(2,1)S(1)}, bf16[64,768]{1,0:T(8,128)(2,1)S(1)}, bf16[64,768]{1,0:T(8,128)(2,1)S(1)}, bf16[64,768]{1,0:T(8,128)(2,1)S(1)}, bf16[64,768]{1,0:T(8,128)(2,1)S(1)}) custom-call(s32[2]{0:T(128)S(1)} %copy-done.7, bf16[64,3072]{1,0:T(8,128)(2,1)S(1)} %copy-done.1, bf16[2304,128]{1,0:T(8,128)(2,1)S(1)} %get-tuple-element.32.heads_ref, ...), custom_call_target="tpu_custom_call" | custom-call | tf_op jit(solution)/shard_map/pallas_call | solution.py:370
  14.5 1.9 %collective-permute-start.3 = (bf16[64,768]{1,0:T(8,128)(2,1)S(1)}, bf16[64,768]{1,0:T(8,128)(2,1)S(1)}, u32[]{:S(2)}, u32[]{:S(2)}) collective-permute-start(bf16[64,768]{1,0:T(8,128)(2,1)S(1)} %get-tuple-element.38), channel_id=1, source_target_pairs={{0,4},{4,0},{8,12},{12,8},{1,5},{5,1},{9,13},{13,9},{2,6},{6,2},{1... | collective-permute-start | bytes 294920 | tf_op jit(solution)/shard_map/ppermute | solution.py:735
  16.4 2.0 %collective-permute-start.4 = (bf16[64,768]{1,0:T(8,128)(2,1)S(1)}, bf16[64,768]{1,0:T(8,128)(2,1)S(1)}, u32[]{:S(2)}, u32[]{:S(2)}) collective-permute-start(bf16[64,768]{1,0:T(8,128)(2,1)S(1)} %get-tuple-element.39), channel_id=1, source_target_pairs={{0,8},{4,12},{8,0},{12,4},{1,9},{5,13},{9,1},{13,5},{2,10},{6,14},... | collective-permute-start | bytes 294920 | tf_op jit(solution)/shard_map/ppermute | solution.py:735
  19.0 3.8 %shard_map.135 = (bf16[3072,2304]{1,0:T(8,128)(2,1)S(1)}, f32[1,2304]{1,0:T(1,128)S(1)}) custom-call(bf16[64,768]{1,0:T(8,128)(2,1)S(1)} %get-tuple-element.34.after_ref.own_ref, bf16[2304,3072]{1,0:T(8,128)(2,1)S(1)} %bitcast.8, bf16[2304,128]{1,0:T(8,128)(2,1)S(1)} %get-tuple-element.32.heads_ref), custom_call_target="tpu_custom_call" | custom-call | flops 5000000000 | tf_op jit(solution)/shard_map/pallas_call | solution.py:395
  22.9 3.4 %collective-permute-done.4.refs_2_ = bf16[64,768]{1,0:T(8,128)(2,1)S(1)} collective-permute-done((bf16[64,768]{1,0:T(8,128)(2,1)S(1)}, bf16[64,768]{1,0:T(8,128)(2,1)S(1)}, u32[]{:S(2)}, u32[]{:S(2)}) %collective-permute-start.4) | collective-permute-done | bytes 98336 | tf_op jit(solution)/shard_map/ppermute | solution.py:735
  26.4 1.6 %collective-permute-start.8 = (bf16[64,768]{1,0:T(8,128)(2,1)S(1)}, bf16[64,768]{1,0:T(8,128)(2,1)S(1)}, u32[]{:S(2)}, u32[]{:S(2)}) collective-permute-start(bf16[64,768]{1,0:T(8,128)(2,1)S(1)} %shard_map.136), channel_id=1, source_target_pairs={{0,2},{2,0},{4,6},{6,4},{8,10},{10,8},{12,14},{14,12},{1,3},{3,1},... | collective-permute-start | bytes 294920 | tf_op jit(solution)/shard_map/ppermute | solution.py:763
  27.9 2.6 %collective-permute-start.7 = (bf16[64,768]{1,0:T(8,128)(2,1)S(1)}, bf16[64,768]{1,0:T(8,128)(2,1)S(1)}, u32[]{:S(2)}, u32[]{:S(2)}) collective-permute-start(bf16[64,768]{1,0:T(8,128)(2,1)S(1)} %shard_map.136), channel_id=1, source_target_pairs={{0,10},{2,8},{4,14},{6,12},{8,2},{10,0},{12,6},{14,4},{1,11},{3,9}... | collective-permute-start | bytes 294920 | tf_op jit(solution)/shard_map/ppermute | solution.py:763
  30.5 1.3 %collective-permute-start.6 = (bf16[64,768]{1,0:T(8,128)(2,1)S(1)}, bf16[64,768]{1,0:T(8,128)(2,1)S(1)}, u32[]{:S(2)}, u32[]{:S(2)}) collective-permute-start(bf16[64,768]{1,0:T(8,128)(2,1)S(1)} %shard_map.136), channel_id=1, source_target_pairs={{0,6},{2,4},{4,2},{6,0},{8,14},{10,12},{12,10},{14,8},{1,7},{3,5},... | collective-permute-start | bytes 294920 | tf_op jit(solution)/shard_map/ppermute | solution.py:763
  31.8 1.3 %collective-permute-start.9 = (bf16[64,768]{1,0:T(8,128)(2,1)S(1)}, bf16[64,768]{1,0:T(8,128)(2,1)S(1)}, u32[]{:S(2)}, u32[]{:S(2)}) collective-permute-start(bf16[64,768]{1,0:T(8,128)(2,1)S(1)} %shard_map.136), channel_id=1, source_target_pairs={{0,14},{2,12},{4,10},{6,8},{8,6},{10,4},{12,2},{14,0},{1,15},{3,13... | collective-permute-start | bytes 294920 | tf_op jit(solution)/shard_map/ppermute | solution.py:763
  33.9 3.1 %collective-permute-done.7.refs_1_.refs_2_ = bf16[64,768]{1,0:T(8,128)(2,1)S(1)} collective-permute-done((bf16[64,768]{1,0:T(8,128)(2,1)S(1)}, bf16[64,768]{1,0:T(8,128)(2,1)S(1)}, u32[]{:S(2)}, u32[]{:S(2)}) %collective-permute-start.7) | collective-permute-done | bytes 98336 | tf_op jit(solution)/shard_map/ppermute | solution.py:763
  37.0 1.4 %shard_map.138 = (f32[64,2304]{1,0:T(8,128)S(1)}, f32[64,1]{1,0:T(8,128)S(1)}) custom-call(f32[3,3072]{1,0:T(4,128)S(1)} %get-tuple-element.31.rows_ref, bf16[3072,2304]{1,0:T(8,128)(2,1)S(1)} %get-tuple-element.35.turned_ref.qkv_ref, bf16[64,768]{1,0:T(8,128)(2,1)S(1)} %collective-permute-done.6.refs_0_.refs_1_, ...), custom_call_target="tpu_custom_call" | custom-call | tf_op jit(solution)/shard_map/pallas_call | solution.py:476
  39.3 2.7 %shard_map.139 = (bf16[16,3072]{1,0:T(8,128)(2,1)S(1)}, bf16[16,3072]{1,0:T(8,128)(2,1)S(1)}, bf16[16,3072]{1,0:T(8,128)(2,1)S(1)}, bf16[16,3072]{1,0:T(8,128)(2,1)S(1)}, bf16[16,3072]{1,0:T(8,128)(2,1)S(1)}) custom-call(s32[2]{0:T(128)S(1)} %copy-done.7, f32[3,3072]{1,0:T(4,128)S(1)} %get-tuple-element.31.rows_ref, ...), custom_call_target="tpu_custom_call" | custom-call | tf_op jit(solution)/shard_map/pallas_call | solution.py:528
  42.0 3.1 %collective-permute-start.10 = (bf16[16,3072]{1,0:T(8,128)(2,1)S(1)}, bf16[16,3072]{1,0:T(8,128)(2,1)S(1)}, u32[]{:S(2)}, u32[]{:S(2)}) collective-permute-start(bf16[16,3072]{1,0:T(8,128)(2,1)S(1)} %get-tuple-element.50), channel_id=1, source_target_pairs={{0,12},{4,8},{8,4},{12,0},{1,13},{5,9},{9,5},{13,1},{2,14},{6,10},... | collective-permute-start | bytes 294920 | tf_op jit(solution)/shard_map/ppermute | solution.py:735
  45.0 1.4 %collective-permute-start.12 = (bf16[16,3072]{1,0:T(8,128)(2,1)S(1)}, bf16[16,3072]{1,0:T(8,128)(2,1)S(1)}, u32[]{:S(2)}, u32[]{:S(2)}) collective-permute-start(bf16[16,3072]{1,0:T(8,128)(2,1)S(1)} %get-tuple-element.53), channel_id=1, source_target_pairs={{0,8},{4,12},{8,0},{12,4},{1,9},{5,13},{9,1},{13,5},{2,10},{6,14},... | collective-permute-start | bytes 294920 | tf_op jit(solution)/shard_map/ppermute | solution.py:735
  46.4 2.1 %collective-permute-done.10.refs_0_.refs_3_ = bf16[16,3072]{1,0:T(8,128)(2,1)S(1)} collective-permute-done((bf16[16,3072]{1,0:T(8,128)(2,1)S(1)}, bf16[16,3072]{1,0:T(8,128)(2,1)S(1)}, u32[]{:S(2)}, u32[]{:S(2)}) %collective-permute-start.10) | collective-permute-done | bytes 98336 | tf_op jit(solution)/shard_map/ppermute | solution.py:735
  48.5 2.8 %collective-permute-done.11.refs_1_ = bf16[16,3072]{1,0:T(8,128)(2,1)S(1)} collective-permute-done((bf16[16,3072]{1,0:T(8,128)(2,1)S(1)}, bf16[16,3072]{1,0:T(8,128)(2,1)S(1)}, u32[]{:S(2)}, u32[]{:S(2)}) %collective-permute-start.11) | collective-permute-done | bytes 98336 | tf_op jit(solution)/shard_map/ppermute | solution.py:735
  51.3 0.9 %shard_map.141 = f32[16,8,128]{2,1,0:T(8,128)} custom-call(f32[3,3072]{1,0:T(4,128)S(1)} %get-tuple-element.31.rows_ref, bf16[16,3072]{1,0:T(8,128)(2,1)S(1)} %get-tuple-element.45.own_ref, bf16[64,3072]{1,0:T(8,128)(2,1)S(1)} %bitcast.12, f32[8,128]{1,0:T(8,128)S(1)} %shard_map.140.far_ref, bf16[16,3072]{1,0:T(8,128)(2,1)S(1)} %get-tuple-element.51.refs_0_, ...), custom_call_target="tpu_custom_call" | custom-call | tf_op jit(solution)/shard_map/pallas_call | solution.py:562
  52.2 3.5 %all-to-all-start = ((f32[16,8,128]{2,1,0:T(8,128)}), f32[16,8,128]{2,1,0:T(8,128)S(1)}, u32[]{:S(2)}, u32[]{:S(2)}) async-start(f32[16,8,128]{2,1,0:T(8,128)} %shard_map.141), calls=%async_computation | async-start | bytes 131072 | tf_op jit(solution)/shard_map/all_to_all | solution.py:793
  55.8 2.1 %shard_map.142 = (bf16[64,3584]{1,0:T(8,128)(2,1)S(1)}, bf16[896,256]{1,0:T(8,128)(2,1)S(1)}) custom-call(s32[4]{0:T(128)S(1)} %copy-done.8, bf16[27,16,128]{2,1,0:T(8,128)(2,1)S(1)} %copy-done.5), custom_call_target="tpu_custom_call" | custom-call | tf_op jit(solution)/shard_map/pallas_call | solution.py:624
  57.8 4.8 %all-to-all-done.terms_ref = f32[16,8,128]{2,1,0:T(8,128)S(1)} async-done(((f32[16,8,128]{2,1,0:T(8,128)}), f32[16,8,128]{2,1,0:T(8,128)S(1)}, u32[]{:S(2)}, u32[]{:S(2)}) %all-to-all-start) | async-done | bytes 65568 | tf_op jit(solution)/shard_map/all_to_all | solution.py:793
  62.6 1.2 %shard_map.143 = (f32[2,8,64]{2,1,0:T(8,128)}, bf16[128,128]{1,0:T(8,128)(2,1)}) custom-call(f32[16,8,128]{2,1,0:T(8,128)S(1)} %all-to-all-done.terms_ref, bf16[64,3584]{1,0:T(8,128)(2,1)S(1)} %get-tuple-element.56.chosen_ref, bf16[896,256]{1,0:T(8,128)(2,1)S(1)} %get-tuple-element.57.weights_ref, f32[2,8,64]{2,1,0:T(8,128)S(1)} %shard_map.132.refs_0_, ...), custom_call_target="tpu_custom_call" | custom-call | tf_op jit(solution)/shard_map/pallas_call | solution.py:695
  (35 shorter events, 3.3 us)
Async XLA Ops:
  0.6 7.3 %copy-start.1 = (bf16[64,3072]{1,0:T(8,128)(2,1)S(1)}, bf16[64,3072]{1,0:T(8,128)(2,1)}, u32[]{:S(2)}) copy-start(bf16[64,3072]{1,0:T(8,128)(2,1)} %embed_ref.3) | copy-start | bytes 1179652
  0.6 7.3 %copy-start.6 = (f32[1,1,3,3072]{3,1,2,0:T(1,128)S(1)}, f32[1,1,3,3072]{3,1,2,0:T(1,128)}, u32[]{:S(2)}) copy-start(f32[1,1,3,3072]{3,1,2,0:T(1,128)} %param.17) | copy-start | bytes 110596
  0.7 7.3 %copy-start.2 = (bf16[50,3,3072]{2,0,1:T(8,128)(2,1)S(1)}, bf16[50,3,3072]{2,0,1:T(8,128)(2,1)}, u32[]{:S(2)}) copy-start(bf16[50,3,3072]{2,0,1:T(8,128)(2,1)} %param.16) | copy-start | bytes 2764804
  0.7 7.3 %copy-start = (bf16[1,2304,3072]{2,1,0:T(8,128)(2,1)S(1)}, bf16[1,2304,3072]{2,1,0:T(8,128)(2,1)}, u32[]{:S(2)}) copy-start(bf16[1,2304,3072]{2,1,0:T(8,128)(2,1)} %param.14) | copy-start | bytes 42467332
  1.5 10.5 %copy-start.3 = (bf16[1,1,1,2,32,1536]{5,4,3,2,1,0:T(8,128)(2,1)S(1)}, bf16[1,1,1,2,32,1536]{5,4,3,2,1,0:T(8,128)(2,1)}, u32[]{:S(2)}) copy-start(bf16[1,1,1,2,32,1536]{5,4,3,2,1,0:T(8,128)(2,1)} %param.18) | copy-start | bytes 589828
  1.5 10.5 %copy-start.7 = (s32[2]{0:T(128)S(1)}, s32[2]{0:T(128)}, u32[]{:S(2)}) copy-start(s32[2]{0:T(128)} %order_ref.3) | copy-start | bytes 28
  1.6 10.4 %collective-permute-start = (f32[2,8,64]{2,1,0:T(8,128)S(1)}, f32[2,8,64]{2,1,0:T(8,128)S(1)}, u32[]{:S(2)}, u32[]{:S(2)}) collective-permute-start(f32[2,8,64]{2,1,0:T(8,128)S(1)} %shard_map.132.refs_0_), channel_id=1, source_target_pairs={{0,4},{4,0},{8,12},{12,8},{1,5},{5,1},{9,13},{13,9},{2,6},{6,2},{1... | collective-permute-start | bytes 12296 | tf_op jit(solution)/shard_map/ppermute | solution.py:735
  4.6 7.4 %collective-permute-start.2 = (f32[2,8,64]{2,1,0:T(8,128)S(1)}, f32[2,8,64]{2,1,0:T(8,128)S(1)}, u32[]{:S(2)}, u32[]{:S(2)}) collective-permute-start(f32[2,8,64]{2,1,0:T(8,128)S(1)} %shard_map.132.refs_0_), channel_id=1, source_target_pairs={{0,12},{4,8},{8,4},{12,0},{1,13},{5,9},{9,5},{13,1},{2,14},{6,10},... | collective-permute-start | bytes 12296 | tf_op jit(solution)/shard_map/ppermute | solution.py:735
  7.1 4.9 %collective-permute-start.1 = (f32[2,8,64]{2,1,0:T(8,128)S(1)}, f32[2,8,64]{2,1,0:T(8,128)S(1)}, u32[]{:S(2)}, u32[]{:S(2)}) collective-permute-start(f32[2,8,64]{2,1,0:T(8,128)S(1)} %shard_map.132.refs_0_), channel_id=1, source_target_pairs={{0,8},{4,12},{8,0},{12,4},{1,9},{5,13},{9,1},{13,5},{2,10},{6,14},... | collective-permute-start | bytes 12296 | tf_op jit(solution)/shard_map/ppermute | solution.py:735
  14.5 8.3 %collective-permute-start.3 = (bf16[64,768]{1,0:T(8,128)(2,1)S(1)}, bf16[64,768]{1,0:T(8,128)(2,1)S(1)}, u32[]{:S(2)}, u32[]{:S(2)}) collective-permute-start(bf16[64,768]{1,0:T(8,128)(2,1)S(1)} %get-tuple-element.38), channel_id=1, source_target_pairs={{0,4},{4,0},{8,12},{12,8},{1,5},{5,1},{9,13},{13,9},{2,6},{6,2},{1... | collective-permute-start | bytes 294920 | tf_op jit(solution)/shard_map/ppermute | solution.py:735
  16.4 9.9 %collective-permute-start.4 = (bf16[64,768]{1,0:T(8,128)(2,1)S(1)}, bf16[64,768]{1,0:T(8,128)(2,1)S(1)}, u32[]{:S(2)}, u32[]{:S(2)}) collective-permute-start(bf16[64,768]{1,0:T(8,128)(2,1)S(1)} %get-tuple-element.39), channel_id=1, source_target_pairs={{0,8},{4,12},{8,0},{12,4},{1,9},{5,13},{9,1},{13,5},{2,10},{6,14},... | collective-permute-start | bytes 294920 | tf_op jit(solution)/shard_map/ppermute | solution.py:735
  18.4 7.8 %collective-permute-start.5 = (bf16[64,768]{1,0:T(8,128)(2,1)S(1)}, bf16[64,768]{1,0:T(8,128)(2,1)S(1)}, u32[]{:S(2)}, u32[]{:S(2)}) collective-permute-start(bf16[64,768]{1,0:T(8,128)(2,1)S(1)} %get-tuple-element.40), channel_id=1, source_target_pairs={{0,12},{4,8},{8,4},{12,0},{1,13},{5,9},{9,5},{13,1},{2,14},{6,10},... | collective-permute-start | bytes 294920 | tf_op jit(solution)/shard_map/ppermute | solution.py:735
  26.4 6.8 %collective-permute-start.8 = (bf16[64,768]{1,0:T(8,128)(2,1)S(1)}, bf16[64,768]{1,0:T(8,128)(2,1)S(1)}, u32[]{:S(2)}, u32[]{:S(2)}) collective-permute-start(bf16[64,768]{1,0:T(8,128)(2,1)S(1)} %shard_map.136), channel_id=1, source_target_pairs={{0,2},{2,0},{4,6},{6,4},{8,10},{10,8},{12,14},{14,12},{1,3},{3,1},... | collective-permute-start | bytes 294920 | tf_op jit(solution)/shard_map/ppermute | solution.py:763
  27.9 9.1 %collective-permute-start.7 = (bf16[64,768]{1,0:T(8,128)(2,1)S(1)}, bf16[64,768]{1,0:T(8,128)(2,1)S(1)}, u32[]{:S(2)}, u32[]{:S(2)}) collective-permute-start(bf16[64,768]{1,0:T(8,128)(2,1)S(1)} %shard_map.136), channel_id=1, source_target_pairs={{0,10},{2,8},{4,14},{6,12},{8,2},{10,0},{12,6},{14,4},{1,11},{3,9}... | collective-permute-start | bytes 294920 | tf_op jit(solution)/shard_map/ppermute | solution.py:763
  30.5 6.5 %collective-permute-start.6 = (bf16[64,768]{1,0:T(8,128)(2,1)S(1)}, bf16[64,768]{1,0:T(8,128)(2,1)S(1)}, u32[]{:S(2)}, u32[]{:S(2)}) collective-permute-start(bf16[64,768]{1,0:T(8,128)(2,1)S(1)} %shard_map.136), channel_id=1, source_target_pairs={{0,6},{2,4},{4,2},{6,0},{8,14},{10,12},{12,10},{14,8},{1,7},{3,5},... | collective-permute-start | bytes 294920 | tf_op jit(solution)/shard_map/ppermute | solution.py:763
  31.8 7.4 %collective-permute-start.9 = (bf16[64,768]{1,0:T(8,128)(2,1)S(1)}, bf16[64,768]{1,0:T(8,128)(2,1)S(1)}, u32[]{:S(2)}, u32[]{:S(2)}) collective-permute-start(bf16[64,768]{1,0:T(8,128)(2,1)S(1)} %shard_map.136), channel_id=1, source_target_pairs={{0,14},{2,12},{4,10},{6,8},{8,6},{10,4},{12,2},{14,0},{1,15},{3,13... | collective-permute-start | bytes 294920 | tf_op jit(solution)/shard_map/ppermute | solution.py:763
  37.0 14.3 %copy-start.4 = (bf16[3072,64]{0,1:T(8,128)(2,1)S(1)}, bf16[3072,64]{0,1:T(8,128)(2,1)}, u32[]{:S(2)}) copy-start(bf16[3072,64]{0,1:T(8,128)(2,1)} %param.19) | copy-start | bytes 1179652
  38.4 17.4 %copy-start.5 = (bf16[27,16,128]{2,1,0:T(8,128)(2,1)S(1)}, bf16[27,16,128]{2,1,0:T(8,128)(2,1)}, u32[]{:S(2)}) copy-start(bf16[27,16,128]{2,1,0:T(8,128)(2,1)} %conv_ref) | copy-start | bytes 331780
  38.4 17.4 %copy-start.8 = (s32[4]{0:T(128)S(1)}, s32[4]{0:T(128)}, u32[]{:S(2)}) copy-start(s32[4]{0:T(128)} %slab_ref) | copy-start | bytes 52
  42.0 6.6 %collective-permute-start.10 = (bf16[16,3072]{1,0:T(8,128)(2,1)S(1)}, bf16[16,3072]{1,0:T(8,128)(2,1)S(1)}, u32[]{:S(2)}, u32[]{:S(2)}) collective-permute-start(bf16[16,3072]{1,0:T(8,128)(2,1)S(1)} %get-tuple-element.50), channel_id=1, source_target_pairs={{0,12},{4,8},{8,4},{12,0},{1,13},{5,9},{9,5},{13,1},{2,14},{6,10},... | collective-permute-start | bytes 294920 | tf_op jit(solution)/shard_map/ppermute | solution.py:735
  45.0 6.3 %collective-permute-start.11 = (bf16[16,3072]{1,0:T(8,128)(2,1)S(1)}, bf16[16,3072]{1,0:T(8,128)(2,1)S(1)}, u32[]{:S(2)}, u32[]{:S(2)}) collective-permute-start(bf16[16,3072]{1,0:T(8,128)(2,1)S(1)} %get-tuple-element.52), channel_id=1, source_target_pairs={{0,4},{4,0},{8,12},{12,8},{1,5},{5,1},{9,13},{13,9},{2,6},{6,2},{1... | collective-permute-start | bytes 294920 | tf_op jit(solution)/shard_map/ppermute | solution.py:735
  45.0 6.3 %collective-permute-start.12 = (bf16[16,3072]{1,0:T(8,128)(2,1)S(1)}, bf16[16,3072]{1,0:T(8,128)(2,1)S(1)}, u32[]{:S(2)}, u32[]{:S(2)}) collective-permute-start(bf16[16,3072]{1,0:T(8,128)(2,1)S(1)} %get-tuple-element.53), channel_id=1, source_target_pairs={{0,8},{4,12},{8,0},{12,4},{1,9},{5,13},{9,1},{13,5},{2,10},{6,14},... | collective-permute-start | bytes 294920 | tf_op jit(solution)/shard_map/ppermute | solution.py:735
  52.2 10.4 %all-to-all-start = ((f32[16,8,128]{2,1,0:T(8,128)}), f32[16,8,128]{2,1,0:T(8,128)S(1)}, u32[]{:S(2)}, u32[]{:S(2)}) async-start(f32[16,8,128]{2,1,0:T(8,128)} %shard_map.141), calls=%async_computation | async-start | bytes 131072 | tf_op jit(solution)/shard_map/all_to_all | solution.py:793

commit v11 on v10

--- a/solution.py
+++ b/solution.py
@@ -311,7 +311,7 @@
     weights = [jnp.exp(score - top) for score, top in zip(scores, tops)]
     totals = [jnp.sum(weight, axis=-1, keepdims=True) for weight in weights]
     for head in range(heads):
-        probs = (weights[head] / totals[head]).astype(jnp.bfloat16)
+        probs = (weights[head] * (1.0 / totals[head])).astype(jnp.bfloat16)
         attended[:, head * HEAD_DIM : (head + 1) * HEAD_DIM] = jnp.dot(
             probs, values[head], preferred_element_type=jnp.float32
         ).astype(jnp.bfloat16)
@@ -419,7 +419,7 @@
     )(*values)
 
 
-def block_sum_kernel(rows_ref, own_ref, term_ref, *refs):
+def block_sum_kernel(rows_ref, own_ref, term_ref, mark_ref, *refs):
     part_refs, block_ref = refs[:-1], refs[-1]
     columns = own_ref.shape[1]
     first = pl.multiple_of(lax.axis_index("seq") * columns, columns)
@@ -433,11 +433,11 @@
 def block_sum(mod_rows, own, term, parts):
     return pl.pallas_call(
         block_sum_kernel,
-        in_specs=[whole()] * (3 + len(parts)),
+        in_specs=[whole()] * (4 + len(parts)),
         out_specs=whole(),
         out_shape=jax.ShapeDtypeStruct(own.shape, own.dtype),
         compiler_params=kernel_params(),
-    )(mod_rows, own, term, *parts)
+    )(mod_rows, own, term, met(parts[1:2]), *parts)
 
 
 def scaled_piece(place, k, piece_ref, rows_ref):

time: 64.1 us -> 64.1 us (level)
  no operation moved by 1% of the time
where the time goes in v11:
time: 64.1 us; the launch traced here: 63.8 us
  starting transfers between devices  24.9 us (39%)
  Pallas kernels  20.4 us (32%)
  waiting for transfers between devices  17 us (27%)
  between operations  1.53 us (2%)
    ppermute x9, starting transfers between devices, returned(): lax.ppermute(values[k], 'seq', within(k))  14.6 us
    ppermute x9, waiting for transfers between devices, returned(): lax.ppermute(values[k], 'seq', within(k))  8.31 us
    ppermute x4, starting transfers between devices, shards(): pieces.insert(0, lax.ppermute(block, ('seq', 'segment'), pairs))  6.81 us
    all_to_all x1, waiting for transfers between devices, shards(): lax.all_to_all(terms, peers, split_axis=0, concat_axis=0, tiled=True)  4.75 us
    pallas_call x1, Pallas kernels, prepared(): pl.pallas_call(prepare_kernel, in_specs=[whole(pltpu.SMEM)] + [whole()] *...  4.05 us
    ppermute x4, waiting for transfers between devices, shards(): pieces.insert(0, lax.ppermute(block, ('seq', 'segment'), pairs))  3.94 us
    pallas_call x1, Pallas kernels, turned(): pl.pallas_call(turn_kernel, in_specs=[whole(pl.ANY)] + [whole()] * 2, out...  3.84 us
    all_to_all x1, starting transfers between devices, shards(): lax.all_to_all(terms, peers, split_axis=0, concat_axis=0, tiled=True)  3.5 us
  transfers between devices with their start and end apart: 14, of which 6 were waited for; matrix products, arithmetic and copies ran while one was open for 0% of the time, Pallas kernels for 19%

profile of v11, /device:TPU:0, one launch (start us, length us, event | category | flops | bytes accessed | tf_op | source)
XLA Modules:
  0.0 63.8 jit_solution(5650035160531436341)
XLA Ops:
  1.6 3.1 %collective-permute-start = (f32[2,8,64]{2,1,0:T(8,128)S(1)}, f32[2,8,64]{2,1,0:T(8,128)S(1)}, u32[]{:S(2)}, u32[]{:S(2)}) collective-permute-start(f32[2,8,64]{2,1,0:T(8,128)S(1)} %shard_map.132.refs_0_), channel_id=1, source_target_pairs={{0,4},{4,0},{8,12},{12,8},{1,5},{5,1},{9,13},{13,9},{2,6},{6,2},{1... | collective-permute-start | bytes 12296 | tf_op jit(solution)/shard_map/ppermute | solution.py:735
  4.6 2.5 %collective-permute-start.2 = (f32[2,8,64]{2,1,0:T(8,128)S(1)}, f32[2,8,64]{2,1,0:T(8,128)S(1)}, u32[]{:S(2)}, u32[]{:S(2)}) collective-permute-start(f32[2,8,64]{2,1,0:T(8,128)S(1)} %shard_map.132.refs_0_), channel_id=1, source_target_pairs={{0,12},{4,8},{8,4},{12,0},{1,13},{5,9},{9,5},{13,1},{2,14},{6,10},... | collective-permute-start | bytes 12296 | tf_op jit(solution)/shard_map/ppermute | solution.py:735
  7.9 4.1 %shard_map.131 = (f32[3,3072]{1,0:T(4,128)S(1)}, bf16[2304,128]{1,0:T(8,128)(2,1)S(1)}, bf16[768,3072]{1,0:T(8,128)(2,1)S(1)}) custom-call(s32[1]{0:T(128)S(6)} %copy.14.timestep_ref, bf16[3,50,3072]{2,1,0:T(8,128)(2,1)S(1)} %bitcast.9, f32[3,1,3072]{2,1,0:T(1,128)S(1)} %bitcast.13, bf16[64,3072]{1,0:T(8,128)(2,1)S(1)} %copy-done.1, ...), custom_call_target="tpu_custom_call" | custom-call | tf_op jit(solution)/shard_map/pallas_call | solution.py:254
  12.1 2.5 %shard_map.134 = (bf16[64,768]{1,0:T(8,128)(2,1)S(1)}, bf16[64,768]{1,0:T(8,128)(2,1)S(1)}, bf16[64,768]{1,0:T(8,128)(2,1)S(1)}, bf16[64,768]{1,0:T(8,128)(2,1)S(1)}, bf16[64,768]{1,0:T(8,128)(2,1)S(1)}) custom-call(s32[2]{0:T(128)S(1)} %copy-done.7, bf16[64,3072]{1,0:T(8,128)(2,1)S(1)} %copy-done.1, bf16[2304,128]{1,0:T(8,128)(2,1)S(1)} %get-tuple-element.32.heads_ref, ...), custom_call_target="tpu_custom_call" | custom-call | tf_op jit(solution)/shard_map/pallas_call | solution.py:370
  14.5 1.9 %collective-permute-start.3 = (bf16[64,768]{1,0:T(8,128)(2,1)S(1)}, bf16[64,768]{1,0:T(8,128)(2,1)S(1)}, u32[]{:S(2)}, u32[]{:S(2)}) collective-permute-start(bf16[64,768]{1,0:T(8,128)(2,1)S(1)} %get-tuple-element.37), channel_id=1, source_target_pairs={{0,4},{4,0},{8,12},{12,8},{1,5},{5,1},{9,13},{13,9},{2,6},{6,2},{1... | collective-permute-start | bytes 294920 | tf_op jit(solution)/shard_map/ppermute | solution.py:735
  16.4 2.0 %collective-permute-start.4 = (bf16[64,768]{1,0:T(8,128)(2,1)S(1)}, bf16[64,768]{1,0:T(8,128)(2,1)S(1)}, u32[]{:S(2)}, u32[]{:S(2)}) collective-permute-start(bf16[64,768]{1,0:T(8,128)(2,1)S(1)} %get-tuple-element.39), channel_id=1, source_target_pairs={{0,8},{4,12},{8,0},{12,4},{1,9},{5,13},{9,1},{13,5},{2,10},{6,14},... | collective-permute-start | bytes 294920 | tf_op jit(solution)/shard_map/ppermute | solution.py:735
  19.0 3.8 %shard_map.135 = (bf16[3072,2304]{1,0:T(8,128)(2,1)S(1)}, f32[1,2304]{1,0:T(1,128)S(1)}) custom-call(bf16[64,768]{1,0:T(8,128)(2,1)S(1)} %get-tuple-element.34.after_ref.own_ref, bf16[2304,3072]{1,0:T(8,128)(2,1)S(1)} %bitcast.8, bf16[2304,128]{1,0:T(8,128)(2,1)S(1)} %get-tuple-element.32.heads_ref), custom_call_target="tpu_custom_call" | custom-call | flops 5000000000 | tf_op jit(solution)/shard_map/pallas_call | solution.py:395
  22.9 3.4 %collective-permute-done.4.refs_2_ = bf16[64,768]{1,0:T(8,128)(2,1)S(1)} collective-permute-done((bf16[64,768]{1,0:T(8,128)(2,1)S(1)}, bf16[64,768]{1,0:T(8,128)(2,1)S(1)}, u32[]{:S(2)}, u32[]{:S(2)}) %collective-permute-start.4) | collective-permute-done | bytes 98336 | tf_op jit(solution)/shard_map/ppermute | solution.py:735
  26.4 1.6 %collective-permute-start.8 = (bf16[64,768]{1,0:T(8,128)(2,1)S(1)}, bf16[64,768]{1,0:T(8,128)(2,1)S(1)}, u32[]{:S(2)}, u32[]{:S(2)}) collective-permute-start(bf16[64,768]{1,0:T(8,128)(2,1)S(1)} %shard_map.137), channel_id=1, source_target_pairs={{0,2},{2,0},{4,6},{6,4},{8,10},{10,8},{12,14},{14,12},{1,3},{3,1},... | collective-permute-start | bytes 294920 | tf_op jit(solution)/shard_map/ppermute | solution.py:763
  27.9 2.6 %collective-permute-start.7 = (bf16[64,768]{1,0:T(8,128)(2,1)S(1)}, bf16[64,768]{1,0:T(8,128)(2,1)S(1)}, u32[]{:S(2)}, u32[]{:S(2)}) collective-permute-start(bf16[64,768]{1,0:T(8,128)(2,1)S(1)} %shard_map.137), channel_id=1, source_target_pairs={{0,10},{2,8},{4,14},{6,12},{8,2},{10,0},{12,6},{14,4},{1,11},{3,9}... | collective-permute-start | bytes 294920 | tf_op jit(solution)/shard_map/ppermute | solution.py:763
  30.5 1.3 %collective-permute-start.6 = (bf16[64,768]{1,0:T(8,128)(2,1)S(1)}, bf16[64,768]{1,0:T(8,128)(2,1)S(1)}, u32[]{:S(2)}, u32[]{:S(2)}) collective-permute-start(bf16[64,768]{1,0:T(8,128)(2,1)S(1)} %shard_map.137), channel_id=1, source_target_pairs={{0,6},{2,4},{4,2},{6,0},{8,14},{10,12},{12,10},{14,8},{1,7},{3,5},... | collective-permute-start | bytes 294920 | tf_op jit(solution)/shard_map/ppermute | solution.py:763
  31.9 1.3 %collective-permute-start.9 = (bf16[64,768]{1,0:T(8,128)(2,1)S(1)}, bf16[64,768]{1,0:T(8,128)(2,1)S(1)}, u32[]{:S(2)}, u32[]{:S(2)}) collective-permute-start(bf16[64,768]{1,0:T(8,128)(2,1)S(1)} %shard_map.137), channel_id=1, source_target_pairs={{0,14},{2,12},{4,10},{6,8},{8,6},{10,4},{12,2},{14,0},{1,15},{3,13... | collective-permute-start | bytes 294920 | tf_op jit(solution)/shard_map/ppermute | solution.py:763
  33.9 3.1 %collective-permute-done.7.refs_1_.refs_2_ = bf16[64,768]{1,0:T(8,128)(2,1)S(1)} collective-permute-done((bf16[64,768]{1,0:T(8,128)(2,1)S(1)}, bf16[64,768]{1,0:T(8,128)(2,1)S(1)}, u32[]{:S(2)}, u32[]{:S(2)}) %collective-permute-start.7) | collective-permute-done | bytes 98336 | tf_op jit(solution)/shard_map/ppermute | solution.py:763
  37.0 1.4 %shard_map.139 = (f32[64,2304]{1,0:T(8,128)S(1)}, f32[64,1]{1,0:T(8,128)S(1)}) custom-call(f32[3,3072]{1,0:T(4,128)S(1)} %get-tuple-element.31.rows_ref, bf16[3072,2304]{1,0:T(8,128)(2,1)S(1)} %get-tuple-element.35.turned_ref.qkv_ref, bf16[64,768]{1,0:T(8,128)(2,1)S(1)} %collective-permute-done.6.refs_0_.refs_1_, ...), custom_call_target="tpu_custom_call" | custom-call | tf_op jit(solution)/shard_map/pallas_call | solution.py:476
  39.3 2.7 %shard_map.140 = (bf16[16,3072]{1,0:T(8,128)(2,1)S(1)}, bf16[16,3072]{1,0:T(8,128)(2,1)S(1)}, bf16[16,3072]{1,0:T(8,128)(2,1)S(1)}, bf16[16,3072]{1,0:T(8,128)(2,1)S(1)}, bf16[16,3072]{1,0:T(8,128)(2,1)S(1)}) custom-call(s32[2]{0:T(128)S(1)} %copy-done.7, f32[3,3072]{1,0:T(4,128)S(1)} %get-tuple-element.31.rows_ref, ...), custom_call_target="tpu_custom_call" | custom-call | tf_op jit(solution)/shard_map/pallas_call | solution.py:528
  42.0 3.1 %collective-permute-start.10 = (bf16[16,3072]{1,0:T(8,128)(2,1)S(1)}, bf16[16,3072]{1,0:T(8,128)(2,1)S(1)}, u32[]{:S(2)}, u32[]{:S(2)}) collective-permute-start(bf16[16,3072]{1,0:T(8,128)(2,1)S(1)} %get-tuple-element.50), channel_id=1, source_target_pairs={{0,12},{4,8},{8,4},{12,0},{1,13},{5,9},{9,5},{13,1},{2,14},{6,10},... | collective-permute-start | bytes 294920 | tf_op jit(solution)/shard_map/ppermute | solution.py:735
  45.0 1.4 %collective-permute-start.12 = (bf16[16,3072]{1,0:T(8,128)(2,1)S(1)}, bf16[16,3072]{1,0:T(8,128)(2,1)S(1)}, u32[]{:S(2)}, u32[]{:S(2)}) collective-permute-start(bf16[16,3072]{1,0:T(8,128)(2,1)S(1)} %get-tuple-element.53), channel_id=1, source_target_pairs={{0,8},{4,12},{8,0},{12,4},{1,9},{5,13},{9,1},{13,5},{2,10},{6,14},... | collective-permute-start | bytes 294920 | tf_op jit(solution)/shard_map/ppermute | solution.py:735
  46.4 2.1 %collective-permute-done.10.refs_0_.refs_3_ = bf16[16,3072]{1,0:T(8,128)(2,1)S(1)} collective-permute-done((bf16[16,3072]{1,0:T(8,128)(2,1)S(1)}, bf16[16,3072]{1,0:T(8,128)(2,1)S(1)}, u32[]{:S(2)}, u32[]{:S(2)}) %collective-permute-start.10) | collective-permute-done | bytes 98336 | tf_op jit(solution)/shard_map/ppermute | solution.py:735
  48.5 2.8 %collective-permute-done.11.refs_1_ = bf16[16,3072]{1,0:T(8,128)(2,1)S(1)} collective-permute-done((bf16[16,3072]{1,0:T(8,128)(2,1)S(1)}, bf16[16,3072]{1,0:T(8,128)(2,1)S(1)}, u32[]{:S(2)}, u32[]{:S(2)}) %collective-permute-start.11) | collective-permute-done | bytes 98336 | tf_op jit(solution)/shard_map/ppermute | solution.py:735
  51.3 0.9 %shard_map.142 = f32[16,8,128]{2,1,0:T(8,128)} custom-call(f32[3,3072]{1,0:T(4,128)S(1)} %get-tuple-element.31.rows_ref, bf16[16,3072]{1,0:T(8,128)(2,1)S(1)} %get-tuple-element.45.own_ref, bf16[64,3072]{1,0:T(8,128)(2,1)S(1)} %bitcast.12, f32[8,128]{1,0:T(8,128)S(1)} %shard_map.141.far_ref, bf16[16,3072]{1,0:T(8,128)(2,1)S(1)} %get-tuple-element.51.refs_0_, ...), custom_call_target="tpu_custom_call" | custom-call | tf_op jit(solution)/shard_map/pallas_call | solution.py:562
  52.2 3.5 %all-to-all-start = ((f32[16,8,128]{2,1,0:T(8,128)}), f32[16,8,128]{2,1,0:T(8,128)S(1)}, u32[]{:S(2)}, u32[]{:S(2)}) async-start(f32[16,8,128]{2,1,0:T(8,128)} %shard_map.142), calls=%async_computation | async-start | bytes 131072 | tf_op jit(solution)/shard_map/all_to_all | solution.py:793
  55.8 2.1 %shard_map.143 = (bf16[64,3584]{1,0:T(8,128)(2,1)S(1)}, bf16[896,256]{1,0:T(8,128)(2,1)S(1)}) custom-call(s32[4]{0:T(128)S(1)} %copy-done.8, bf16[27,16,128]{2,1,0:T(8,128)(2,1)S(1)} %copy-done.5), custom_call_target="tpu_custom_call" | custom-call | tf_op jit(solution)/shard_map/pallas_call | solution.py:624
  57.8 4.8 %all-to-all-done.terms_ref = f32[16,8,128]{2,1,0:T(8,128)S(1)} async-done(((f32[16,8,128]{2,1,0:T(8,128)}), f32[16,8,128]{2,1,0:T(8,128)S(1)}, u32[]{:S(2)}, u32[]{:S(2)}) %all-to-all-start) | async-done | bytes 65568 | tf_op jit(solution)/shard_map/all_to_all | solution.py:793
  62.6 1.2 %shard_map.144 = (f32[2,8,64]{2,1,0:T(8,128)}, bf16[128,128]{1,0:T(8,128)(2,1)}) custom-call(f32[16,8,128]{2,1,0:T(8,128)S(1)} %all-to-all-done.terms_ref, bf16[64,3584]{1,0:T(8,128)(2,1)S(1)} %get-tuple-element.56.chosen_ref, bf16[896,256]{1,0:T(8,128)(2,1)S(1)} %get-tuple-element.57.weights_ref, f32[2,8,64]{2,1,0:T(8,128)S(1)} %shard_map.132.refs_0_, ...), custom_call_target="tpu_custom_call" | custom-call | tf_op jit(solution)/shard_map/pallas_call | solution.py:695
  (36 shorter events, 3.3 us)
Async XLA Ops:
  0.6 7.3 %copy-start.1 = (bf16[64,3072]{1,0:T(8,128)(2,1)S(1)}, bf16[64,3072]{1,0:T(8,128)(2,1)}, u32[]{:S(2)}) copy-start(bf16[64,3072]{1,0:T(8,128)(2,1)} %embed_ref.3) | copy-start | bytes 1179652
  0.6 7.3 %copy-start.6 = (f32[1,1,3,3072]{3,1,2,0:T(1,128)S(1)}, f32[1,1,3,3072]{3,1,2,0:T(1,128)}, u32[]{:S(2)}) copy-start(f32[1,1,3,3072]{3,1,2,0:T(1,128)} %param.17) | copy-start | bytes 110596
  0.7 7.3 %copy-start.2 = (bf16[50,3,3072]{2,0,1:T(8,128)(2,1)S(1)}, bf16[50,3,3072]{2,0,1:T(8,128)(2,1)}, u32[]{:S(2)}) copy-start(bf16[50,3,3072]{2,0,1:T(8,128)(2,1)} %param.16) | copy-start | bytes 2764804
  0.7 7.3 %copy-start = (bf16[1,2304,3072]{2,1,0:T(8,128)(2,1)S(1)}, bf16[1,2304,3072]{2,1,0:T(8,128)(2,1)}, u32[]{:S(2)}) copy-start(bf16[1,2304,3072]{2,1,0:T(8,128)(2,1)} %param.14) | copy-start | bytes 42467332
  1.5 10.5 %copy-start.3 = (bf16[1,1,1,2,32,1536]{5,4,3,2,1,0:T(8,128)(2,1)S(1)}, bf16[1,1,1,2,32,1536]{5,4,3,2,1,0:T(8,128)(2,1)}, u32[]{:S(2)}) copy-start(bf16[1,1,1,2,32,1536]{5,4,3,2,1,0:T(8,128)(2,1)} %param.18) | copy-start | bytes 589828
  1.5 10.5 %copy-start.7 = (s32[2]{0:T(128)S(1)}, s32[2]{0:T(128)}, u32[]{:S(2)}) copy-start(s32[2]{0:T(128)} %order_ref.3) | copy-start | bytes 28
  1.6 10.4 %collective-permute-start = (f32[2,8,64]{2,1,0:T(8,128)S(1)}, f32[2,8,64]{2,1,0:T(8,128)S(1)}, u32[]{:S(2)}, u32[]{:S(2)}) collective-permute-start(f32[2,8,64]{2,1,0:T(8,128)S(1)} %shard_map.132.refs_0_), channel_id=1, source_target_pairs={{0,4},{4,0},{8,12},{12,8},{1,5},{5,1},{9,13},{13,9},{2,6},{6,2},{1... | collective-permute-start | bytes 12296 | tf_op jit(solution)/shard_map/ppermute | solution.py:735
  4.6 7.4 %collective-permute-start.2 = (f32[2,8,64]{2,1,0:T(8,128)S(1)}, f32[2,8,64]{2,1,0:T(8,128)S(1)}, u32[]{:S(2)}, u32[]{:S(2)}) collective-permute-start(f32[2,8,64]{2,1,0:T(8,128)S(1)} %shard_map.132.refs_0_), channel_id=1, source_target_pairs={{0,12},{4,8},{8,4},{12,0},{1,13},{5,9},{9,5},{13,1},{2,14},{6,10},... | collective-permute-start | bytes 12296 | tf_op jit(solution)/shard_map/ppermute | solution.py:735
  7.1 4.9 %collective-permute-start.1 = (f32[2,8,64]{2,1,0:T(8,128)S(1)}, f32[2,8,64]{2,1,0:T(8,128)S(1)}, u32[]{:S(2)}, u32[]{:S(2)}) collective-permute-start(f32[2,8,64]{2,1,0:T(8,128)S(1)} %shard_map.132.refs_0_), channel_id=1, source_target_pairs={{0,8},{4,12},{8,0},{12,4},{1,9},{5,13},{9,1},{13,5},{2,10},{6,14},... | collective-permute-start | bytes 12296 | tf_op jit(solution)/shard_map/ppermute | solution.py:735
  14.5 8.3 %collective-permute-start.3 = (bf16[64,768]{1,0:T(8,128)(2,1)S(1)}, bf16[64,768]{1,0:T(8,128)(2,1)S(1)}, u32[]{:S(2)}, u32[]{:S(2)}) collective-permute-start(bf16[64,768]{1,0:T(8,128)(2,1)S(1)} %get-tuple-element.37), channel_id=1, source_target_pairs={{0,4},{4,0},{8,12},{12,8},{1,5},{5,1},{9,13},{13,9},{2,6},{6,2},{1... | collective-permute-start | bytes 294920 | tf_op jit(solution)/shard_map/ppermute | solution.py:735
  16.4 9.9 %collective-permute-start.4 = (bf16[64,768]{1,0:T(8,128)(2,1)S(1)}, bf16[64,768]{1,0:T(8,128)(2,1)S(1)}, u32[]{:S(2)}, u32[]{:S(2)}) collective-permute-start(bf16[64,768]{1,0:T(8,128)(2,1)S(1)} %get-tuple-element.39), channel_id=1, source_target_pairs={{0,8},{4,12},{8,0},{12,4},{1,9},{5,13},{9,1},{13,5},{2,10},{6,14},... | collective-permute-start | bytes 294920 | tf_op jit(solution)/shard_map/ppermute | solution.py:735
  18.4 7.8 %collective-permute-start.5 = (bf16[64,768]{1,0:T(8,128)(2,1)S(1)}, bf16[64,768]{1,0:T(8,128)(2,1)S(1)}, u32[]{:S(2)}, u32[]{:S(2)}) collective-permute-start(bf16[64,768]{1,0:T(8,128)(2,1)S(1)} %get-tuple-element.40), channel_id=1, source_target_pairs={{0,12},{4,8},{8,4},{12,0},{1,13},{5,9},{9,5},{13,1},{2,14},{6,10},... | collective-permute-start | bytes 294920 | tf_op jit(solution)/shard_map/ppermute | solution.py:735
  26.4 6.8 %collective-permute-start.8 = (bf16[64,768]{1,0:T(8,128)(2,1)S(1)}, bf16[64,768]{1,0:T(8,128)(2,1)S(1)}, u32[]{:S(2)}, u32[]{:S(2)}) collective-permute-start(bf16[64,768]{1,0:T(8,128)(2,1)S(1)} %shard_map.137), channel_id=1, source_target_pairs={{0,2},{2,0},{4,6},{6,4},{8,10},{10,8},{12,14},{14,12},{1,3},{3,1},... | collective-permute-start | bytes 294920 | tf_op jit(solution)/shard_map/ppermute | solution.py:763
  27.9 9.1 %collective-permute-start.7 = (bf16[64,768]{1,0:T(8,128)(2,1)S(1)}, bf16[64,768]{1,0:T(8,128)(2,1)S(1)}, u32[]{:S(2)}, u32[]{:S(2)}) collective-permute-start(bf16[64,768]{1,0:T(8,128)(2,1)S(1)} %shard_map.137), channel_id=1, source_target_pairs={{0,10},{2,8},{4,14},{6,12},{8,2},{10,0},{12,6},{14,4},{1,11},{3,9}... | collective-permute-start | bytes 294920 | tf_op jit(solution)/shard_map/ppermute | solution.py:763
  30.5 6.5 %collective-permute-start.6 = (bf16[64,768]{1,0:T(8,128)(2,1)S(1)}, bf16[64,768]{1,0:T(8,128)(2,1)S(1)}, u32[]{:S(2)}, u32[]{:S(2)}) collective-permute-start(bf16[64,768]{1,0:T(8,128)(2,1)S(1)} %shard_map.137), channel_id=1, source_target_pairs={{0,6},{2,4},{4,2},{6,0},{8,14},{10,12},{12,10},{14,8},{1,7},{3,5},... | collective-permute-start | bytes 294920 | tf_op jit(solution)/shard_map/ppermute | solution.py:763
  31.9 7.4 %collective-permute-start.9 = (bf16[64,768]{1,0:T(8,128)(2,1)S(1)}, bf16[64,768]{1,0:T(8,128)(2,1)S(1)}, u32[]{:S(2)}, u32[]{:S(2)}) collective-permute-start(bf16[64,768]{1,0:T(8,128)(2,1)S(1)} %shard_map.137), channel_id=1, source_target_pairs={{0,14},{2,12},{4,10},{6,8},{8,6},{10,4},{12,2},{14,0},{1,15},{3,13... | collective-permute-start | bytes 294920 | tf_op jit(solution)/shard_map/ppermute | solution.py:763
  37.0 14.3 %copy-start.4 = (bf16[3072,64]{0,1:T(8,128)(2,1)S(1)}, bf16[3072,64]{0,1:T(8,128)(2,1)}, u32[]{:S(2)}) copy-start(bf16[3072,64]{0,1:T(8,128)(2,1)} %param.19) | copy-start | bytes 1179652
  38.4 17.4 %copy-start.5 = (bf16[27,16,128]{2,1,0:T(8,128)(2,1)S(1)}, bf16[27,16,128]{2,1,0:T(8,128)(2,1)}, u32[]{:S(2)}) copy-start(bf16[27,16,128]{2,1,0:T(8,128)(2,1)} %conv_ref) | copy-start | bytes 331780
  38.4 17.4 %copy-start.8 = (s32[4]{0:T(128)S(1)}, s32[4]{0:T(128)}, u32[]{:S(2)}) copy-start(s32[4]{0:T(128)} %slab_ref) | copy-start | bytes 52
  42.0 6.6 %collective-permute-start.10 = (bf16[16,3072]{1,0:T(8,128)(2,1)S(1)}, bf16[16,3072]{1,0:T(8,128)(2,1)S(1)}, u32[]{:S(2)}, u32[]{:S(2)}) collective-permute-start(bf16[16,3072]{1,0:T(8,128)(2,1)S(1)} %get-tuple-element.50), channel_id=1, source_target_pairs={{0,12},{4,8},{8,4},{12,0},{1,13},{5,9},{9,5},{13,1},{2,14},{6,10},... | collective-permute-start | bytes 294920 | tf_op jit(solution)/shard_map/ppermute | solution.py:735
  45.0 6.3 %collective-permute-start.11 = (bf16[16,3072]{1,0:T(8,128)(2,1)S(1)}, bf16[16,3072]{1,0:T(8,128)(2,1)S(1)}, u32[]{:S(2)}, u32[]{:S(2)}) collective-permute-start(bf16[16,3072]{1,0:T(8,128)(2,1)S(1)} %get-tuple-element.52), channel_id=1, source_target_pairs={{0,4},{4,0},{8,12},{12,8},{1,5},{5,1},{9,13},{13,9},{2,6},{6,2},{1... | collective-permute-start | bytes 294920 | tf_op jit(solution)/shard_map/ppermute | solution.py:735
  45.0 6.3 %collective-permute-start.12 = (bf16[16,3072]{1,0:T(8,128)(2,1)S(1)}, bf16[16,3072]{1,0:T(8,128)(2,1)S(1)}, u32[]{:S(2)}, u32[]{:S(2)}) collective-permute-start(bf16[16,3072]{1,0:T(8,128)(2,1)S(1)} %get-tuple-element.53), channel_id=1, source_target_pairs={{0,8},{4,12},{8,0},{12,4},{1,9},{5,13},{9,1},{13,5},{2,10},{6,14},... | collective-permute-start | bytes 294920 | tf_op jit(solution)/shard_map/ppermute | solution.py:735
  52.2 10.4 %all-to-all-start = ((f32[16,8,128]{2,1,0:T(8,128)}), f32[16,8,128]{2,1,0:T(8,128)S(1)}, u32[]{:S(2)}, u32[]{:S(2)}) async-start(f32[16,8,128]{2,1,0:T(8,128)} %shard_map.142), calls=%async_computation | async-start | bytes 131072 | tf_op jit(solution)/shard_map/all_to_all | solution.py:793

commit v12 on v10

--- a/solution.py
+++ b/solution.py
@@ -311,7 +311,7 @@
     weights = [jnp.exp(score - top) for score, top in zip(scores, tops)]
     totals = [jnp.sum(weight, axis=-1, keepdims=True) for weight in weights]
     for head in range(heads):
-        probs = (weights[head] / totals[head]).astype(jnp.bfloat16)
+        probs = (weights[head] * (1.0 / totals[head])).astype(jnp.bfloat16)
         attended[:, head * HEAD_DIM : (head + 1) * HEAD_DIM] = jnp.dot(
             probs, values[head], preferred_element_type=jnp.float32
         ).astype(jnp.bfloat16)

time: 64.1 us -> 64.1 us (level)
  no operation moved by 1% of the time
where the time goes in v12:
time: 64.1 us; the launch traced here: 63.8 us
  starting transfers between devices  24.9 us (39%)
  Pallas kernels  20.4 us (32%)
  waiting for transfers between devices  17 us (27%)
  between operations  1.52 us (2%)
    ppermute x9, starting transfers between devices, returned(): lax.ppermute(values[k], 'seq', within(k))  14.6 us
    ppermute x9, waiting for transfers between devices, returned(): lax.ppermute(values[k], 'seq', within(k))  8.32 us
    ppermute x4, starting transfers between devices, shards(): pieces.insert(0, lax.ppermute(block, ('seq', 'segment'), pairs))  6.81 us
    all_to_all x1, waiting for transfers between devices, shards(): lax.all_to_all(terms, peers, split_axis=0, concat_axis=0, tiled=True)  4.75 us
    pallas_call x1, Pallas kernels, prepared(): pl.pallas_call(prepare_kernel, in_specs=[whole(pltpu.SMEM)] + [whole()] *...  4.05 us
    ppermute x4, waiting for transfers between devices, shards(): pieces.insert(0, lax.ppermute(block, ('seq', 'segment'), pairs))  3.94 us
    pallas_call x1, Pallas kernels, turned(): pl.pallas_call(turn_kernel, in_specs=[whole(pl.ANY)] + [whole()] * 2, out...  3.84 us
    all_to_all x1, starting transfers between devices, shards(): lax.all_to_all(terms, peers, split_axis=0, concat_axis=0, tiled=True)  3.5 us
  transfers between devices with their start and end apart: 14, of which 6 were waited for; matrix products, arithmetic and copies ran while one was open for 0% of the time, Pallas kernels for 19%

profile of v12, /device:TPU:0, one launch (start us, length us, event | category | flops | bytes accessed | tf_op | source)
XLA Modules:
  0.0 63.8 jit_solution(7493446078129857322)
XLA Ops:
  1.6 3.1 %collective-permute-start = (f32[2,8,64]{2,1,0:T(8,128)S(1)}, f32[2,8,64]{2,1,0:T(8,128)S(1)}, u32[]{:S(2)}, u32[]{:S(2)}) collective-permute-start(f32[2,8,64]{2,1,0:T(8,128)S(1)} %shard_map.132.refs_0_), channel_id=1, source_target_pairs={{0,4},{4,0},{8,12},{12,8},{1,5},{5,1},{9,13},{13,9},{2,6},{6,2},{1... | collective-permute-start | bytes 12296 | tf_op jit(solution)/shard_map/ppermute | solution.py:735
  4.6 2.5 %collective-permute-start.2 = (f32[2,8,64]{2,1,0:T(8,128)S(1)}, f32[2,8,64]{2,1,0:T(8,128)S(1)}, u32[]{:S(2)}, u32[]{:S(2)}) collective-permute-start(f32[2,8,64]{2,1,0:T(8,128)S(1)} %shard_map.132.refs_0_), channel_id=1, source_target_pairs={{0,12},{4,8},{8,4},{12,0},{1,13},{5,9},{9,5},{13,1},{2,14},{6,10},... | collective-permute-start | bytes 12296 | tf_op jit(solution)/shard_map/ppermute | solution.py:735
  7.9 4.1 %shard_map.131 = (f32[3,3072]{1,0:T(4,128)S(1)}, bf16[2304,128]{1,0:T(8,128)(2,1)S(1)}, bf16[768,3072]{1,0:T(8,128)(2,1)S(1)}) custom-call(s32[1]{0:T(128)S(6)} %copy.14.timestep_ref, bf16[3,50,3072]{2,1,0:T(8,128)(2,1)S(1)} %bitcast.9, f32[3,1,3072]{2,1,0:T(1,128)S(1)} %bitcast.13, bf16[64,3072]{1,0:T(8,128)(2,1)S(1)} %copy-done.1, ...), custom_call_target="tpu_custom_call" | custom-call | tf_op jit(solution)/shard_map/pallas_call | solution.py:254
  12.1 2.5 %shard_map.134 = (bf16[64,768]{1,0:T(8,128)(2,1)S(1)}, bf16[64,768]{1,0:T(8,128)(2,1)S(1)}, bf16[64,768]{1,0:T(8,128)(2,1)S(1)}, bf16[64,768]{1,0:T(8,128)(2,1)S(1)}, bf16[64,768]{1,0:T(8,128)(2,1)S(1)}) custom-call(s32[2]{0:T(128)S(1)} %copy-done.7, bf16[64,3072]{1,0:T(8,128)(2,1)S(1)} %copy-done.1, bf16[2304,128]{1,0:T(8,128)(2,1)S(1)} %get-tuple-element.32.heads_ref, ...), custom_call_target="tpu_custom_call" | custom-call | tf_op jit(solution)/shard_map/pallas_call | solution.py:370
  14.5 1.9 %collective-permute-start.3 = (bf16[64,768]{1,0:T(8,128)(2,1)S(1)}, bf16[64,768]{1,0:T(8,128)(2,1)S(1)}, u32[]{:S(2)}, u32[]{:S(2)}) collective-permute-start(bf16[64,768]{1,0:T(8,128)(2,1)S(1)} %get-tuple-element.38), channel_id=1, source_target_pairs={{0,4},{4,0},{8,12},{12,8},{1,5},{5,1},{9,13},{13,9},{2,6},{6,2},{1... | collective-permute-start | bytes 294920 | tf_op jit(solution)/shard_map/ppermute | solution.py:735
  16.4 2.0 %collective-permute-start.4 = (bf16[64,768]{1,0:T(8,128)(2,1)S(1)}, bf16[64,768]{1,0:T(8,128)(2,1)S(1)}, u32[]{:S(2)}, u32[]{:S(2)}) collective-permute-start(bf16[64,768]{1,0:T(8,128)(2,1)S(1)} %get-tuple-element.39), channel_id=1, source_target_pairs={{0,8},{4,12},{8,0},{12,4},{1,9},{5,13},{9,1},{13,5},{2,10},{6,14},... | collective-permute-start | bytes 294920 | tf_op jit(solution)/shard_map/ppermute | solution.py:735
  19.0 3.8 %shard_map.135 = (bf16[3072,2304]{1,0:T(8,128)(2,1)S(1)}, f32[1,2304]{1,0:T(1,128)S(1)}) custom-call(bf16[64,768]{1,0:T(8,128)(2,1)S(1)} %get-tuple-element.34.after_ref.own_ref, bf16[2304,3072]{1,0:T(8,128)(2,1)S(1)} %bitcast.8, bf16[2304,128]{1,0:T(8,128)(2,1)S(1)} %get-tuple-element.32.heads_ref), custom_call_target="tpu_custom_call" | custom-call | flops 5000000000 | tf_op jit(solution)/shard_map/pallas_call | solution.py:395
  22.9 3.4 %collective-permute-done.4.refs_2_ = bf16[64,768]{1,0:T(8,128)(2,1)S(1)} collective-permute-done((bf16[64,768]{1,0:T(8,128)(2,1)S(1)}, bf16[64,768]{1,0:T(8,128)(2,1)S(1)}, u32[]{:S(2)}, u32[]{:S(2)}) %collective-permute-start.4) | collective-permute-done | bytes 98336 | tf_op jit(solution)/shard_map/ppermute | solution.py:735
  26.4 1.6 %collective-permute-start.8 = (bf16[64,768]{1,0:T(8,128)(2,1)S(1)}, bf16[64,768]{1,0:T(8,128)(2,1)S(1)}, u32[]{:S(2)}, u32[]{:S(2)}) collective-permute-start(bf16[64,768]{1,0:T(8,128)(2,1)S(1)} %shard_map.136), channel_id=1, source_target_pairs={{0,2},{2,0},{4,6},{6,4},{8,10},{10,8},{12,14},{14,12},{1,3},{3,1},... | collective-permute-start | bytes 294920 | tf_op jit(solution)/shard_map/ppermute | solution.py:763
  27.9 2.6 %collective-permute-start.7 = (bf16[64,768]{1,0:T(8,128)(2,1)S(1)}, bf16[64,768]{1,0:T(8,128)(2,1)S(1)}, u32[]{:S(2)}, u32[]{:S(2)}) collective-permute-start(bf16[64,768]{1,0:T(8,128)(2,1)S(1)} %shard_map.136), channel_id=1, source_target_pairs={{0,10},{2,8},{4,14},{6,12},{8,2},{10,0},{12,6},{14,4},{1,11},{3,9}... | collective-permute-start | bytes 294920 | tf_op jit(solution)/shard_map/ppermute | solution.py:763
  30.5 1.3 %collective-permute-start.6 = (bf16[64,768]{1,0:T(8,128)(2,1)S(1)}, bf16[64,768]{1,0:T(8,128)(2,1)S(1)}, u32[]{:S(2)}, u32[]{:S(2)}) collective-permute-start(bf16[64,768]{1,0:T(8,128)(2,1)S(1)} %shard_map.136), channel_id=1, source_target_pairs={{0,6},{2,4},{4,2},{6,0},{8,14},{10,12},{12,10},{14,8},{1,7},{3,5},... | collective-permute-start | bytes 294920 | tf_op jit(solution)/shard_map/ppermute | solution.py:763
  31.8 1.3 %collective-permute-start.9 = (bf16[64,768]{1,0:T(8,128)(2,1)S(1)}, bf16[64,768]{1,0:T(8,128)(2,1)S(1)}, u32[]{:S(2)}, u32[]{:S(2)}) collective-permute-start(bf16[64,768]{1,0:T(8,128)(2,1)S(1)} %shard_map.136), channel_id=1, source_target_pairs={{0,14},{2,12},{4,10},{6,8},{8,6},{10,4},{12,2},{14,0},{1,15},{3,13... | collective-permute-start | bytes 294920 | tf_op jit(solution)/shard_map/ppermute | solution.py:763
  33.9 3.1 %collective-permute-done.7.refs_1_.refs_2_ = bf16[64,768]{1,0:T(8,128)(2,1)S(1)} collective-permute-done((bf16[64,768]{1,0:T(8,128)(2,1)S(1)}, bf16[64,768]{1,0:T(8,128)(2,1)S(1)}, u32[]{:S(2)}, u32[]{:S(2)}) %collective-permute-start.7) | collective-permute-done | bytes 98336 | tf_op jit(solution)/shard_map/ppermute | solution.py:763
  37.0 1.4 %shard_map.138 = (f32[64,2304]{1,0:T(8,128)S(1)}, f32[64,1]{1,0:T(8,128)S(1)}) custom-call(f32[3,3072]{1,0:T(4,128)S(1)} %get-tuple-element.31.rows_ref, bf16[3072,2304]{1,0:T(8,128)(2,1)S(1)} %get-tuple-element.35.turned_ref.qkv_ref, bf16[64,768]{1,0:T(8,128)(2,1)S(1)} %collective-permute-done.6.refs_0_.refs_1_, ...), custom_call_target="tpu_custom_call" | custom-call | tf_op jit(solution)/shard_map/pallas_call | solution.py:476
  39.3 2.7 %shard_map.139 = (bf16[16,3072]{1,0:T(8,128)(2,1)S(1)}, bf16[16,3072]{1,0:T(8,128)(2,1)S(1)}, bf16[16,3072]{1,0:T(8,128)(2,1)S(1)}, bf16[16,3072]{1,0:T(8,128)(2,1)S(1)}, bf16[16,3072]{1,0:T(8,128)(2,1)S(1)}) custom-call(s32[2]{0:T(128)S(1)} %copy-done.7, f32[3,3072]{1,0:T(4,128)S(1)} %get-tuple-element.31.rows_ref, ...), custom_call_target="tpu_custom_call" | custom-call | tf_op jit(solution)/shard_map/pallas_call | solution.py:528
  42.0 3.1 %collective-permute-start.10 = (bf16[16,3072]{1,0:T(8,128)(2,1)S(1)}, bf16[16,3072]{1,0:T(8,128)(2,1)S(1)}, u32[]{:S(2)}, u32[]{:S(2)}) collective-permute-start(bf16[16,3072]{1,0:T(8,128)(2,1)S(1)} %get-tuple-element.50), channel_id=1, source_target_pairs={{0,12},{4,8},{8,4},{12,0},{1,13},{5,9},{9,5},{13,1},{2,14},{6,10},... | collective-permute-start | bytes 294920 | tf_op jit(solution)/shard_map/ppermute | solution.py:735
  45.0 1.4 %collective-permute-start.12 = (bf16[16,3072]{1,0:T(8,128)(2,1)S(1)}, bf16[16,3072]{1,0:T(8,128)(2,1)S(1)}, u32[]{:S(2)}, u32[]{:S(2)}) collective-permute-start(bf16[16,3072]{1,0:T(8,128)(2,1)S(1)} %get-tuple-element.53), channel_id=1, source_target_pairs={{0,8},{4,12},{8,0},{12,4},{1,9},{5,13},{9,1},{13,5},{2,10},{6,14},... | collective-permute-start | bytes 294920 | tf_op jit(solution)/shard_map/ppermute | solution.py:735
  46.4 2.1 %collective-permute-done.10.refs_0_.refs_3_ = bf16[16,3072]{1,0:T(8,128)(2,1)S(1)} collective-permute-done((bf16[16,3072]{1,0:T(8,128)(2,1)S(1)}, bf16[16,3072]{1,0:T(8,128)(2,1)S(1)}, u32[]{:S(2)}, u32[]{:S(2)}) %collective-permute-start.10) | collective-permute-done | bytes 98336 | tf_op jit(solution)/shard_map/ppermute | solution.py:735
  48.5 2.8 %collective-permute-done.11.refs_1_ = bf16[16,3072]{1,0:T(8,128)(2,1)S(1)} collective-permute-done((bf16[16,3072]{1,0:T(8,128)(2,1)S(1)}, bf16[16,3072]{1,0:T(8,128)(2,1)S(1)}, u32[]{:S(2)}, u32[]{:S(2)}) %collective-permute-start.11) | collective-permute-done | bytes 98336 | tf_op jit(solution)/shard_map/ppermute | solution.py:735
  51.3 0.9 %shard_map.141 = f32[16,8,128]{2,1,0:T(8,128)} custom-call(f32[3,3072]{1,0:T(4,128)S(1)} %get-tuple-element.31.rows_ref, bf16[16,3072]{1,0:T(8,128)(2,1)S(1)} %get-tuple-element.45.own_ref, bf16[64,3072]{1,0:T(8,128)(2,1)S(1)} %bitcast.12, f32[8,128]{1,0:T(8,128)S(1)} %shard_map.140.far_ref, bf16[16,3072]{1,0:T(8,128)(2,1)S(1)} %get-tuple-element.51.refs_0_, ...), custom_call_target="tpu_custom_call" | custom-call | tf_op jit(solution)/shard_map/pallas_call | solution.py:562
  52.2 3.5 %all-to-all-start = ((f32[16,8,128]{2,1,0:T(8,128)}), f32[16,8,128]{2,1,0:T(8,128)S(1)}, u32[]{:S(2)}, u32[]{:S(2)}) async-start(f32[16,8,128]{2,1,0:T(8,128)} %shard_map.141), calls=%async_computation | async-start | bytes 131072 | tf_op jit(solution)/shard_map/all_to_all | solution.py:793
  55.8 2.1 %shard_map.142 = (bf16[64,3584]{1,0:T(8,128)(2,1)S(1)}, bf16[896,256]{1,0:T(8,128)(2,1)S(1)}) custom-call(s32[4]{0:T(128)S(1)} %copy-done.8, bf16[27,16,128]{2,1,0:T(8,128)(2,1)S(1)} %copy-done.5), custom_call_target="tpu_custom_call" | custom-call | tf_op jit(solution)/shard_map/pallas_call | solution.py:624
  57.8 4.8 %all-to-all-done.terms_ref = f32[16,8,128]{2,1,0:T(8,128)S(1)} async-done(((f32[16,8,128]{2,1,0:T(8,128)}), f32[16,8,128]{2,1,0:T(8,128)S(1)}, u32[]{:S(2)}, u32[]{:S(2)}) %all-to-all-start) | async-done | bytes 65568 | tf_op jit(solution)/shard_map/all_to_all | solution.py:793
  62.6 1.2 %shard_map.143 = (f32[2,8,64]{2,1,0:T(8,128)}, bf16[128,128]{1,0:T(8,128)(2,1)}) custom-call(f32[16,8,128]{2,1,0:T(8,128)S(1)} %all-to-all-done.terms_ref, bf16[64,3584]{1,0:T(8,128)(2,1)S(1)} %get-tuple-element.56.chosen_ref, bf16[896,256]{1,0:T(8,128)(2,1)S(1)} %get-tuple-element.57.weights_ref, f32[2,8,64]{2,1,0:T(8,128)S(1)} %shard_map.132.refs_0_, ...), custom_call_target="tpu_custom_call" | custom-call | tf_op jit(solution)/shard_map/pallas_call | solution.py:695
  (35 shorter events, 3.3 us)
Async XLA Ops:
  0.6 7.3 %copy-start.1 = (bf16[64,3072]{1,0:T(8,128)(2,1)S(1)}, bf16[64,3072]{1,0:T(8,128)(2,1)}, u32[]{:S(2)}) copy-start(bf16[64,3072]{1,0:T(8,128)(2,1)} %embed_ref.3) | copy-start | bytes 1179652
  0.6 7.3 %copy-start.6 = (f32[1,1,3,3072]{3,1,2,0:T(1,128)S(1)}, f32[1,1,3,3072]{3,1,2,0:T(1,128)}, u32[]{:S(2)}) copy-start(f32[1,1,3,3072]{3,1,2,0:T(1,128)} %param.17) | copy-start | bytes 110596
  0.7 7.3 %copy-start.2 = (bf16[50,3,3072]{2,0,1:T(8,128)(2,1)S(1)}, bf16[50,3,3072]{2,0,1:T(8,128)(2,1)}, u32[]{:S(2)}) copy-start(bf16[50,3,3072]{2,0,1:T(8,128)(2,1)} %param.16) | copy-start | bytes 2764804
  0.7 7.3 %copy-start = (bf16[1,2304,3072]{2,1,0:T(8,128)(2,1)S(1)}, bf16[1,2304,3072]{2,1,0:T(8,128)(2,1)}, u32[]{:S(2)}) copy-start(bf16[1,2304,3072]{2,1,0:T(8,128)(2,1)} %param.14) | copy-start | bytes 42467332
  1.5 10.5 %copy-start.3 = (bf16[1,1,1,2,32,1536]{5,4,3,2,1,0:T(8,128)(2,1)S(1)}, bf16[1,1,1,2,32,1536]{5,4,3,2,1,0:T(8,128)(2,1)}, u32[]{:S(2)}) copy-start(bf16[1,1,1,2,32,1536]{5,4,3,2,1,0:T(8,128)(2,1)} %param.18) | copy-start | bytes 589828
  1.5 10.5 %copy-start.7 = (s32[2]{0:T(128)S(1)}, s32[2]{0:T(128)}, u32[]{:S(2)}) copy-start(s32[2]{0:T(128)} %order_ref.3) | copy-start | bytes 28
  1.6 10.4 %collective-permute-start = (f32[2,8,64]{2,1,0:T(8,128)S(1)}, f32[2,8,64]{2,1,0:T(8,128)S(1)}, u32[]{:S(2)}, u32[]{:S(2)}) collective-permute-start(f32[2,8,64]{2,1,0:T(8,128)S(1)} %shard_map.132.refs_0_), channel_id=1, source_target_pairs={{0,4},{4,0},{8,12},{12,8},{1,5},{5,1},{9,13},{13,9},{2,6},{6,2},{1... | collective-permute-start | bytes 12296 | tf_op jit(solution)/shard_map/ppermute | solution.py:735
  4.6 7.4 %collective-permute-start.2 = (f32[2,8,64]{2,1,0:T(8,128)S(1)}, f32[2,8,64]{2,1,0:T(8,128)S(1)}, u32[]{:S(2)}, u32[]{:S(2)}) collective-permute-start(f32[2,8,64]{2,1,0:T(8,128)S(1)} %shard_map.132.refs_0_), channel_id=1, source_target_pairs={{0,12},{4,8},{8,4},{12,0},{1,13},{5,9},{9,5},{13,1},{2,14},{6,10},... | collective-permute-start | bytes 12296 | tf_op jit(solution)/shard_map/ppermute | solution.py:735
  7.1 4.9 %collective-permute-start.1 = (f32[2,8,64]{2,1,0:T(8,128)S(1)}, f32[2,8,64]{2,1,0:T(8,128)S(1)}, u32[]{:S(2)}, u32[]{:S(2)}) collective-permute-start(f32[2,8,64]{2,1,0:T(8,128)S(1)} %shard_map.132.refs_0_), channel_id=1, source_target_pairs={{0,8},{4,12},{8,0},{12,4},{1,9},{5,13},{9,1},{13,5},{2,10},{6,14},... | collective-permute-start | bytes 12296 | tf_op jit(solution)/shard_map/ppermute | solution.py:735
  14.5 8.3 %collective-permute-start.3 = (bf16[64,768]{1,0:T(8,128)(2,1)S(1)}, bf16[64,768]{1,0:T(8,128)(2,1)S(1)}, u32[]{:S(2)}, u32[]{:S(2)}) collective-permute-start(bf16[64,768]{1,0:T(8,128)(2,1)S(1)} %get-tuple-element.38), channel_id=1, source_target_pairs={{0,4},{4,0},{8,12},{12,8},{1,5},{5,1},{9,13},{13,9},{2,6},{6,2},{1... | collective-permute-start | bytes 294920 | tf_op jit(solution)/shard_map/ppermute | solution.py:735
  16.4 9.9 %collective-permute-start.4 = (bf16[64,768]{1,0:T(8,128)(2,1)S(1)}, bf16[64,768]{1,0:T(8,128)(2,1)S(1)}, u32[]{:S(2)}, u32[]{:S(2)}) collective-permute-start(bf16[64,768]{1,0:T(8,128)(2,1)S(1)} %get-tuple-element.39), channel_id=1, source_target_pairs={{0,8},{4,12},{8,0},{12,4},{1,9},{5,13},{9,1},{13,5},{2,10},{6,14},... | collective-permute-start | bytes 294920 | tf_op jit(solution)/shard_map/ppermute | solution.py:735
  18.4 7.8 %collective-permute-start.5 = (bf16[64,768]{1,0:T(8,128)(2,1)S(1)}, bf16[64,768]{1,0:T(8,128)(2,1)S(1)}, u32[]{:S(2)}, u32[]{:S(2)}) collective-permute-start(bf16[64,768]{1,0:T(8,128)(2,1)S(1)} %get-tuple-element.40), channel_id=1, source_target_pairs={{0,12},{4,8},{8,4},{12,0},{1,13},{5,9},{9,5},{13,1},{2,14},{6,10},... | collective-permute-start | bytes 294920 | tf_op jit(solution)/shard_map/ppermute | solution.py:735
  26.4 6.8 %collective-permute-start.8 = (bf16[64,768]{1,0:T(8,128)(2,1)S(1)}, bf16[64,768]{1,0:T(8,128)(2,1)S(1)}, u32[]{:S(2)}, u32[]{:S(2)}) collective-permute-start(bf16[64,768]{1,0:T(8,128)(2,1)S(1)} %shard_map.136), channel_id=1, source_target_pairs={{0,2},{2,0},{4,6},{6,4},{8,10},{10,8},{12,14},{14,12},{1,3},{3,1},... | collective-permute-start | bytes 294920 | tf_op jit(solution)/shard_map/ppermute | solution.py:763
  27.9 9.1 %collective-permute-start.7 = (bf16[64,768]{1,0:T(8,128)(2,1)S(1)}, bf16[64,768]{1,0:T(8,128)(2,1)S(1)}, u32[]{:S(2)}, u32[]{:S(2)}) collective-permute-start(bf16[64,768]{1,0:T(8,128)(2,1)S(1)} %shard_map.136), channel_id=1, source_target_pairs={{0,10},{2,8},{4,14},{6,12},{8,2},{10,0},{12,6},{14,4},{1,11},{3,9}... | collective-permute-start | bytes 294920 | tf_op jit(solution)/shard_map/ppermute | solution.py:763
  30.5 6.5 %collective-permute-start.6 = (bf16[64,768]{1,0:T(8,128)(2,1)S(1)}, bf16[64,768]{1,0:T(8,128)(2,1)S(1)}, u32[]{:S(2)}, u32[]{:S(2)}) collective-permute-start(bf16[64,768]{1,0:T(8,128)(2,1)S(1)} %shard_map.136), channel_id=1, source_target_pairs={{0,6},{2,4},{4,2},{6,0},{8,14},{10,12},{12,10},{14,8},{1,7},{3,5},... | collective-permute-start | bytes 294920 | tf_op jit(solution)/shard_map/ppermute | solution.py:763
  31.8 7.4 %collective-permute-start.9 = (bf16[64,768]{1,0:T(8,128)(2,1)S(1)}, bf16[64,768]{1,0:T(8,128)(2,1)S(1)}, u32[]{:S(2)}, u32[]{:S(2)}) collective-permute-start(bf16[64,768]{1,0:T(8,128)(2,1)S(1)} %shard_map.136), channel_id=1, source_target_pairs={{0,14},{2,12},{4,10},{6,8},{8,6},{10,4},{12,2},{14,0},{1,15},{3,13... | collective-permute-start | bytes 294920 | tf_op jit(solution)/shard_map/ppermute | solution.py:763
  37.0 14.3 %copy-start.4 = (bf16[3072,64]{0,1:T(8,128)(2,1)S(1)}, bf16[3072,64]{0,1:T(8,128)(2,1)}, u32[]{:S(2)}) copy-start(bf16[3072,64]{0,1:T(8,128)(2,1)} %param.19) | copy-start | bytes 1179652
  38.4 17.4 %copy-start.5 = (bf16[27,16,128]{2,1,0:T(8,128)(2,1)S(1)}, bf16[27,16,128]{2,1,0:T(8,128)(2,1)}, u32[]{:S(2)}) copy-start(bf16[27,16,128]{2,1,0:T(8,128)(2,1)} %conv_ref) | copy-start | bytes 331780
  38.4 17.4 %copy-start.8 = (s32[4]{0:T(128)S(1)}, s32[4]{0:T(128)}, u32[]{:S(2)}) copy-start(s32[4]{0:T(128)} %slab_ref) | copy-start | bytes 52
  42.0 6.6 %collective-permute-start.10 = (bf16[16,3072]{1,0:T(8,128)(2,1)S(1)}, bf16[16,3072]{1,0:T(8,128)(2,1)S(1)}, u32[]{:S(2)}, u32[]{:S(2)}) collective-permute-start(bf16[16,3072]{1,0:T(8,128)(2,1)S(1)} %get-tuple-element.50), channel_id=1, source_target_pairs={{0,12},{4,8},{8,4},{12,0},{1,13},{5,9},{9,5},{13,1},{2,14},{6,10},... | collective-permute-start | bytes 294920 | tf_op jit(solution)/shard_map/ppermute | solution.py:735
  45.0 6.3 %collective-permute-start.11 = (bf16[16,3072]{1,0:T(8,128)(2,1)S(1)}, bf16[16,3072]{1,0:T(8,128)(2,1)S(1)}, u32[]{:S(2)}, u32[]{:S(2)}) collective-permute-start(bf16[16,3072]{1,0:T(8,128)(2,1)S(1)} %get-tuple-element.52), channel_id=1, source_target_pairs={{0,4},{4,0},{8,12},{12,8},{1,5},{5,1},{9,13},{13,9},{2,6},{6,2},{1... | collective-permute-start | bytes 294920 | tf_op jit(solution)/shard_map/ppermute | solution.py:735
  45.0 6.3 %collective-permute-start.12 = (bf16[16,3072]{1,0:T(8,128)(2,1)S(1)}, bf16[16,3072]{1,0:T(8,128)(2,1)S(1)}, u32[]{:S(2)}, u32[]{:S(2)}) collective-permute-start(bf16[16,3072]{1,0:T(8,128)(2,1)S(1)} %get-tuple-element.53), channel_id=1, source_target_pairs={{0,8},{4,12},{8,0},{12,4},{1,9},{5,13},{9,1},{13,5},{2,10},{6,14},... | collective-permute-start | bytes 294920 | tf_op jit(solution)/shard_map/ppermute | solution.py:735
  52.2 10.4 %all-to-all-start = ((f32[16,8,128]{2,1,0:T(8,128)}), f32[16,8,128]{2,1,0:T(8,128)S(1)}, u32[]{:S(2)}, u32[]{:S(2)}) async-start(f32[16,8,128]{2,1,0:T(8,128)} %shard_map.141), calls=%async_computation | async-start | bytes 131072 | tf_op jit(solution)/shard_map/all_to_all | solution.py:793
